TPU v7x, 32 devices: a whole 2x2x4 slice. The times are simulated.
32 devices in a mesh: head: 4 (over y, core), inner: 4 (over z), outer: 2 (over x).
Axes of the slice: x: 2, y: 2, z: 4, core: 2. Of those that a mesh axis runs over, the one named last changes fastest.
Arguments:
- queries: bfloat16 [4096, 8192], P(('inner', 'outer', 'head')), may hold values from -12.816310409006173 to 12.816310409006173
- keys: bfloat16 [4096, 1024], P(('inner', 'outer', 'head')), may hold values from -4 to 4
- values: bfloat16 [4096, 1024], P(('inner', 'outer', 'head')), may hold values from -6 to 6
- dout: bfloat16 [4096, 8192], P(('inner', 'outer', 'head')), may hold values from -6 to 6
- doc_lengths: int32 [32], replicated, may hold values from 1 to 256, 4096 in all
- span_order: int32 [16], replicated, may hold values from 0 to 15, as said below
Outputs:
- attended: bfloat16 [4096, 8192], P(('inner', 'outer', 'head'))
- entropy: float32 [4096, 64], P(('inner', 'outer'), 'head')
- grad_query: bfloat16 [4096, 8192], P(('inner', 'outer', 'head'))
- grad_key: bfloat16 [4096, 1024], P(('inner', 'outer', 'head'))
- grad_value: bfloat16 [4096, 1024], P(('inner', 'outer', 'head'))
Inputs may be any that keep to these rules, and one draw needn't show every extreme that they name: `doc_lengths`: the 32 documents lie one after another over the 4096 positions of the sequence; the lengths sum to 4096 and the longest is exactly 256. Stored rows b * 256 to (b + 1) * 256 - 1 hold the sequence positions span_order[b] * 256 onward, in order; stored blocks 2 i and 2 i + 1 hold the spans i and 15 - i, in either order.
All inputs are finite; a program needn't handle non-finite values.
Results may differ from a plain program's by a relative error of at most 0.03.
Values may be sent and summed in bfloat16 or wider, within the bound.
No kernel may reach another device: no remote copies, remote signals or barrier semaphores. Data moves between devices by JAX's collectives and lax.ppermute only.
A program may use at most 128 MiB of HBM per device.

v0:
```python
import functools
import math

import jax
import jax.numpy as jnp
from jax import lax
from jax.experimental import pallas as pl
from jax.experimental.pallas import tpu as pltpu
from jax.sharding import PartitionSpec as P

QUERY_HEADS = 64
KEY_VALUE_HEADS = 8
HEAD_WIDTH = 128
GROUP = QUERY_HEADS // KEY_VALUE_HEADS
SCALE = 1.0 / math.sqrt(HEAD_WIDTH)
MASKED = -1e30
CONTEXT = ("inner", "outer")
CHUNKS = 1
NT = (((1,), (1,)), ((), ()))
NN = (((1,), (0,)), ((), ()))


def attention_kernel(units, doc_ref, first_ref, q_ref, do_ref, *refs):
    unit_refs = refs[:units]
    att_ref, dq_ref, ent_ref, own_ref = refs[units : units + 4]
    term_refs = refs[units + 4 : 2 * units + 3]
    bias_ref, pb_ref, ds_ref, qs_ref, dos_ref = refs[2 * units + 3 :]
    rows = q_ref.shape[0]
    window = units * rows
    g = pl.program_id(0)
    count = own_ref.shape[1] // (2 * HEAD_WIDTH)

    @pl.when(g == 0)
    def _():
        first = first_ref[0]
        q_pos = first + lax.broadcasted_iota(jnp.int32, (1, rows), 1)

        def step(index, carry):
            at, start = carry
            return at + doc_ref[index], jnp.where(at <= q_pos, at, start)

        _, start = lax.fori_loop(
            0, doc_ref.shape[0], step, (jnp.int32(0), jnp.zeros((1, rows), jnp.int32))
        )
        k_pos = first - (units - 1) * rows + lax.broadcasted_iota(jnp.int32, (window, rows), 0)
        bias_ref[...] = jnp.where((k_pos >= start) & (k_pos <= q_pos), 0.0, MASKED)

    half = count // 2
    base = (g // half) * count + g % half
    k_cols = pl.ds(pl.multiple_of(base * HEAD_WIDTH, HEAD_WIDTH), HEAD_WIDTH)
    v_cols = pl.ds(pl.multiple_of((base + half) * HEAD_WIDTH, HEAD_WIDTH), HEAD_WIDTH)
    k_rows = jnp.concatenate([unit[:, k_cols] for unit in unit_refs], axis=0)
    v_rows = jnp.concatenate([unit[:, v_cols] for unit in unit_refs], axis=0)
    heads = [slice(h * HEAD_WIDTH, (h + 1) * HEAD_WIDTH) for h in range(GROUP)]
    spots = [slice(h * rows, (h + 1) * rows) for h in range(GROUP)]
    for head, spot in zip(heads, spots):
        qs_ref[spot, :] = q_ref[:, head]
        dos_ref[spot, :] = do_ref[:, head]
    q_all = qs_ref[...]
    do_all = dos_ref[...]
    bias = jnp.concatenate([bias_ref[...]] * GROUP, axis=1)
    s = lax.dot_general(k_rows, q_all, NT, preferred_element_type=jnp.float32) + bias
    top = jnp.max(s, axis=0, keepdims=True)
    t = (s - top) * (SCALE * math.log2(math.e))
    e = jnp.exp2(t)
    total = jnp.sum(e, axis=0, keepdims=True)
    inv = 1.0 / total
    entropy = jnp.log(total) - jnp.sum(e * t, axis=0, keepdims=True) * inv * math.log(2.0)
    for h, spot in enumerate(spots):
        ent_ref[h : h + 1, :] = entropy[:, spot]
    p = e * inv
    pb = p.astype(jnp.bfloat16)
    pb_ref[...] = pb
    out = lax.dot_general(v_rows.T, pb, NN, preferred_element_type=jnp.float32)
    out = out.astype(jnp.bfloat16).T
    dp = lax.dot_general(v_rows, do_all, NT, preferred_element_type=jnp.float32)
    delta = jnp.sum(p * dp, axis=0, keepdims=True)
    ds = (p * (dp - delta)).astype(jnp.bfloat16)
    ds_ref[...] = ds
    dq = lax.dot_general(k_rows.T, ds, NN, preferred_element_type=jnp.float32)
    dq = (dq * SCALE).astype(jnp.bfloat16).T
    for head, spot in zip(heads, spots):
        att_ref[:, head] = out[spot, :]
        dq_ref[:, head] = dq[spot, :]
    dv = lax.dot_general(pb_ref[...], do_all, NN, preferred_element_type=jnp.float32)
    dk = lax.dot_general(ds_ref[...], q_all, NN, preferred_element_type=jnp.float32) * SCALE
    own_ref[:, k_cols] = dk[window - rows :]
    own_ref[:, v_cols] = dv[window - rows :]
    for index, term in enumerate(term_refs):
        part = slice(index * rows, (index + 1) * rows)
        term[:, k_cols] = dk[part].astype(jnp.bfloat16)
        term[:, v_cols] = dv[part].astype(jnp.bfloat16)


def attention(doc_lengths, first, queries, dout, unit_rows, chunk, earlier):
    rows = queries.shape[0]
    units = len(unit_rows)
    window = units * rows
    width = unit_rows[0].shape[1]
    count = width // (2 * HEAD_WIDTH)
    whole = pl.BlockSpec((rows, width), lambda g, *_: (0, 0))
    block = pl.BlockSpec((rows, GROUP * HEAD_WIDTH), lambda g, *_: (0, chunk * count + g))
    aliases = {4 + units: 0, 5 + units: 1} if earlier else {}

    def kernel(doc_ref, first_ref, q_ref, do_ref, *refs):
        kept = refs[:units] + refs[units + len(earlier) :]
        attention_kernel(units, doc_ref, first_ref, q_ref, do_ref, *kept)

    wide = jax.ShapeDtypeStruct(queries.shape, jnp.bfloat16)
    return pl.pallas_call(
        kernel,
        grid_spec=pltpu.PrefetchScalarGridSpec(
            num_scalar_prefetch=2,
            grid=(count,),
            in_specs=[block, block]
            + [whole] * units
            + [pl.BlockSpec(memory_space=pl.ANY)] * len(earlier),
            out_specs=[block, block, pl.BlockSpec((GROUP, rows), lambda g, *_: (g, 0))]
            + [whole] * units,
            scratch_shapes=[
                pltpu.VMEM((window, rows), jnp.float32),
                pltpu.VMEM((window, GROUP * rows), jnp.bfloat16),
                pltpu.VMEM((window, GROUP * rows), jnp.bfloat16),
                pltpu.VMEM((GROUP * rows, HEAD_WIDTH), jnp.bfloat16),
                pltpu.VMEM((GROUP * rows, HEAD_WIDTH), jnp.bfloat16),
            ],
        ),
        out_shape=[
            wide,
            wide,
            jax.ShapeDtypeStruct((count * GROUP, rows), jnp.float32),
            jax.ShapeDtypeStruct((rows, width), jnp.float32),
        ]
        + [jax.ShapeDtypeStruct((rows, width), jnp.bfloat16)] * (units - 1),
        input_output_aliases=aliases,
        compiler_params=pltpu.CompilerParams(vmem_limit_bytes=40 * 2**20),
        cost_estimate=pl.CostEstimate(
            flops=12 * count * window * GROUP * rows * HEAD_WIDTH,
            bytes_accessed=16 * count * GROUP * rows * HEAD_WIDTH,
            transcendentals=count * window * GROUP * rows,
        ),
    )(doc_lengths, first, queries, dout, *unit_rows, *earlier)


def along_context(value, steps):
    size = lax.axis_size(CONTEXT)
    low, high = max(0, -steps), min(size, size - steps)
    return lax.ppermute(value, CONTEXT, [(s, s + steps) for s in range(low, high)])


def body(queries, keys, values, dout, doc_lengths, span_order):
    rows = queries.shape[0]
    size = lax.axis_size("head")
    subs = size // 2
    here = lax.axis_index("head")
    side, sub = here // subs, here % subs
    context = lax.axis_index(CONTEXT)
    is_top = context == lax.axis_size(CONTEXT) - 1
    span = lax.dynamic_index_in_dim(span_order, 2 * context + side, keepdims=False)
    is_low = span == context
    first = ((span * subs + sub) * rows).reshape(1)
    across = [(j, (j + subs) % size) for j in range(size)]

    def around(value, steps):
        pairs = [(j, j // subs * subs + (j + steps) % subs) for j in range(size)]
        return lax.ppermute(value, "head", pairs)

    half_width = keys.shape[1] // (2 * CHUNKS)

    def packed(chunk):
        parts = []
        for half in range(2):
            cols = slice((2 * chunk + half) * half_width, (2 * chunk + half + 1) * half_width)
            parts += [keys[:, cols], values[:, cols]]
        return jnp.concatenate(parts, axis=1)

    def halves(value):
        left, right = jnp.split(value, 2, axis=1)
        return jnp.where(side == 0, left, right), jnp.where(side == 0, right, left)

    def joined(mine, other):
        return jnp.concatenate(
            [jnp.where(side == 0, mine, other), jnp.where(side == 0, other, mine)], axis=1
        )

    def swap_if(condition, one, two):
        return jnp.where(condition, one, two), jnp.where(condition, two, one)

    def earlier_span(own):
        keep, give = halves(own)
        got = lax.ppermute(give, "head", across)
        low, high = swap_if(is_low, keep, got)
        from_below = along_context(low, 1)
        from_above = jnp.where(is_top, low, along_context(high, -1))
        mine, theirs = swap_if(is_low, from_below, from_above)
        return joined(mine, lax.ppermute(theirs, "head", across))

    def key_window(own):
        before = earlier_span(own)
        near = [
            around(jnp.where(sub + steps < subs, own, before), steps)
            for steps in range(subs - 1, 0, -1)
        ]
        return [before] + near + [own]

    def returned(own, terms):
        before = terms[0].astype(jnp.float32)
        for index, steps in enumerate(range(subs - 1, 0, -1)):
            got = around(terms[index + 1], -steps).astype(jnp.float32)
            within = sub + steps < subs
            own = own + jnp.where(within, got, 0.0)
            before = before + jnp.where(within, 0.0, got)
        keep, give = halves(before.astype(jnp.bfloat16))
        got = lax.ppermute(give, "head", across)
        low, high = swap_if(is_low, keep, got)
        from_upper = jnp.where(is_top, high, along_context(low, -1))
        from_lower = along_context(high, 1)
        mine, theirs = swap_if(is_low, from_upper, from_lower)
        other = lax.ppermute(theirs, "head", across)
        return (own + joined(mine, other).astype(jnp.float32)).astype(jnp.bfloat16)

    windows = [key_window(packed(chunk)) for chunk in range(CHUNKS)]
    earlier = []
    entropies, grads = [], []
    for chunk, window in enumerate(windows):
        results = attention(doc_lengths, first, queries, dout, window, chunk, earlier)
        earlier = results[:2]
        entropies.append(results[2])
        grads.append(returned(results[3], results[4:]))
    attended, grad_query = earlier
    entropy = lax.all_to_all(
        jnp.concatenate(entropies, axis=0).T, "head", split_axis=1, concat_axis=0, tiled=True
    )
    grad_key, grad_value = [], []
    for grad in grads:
        parts = jnp.split(grad, 4, axis=1)
        grad_key += [parts[0], parts[2]]
        grad_value += [parts[1], parts[3]]
    return (
        attended,
        entropy,
        grad_query,
        jnp.concatenate(grad_key, axis=1),
        jnp.concatenate(grad_value, axis=1),
    )


def solution(mesh):
    rows = P(("inner", "outer", "head"), None)
    return jax.shard_map(
        body,
        mesh=mesh,
        in_specs=(rows, rows, rows, rows, P(), P()),
        out_specs=(rows, P(("inner", "outer"), "head"), rows, rows, rows),
        check_vma=False,
    )
```

profile of v0, /device:TPU:0, one launch (start us, length us, event | category | flops | bytes accessed | tf_op | source)
XLA Modules:
  0.0 98.0 jit_solution(10437744791998978463)
XLA Ops:
  0.6 1.1 %fusion.6 = (bf16[128,512]{1,0:T(8,128)(2,1)S(1)}, bf16[128,512]{1,0:T(8,128)(2,1)S(1)}, bf16[128,512]{1,0:T(8,128)(2,1)S(1)}, bf16[128,512]{1,0:T(8,128)(2,1)S(1)}) fusion(bf16[128,1024]{1,0:T(8,128)(2,1)} %param.7, bf16[128,1024]{1,0:T(8,128)(2,1)} %param.8), kind=kLoop, calls=%fused_computation.34 | loop fusion | bytes 1048576 | tf_op jit(solution)/shard_map/slice | solution.py:174
  1.8 0.0 copy-start.3
  1.8 0.1 broadcast_select_fusion.17
  1.9 3.0 %collective-permute-start = (bf16[128,1024]{1,0:T(8,128)(2,1)S(1)}, bf16[128,1024]{1,0:T(8,128)(2,1)S(1)}, u32[]{:S(2)}, u32[]{:S(2)}) collective-permute-start(bf16[128,1024]{1,0:T(8,128)(2,1)S(1)} %broadcast_select_fusion.17), channel_id=1, source_target_pairs={{0,16},{8,24},{16,0},{24,8},{1,17},{9,25},{17,1},{25,9},{2,18},{10... | collective-permute-start | bytes 786440 | tf_op jit(solution)/shard_map/ppermute | solution.py:191
  4.9 1.2 %dynamic_slice.4 = s32[1]{0:T(128)} dynamic-slice(s32[16]{0:T(128)} %param.11, s32[]{:T(128)S(6)} %select_n.116), dynamic_slice_sizes={1} | dynamic-slice | bytes 12 | tf_op jit(solution)/shard_map/jit(dynamic_index_in_dim)/dynamic_slice | solution.py:159
  6.8 4.4 %collective-permute-done = bf16[128,1024]{1,0:T(8,128)(2,1)S(1)} collective-permute-done((bf16[128,1024]{1,0:T(8,128)(2,1)S(1)}, bf16[128,1024]{1,0:T(8,128)(2,1)S(1)}, u32[]{:S(2)}, u32[]{:S(2)}) %collective-permute-start) | collective-permute-done | bytes 262176 | tf_op jit(solution)/shard_map/ppermute | solution.py:191
  11.2 0.1 broadcast_select_fusion.9
  11.3 1.3 %collective-permute-start.2 = (bf16[128,1024]{1,0:T(8,128)(2,1)S(1)}, bf16[128,1024]{1,0:T(8,128)(2,1)S(1)}, u32[]{:S(2)}, u32[]{:S(2)}) collective-permute-start(bf16[128,1024]{1,0:T(8,128)(2,1)S(1)} %get-tuple-element.27), channel_id=1, source_target_pairs={{1,0},{2,1},{3,2},{4,3},{5,4},{6,5},{7,6},{9,8},{10,9},{11,10},{12... | collective-permute-start | bytes 786440 | tf_op jit(solution)/shard_map/ppermute | solution.py:148
  12.6 4.6 %collective-permute-start.1 = (bf16[128,1024]{1,0:T(8,128)(2,1)S(1)}, bf16[128,1024]{1,0:T(8,128)(2,1)S(1)}, u32[]{:S(2)}, u32[]{:S(2)}) collective-permute-start(bf16[128,1024]{1,0:T(8,128)(2,1)S(1)} %get-tuple-element.28), channel_id=1, source_target_pairs={{0,1},{1,2},{2,3},{3,4},{4,5},{5,6},{6,7},{8,9},{9,10},{10,11},{11... | collective-permute-start | bytes 786440 | tf_op jit(solution)/shard_map/ppermute | solution.py:148
  17.2 3.5 %collective-permute-done.2 = bf16[128,1024]{1,0:T(8,128)(2,1)S(1)} collective-permute-done((bf16[128,1024]{1,0:T(8,128)(2,1)S(1)}, bf16[128,1024]{1,0:T(8,128)(2,1)S(1)}, u32[]{:S(2)}, u32[]{:S(2)}) %collective-permute-start.2) | collective-permute-done | bytes 262176 | tf_op jit(solution)/shard_map/ppermute | solution.py:148
  20.7 5.4 %collective-permute-done.1 = bf16[128,1024]{1,0:T(8,128)(2,1)S(1)} collective-permute-done((bf16[128,1024]{1,0:T(8,128)(2,1)S(1)}, bf16[128,1024]{1,0:T(8,128)(2,1)S(1)}, u32[]{:S(2)}, u32[]{:S(2)}) %collective-permute-start.1) | collective-permute-done | bytes 262176 | tf_op jit(solution)/shard_map/ppermute | solution.py:148
  26.1 0.0 copy-done.3
  26.1 0.1 broadcast_select_fusion.7
  26.2 0.0 copy-start
  26.2 0.0 copy-start.2
  26.2 1.6 %collective-permute-start.3 = (bf16[128,1024]{1,0:T(8,128)(2,1)S(1)}, bf16[128,1024]{1,0:T(8,128)(2,1)S(1)}, u32[]{:S(2)}, u32[]{:S(2)}) collective-permute-start(bf16[128,1024]{1,0:T(8,128)(2,1)S(1)} %get-tuple-element.19), channel_id=1, source_target_pairs={{0,16},{8,24},{16,0},{24,8},{1,17},{9,25},{17,1},{25,9},{2,18},{10... | collective-permute-start | bytes 786440 | tf_op jit(solution)/shard_map/ppermute | solution.py:196
  27.8 6.7 %collective-permute-done.3 = bf16[128,1024]{1,0:T(8,128)(2,1)S(1)} collective-permute-done((bf16[128,1024]{1,0:T(8,128)(2,1)S(1)}, bf16[128,1024]{1,0:T(8,128)(2,1)S(1)}, u32[]{:S(2)}, u32[]{:S(2)}) %collective-permute-start.3) | collective-permute-done | bytes 262176 | tf_op jit(solution)/shard_map/ppermute | solution.py:196
  34.6 1.9 %pad_maximum_fusion.1 = (bf16[128,2048]{1,0:T(8,128)(2,1)S(1)}, bf16[128,2048]{1,0:T(8,128)(2,1)}, bf16[128,2048]{1,0:T(8,128)(2,1)S(1)}) fusion(bf16[128,512]{1,0:T(8,128)(2,1)S(1)} %get-tuple-element.40, bf16[128,512]{1,0:T(8,128)(2,1)S(1)} %get-tuple-element.37, bf16[128,512]{1,0:T(8,128)(2,1)} %copy-done.3, bf16[128,512]{1,0:T(8,128)(2,1)S(1)} %get-tuple-element.36, ...), kind=kLoop, calls=%fused_computation.8 | loop fusion | flops 3407872 | bytes 2621441 | tf_op jit(solution)/shard_map/concatenate | solution.py:175
  36.5 0.0 collective-permute-start.4
  37.1 1.6 %collective-permute-done.4.refs_1_ = bf16[128,2048]{1,0:T(8,128)(2,1)} collective-permute-done((bf16[128,2048]{1,0:T(8,128)(2,1)}, bf16[128,2048]{1,0:T(8,128)(2,1)}, u32[]{:S(2)}, u32[]{:S(2)}) %collective-permute-start.4) | collective-permute-done | bytes 524320 | tf_op jit(solution)/shard_map/ppermute | solution.py:166
  38.7 0.0 copy-done
  38.7 0.0 copy-done.2
  38.7 0.0 copy-start.1
  38.7 1.6 %copy-done.1 = bf16[128,8192]{1,0:T(8,128)(2,1)S(1)} copy-done((bf16[128,8192]{1,0:T(8,128)(2,1)S(1)}, bf16[128,8192]{1,0:T(8,128)(2,1)}, u32[]{:S(2)}) %copy-start.1) | copy-done | bytes 2097176
  40.3 20.1 %shard_map.101 = (bf16[128,8192]{1,0:T(8,128)(2,1)}, bf16[128,8192]{1,0:T(8,128)(2,1)}, f32[64,128]{1,0:T(8,128)S(1)}, f32[128,2048]{1,0:T(8,128)S(1)}, bf16[128...) custom-call(s32[32]{0:T(128)S(1)} %copy-done.2, s32[1]{0:T(128)} %bitcast.1.first_ref, ...), custom_call_target="tpu_custom_call" | custom-call | flops 4831838208 | bytes 16777216 | tf_op jit(solution)/shard_map/pallas_call | solution.py:110
  60.4 0.1 collective-permute-start.5
  60.5 1.8 %collective-permute-done.5 = bf16[128,2048]{1,0:T(8,128)(2,1)S(1)} collective-permute-done((bf16[128,2048]{1,0:T(8,128)(2,1)S(1)}, bf16[128,2048]{1,0:T(8,128)(2,1)S(1)}, u32[]{:S(2)}, u32[]{:S(2)}) %collective-permute-start.5) | collective-permute-done | bytes 524320 | tf_op jit(solution)/shard_map/ppermute | solution.py:166
  62.3 0.2 fusion.4
  62.5 1.6 %collective-permute-start.6 = (bf16[128,1024]{1,0:T(8,128)(2,1)S(1)}, bf16[128,1024]{1,0:T(8,128)(2,1)S(1)}, u32[]{:S(2)}, u32[]{:S(2)}) collective-permute-start(bf16[128,1024]{1,0:T(8,128)(2,1)S(1)} %broadcast_select_fusion.14), channel_id=1, source_target_pairs={{0,16},{8,24},{16,0},{24,8},{1,17},{9,25},{17,1},{25,9},{2,18},{10... | collective-permute-start | bytes 786440 | tf_op jit(solution)/shard_map/ppermute | solution.py:214
  64.1 6.8 %collective-permute-done.6 = bf16[128,1024]{1,0:T(8,128)(2,1)S(1)} collective-permute-done((bf16[128,1024]{1,0:T(8,128)(2,1)S(1)}, bf16[128,1024]{1,0:T(8,128)(2,1)S(1)}, u32[]{:S(2)}, u32[]{:S(2)}) %collective-permute-start.6) | collective-permute-done | bytes 262176 | tf_op jit(solution)/shard_map/ppermute | solution.py:214
  70.9 0.1 broadcast_select_fusion.5
  71.0 1.3 %collective-permute-start.7 = (bf16[128,1024]{1,0:T(8,128)(2,1)S(1)}, bf16[128,1024]{1,0:T(8,128)(2,1)S(1)}, u32[]{:S(2)}, u32[]{:S(2)}) collective-permute-start(bf16[128,1024]{1,0:T(8,128)(2,1)S(1)} %get-tuple-element.23), channel_id=1, source_target_pairs={{1,0},{2,1},{3,2},{4,3},{5,4},{6,5},{7,6},{9,8},{10,9},{11,10},{12... | collective-permute-start | bytes 786440 | tf_op jit(solution)/shard_map/ppermute | solution.py:148
  72.3 5.0 %collective-permute-start.8 = (bf16[128,1024]{1,0:T(8,128)(2,1)S(1)}, bf16[128,1024]{1,0:T(8,128)(2,1)S(1)}, u32[]{:S(2)}, u32[]{:S(2)}) collective-permute-start(bf16[128,1024]{1,0:T(8,128)(2,1)S(1)} %get-tuple-element.24), channel_id=1, source_target_pairs={{0,1},{1,2},{2,3},{3,4},{4,5},{5,6},{6,7},{8,9},{9,10},{10,11},{11... | collective-permute-start | bytes 786440 | tf_op jit(solution)/shard_map/ppermute | solution.py:148
  77.3 3.8 %collective-permute-done.7 = bf16[128,1024]{1,0:T(8,128)(2,1)S(1)} collective-permute-done((bf16[128,1024]{1,0:T(8,128)(2,1)S(1)}, bf16[128,1024]{1,0:T(8,128)(2,1)S(1)}, u32[]{:S(2)}, u32[]{:S(2)}) %collective-permute-start.7) | collective-permute-done | bytes 262176 | tf_op jit(solution)/shard_map/ppermute | solution.py:148
  81.1 5.8 %collective-permute-done.8 = bf16[128,1024]{1,0:T(8,128)(2,1)S(1)} collective-permute-done((bf16[128,1024]{1,0:T(8,128)(2,1)S(1)}, bf16[128,1024]{1,0:T(8,128)(2,1)S(1)}, u32[]{:S(2)}, u32[]{:S(2)}) %collective-permute-start.8) | collective-permute-done | bytes 262176 | tf_op jit(solution)/shard_map/ppermute | solution.py:148
  86.9 1.6 %collective-permute-start.9 = (bf16[128,1024]{1,0:T(8,128)(2,1)S(1)}, bf16[128,1024]{1,0:T(8,128)(2,1)S(1)}, u32[]{:S(2)}, u32[]{:S(2)}) collective-permute-start(bf16[128,1024]{1,0:T(8,128)(2,1)S(1)} %get-tuple-element.17), channel_id=1, source_target_pairs={{0,16},{8,24},{16,0},{24,8},{1,17},{9,25},{17,1},{25,9},{2,18},{10... | collective-permute-start | bytes 786440 | tf_op jit(solution)/shard_map/ppermute | solution.py:219
  88.5 7.1 %all_to_all.19 = f32[128,4,16]{0,2,1:T(8,128)S(1)} all-to-all(f32[128,4,16]{0,2,1:T(8,128)S(1)} %bitcast.11), channel_id=1, replica_groups=mesh['head'=4,'inner'=4,'outer'=2] {'head'}, dimensions={1} | all-to-all | bytes 65536 | tf_op jit(solution)/shard_map/all_to_all | solution.py:231
  95.6 0.6 copy_bitcast_fusion
  96.2 0.0 collective-permute-done.9
  96.3 0.2 fusion.2
  96.5 0.7 pad_maximum_fusion.5
  97.3 0.7 pad_maximum_fusion.4
  (5 shorter events, 0.2 us)
Async XLA Ops:
  1.8 24.4 %copy-start.3 = (bf16[128,512]{1,0:T(8,128)(2,1)}, bf16[128,512]{1,0:T(8,128)(2,1)S(1)}, u32[]{:S(2)}) copy-start(bf16[128,512]{1,0:T(8,128)(2,1)S(1)} %get-tuple-element.41) | copy-start | bytes 393220
  1.9 9.3 %collective-permute-start = (bf16[128,1024]{1,0:T(8,128)(2,1)S(1)}, bf16[128,1024]{1,0:T(8,128)(2,1)S(1)}, u32[]{:S(2)}, u32[]{:S(2)}) collective-permute-start(bf16[128,1024]{1,0:T(8,128)(2,1)S(1)} %broadcast_select_fusion.17), channel_id=1, source_target_pairs={{0,16},{8,24},{16,0},{24,8},{1,17},{9,25},{17,1},{25,9},{2,18},{10... | collective-permute-start | bytes 786440 | tf_op jit(solution)/shard_map/ppermute | solution.py:191
  11.3 9.4 %collective-permute-start.2 = (bf16[128,1024]{1,0:T(8,128)(2,1)S(1)}, bf16[128,1024]{1,0:T(8,128)(2,1)S(1)}, u32[]{:S(2)}, u32[]{:S(2)}) collective-permute-start(bf16[128,1024]{1,0:T(8,128)(2,1)S(1)} %get-tuple-element.27), channel_id=1, source_target_pairs={{1,0},{2,1},{3,2},{4,3},{5,4},{6,5},{7,6},{9,8},{10,9},{11,10},{12... | collective-permute-start | bytes 786440 | tf_op jit(solution)/shard_map/ppermute | solution.py:148
  12.6 13.5 %collective-permute-start.1 = (bf16[128,1024]{1,0:T(8,128)(2,1)S(1)}, bf16[128,1024]{1,0:T(8,128)(2,1)S(1)}, u32[]{:S(2)}, u32[]{:S(2)}) collective-permute-start(bf16[128,1024]{1,0:T(8,128)(2,1)S(1)} %get-tuple-element.28), channel_id=1, source_target_pairs={{0,1},{1,2},{2,3},{3,4},{4,5},{5,6},{6,7},{8,9},{9,10},{10,11},{11... | collective-permute-start | bytes 786440 | tf_op jit(solution)/shard_map/ppermute | solution.py:148
  26.2 12.5 %copy-start = (bf16[128,8192]{1,0:T(8,128)(2,1)S(1)}, bf16[128,8192]{1,0:T(8,128)(2,1)}, u32[]{:S(2)}) copy-start(bf16[128,8192]{1,0:T(8,128)(2,1)} %q_ref.1) | copy-start | bytes 6291460
  26.2 12.5 %copy-start.2 = (s32[32]{0:T(128)S(1)}, s32[32]{0:T(128)}, u32[]{:S(2)}) copy-start(s32[32]{0:T(128)} %doc_ref.1) | copy-start | bytes 388
  26.2 8.3 %collective-permute-start.3 = (bf16[128,1024]{1,0:T(8,128)(2,1)S(1)}, bf16[128,1024]{1,0:T(8,128)(2,1)S(1)}, u32[]{:S(2)}, u32[]{:S(2)}) collective-permute-start(bf16[128,1024]{1,0:T(8,128)(2,1)S(1)} %get-tuple-element.19), channel_id=1, source_target_pairs={{0,16},{8,24},{16,0},{24,8},{1,17},{9,25},{17,1},{25,9},{2,18},{10... | collective-permute-start | bytes 786440 | tf_op jit(solution)/shard_map/ppermute | solution.py:196
  36.5 2.3 %collective-permute-start.4 = (bf16[128,2048]{1,0:T(8,128)(2,1)}, bf16[128,2048]{1,0:T(8,128)(2,1)}, u32[]{:S(2)}, u32[]{:S(2)}) collective-permute-start(bf16[128,2048]{1,0:T(8,128)(2,1)} %get-tuple-element.34), channel_id=1, source_target_pairs={{0,8},{8,0},{16,24},{24,16},{1,9},{9,1},{17,25},{25,17},{2,10},{10... | collective-permute-start | bytes 1572872 | tf_op jit(solution)/shard_map/ppermute | solution.py:166
  38.7 1.6 %copy-start.1 = (bf16[128,8192]{1,0:T(8,128)(2,1)S(1)}, bf16[128,8192]{1,0:T(8,128)(2,1)}, u32[]{:S(2)}) copy-start(bf16[128,8192]{1,0:T(8,128)(2,1)} %do_ref.1) | copy-start | bytes 6291460
  60.4 1.9 %collective-permute-start.5 = (bf16[128,2048]{1,0:T(8,128)(2,1)S(1)}, bf16[128,2048]{1,0:T(8,128)(2,1)S(1)}, u32[]{:S(2)}, u32[]{:S(2)}) collective-permute-start(bf16[128,2048]{1,0:T(8,128)(2,1)S(1)} %get-tuple-element.15), channel_id=1, source_target_pairs={{0,8},{8,0},{16,24},{24,16},{1,9},{9,1},{17,25},{25,17},{2,10},{10... | collective-permute-start | bytes 1572872 | tf_op jit(solution)/shard_map/ppermute | solution.py:166
  62.5 8.4 %collective-permute-start.6 = (bf16[128,1024]{1,0:T(8,128)(2,1)S(1)}, bf16[128,1024]{1,0:T(8,128)(2,1)S(1)}, u32[]{:S(2)}, u32[]{:S(2)}) collective-permute-start(bf16[128,1024]{1,0:T(8,128)(2,1)S(1)} %broadcast_select_fusion.14), channel_id=1, source_target_pairs={{0,16},{8,24},{16,0},{24,8},{1,17},{9,25},{17,1},{25,9},{2,18},{10... | collective-permute-start | bytes 786440 | tf_op jit(solution)/shard_map/ppermute | solution.py:214
  71.0 10.2 %collective-permute-start.7 = (bf16[128,1024]{1,0:T(8,128)(2,1)S(1)}, bf16[128,1024]{1,0:T(8,128)(2,1)S(1)}, u32[]{:S(2)}, u32[]{:S(2)}) collective-permute-start(bf16[128,1024]{1,0:T(8,128)(2,1)S(1)} %get-tuple-element.23), channel_id=1, source_target_pairs={{1,0},{2,1},{3,2},{4,3},{5,4},{6,5},{7,6},{9,8},{10,9},{11,10},{12... | collective-permute-start | bytes 786440 | tf_op jit(solution)/shard_map/ppermute | solution.py:148
  72.3 14.6 %collective-permute-start.8 = (bf16[128,1024]{1,0:T(8,128)(2,1)S(1)}, bf16[128,1024]{1,0:T(8,128)(2,1)S(1)}, u32[]{:S(2)}, u32[]{:S(2)}) collective-permute-start(bf16[128,1024]{1,0:T(8,128)(2,1)S(1)} %get-tuple-element.24), channel_id=1, source_target_pairs={{0,1},{1,2},{2,3},{3,4},{4,5},{5,6},{6,7},{8,9},{9,10},{10,11},{11... | collective-permute-start | bytes 786440 | tf_op jit(solution)/shard_map/ppermute | solution.py:148
  86.9 9.3 %collective-permute-start.9 = (bf16[128,1024]{1,0:T(8,128)(2,1)S(1)}, bf16[128,1024]{1,0:T(8,128)(2,1)S(1)}, u32[]{:S(2)}, u32[]{:S(2)}) collective-permute-start(bf16[128,1024]{1,0:T(8,128)(2,1)S(1)} %get-tuple-element.17), channel_id=1, source_target_pairs={{0,16},{8,24},{16,0},{24,8},{1,17},{9,25},{17,1},{25,9},{2,18},{10... | collective-permute-start | bytes 786440 | tf_op jit(solution)/shard_map/ppermute | solution.py:219
where the time goes:
time: 98.4 us; the launch traced here: 98 us
  waiting for transfers between devices  39.9 us (41%)
  starting transfers between devices  20.1 us (20%)
  Pallas kernels  20.1 us (20%)
  blocking collectives  7.07 us (7%)
  local copies, waits for them, and re-layouts  4.64 us (5%)
  other arithmetic  4.2 us (4%)
  between operations  2.09 us (2%)
    pallas_call x1, Pallas kernels, attention(): pl.pallas_call(kernel, grid_spec=pltpu.PrefetchScalarGridSpec(num_scalar_...  20.1 us
    ppermute x4, waiting for transfers between devices, along_context(): lax.ppermute(value, CONTEXT, [(s, s + steps) for s in range(low, high)])  18.5 us
    ppermute x4, starting transfers between devices, along_context(): lax.ppermute(value, CONTEXT, [(s, s + steps) for s in range(low, high)])  12.2 us
    all_to_all x1, blocking collectives, body(): lax.all_to_all(jnp.concatenate(entropies, axis=0).T, 'head', split_axis=1...  7.07 us
    ppermute x1, waiting for transfers between devices, returned(): got = lax.ppermute(give, 'head', across)  6.83 us
    ppermute x1, waiting for transfers between devices, earlier_span(): return joined(mine, lax.ppermute(theirs, 'head', across))  6.71 us
    ppermute x1, waiting for transfers between devices, earlier_span(): got = lax.ppermute(give, 'head', across)  4.41 us
    ppermute x2, waiting for transfers between devices, around(): return lax.ppermute(value, 'head', pairs)  3.36 us
  transfers between devices with their start and end apart: 10, of which 9 were waited for; matrix products, arithmetic and copies ran while one was open for 2% of the time, Pallas kernels for 0%

commit v1 on v0

v1 whole, which is shorter than its diff:
```python
import math

import jax
import jax.numpy as jnp
from jax import lax
from jax.experimental import pallas as pl
from jax.experimental.pallas import tpu as pltpu
from jax.sharding import PartitionSpec as P

QUERY_HEADS = 64
KEY_VALUE_HEADS = 8
WIDTH = 128
GROUP = QUERY_HEADS // KEY_VALUE_HEADS
SCALE = 1.0 / math.sqrt(WIDTH)
MASKED = -1e30
CONTEXT = ("inner", "outer")
CHUNKS = 2
NT = (((1,), (1,)), ((), ()))
NN = (((1,), (0,)), ((), ()))


def dot(left, right, dims):
    return lax.dot_general(left, right, dims, preferred_element_type=jnp.float32)


def attention_kernel(near, doc_ref, first_ref, q_ref, do_ref, *refs):
    units = near + 2
    kv_refs, refs = refs[: 2 * units], refs[2 * units :]
    att_ref, dq_ref, ent_ref = refs[:3]
    term_refs, refs = refs[3 : 3 + 2 * units], refs[3 + 2 * units :]
    bias_ref, pb_ref, ds_ref, qs_ref, dos_ref = refs
    rows = q_ref.shape[0]
    window = units * rows
    heads = [slice(h * WIDTH, (h + 1) * WIDTH) for h in range(GROUP)]
    spots = [slice(h * rows, (h + 1) * rows) for h in range(GROUP)]

    @pl.when(pl.program_id(0) == 0)
    def _():
        first = first_ref[0]
        q_pos = first + lax.broadcasted_iota(jnp.int32, (1, rows), 1)

        def step(index, carry):
            at, start = carry
            return at + doc_ref[index], jnp.where(at <= q_pos, at, start)

        _, start = lax.fori_loop(
            0, doc_ref.shape[0], step, (jnp.int32(0), jnp.zeros((1, rows), jnp.int32))
        )
        k_pos = first - (units - 1) * rows + lax.broadcasted_iota(jnp.int32, (window, rows), 0)
        bias_ref[...] = jnp.where((k_pos >= start) & (k_pos <= q_pos), 0.0, MASKED)

    k_rows = jnp.concatenate([ref[...] for ref in kv_refs[:units]], axis=0)
    v_rows = jnp.concatenate([ref[...] for ref in kv_refs[units:]], axis=0)
    for head, spot in zip(heads, spots):
        qs_ref[spot, :] = q_ref[:, head]
        dos_ref[spot, :] = do_ref[:, head]
    scores = dot(k_rows, qs_ref[...], NT)
    dprobs = dot(v_rows, dos_ref[...], NT)
    for h in range(0, GROUP, 2):
        cols = slice(h * rows, (h + 2) * rows)
        s = scores[:, cols] + jnp.concatenate([bias_ref[...]] * 2, axis=1)
        t = (s - jnp.max(s, axis=0, keepdims=True)) * (SCALE * math.log2(math.e))
        e = jnp.exp2(t)
        total = jnp.sum(e, axis=0, keepdims=True)
        inv = 1.0 / total
        entropy = jnp.log(total) - jnp.sum(e * t, axis=0, keepdims=True) * inv * math.log(2.0)
        ent_ref[h : h + 1, :] = entropy[:, :rows]
        ent_ref[h + 1 : h + 2, :] = entropy[:, rows:]
        p = e * inv
        pb_ref[:, cols] = p.astype(jnp.bfloat16)
        dp = dprobs[:, cols]
        delta = jnp.sum(p * dp, axis=0, keepdims=True)
        ds_ref[:, cols] = (p * (dp - delta)).astype(jnp.bfloat16)
    out = dot(v_rows.T, pb_ref[...], NN).astype(jnp.bfloat16).T
    dq = (dot(k_rows.T, ds_ref[...], NN) * SCALE).astype(jnp.bfloat16).T
    for head, spot in zip(heads, spots):
        att_ref[:, head] = out[spot, :]
        dq_ref[:, head] = dq[spot, :]
    dv = dot(pb_ref[...], dos_ref[...], NN)
    dk = dot(ds_ref[...], qs_ref[...], NN) * SCALE
    for index in range(units):
        part = slice(index * rows, (index + 1) * rows)
        term_refs[index][...] = dk[part].astype(term_refs[index].dtype)
        term_refs[units + index][...] = dv[part].astype(term_refs[units + index].dtype)


def attention(doc_lengths, first, queries, dout, own, before, near, chunk, earlier):
    rows = queries.shape[0]
    units = len(near) + 2
    window = units * rows
    count = KEY_VALUE_HEADS // CHUNKS
    block = pl.BlockSpec((rows, GROUP * WIDTH), lambda g, *_: (0, chunk * count + g))
    of_own = pl.BlockSpec((rows, WIDTH), lambda g, *_: (0, chunk * count + g))
    left = pl.BlockSpec((rows, WIDTH), lambda g, *_: (0, g))
    right = pl.BlockSpec((rows, WIDTH), lambda g, *_: (0, count + g))
    keys = [before[0], *near, own[0]]
    values = [before[1], *near, own[1]]
    stay = pl.BlockSpec(memory_space=pl.ANY)

    def kernel(doc_ref, first_ref, q_ref, do_ref, *refs):
        kept = refs[: 2 * units] + refs[2 * units + len(earlier) :]
        attention_kernel(len(near), doc_ref, first_ref, q_ref, do_ref, *kept)

    wide = jax.ShapeDtypeStruct(queries.shape, jnp.bfloat16)
    narrow = [jax.ShapeDtypeStruct((rows, count * WIDTH), jnp.bfloat16)] * (units - 1)
    narrow.append(jax.ShapeDtypeStruct((rows, count * WIDTH), jnp.float32))
    results = pl.pallas_call(
        kernel,
        grid_spec=pltpu.PrefetchScalarGridSpec(
            num_scalar_prefetch=2,
            grid=(count,),
            in_specs=[block, block]
            + [left] * (units - 1)
            + [of_own, left]
            + [right] * len(near)
            + [of_own]
            + [stay] * len(earlier),
            out_specs=[block, block, pl.BlockSpec((GROUP, rows), lambda g, *_: (g, 0))]
            + [left] * (2 * units),
            scratch_shapes=[
                pltpu.VMEM((window, rows), jnp.float32),
                pltpu.VMEM((window, GROUP * rows), jnp.bfloat16),
                pltpu.VMEM((window, GROUP * rows), jnp.bfloat16),
                pltpu.VMEM((GROUP * rows, WIDTH), jnp.bfloat16),
                pltpu.VMEM((GROUP * rows, WIDTH), jnp.bfloat16),
            ],
        ),
        out_shape=[wide, wide, jax.ShapeDtypeStruct((count * GROUP, rows), jnp.float32)]
        + narrow * 2,
        input_output_aliases={4 + 2 * units: 0, 5 + 2 * units: 1} if earlier else {},
        compiler_params=pltpu.CompilerParams(vmem_limit_bytes=32 * 2**20),
        cost_estimate=pl.CostEstimate(
            flops=12 * count * window * GROUP * rows * WIDTH,
            bytes_accessed=16 * count * GROUP * rows * WIDTH,
            transcendentals=count * window * GROUP * rows,
        ),
    )(doc_lengths, first, queries, dout, *keys, *values, *earlier)
    terms = results[3:]
    return results[:2], results[2], terms[:units], terms[units:]


def body(queries, keys, values, dout, doc_lengths, span_order):
    rows = queries.shape[0]
    size = lax.axis_size("head")
    subs = size // 2
    here = lax.axis_index("head")
    side, sub = here // subs, here % subs
    contexts = lax.axis_size(CONTEXT)
    context = lax.axis_index(CONTEXT)
    is_top = context == contexts - 1
    span = lax.dynamic_index_in_dim(span_order, 2 * context + side, keepdims=False)
    is_low = span == context
    in_step = is_low == (context % 2 == 0)
    first = ((span * subs + sub) * rows).reshape(1)
    width = keys.shape[1] // CHUNKS

    def across(value):
        return lax.ppermute(value, "head", [(j, (j + subs) % size) for j in range(size)])

    def around(value, steps):
        pairs = [(j, j // subs * subs + (j + steps) % subs) for j in range(size)]
        return lax.ppermute(value, "head", pairs)

    def edges(value, start):
        pairs = [(c, c + 1) for c in range(start, contexts - 1, 2)]
        return lax.ppermute(value, CONTEXT, pairs + [(b, a) for a, b in pairs])

    def choose(condition, one, two):
        return jnp.where(condition, one, two), jnp.where(condition, two, one)

    def moved(key_part, value_part, backward):
        keep, give = choose(side == 0, key_part, value_part)
        got = across(give)
        upward = is_low != backward
        even_out, odd_out = choose(upward == (context % 2 == 0), keep, got)
        even_in = edges(even_out, 0)
        odd_in = jnp.where(is_top, choose(is_low != backward, keep, got)[0], edges(odd_out, 1))
        mine, theirs = choose(in_step, *((even_in, odd_in) if backward else (odd_in, even_in)))
        return choose(side == 0, mine, across(theirs))

    def key_window(chunk):
        cols = slice(chunk * width, (chunk + 1) * width)
        before = moved(keys[:, cols], values[:, cols], False)
        own_both = jnp.concatenate([keys[:, cols], values[:, cols]], axis=1)
        before_both = jnp.concatenate(before, axis=1)
        near = [
            around(jnp.where(sub + steps < subs, own_both, before_both), steps)
            for steps in range(subs - 1, 0, -1)
        ]
        return before, near

    def returned(dk, dv):
        own = [dk[-1], dv[-1]]
        before = [dk[0].astype(jnp.float32), dv[0].astype(jnp.float32)]
        for index, steps in enumerate(range(subs - 1, 0, -1)):
            got = around(jnp.concatenate([dk[index + 1], dv[index + 1]], axis=1), -steps)
            within = sub + steps < subs
            for which, part in enumerate(jnp.split(got.astype(jnp.float32), 2, axis=1)):
                own[which] = own[which] + jnp.where(within, part, 0.0)
                before[which] = before[which] + jnp.where(within, 0.0, part)
        back = moved(before[0].astype(jnp.bfloat16), before[1].astype(jnp.bfloat16), True)
        return [
            (mine + theirs.astype(jnp.float32)).astype(jnp.bfloat16)
            for mine, theirs in zip(own, back)
        ]

    windows = [key_window(chunk) for chunk in range(CHUNKS)]
    wide = []
    entropies, grads = [], []
    for chunk, window in enumerate(windows):
        wide, entropy, dk, dv = attention(
            doc_lengths, first, queries, dout, (keys, values), *window, chunk, wide
        )
        entropies.append(entropy)
        grads.append(returned(dk, dv))
    attended, grad_query = wide
    entropy = lax.all_to_all(
        jnp.concatenate(entropies, axis=0).T, "head", split_axis=1, concat_axis=0, tiled=True
    )
    grad_key, grad_value = [jnp.concatenate(parts, axis=1) for parts in zip(*grads)]
    return attended, entropy, grad_query, grad_key, grad_value


def solution(mesh):
    rows = P(("inner", "outer", "head"), None)
    return jax.shard_map(
        body,
        mesh=mesh,
        in_specs=(rows, rows, rows, rows, P(), P()),
        out_specs=(rows, P(("inner", "outer"), "head"), rows, rows, rows),
        check_vma=False,
    )
```

time: 98.4 us -> 87.1 us (0.89)
  waiting for transfers between devices: 39.9 us -> 24 us
  starting transfers between devices: 20.1 us -> 33.3 us
  blocking collectives: 7.07 us -> 0 us
  local copies, waits for them, and re-layouts: 4.64 us -> 1.88 us
    ppermute x8 -> x16, waiting for transfers between devices: 36.5 us -> 20.6 us  [the longest x8 15.2 us: across(): lax.ppermute(value, 'head', [(j, (j + subs) % size) for j in range(size)])]
    ppermute x8 -> x16, starting transfers between devices: 20 us -> 28.8 us  [the longest x8 19.9 us: edges(): return lax.ppermute(value, CONTEXT, pairs + [(b, a) for a, b in pairs])]
    all_to_all x1 -> x0, blocking collectives: 7.07 us -> none  [body(): lax.all_to_all(jnp.concatenate(entropies, axis=0).T, 'head', split_axis=1...]
    ppermute x2 -> x4, waiting for transfers between devices: 3.36 us -> 0.01 us  [around(): return lax.ppermute(value, 'head', pairs)]
    all_to_all x0 -> x1, waiting for transfers between devices: none -> 3.35 us  [body(): lax.all_to_all(jnp.concatenate(entropies, axis=0).T, 'head', split_axis=1...]
    all_to_all x0 -> x1, starting transfers between devices: none -> 3.26 us  [body(): lax.all_to_all(jnp.concatenate(entropies, axis=0).T, 'head', split_axis=1...]
    select_n x8 -> x19, other arithmetic: 0.49 us -> 2.82 us  [the longest x17 2.69 us: choose(): return (jnp.where(condition, one, two), jnp.where(condition, two, one))]
    concatenate x3 -> x4, other arithmetic: 3.32 us -> 1.51 us  [the longest x1 0.86 us: body(): jnp.concatenate(parts, axis=1)]
  transfers between devices with their start and end apart: 10 -> 21, of which waited for: 9 -> 11; matrix products, arithmetic and copies ran while one was open for 2% -> 4% of each run, Pallas kernels for 0% -> 23%
where the time goes in v1:
time: 87.1 us; the launch traced here: 86.1 us
  starting transfers between devices  33.3 us (38%)
  waiting for transfers between devices  24 us (28%)
  Pallas kernels  20 us (23%)
  other arithmetic  4.72 us (5%)
  between operations  2.24 us (3%)
  local copies, waits for them, and re-layouts  1.88 us (2%)
    pallas_call x2, Pallas kernels, attention(): pl.pallas_call(kernel, grid_spec=pltpu.PrefetchScalarGridSpec(num_scalar_...  20 us
    ppermute x8, starting transfers between devices, edges(): return lax.ppermute(value, CONTEXT, pairs + [(b, a) for a, b in pairs])  19.9 us
    ppermute x8, waiting for transfers between devices, across(): lax.ppermute(value, 'head', [(j, (j + subs) % size) for j in range(size)])  15.2 us
    ppermute x8, starting transfers between devices, across(): lax.ppermute(value, 'head', [(j, (j + subs) % size) for j in range(size)])  8.83 us
    ppermute x8, waiting for transfers between devices, edges(): return lax.ppermute(value, CONTEXT, pairs + [(b, a) for a, b in pairs])  5.36 us
    all_to_all x1, waiting for transfers between devices, body(): lax.all_to_all(jnp.concatenate(entropies, axis=0).T, 'head', split_axis=1...  3.35 us
    all_to_all x1, starting transfers between devices, body(): lax.all_to_all(jnp.concatenate(entropies, axis=0).T, 'head', split_axis=1...  3.26 us
    select_n x17, other arithmetic, choose(): return (jnp.where(condition, one, two), jnp.where(condition, two, one))  2.69 us
  transfers between devices with their start and end apart: 21, of which 11 were waited for; matrix products, arithmetic and copies ran while one was open for 4% of the time, Pallas kernels for 23%

profile of v1, /device:TPU:0, one launch (start us, length us, event | category | flops | bytes accessed | tf_op | source)
XLA Modules:
  0.0 86.1 jit_solution(18334577797384343585)
XLA Ops:
  0.6 0.0 copy-start
  0.6 0.0 copy-start.1
  0.7 1.0 %broadcast_select_fusion.22 = bf16[128,512]{1,0:T(8,128)(2,1)S(1)} fusion(pred[]{:T(512)S(6)} %eq.19, bf16[128,1024]{1,0:T(8,128)(2,1)} %refs_5_.3, bf16[128,1024]{1,0:T(8,128)(2,1)} %refs_2_.3), kind=kLoop, calls=%fused_computation.40 | loop fusion | flops 65536 | bytes 393217 | tf_op jit(solution)/shard_map/jit(_where)/select_n | solution.py:169
  1.7 3.0 %collective-permute-start.5 = (bf16[128,512]{1,0:T(8,128)(2,1)S(1)}, bf16[128,512]{1,0:T(8,128)(2,1)S(1)}, u32[]{:S(2)}, u32[]{:S(2)}) collective-permute-start(bf16[128,512]{1,0:T(8,128)(2,1)S(1)} %broadcast_select_fusion.22), channel_id=1, source_target_pairs={{0,16},{8,24},{16,0},{24,8},{1,17},{9,25},{17,1},{25,9},{2,18},{10... | collective-permute-start | bytes 393224 | tf_op jit(solution)/shard_map/ppermute | solution.py:158
  4.7 1.2 %dynamic_slice.4 = s32[1]{0:T(128)} dynamic-slice(s32[16]{0:T(128)} %param.11, s32[]{:T(128)S(6)} %select_n.252), dynamic_slice_sizes={1} | dynamic-slice | bytes 12 | tf_op jit(solution)/shard_map/jit(dynamic_index_in_dim)/dynamic_slice | solution.py:151
  7.3 0.9 %collective-permute-done.5 = bf16[128,512]{1,0:T(8,128)(2,1)S(1)} collective-permute-done((bf16[128,512]{1,0:T(8,128)(2,1)S(1)}, bf16[128,512]{1,0:T(8,128)(2,1)S(1)}, u32[]{:S(2)}, u32[]{:S(2)}) %collective-permute-start.5) | collective-permute-done | bytes 131104 | tf_op jit(solution)/shard_map/ppermute | solution.py:158
  8.2 1.1 %broadcast_select_fusion.11 = (bf16[128,512]{1,0:T(8,128)(2,1)S(1)}, bf16[128,512]{1,0:T(8,128)(2,1)S(1)}, bf16[128,512]{1,0:T(8,128)(2,1)S(1)}, bf16[128,512]{1,0:T(8,128)(2,1)S(1)}) fusion(bf16[128,512]{1,0:T(8,128)(2,1)S(1)} %collective-permute-done.5, pred[]{:T(512)S(6)} %eq.42, bf16[128,1024]{1,0:T(8,128)(2,1)} %refs_5_.3, ...), kind=kLoop, calls=%fused_computation.29 | loop fusion | flops 196608 | bytes 1179650 | tf_op jit(solution)/shard_map/jit(_where)/select_n | solution.py:169
  9.4 1.8 %collective-permute-start = (bf16[128,512]{1,0:T(8,128)(2,1)S(1)}, bf16[128,512]{1,0:T(8,128)(2,1)S(1)}, u32[]{:S(2)}, u32[]{:S(2)}) collective-permute-start(bf16[128,512]{1,0:T(8,128)(2,1)S(1)} %get-tuple-element.67), channel_id=1, source_target_pairs={{0,16},{8,24},{16,0},{24,8},{1,17},{9,25},{17,1},{25,9},{2,18},{10... | collective-permute-start | bytes 393224 | tf_op jit(solution)/shard_map/ppermute | solution.py:158
  11.2 1.6 %collective-permute-start.7 = (bf16[128,512]{1,0:T(8,128)(2,1)S(1)}, bf16[128,512]{1,0:T(8,128)(2,1)S(1)}, u32[]{:S(2)}, u32[]{:S(2)}) collective-permute-start(bf16[128,512]{1,0:T(8,128)(2,1)S(1)} %broadcast_select_fusion.10), channel_id=1, source_target_pairs={{0,1},{2,3},{4,5},{6,7},{1,0},{3,2},{5,4},{7,6},{8,9},{10,11},{12,... | collective-permute-start | bytes 393224 | tf_op jit(solution)/shard_map/ppermute | solution.py:166
  12.8 0.7 collective-permute-start.6
  13.4 1.0 %collective-permute-done = bf16[128,512]{1,0:T(8,128)(2,1)S(1)} collective-permute-done((bf16[128,512]{1,0:T(8,128)(2,1)S(1)}, bf16[128,512]{1,0:T(8,128)(2,1)S(1)}, u32[]{:S(2)}, u32[]{:S(2)}) %collective-permute-start) | collective-permute-done | bytes 131104 | tf_op jit(solution)/shard_map/ppermute | solution.py:158
  14.5 3.4 %collective-permute-start.2 = (bf16[128,512]{1,0:T(8,128)(2,1)S(1)}, bf16[128,512]{1,0:T(8,128)(2,1)S(1)}, u32[]{:S(2)}, u32[]{:S(2)}) collective-permute-start(bf16[128,512]{1,0:T(8,128)(2,1)S(1)} %broadcast_select_fusion.14), channel_id=1, source_target_pairs={{0,1},{2,3},{4,5},{6,7},{1,0},{3,2},{5,4},{7,6},{8,9},{10,11},{12,... | collective-permute-start | bytes 393224 | tf_op jit(solution)/shard_map/ppermute | solution.py:166
  17.9 0.8 collective-permute-start.1
  18.7 0.6 collective-permute-start.8
  19.3 3.0 %collective-permute-done.2 = bf16[128,512]{1,0:T(8,128)(2,1)S(1)} collective-permute-done((bf16[128,512]{1,0:T(8,128)(2,1)S(1)}, bf16[128,512]{1,0:T(8,128)(2,1)S(1)}, u32[]{:S(2)}, u32[]{:S(2)}) %collective-permute-start.2) | collective-permute-done | bytes 131104 | tf_op jit(solution)/shard_map/ppermute | solution.py:166
  22.4 0.6 collective-permute-start.3
  23.0 0.8 collective-permute-done.8
  23.8 0.1 maximum_select_fusion.1
  23.9 0.1 collective-permute-start.9
  24.0 3.5 %collective-permute-done.3 = bf16[128,512]{1,0:T(8,128)(2,1)S(1)} collective-permute-done((bf16[128,512]{1,0:T(8,128)(2,1)S(1)}, bf16[128,512]{1,0:T(8,128)(2,1)S(1)}, u32[]{:S(2)}, u32[]{:S(2)}) %collective-permute-start.3) | collective-permute-done | bytes 131104 | tf_op jit(solution)/shard_map/ppermute | solution.py:158
  27.5 0.1 maximum_select_fusion
  27.5 0.1 collective-permute-start.4
  27.6 10.0 %shard_map.101 = (bf16[128,8192]{1,0:T(8,128)(2,1)}, bf16[128,8192]{1,0:T(8,128)(2,1)}, f32[32,128]{1,0:T(8,128)S(1)}, bf16[128,512]{1,0:T(8,128)(2,1)S(1)}, bf1...) custom-call(s32[32]{0:T(128)S(1)} %copy-done.4, ...), custom_call_target="tpu_custom_call" | custom-call | flops 2415919104 | bytes 8388608 | tf_op jit(solution)/shard_map/pallas_call | solution.py:107
  37.7 0.6 collective-permute-start.10
  38.2 10.0 %shard_map.102 = (bf16[128,8192]{1,0:T(8,128)(2,1)}, bf16[128,8192]{1,0:T(8,128)(2,1)}, f32[32,128]{1,0:T(8,128)S(1)}, bf16[128,512]{1,0:T(8,128)(2,1)S(1)}, bf1...) custom-call(s32[32]{0:T(128)S(1)} %copy-done.4, ...), custom_call_target="tpu_custom_call", output_to_operand_aliasing={{0}: (10, {}), {1}: (11, {})} | custom-call | flops 2415919104 | bytes 8388608 | tf_op jit(solution)/shard_map/pallas_call | solution.py:107
  48.2 0.6 pad_maximum_fusion.4
  48.8 3.3 %all-to-all-start = ((f32[128,4,16]{0,2,1:T(8,128)}), f32[128,4,16]{0,2,1:T(8,128)S(1)}, u32[]{:S(2)}, u32[]{:S(2)}) async-start(f32[128,4,16]{0,2,1:T(8,128)} %bitcast.3), calls=%async_computation | async-start | bytes 65536 | tf_op jit(solution)/shard_map/all_to_all | solution.py:217
  52.1 0.5 collective-permute-start.15
  52.7 3.4 %all-to-all-done = f32[128,4,16]{0,2,1:T(8,128)S(1)} async-done(((f32[128,4,16]{0,2,1:T(8,128)}), f32[128,4,16]{0,2,1:T(8,128)S(1)}, u32[]{:S(2)}, u32[]{:S(2)}) %all-to-all-start) | async-done | bytes 32800 | tf_op jit(solution)/shard_map/all_to_all | solution.py:217
  56.0 0.6 copy_bitcast_fusion
  56.7 0.1 broadcast_select_fusion.18
  56.8 0.1 collective-permute-start.11
  56.9 0.1 broadcast_select_fusion.16
  57.0 2.1 %collective-permute-start.16 = (bf16[128,512]{1,0:T(8,128)(2,1)S(1)}, bf16[128,512]{1,0:T(8,128)(2,1)S(1)}, u32[]{:S(2)}, u32[]{:S(2)}) collective-permute-start(bf16[128,512]{1,0:T(8,128)(2,1)S(1)} %get-tuple-element.52), channel_id=1, source_target_pairs={{0,16},{8,24},{16,0},{24,8},{1,17},{9,25},{17,1},{25,9},{2,18},{10... | collective-permute-start | bytes 393224 | tf_op jit(solution)/shard_map/ppermute | solution.py:158
  59.1 4.2 %collective-permute-done.11 = bf16[128,512]{1,0:T(8,128)(2,1)S(1)} collective-permute-done((bf16[128,512]{1,0:T(8,128)(2,1)S(1)}, bf16[128,512]{1,0:T(8,128)(2,1)S(1)}, u32[]{:S(2)}, u32[]{:S(2)}) %collective-permute-start.11) | collective-permute-done | bytes 131104 | tf_op jit(solution)/shard_map/ppermute | solution.py:158
  63.3 0.7 collective-permute-start.13
  64.0 7.9 %collective-permute-start.12 = (bf16[128,512]{1,0:T(8,128)(2,1)S(1)}, bf16[128,512]{1,0:T(8,128)(2,1)S(1)}, u32[]{:S(2)}, u32[]{:S(2)}) collective-permute-start(bf16[128,512]{1,0:T(8,128)(2,1)S(1)} %get-tuple-element.43), channel_id=1, source_target_pairs={{0,1},{2,3},{4,5},{6,7},{1,0},{3,2},{5,4},{7,6},{8,9},{10,11},{12,... | collective-permute-start | bytes 393224 | tf_op jit(solution)/shard_map/ppermute | solution.py:166
  71.9 0.7 collective-permute-start.18
  72.6 4.3 %collective-permute-start.17 = (bf16[128,512]{1,0:T(8,128)(2,1)S(1)}, bf16[128,512]{1,0:T(8,128)(2,1)S(1)}, u32[]{:S(2)}, u32[]{:S(2)}) collective-permute-start(bf16[128,512]{1,0:T(8,128)(2,1)S(1)} %get-tuple-element.50), channel_id=1, source_target_pairs={{0,1},{2,3},{4,5},{6,7},{1,0},{3,2},{5,4},{7,6},{8,9},{10,11},{12,... | collective-permute-start | bytes 393224 | tf_op jit(solution)/shard_map/ppermute | solution.py:166
  76.9 0.8 collective-permute-done.12
  77.8 0.6 collective-permute-start.14
  78.4 1.5 %collective-permute-done.17 = bf16[128,512]{1,0:T(8,128)(2,1)S(1)} collective-permute-done((bf16[128,512]{1,0:T(8,128)(2,1)S(1)}, bf16[128,512]{1,0:T(8,128)(2,1)S(1)}, u32[]{:S(2)}, u32[]{:S(2)}) %collective-permute-start.17) | collective-permute-done | bytes 131104 | tf_op jit(solution)/shard_map/ppermute | solution.py:166
  79.9 0.1 collective-permute-start.19
  80.0 3.6 %collective-permute-done.14 = bf16[128,512]{1,0:T(8,128)(2,1)S(1)} collective-permute-done((bf16[128,512]{1,0:T(8,128)(2,1)S(1)}, bf16[128,512]{1,0:T(8,128)(2,1)S(1)}, u32[]{:S(2)}, u32[]{:S(2)}) %collective-permute-start.14) | collective-permute-done | bytes 131104 | tf_op jit(solution)/shard_map/ppermute | solution.py:158
  83.6 0.1 add_convert_fusion.1
  83.8 1.3 %collective-permute-done.19 = bf16[128,512]{1,0:T(8,128)(2,1)S(1)} collective-permute-done((bf16[128,512]{1,0:T(8,128)(2,1)S(1)}, bf16[128,512]{1,0:T(8,128)(2,1)S(1)}, u32[]{:S(2)}, u32[]{:S(2)}) %collective-permute-start.19) | collective-permute-done | bytes 131104 | tf_op jit(solution)/shard_map/ppermute | solution.py:158
  85.0 0.1 add_convert_fusion
  85.2 0.9 pad_maximum_fusion.2
  (35 shorter events, 0.5 us)
Async XLA Ops:
  0.6 13.8 %copy-start = (bf16[128,1024]{1,0:T(8,128)(2,1)S(1)}, bf16[128,1024]{1,0:T(8,128)(2,1)}, u32[]{:S(2)}) copy-start(bf16[128,1024]{1,0:T(8,128)(2,1)} %refs_5_.3) | copy-start | bytes 786436
  0.6 13.8 %copy-start.1 = (bf16[128,1024]{1,0:T(8,128)(2,1)S(1)}, bf16[128,1024]{1,0:T(8,128)(2,1)}, u32[]{:S(2)}) copy-start(bf16[128,1024]{1,0:T(8,128)(2,1)} %refs_2_.3) | copy-start | bytes 786436
  1.7 6.5 %collective-permute-start.5 = (bf16[128,512]{1,0:T(8,128)(2,1)S(1)}, bf16[128,512]{1,0:T(8,128)(2,1)S(1)}, u32[]{:S(2)}, u32[]{:S(2)}) collective-permute-start(bf16[128,512]{1,0:T(8,128)(2,1)S(1)} %broadcast_select_fusion.22), channel_id=1, source_target_pairs={{0,16},{8,24},{16,0},{24,8},{1,17},{9,25},{17,1},{25,9},{2,18},{10... | collective-permute-start | bytes 393224 | tf_op jit(solution)/shard_map/ppermute | solution.py:158
  9.4 5.0 %collective-permute-start = (bf16[128,512]{1,0:T(8,128)(2,1)S(1)}, bf16[128,512]{1,0:T(8,128)(2,1)S(1)}, u32[]{:S(2)}, u32[]{:S(2)}) collective-permute-start(bf16[128,512]{1,0:T(8,128)(2,1)S(1)} %get-tuple-element.67), channel_id=1, source_target_pairs={{0,16},{8,24},{16,0},{24,8},{1,17},{9,25},{17,1},{25,9},{2,18},{10... | collective-permute-start | bytes 393224 | tf_op jit(solution)/shard_map/ppermute | solution.py:158
  11.2 7.5 %collective-permute-start.7 = (bf16[128,512]{1,0:T(8,128)(2,1)S(1)}, bf16[128,512]{1,0:T(8,128)(2,1)S(1)}, u32[]{:S(2)}, u32[]{:S(2)}) collective-permute-start(bf16[128,512]{1,0:T(8,128)(2,1)S(1)} %broadcast_select_fusion.10), channel_id=1, source_target_pairs={{0,1},{2,3},{4,5},{6,7},{1,0},{3,2},{5,4},{7,6},{8,9},{10,11},{12,... | collective-permute-start | bytes 393224 | tf_op jit(solution)/shard_map/ppermute | solution.py:166
  12.8 5.9 %collective-permute-start.6 = (bf16[128,512]{1,0:T(8,128)(2,1)S(1)}, bf16[128,512]{1,0:T(8,128)(2,1)S(1)}, u32[]{:S(2)}, u32[]{:S(2)}) collective-permute-start(bf16[128,512]{1,0:T(8,128)(2,1)S(1)} %get-tuple-element.57), channel_id=1, source_target_pairs={{1,2},{3,4},{5,6},{2,1},{4,3},{6,5},{9,10},{11,12},{13,14},{10,9},... | collective-permute-start | bytes 393224 | tf_op jit(solution)/shard_map/ppermute | solution.py:166
  14.5 7.9 %collective-permute-start.2 = (bf16[128,512]{1,0:T(8,128)(2,1)S(1)}, bf16[128,512]{1,0:T(8,128)(2,1)S(1)}, u32[]{:S(2)}, u32[]{:S(2)}) collective-permute-start(bf16[128,512]{1,0:T(8,128)(2,1)S(1)} %broadcast_select_fusion.14), channel_id=1, source_target_pairs={{0,1},{2,3},{4,5},{6,7},{1,0},{3,2},{5,4},{7,6},{8,9},{10,11},{12,... | collective-permute-start | bytes 393224 | tf_op jit(solution)/shard_map/ppermute | solution.py:166
  17.9 9.7 %copy-start.2 = (bf16[128,8192]{1,0:T(8,128)(2,1)S(1)}, bf16[128,8192]{1,0:T(8,128)(2,1)}, u32[]{:S(2)}) copy-start(bf16[128,8192]{1,0:T(8,128)(2,1)} %q_ref.3) | copy-start | bytes 6291460
  17.9 9.7 %copy-start.3 = (bf16[128,8192]{1,0:T(8,128)(2,1)S(1)}, bf16[128,8192]{1,0:T(8,128)(2,1)}, u32[]{:S(2)}) copy-start(bf16[128,8192]{1,0:T(8,128)(2,1)} %do_ref.3) | copy-start | bytes 6291460
  17.9 9.8 %copy-start.4 = (s32[32]{0:T(128)S(1)}, s32[32]{0:T(128)}, u32[]{:S(2)}) copy-start(s32[32]{0:T(128)} %doc_ref.3) | copy-start | bytes 388
  17.9 4.5 %collective-permute-start.1 = (bf16[128,512]{1,0:T(8,128)(2,1)S(1)}, bf16[128,512]{1,0:T(8,128)(2,1)S(1)}, u32[]{:S(2)}, u32[]{:S(2)}) collective-permute-start(bf16[128,512]{1,0:T(8,128)(2,1)S(1)} %get-tuple-element.61), channel_id=1, source_target_pairs={{1,2},{3,4},{5,6},{2,1},{4,3},{6,5},{9,10},{11,12},{13,14},{10,9},... | collective-permute-start | bytes 393224 | tf_op jit(solution)/shard_map/ppermute | solution.py:166
  18.7 5.0 %collective-permute-start.8 = (bf16[128,512]{1,0:T(8,128)(2,1)S(1)}, bf16[128,512]{1,0:T(8,128)(2,1)S(1)}, u32[]{:S(2)}, u32[]{:S(2)}) collective-permute-start(bf16[128,512]{1,0:T(8,128)(2,1)S(1)} %get-tuple-element.55), channel_id=1, source_target_pairs={{0,16},{8,24},{16,0},{24,8},{1,17},{9,25},{17,1},{25,9},{2,18},{10... | collective-permute-start | bytes 393224 | tf_op jit(solution)/shard_map/ppermute | solution.py:158
  22.4 5.0 %collective-permute-start.3 = (bf16[128,512]{1,0:T(8,128)(2,1)S(1)}, bf16[128,512]{1,0:T(8,128)(2,1)S(1)}, u32[]{:S(2)}, u32[]{:S(2)}) collective-permute-start(bf16[128,512]{1,0:T(8,128)(2,1)S(1)} %get-tuple-element.59), channel_id=1, source_target_pairs={{0,16},{8,24},{16,0},{24,8},{1,17},{9,25},{17,1},{25,9},{2,18},{10... | collective-permute-start | bytes 393224 | tf_op jit(solution)/shard_map/ppermute | solution.py:158
  23.9 3.7 %collective-permute-start.9 = (bf16[128,1024]{1,0:T(8,128)(2,1)S(1)}, bf16[128,1024]{1,0:T(8,128)(2,1)S(1)}, u32[]{:S(2)}, u32[]{:S(2)}) collective-permute-start(bf16[128,1024]{1,0:T(8,128)(2,1)S(1)} %maximum_select_fusion.1), channel_id=1, source_target_pairs={{0,8},{8,0},{16,24},{24,16},{1,9},{9,1},{17,25},{25,17},{2,10},{10... | collective-permute-start | bytes 786440 | tf_op jit(solution)/shard_map/ppermute | solution.py:162
  27.5 10.7 %collective-permute-start.4 = (bf16[128,1024]{1,0:T(8,128)(2,1)S(1)}, bf16[128,1024]{1,0:T(8,128)(2,1)S(1)}, u32[]{:S(2)}, u32[]{:S(2)}) collective-permute-start(bf16[128,1024]{1,0:T(8,128)(2,1)S(1)} %maximum_select_fusion), channel_id=1, source_target_pairs={{0,8},{8,0},{16,24},{24,16},{1,9},{9,1},{17,25},{25,17},{2,10},{10... | collective-permute-start | bytes 786440 | tf_op jit(solution)/shard_map/ppermute | solution.py:162
  37.7 19.0 %collective-permute-start.10 = (bf16[128,1024]{1,0:T(8,128)(2,1)S(1)}, bf16[128,1024]{1,0:T(8,128)(2,1)S(1)}, u32[]{:S(2)}, u32[]{:S(2)}) collective-permute-start(bf16[128,1024]{1,0:T(8,128)(2,1)S(1)} %pad_maximum_fusion), channel_id=1, source_target_pairs={{0,8},{8,0},{16,24},{24,16},{1,9},{9,1},{17,25},{25,17},{2,10},{10... | collective-permute-start | bytes 786440 | tf_op jit(solution)/shard_map/ppermute | solution.py:162
  48.8 7.2 %all-to-all-start = ((f32[128,4,16]{0,2,1:T(8,128)}), f32[128,4,16]{0,2,1:T(8,128)S(1)}, u32[]{:S(2)}, u32[]{:S(2)}) async-start(f32[128,4,16]{0,2,1:T(8,128)} %bitcast.3), calls=%async_computation | async-start | bytes 65536 | tf_op jit(solution)/shard_map/all_to_all | solution.py:217
  52.1 4.7 %collective-permute-start.15 = (bf16[128,1024]{1,0:T(8,128)(2,1)S(1)}, bf16[128,1024]{1,0:T(8,128)(2,1)S(1)}, u32[]{:S(2)}, u32[]{:S(2)}) collective-permute-start(bf16[128,1024]{1,0:T(8,128)(2,1)S(1)} %pad_maximum_fusion.1), channel_id=1, source_target_pairs={{0,8},{8,0},{16,24},{24,16},{1,9},{9,1},{17,25},{25,17},{2,10},{10... | collective-permute-start | bytes 786440 | tf_op jit(solution)/shard_map/ppermute | solution.py:162
  56.8 6.5 %collective-permute-start.11 = (bf16[128,512]{1,0:T(8,128)(2,1)S(1)}, bf16[128,512]{1,0:T(8,128)(2,1)S(1)}, u32[]{:S(2)}, u32[]{:S(2)}) collective-permute-start(bf16[128,512]{1,0:T(8,128)(2,1)S(1)} %get-tuple-element.45), channel_id=1, source_target_pairs={{0,16},{8,24},{16,0},{24,8},{1,17},{9,25},{17,1},{25,9},{2,18},{10... | collective-permute-start | bytes 393224 | tf_op jit(solution)/shard_map/ppermute | solution.py:158
  57.0 14.9 %collective-permute-start.16 = (bf16[128,512]{1,0:T(8,128)(2,1)S(1)}, bf16[128,512]{1,0:T(8,128)(2,1)S(1)}, u32[]{:S(2)}, u32[]{:S(2)}) collective-permute-start(bf16[128,512]{1,0:T(8,128)(2,1)S(1)} %get-tuple-element.52), channel_id=1, source_target_pairs={{0,16},{8,24},{16,0},{24,8},{1,17},{9,25},{17,1},{25,9},{2,18},{10... | collective-permute-start | bytes 393224 | tf_op jit(solution)/shard_map/ppermute | solution.py:158
  63.3 13.6 %collective-permute-start.13 = (bf16[128,512]{1,0:T(8,128)(2,1)S(1)}, bf16[128,512]{1,0:T(8,128)(2,1)S(1)}, u32[]{:S(2)}, u32[]{:S(2)}) collective-permute-start(bf16[128,512]{1,0:T(8,128)(2,1)S(1)} %broadcast_select_fusion.2), channel_id=1, source_target_pairs={{1,2},{3,4},{5,6},{2,1},{4,3},{6,5},{9,10},{11,12},{13,14},{10,9},... | collective-permute-start | bytes 393224 | tf_op jit(solution)/shard_map/ppermute | solution.py:166
  64.0 13.8 %collective-permute-start.12 = (bf16[128,512]{1,0:T(8,128)(2,1)S(1)}, bf16[128,512]{1,0:T(8,128)(2,1)S(1)}, u32[]{:S(2)}, u32[]{:S(2)}) collective-permute-start(bf16[128,512]{1,0:T(8,128)(2,1)S(1)} %get-tuple-element.43), channel_id=1, source_target_pairs={{0,1},{2,3},{4,5},{6,7},{1,0},{3,2},{5,4},{7,6},{8,9},{10,11},{12,... | collective-permute-start | bytes 393224 | tf_op jit(solution)/shard_map/ppermute | solution.py:166
  71.9 6.5 %collective-permute-start.18 = (bf16[128,512]{1,0:T(8,128)(2,1)S(1)}, bf16[128,512]{1,0:T(8,128)(2,1)S(1)}, u32[]{:S(2)}, u32[]{:S(2)}) collective-permute-start(bf16[128,512]{1,0:T(8,128)(2,1)S(1)} %broadcast_select_fusion), channel_id=1, source_target_pairs={{1,2},{3,4},{5,6},{2,1},{4,3},{6,5},{9,10},{11,12},{13,14},{10,9},... | collective-permute-start | bytes 393224 | tf_op jit(solution)/shard_map/ppermute | solution.py:166
  72.6 7.3 %collective-permute-start.17 = (bf16[128,512]{1,0:T(8,128)(2,1)S(1)}, bf16[128,512]{1,0:T(8,128)(2,1)S(1)}, u32[]{:S(2)}, u32[]{:S(2)}) collective-permute-start(bf16[128,512]{1,0:T(8,128)(2,1)S(1)} %get-tuple-element.50), channel_id=1, source_target_pairs={{0,1},{2,3},{4,5},{6,7},{1,0},{3,2},{5,4},{7,6},{8,9},{10,11},{12,... | collective-permute-start | bytes 393224 | tf_op jit(solution)/shard_map/ppermute | solution.py:166
  77.8 5.8 %collective-permute-start.14 = (bf16[128,512]{1,0:T(8,128)(2,1)S(1)}, bf16[128,512]{1,0:T(8,128)(2,1)S(1)}, u32[]{:S(2)}, u32[]{:S(2)}) collective-permute-start(bf16[128,512]{1,0:T(8,128)(2,1)S(1)} %get-tuple-element.41), channel_id=1, source_target_pairs={{0,16},{8,24},{16,0},{24,8},{1,17},{9,25},{17,1},{25,9},{2,18},{10... | collective-permute-start | bytes 393224 | tf_op jit(solution)/shard_map/ppermute | solution.py:158
  79.9 5.1 %collective-permute-start.19 = (bf16[128,512]{1,0:T(8,128)(2,1)S(1)}, bf16[128,512]{1,0:T(8,128)(2,1)S(1)}, u32[]{:S(2)}, u32[]{:S(2)}) collective-permute-start(bf16[128,512]{1,0:T(8,128)(2,1)S(1)} %get-tuple-element.48), channel_id=1, source_target_pairs={{0,16},{8,24},{16,0},{24,8},{1,17},{9,25},{17,1},{25,9},{2,18},{10... | collective-permute-start | bytes 393224 | tf_op jit(solution)/shard_map/ppermute | solution.py:158

commit v2 on v1

v2 whole, which is shorter than its diff:
```python
import functools
import math

import jax
import jax.numpy as jnp
from jax import lax
from jax.experimental import pallas as pl
from jax.experimental.pallas import tpu as pltpu
from jax.sharding import PartitionSpec as P

QUERY_HEADS = 64
KEY_VALUE_HEADS = 8
WIDTH = 128
GROUP = QUERY_HEADS // KEY_VALUE_HEADS
SCALE = 1.0 / math.sqrt(WIDTH)
MASKED = -1e30
CONTEXT = ("inner", "outer")
CHUNKS = 1
UNROLL = 2
EXTRA = 16
BEHIND = (2, 4, 2)
LOG2E = math.log2(math.e)
VMEM_SMALL = 8 * 2**20
VMEM_LARGE = 16 * 2**20
NT = (((1,), (1,)), ((), ()))
NN = (((1,), (0,)), ((), ()))


def dot(left, right, dims):
    return lax.dot_general(left, right, dims, preferred_element_type=jnp.float32)


def lanes(index, width=WIDTH):
    if isinstance(index, int):
        return slice(index * width, (index + 1) * width)
    return pl.ds(pl.multiple_of(index * width, WIDTH), width)


def group_rows(ref, g):
    return jnp.concatenate([ref[:, lanes(g * GROUP + h)] for h in range(GROUP)], axis=0)


def tiled(bias):
    return jnp.concatenate([bias] * GROUP, axis=1)


def own_kernel(bias_ref, *refs):
    sources, refs = refs[:4], refs[4:]
    loaded, (stat_ref, sems) = refs[:4], refs[4:]
    q_ref, do_ref, k_ref, v_ref = loaded
    rows = q_ref.shape[0]
    last = bias_ref.shape[0] - rows
    heads = k_ref.shape[1] // WIDTH
    narrow = [pltpu.make_async_copy(sources[i], loaded[i], sems.at[i, 0]) for i in (2, 3)]

    def wide(g):
        cols = lanes(g, GROUP * WIDTH)
        return [
            pltpu.make_async_copy(sources[i].at[:, cols], loaded[i].at[:, cols], sems.at[i, g])
            for i in (0, 1)
        ]

    copies = narrow + [copy for g in range(heads) for copy in wide(g)]
    for copy in copies:
        copy.start()
    for copy in narrow:
        copy.wait()

    def step(g, _):
        for copy in wide(g):
            copy.wait()
        s = dot(k_ref[:, lanes(g)], group_rows(q_ref, g), NT) + tiled(bias_ref[last:, :])
        dp = dot(v_ref[:, lanes(g)], group_rows(do_ref, g), NT)
        top = jnp.max(s, axis=0, keepdims=True)
        t = (s - top) * (SCALE * LOG2E)
        e = jnp.exp2(t)
        stat_ref[g, 0:1, :] = top
        stat_ref[g, 1:2, :] = jnp.sum(e, axis=0, keepdims=True)
        stat_ref[g, 2:3, :] = jnp.sum(e * t, axis=0, keepdims=True)
        stat_ref[g, 3:4, :] = jnp.sum(e * dp, axis=0, keepdims=True)
        return 0

    lax.fori_loop(0, heads, step, 0)


def earlier_kernel(start, count, near, q_ref, do_ref, bias_ref, first_k, first_v, *refs):
    near_refs, (stat_ref, *refs) = refs[:near], refs[near:]
    ent_ref, row_ref, p_ref, ds_ref = refs[:4]
    dk_refs, dv_refs = refs[4 : 5 + near], refs[5 + near :]
    rows = q_ref.shape[0]
    width = first_k.shape[1] // WIDTH
    window = (near + 1) * rows

    def head(at, _):
        g = start + at
        k_rows = jnp.concatenate(
            [first_k[:, lanes(at)], *[ref[:, lanes(at)] for ref in near_refs]], axis=0
        )
        v_rows = jnp.concatenate(
            [first_v[:, lanes(at)], *[ref[:, lanes(at + width)] for ref in near_refs]], axis=0
        )
        q_all, do_all = group_rows(q_ref, g), group_rows(do_ref, g)
        s = dot(k_rows, q_all, NT) + tiled(bias_ref[:window, :])
        dp = dot(v_rows, do_all, NT)
        own_top, own_total = stat_ref[g, 0:1, :], stat_ref[g, 1:2, :]
        top = jnp.maximum(jnp.max(s, axis=0, keepdims=True), own_top)
        t = (s - top) * (SCALE * LOG2E)
        e = jnp.exp2(t)
        shift = (own_top - top) * (SCALE * LOG2E)
        ratio = jnp.exp2(shift)
        total = own_total * ratio + jnp.sum(e, axis=0, keepdims=True)
        inv = 1.0 / total
        spread = (stat_ref[g, 2:3, :] + shift * own_total) * ratio
        spread = spread + jnp.sum(e * t, axis=0, keepdims=True)
        entropy = jnp.log(total) - spread * inv * math.log(2.0)
        for h in range(GROUP):
            ent_ref[at, h : h + 1, :] = entropy[:, h * rows : (h + 1) * rows]
        delta = stat_ref[g, 3:4, :] * ratio + jnp.sum(e * dp, axis=0, keepdims=True)
        delta = delta * inv
        row_ref[at, 0:1, :] = top * (SCALE * LOG2E) + jnp.log2(total)
        row_ref[at, 1:2, :] = delta
        p = e * inv
        pb = p.astype(jnp.bfloat16)
        ds = (p * (dp - delta)).astype(jnp.bfloat16)
        p_ref[at] = pb
        ds_ref[at] = ds
        dv = dot(pb, do_all, NN)
        dk = dot(ds, q_all, NN) * SCALE
        for unit in range(near + 1):
            part = slice(unit * rows, (unit + 1) * rows)
            dk_refs[unit][:, lanes(at)] = dk[part].astype(jnp.bfloat16)
            dv_refs[unit][:, lanes(at)] = dv[part].astype(jnp.bfloat16)

        return 0

    lax.fori_loop(0, count, head, 0, unroll=UNROLL)


def rest_kernel(start, skip, near, q_ref, do_ref, bias_ref, first_k, first_v, *refs):
    near_refs, (own_k, own_v), refs = refs[:near], refs[near : near + 2], refs[near + 2 :]
    row_ref, p_ref, ds_ref, att_ref, dq_ref, dk_ref, dv_ref = refs
    rows = q_ref.shape[0]
    width = first_k.shape[1] // WIDTH
    last = bias_ref.shape[0] - rows
    index = pl.program_id(0)
    at, g = skip + index, start + skip + index
    own_keys, own_values = own_k[:, lanes(g)], own_v[:, lanes(g)]
    k_rows = jnp.concatenate(
        [first_k[:, lanes(at)], *[ref[:, lanes(at)] for ref in near_refs], own_keys], axis=0
    )
    v_rows = jnp.concatenate(
        [first_v[:, lanes(at)], *[ref[:, lanes(at + width)] for ref in near_refs], own_values],
        axis=0,
    )
    q_all, do_all = group_rows(q_ref, g), group_rows(do_ref, g)
    s = dot(own_keys, q_all, NT) + tiled(bias_ref[last:, :])
    dp = dot(own_values, do_all, NT)
    p = jnp.exp2(s * (SCALE * LOG2E) - row_ref[at, 0:1, :])
    pb = p.astype(jnp.bfloat16)
    ds = (p * (dp - row_ref[at, 1:2, :])).astype(jnp.bfloat16)
    dv_ref[:, lanes(index)] = dot(pb, do_all, NN)
    dk_ref[:, lanes(index)] = dot(ds, q_all, NN) * SCALE
    p_all = jnp.concatenate([p_ref[at], pb], axis=0)
    ds_all = jnp.concatenate([ds_ref[at], ds], axis=0)
    out = dot(v_rows.T, p_all, NN).astype(jnp.bfloat16).T
    dq = (dot(k_rows.T, ds_all, NN) * SCALE).astype(jnp.bfloat16).T
    for h in range(GROUP):
        spot = slice(h * rows, (h + 1) * rows)
        att_ref[:, lanes(h)] = out[spot, :]
        dq_ref[:, lanes(h)] = dq[spot, :]


def whole(count, space=pltpu.VMEM):
    return [pl.BlockSpec(memory_space=space)] * count


def near_by(value):
    return pltpu.with_memory_space_constraint(value, pltpu.VMEM)


def in_scalars(value):
    return pltpu.with_memory_space_constraint(value, pltpu.SMEM)


def small(kernel, flags, inputs, outs, behind=()):
    def body(*refs):
        kernel(*refs[: 1 + len(inputs)], *refs[1 + len(inputs) + len(behind) :])

    return pl.pallas_call(
        body,
        in_specs=whole(1, pltpu.SMEM) + whole(len(inputs)) + whole(len(behind), pl.ANY),
        out_specs=whole(len(outs)),
        out_shape=[pltpu.VMEM(shape, dtype) for shape, dtype in outs],
        compiler_params=pltpu.CompilerParams(vmem_limit_bytes=VMEM_SMALL),
    )(in_scalars(flags), *[near_by(value) for value in inputs], *behind)


def cost(count, rows, products):
    return pl.CostEstimate(
        flops=16 * products * count * rows * GROUP * rows * WIDTH,
        bytes_accessed=1,
        transcendentals=0,
    )


def large(kernel, inputs, outs, price, behind=()):
    def body(*refs):
        kernel(*refs[: len(inputs)], *refs[len(inputs) + len(behind) :])

    return pl.pallas_call(
        body,
        in_specs=whole(len(inputs)) + whole(len(behind), pl.ANY),
        out_specs=whole(len(outs)),
        out_shape=[pltpu.VMEM(shape, dtype) for shape, dtype in outs],
        compiler_params=pltpu.CompilerParams(vmem_limit_bytes=VMEM_LARGE),
        cost_estimate=price,
    )(*[near_by(value) for value in inputs], *behind)


def far(value):
    return pltpu.with_memory_space_constraint(value, pltpu.HBM)


def own_sums(bias, *arrays):
    rows = arrays[0].shape[0]
    heads = arrays[2].shape[1] // WIDTH
    return pl.pallas_call(
        own_kernel,
        in_specs=whole(1) + whole(4, pl.ANY),
        out_specs=whole(5),
        out_shape=[pltpu.VMEM(array.shape, array.dtype) for array in arrays]
        + [pltpu.VMEM((heads, 8, GROUP * rows), jnp.float32)],
        scratch_shapes=[pltpu.SemaphoreType.DMA((4, heads))],
        compiler_params=pltpu.CompilerParams(vmem_limit_bytes=VMEM_LARGE),
        cost_estimate=cost(heads, rows, 2),
    )(near_by(bias), *[far(array) for array in arrays])


def earlier_terms(queries, dout, bias, before, near, stats, start, behind=()):
    rows = queries.shape[0]
    units = len(near) + 1
    count = before[0].shape[1] // WIDTH
    wide = (count, units * rows, GROUP * rows)
    outs = [
        ((count, GROUP, rows), jnp.float32),
        ((count, 8, GROUP * rows), jnp.float32),
        (wide, jnp.bfloat16),
        (wide, jnp.bfloat16),
    ] + [((rows, count * WIDTH), jnp.bfloat16)] * (2 * units)
    kernel = functools.partial(earlier_kernel, start, count, len(near))
    inputs = [queries, dout, bias, *before, *near, stats]
    results = large(kernel, inputs, outs, cost(count, rows, 4 * units), behind)
    return results[0], results[1:4], results[4 : 4 + units], results[4 + units :]


def the_rest(queries, dout, bias, before, near, own, kept, start, skip, count, earlier, behind=()):
    rows = queries.shape[0]
    block = pl.BlockSpec((rows, GROUP * WIDTH), lambda g: (0, start + skip + g))
    inputs = [near_by(v) for v in (queries, dout, bias, *before, *near, *own, *kept)]
    extra = [*earlier, *behind]

    def kernel(*refs):
        refs = refs[: len(inputs)] + refs[len(inputs) + len(extra) :]
        rest_kernel(start, skip, len(near), *refs)

    wide = jax.ShapeDtypeStruct(queries.shape, jnp.bfloat16)
    results = pl.pallas_call(
        kernel,
        grid=(count,),
        in_specs=whole(len(inputs)) + whole(len(extra), pl.ANY),
        out_specs=[block, block] + whole(2),
        out_shape=[wide, wide] + [pltpu.VMEM((rows, count * WIDTH), jnp.float32)] * 2,
        input_output_aliases={len(inputs): 0, len(inputs) + 1: 1} if earlier else {},
        compiler_params=pltpu.CompilerParams(vmem_limit_bytes=VMEM_LARGE),
        cost_estimate=cost(count, rows, 10),
    )(*inputs, *extra)
    return results[:2], results[2:]


def route(flag, first, second, one, two):
    @pl.when(flag != 0)
    def _():
        one[...] = first[...]
        two[...] = second[...]

    @pl.when(flag == 0)
    def _():
        one[...] = second[...]
        two[...] = first[...]


def body(queries, keys, values, dout, doc_lengths, span_order):
    rows = queries.shape[0]
    size = lax.axis_size("head")
    subs = size // 2
    here = lax.axis_index("head")
    side, sub = here // subs, here % subs
    contexts = lax.axis_size(CONTEXT)
    context = lax.axis_index(CONTEXT)
    place = jnp.stack([context, side, sub, context % 2]).astype(jnp.int32)

    def place_flags(place, spans, flag):
        span = spans[2 * place[0] + place[1]]
        flag[0] = (span * subs + place[2]) * rows
        for index in (1, 2):
            flag[index] = place[index]
        flag[3] = (span == place[0]).astype(jnp.int32)
        flag[4] = place[3]
        flag[5] = (place[0] == contexts - 1).astype(jnp.int32)

    flags = pl.pallas_call(
        place_flags,
        in_specs=whole(2, pltpu.SMEM),
        out_specs=whole(1, pltpu.SMEM)[0],
        out_shape=pltpu.SMEM((6,), jnp.int32),
    )(place, span_order)
    width = keys.shape[1] // CHUNKS
    half = ((rows, width), jnp.bfloat16)

    def across(value):
        return lax.ppermute(value, "head", [(j, (j + subs) % size) for j in range(size)])

    def around(value, steps):
        pairs = [(j, j // subs * subs + (j + steps) % subs) for j in range(size)]
        return lax.ppermute(value, "head", pairs)

    def edges(value, start):
        pairs = [(c, c + 1) for c in range(start, contexts - 1, 2)]
        return lax.ppermute(value, CONTEXT, pairs + [(b, a) for a, b in pairs])

    def pick_in(place, keys, values, give, sem):
        for flag, source in ((0, values), (1, keys)):

            @pl.when(place[1] == flag)
            def _(source=source):
                copy = pltpu.make_async_copy(source, give, sem)
                copy.start()
                copy.wait()

    give = pl.pallas_call(
        pick_in,
        in_specs=whole(1, pltpu.SMEM) + whole(2, pl.ANY),
        out_specs=whole(1)[0],
        out_shape=pltpu.VMEM(keys.shape, keys.dtype),
        scratch_shapes=[pltpu.SemaphoreType.DMA],
        compiler_params=pltpu.CompilerParams(vmem_limit_bytes=VMEM_SMALL),
    )(place, far(keys), far(values))

    def mask(flag, doc_ref, bias_ref):
        first = flag[0]
        window = bias_ref.shape[0]
        q_pos = first + lax.broadcasted_iota(jnp.int32, (1, rows), 1)

        def step(index, carry):
            at, start = carry
            return at + doc_ref[index], jnp.where(at <= q_pos, at, start)

        _, start = lax.fori_loop(
            0, doc_ref.shape[0], step, (jnp.int32(0), jnp.zeros((1, rows), jnp.int32))
        )
        k_pos = first + rows - window + lax.broadcasted_iota(jnp.int32, (window, rows), 0)
        bias_ref[...] = jnp.where((k_pos >= start) & (k_pos <= q_pos), 0.0, MASKED)

    bias = pl.pallas_call(
        mask,
        in_specs=whole(2, pltpu.SMEM),
        out_specs=whole(1)[0],
        out_shape=pltpu.VMEM(((subs + 1) * rows, rows), jnp.float32),
        compiler_params=pltpu.CompilerParams(vmem_limit_bytes=VMEM_SMALL),
    )(in_scalars(flags), doc_lengths)

    def out_of_step(flag, backward):
        return (flag[3] + flag[4] + (1 if backward else 0)) % 2

    def edge_parts(own, got, backward, behind=()):
        def kernel(flag, *refs):
            own, (got, even, odd) = refs[:-3], refs[-3:]
            for which, keep in enumerate(own):

                @pl.when((flag[1] == which) | (len(own) == 1))
                def _(keep=keep):
                    route(out_of_step(flag, backward), keep, got.at[:rows], even, odd)

        return small(kernel, flags, [*own, got], [half, half], behind)

    def edge_done(own, got, even, odd, backward, behind=()):
        def kernel(flag, *refs):
            own, (got, even, odd, mine, theirs) = refs[:-5], refs[-5:]
            takes_odd = (flag[3] + flag[4]) % 2
            if backward:
                takes_odd = 1 - takes_odd

            @pl.when(flag[5] == 0)
            def _():
                route(takes_odd, odd, even, mine, theirs)

            kept = (flag[3] + (1 if backward else 0)) % 2
            for which, keep in enumerate(own):

                @pl.when((flag[5] != 0) & (kept != 0) & ((flag[1] == which) | (len(own) == 1)))
                def _(keep=keep):
                    route(takes_odd, keep, even, mine, theirs)

            @pl.when((flag[5] != 0) & (kept == 0))
            def _():
                route(takes_odd, got.at[:rows], even, mine, theirs)

        return small(kernel, flags, [*own, got, even, odd], [half, half], behind)

    def window_parts(own, mine, other, behind=()):
        def kernel(flag, own_key, own_value, mine, other, key, value, *sent):
            route(flag[1], other, mine, key, value)
            for index, out in enumerate(sent):
                inside = flag[2] + (subs - 1 - index) < subs

                @pl.when(inside)
                def _():
                    out[:, :width] = own_key[...]
                    out[:, width:] = own_value[...]

                @pl.when(jnp.logical_not(inside))
                def _():
                    out[:, :width] = key[...]
                    out[:, width:] = value[...]

        both = ((rows, 2 * width), jnp.bfloat16)
        outs = small(kernel, flags, [*own, mine, other], [half, half] + [both] * (subs - 1), behind)
        return outs[:2], [around(out, subs - 1 - i) for i, out in enumerate(outs[2:])]

    per_device = KEY_VALUE_HEADS // size

    def two_parts(out, lo, block):
        block = block.reshape(-1, rows)
        if block.shape[0] < EXTRA:
            fill = jnp.zeros((EXTRA - block.shape[0], rows), jnp.float32)
            block = jnp.concatenate([block, fill], axis=0)
        high = block.astype(jnp.bfloat16)
        out[rows:, lo : lo + rows] = high
        lo += WIDTH
        out[rows:, lo : lo + rows] = (block - high.astype(jnp.float32)).astype(jnp.bfloat16)

    def one_part(ref, lo):
        high, low = ref[rows:, lo : lo + rows], ref[rows:, lo + WIDTH : lo + WIDTH + rows]
        return high.astype(jnp.float32) + low.astype(jnp.float32)

    def near_terms(dk, dv, entropies):
        def kernel(flag, ent, *refs):
            for index in range(subs - 1):
                out = refs[2 * (subs - 1) + index]
                out[:rows, :width] = refs[index][...]
                out[:rows, width:] = refs[subs - 1 + index][...]
                to = lax.rem(flag[2] + index + 1, subs)
                for which in range(2):
                    block = ent[pl.ds((which * subs + to) * per_device, per_device)]
                    two_parts(out, 2 * which * WIDTH, block)

        both = ((rows + EXTRA, 2 * width), jnp.bfloat16)
        outs = small(kernel, flags, [entropies, *dk[1:], *dv[1:]], [both] * (subs - 1))
        return [around(out, index + 1 - subs) for index, out in enumerate(outs)]

    def collect(dk, dv, entropies, arrived, behind=()):
        def kernel(flag, dk, dv, ent, *refs):
            got = refs[: subs - 1]
            keep, give, own_key, own_value, ent_out = refs[subs - 1 :]
            for which, term, own in ((0, dk, own_key), (1, dv, own_value)):
                before = term[...].astype(jnp.float32)
                mine = jnp.zeros_like(before)
                for index, ref in enumerate(got):
                    part = ref[:rows, which * width : (which + 1) * width].astype(jnp.float32)
                    within = flag[2] + (subs - 1 - index) < subs
                    mine = mine + jnp.where(within, part, 0.0)
                    before = before + jnp.where(within, 0.0, part)
                own[...] = mine
                before = before.astype(jnp.bfloat16)

                @pl.when(flag[1] == which)
                def _():
                    keep[...] = before

                @pl.when(flag[1] != which)
                def _():
                    give[:rows, :] = before

            for which in range(2):
                block = ent[pl.ds((which * subs + flag[2]) * per_device, per_device)]
                blocks = [block.reshape(-1, rows)]
                blocks += [one_part(ref, 2 * which * WIDTH)[: blocks[0].shape[0]] for ref in got]

                @pl.when(flag[1] == which)
                def _(blocks=blocks):
                    for index, block in enumerate(blocks):
                        ent_out[index] = block

                @pl.when(flag[1] != which)
                def _(blocks=blocks):
                    for index, block in enumerate(blocks):
                        two_parts(give, 2 * index * WIDTH, block)

        full = ((rows, width), jnp.float32)
        kept = ((subs, per_device * GROUP, rows), jnp.float32)
        given = ((rows + EXTRA, width), jnp.bfloat16)
        inputs = [dk[0], dv[0], entropies, *arrived]
        return small(kernel, flags, inputs, [half, given, full, full, kept], behind)

    def finish(own_key, own_value, pieces, mine, other, entropies, got):
        spots = [0]
        for dk, dv in pieces:
            spots.append(spots[-1] + dk.shape[1])
        local = [own_key, own_value, mine, other, *[term for piece in pieces for term in piece]]
        local += [entropies, got]
        count = per_device * GROUP

        def kernel(flag, own_key, own_value, mine, other, *refs):
            terms, refs = refs[: 2 * len(pieces)], refs[2 * len(pieces) :]
            ent, got, out_key, out_value, out_ent = refs
            is_key = flag[1] == 0
            for index in range(len(pieces)):
                cols = slice(spots[index], spots[index + 1])
                here = mine[:, cols].astype(jnp.float32)
                there = other[:, cols].astype(jnp.float32)
                for out, own, term, back in (
                    (out_key, own_key, terms[2 * index], jnp.where(is_key, here, there)),
                    (out_value, own_value, terms[2 * index + 1], jnp.where(is_key, there, here)),
                ):
                    out[:, cols] = (own[:, cols] + term[...] + back).astype(jnp.bfloat16)
            for index in range(subs):
                steps = 0 if index == 0 else subs - index
                source = lax.rem(flag[2] + steps, subs)
                for way, block in ((flag[1], ent[index]), (1 - flag[1], one_part(got, 2 * index * WIDTH))):
                    for spot in range(size):

                        @pl.when(way * subs + source == spot)
                        def _(spot=spot, block=block):
                            out_ent[:, spot * rows : (spot + 1) * rows] = block[:count]

        return pl.pallas_call(
            kernel,
            grid=(1,),
            in_specs=whole(1, pltpu.SMEM) + whole(len(local)),
            out_specs=[pl.BlockSpec((rows, width), lambda g: (0, 0))] * 2
            + [pl.BlockSpec((count, size * rows), lambda g: (0, 0))],
            out_shape=[jax.ShapeDtypeStruct(keys.shape, jnp.bfloat16)] * 2
            + [jax.ShapeDtypeStruct((count, size * rows), jnp.float32)],
            compiler_params=pltpu.CompilerParams(vmem_limit_bytes=VMEM_SMALL),
        )(in_scalars(flags), *[near_by(v) for v in local])

    def travel(keep, got, backward, behind=()):
        even, odd = edge_parts(keep, got, backward, behind)
        return edges(even, 0), edges(odd, 1)

    def land(keep, got, even, odd, backward, behind=()):
        mine, theirs = edge_done(keep, got, even, odd, backward, behind)
        return mine, across(theirs)

    got = across(give)
    q_near, do_near, *own, stats = own_sums(bias, queries, dout, keys, values)
    even, odd = travel(own, got, False, [stats])
    mine, other = land(own, got, even, odd, False)
    before, near = window_parts(own, mine, other)
    entropies, kept, dk, dv = earlier_terms(q_near, do_near, bias, before, near, stats, 0)
    arrived = near_terms(dk, dv, entropies)
    keep, give, own_key, own_value, entropies = collect(dk, dv, entropies, arrived)
    got = across(give)
    wide, pieces, done = [], [], 0
    for count in BEHIND:
        wide, piece = the_rest(
            q_near, do_near, bias, before, near, own, kept, 0, done, count, wide, [give]
        )
        pieces.append(piece)
        done += count
    even, odd = travel([keep], got, True, pieces[0][:1])
    mine, other = land([keep], got, even, odd, True, pieces[1][:1])
    grad_key, grad_value, entropy = finish(
        own_key, own_value, pieces, mine, other, entropies, got
    )
    return wide[0], entropy.T, wide[1], grad_key, grad_value


def solution(mesh):
    rows = P(("inner", "outer", "head"), None)
    return jax.shard_map(
        body,
        mesh=mesh,
        in_specs=(rows, rows, rows, rows, P(), P()),
        out_specs=(rows, P(("inner", "outer"), "head"), rows, rows, rows),
        check_vma=False,
    )
```

time: 87.1 us -> 75.9 us (0.87); the launches traced: 86.1 us -> 75.7 us
  starting transfers between devices: 33.3 us -> 10.1 us
  waiting for transfers between devices: 24 us -> 36.4 us
  Pallas kernels: 20 us -> 27.8 us
  other arithmetic: 4.72 us -> 0.08 us
  between operations: 2.24 us -> 0.8 us
  local copies, waits for them, and re-layouts: 1.88 us -> 0.65 us
    ppermute x8 -> x4, starting transfers between devices: 19.9 us -> 5.44 us  [edges(): return lax.ppermute(value, CONTEXT, pairs + [(b, a) for a, b in pairs])]
    ppermute x8 -> x4, waiting for transfers between devices: 5.36 us -> 16 us  [edges(): return lax.ppermute(value, CONTEXT, pairs + [(b, a) for a, b in pairs])]
    pallas_call x2 -> x16, Pallas kernels: 20 us -> 27.8 us  [the longest x1 9.14 us: large(): pl.pallas_call(body, in_specs=whole(len(inputs)) + whole(len(behind), pl....]
    ppermute x8 -> x4, starting transfers between devices: 8.83 us -> 4.34 us  [across(): lax.ppermute(value, 'head', [(j, (j + subs) % size) for j in range(size)])]
    ppermute x4 -> x2, waiting for transfers between devices: 0.01 us -> 3.76 us  [around(): return lax.ppermute(value, 'head', pairs)]
    all_to_all x1 -> x0, waiting for transfers between devices: 3.35 us -> none  [body(): lax.all_to_all(jnp.concatenate(entropies, axis=0).T, 'head', split_axis=1...]
    all_to_all x1 -> x0, starting transfers between devices: 3.26 us -> none  [body(): lax.all_to_all(jnp.concatenate(entropies, axis=0).T, 'head', split_axis=1...]
    select_n x19 -> x0, other arithmetic: 2.82 us -> none  [the longest x17 2.69 us: choose(): return (jnp.where(condition, one, two), jnp.where(condition, two, one))]
  transfers between devices with their start and end apart: 21 -> 10, of which waited for: 11 -> 7; matrix products, arithmetic and copies ran while one was open for 4% -> 0% of each run, Pallas kernels for 23% -> 20%
where the time goes in v2:
time: 75.9 us; the launch traced here: 75.7 us
  waiting for transfers between devices  36.4 us (48%)
  Pallas kernels  27.8 us (37%)
  starting transfers between devices  10.1 us (13%)
  between operations  0.8 us (1%)
    ppermute x4, waiting for transfers between devices, across(): lax.ppermute(value, 'head', [(j, (j + subs) % size) for j in range(size)])  16.6 us
    ppermute x4, waiting for transfers between devices, edges(): return lax.ppermute(value, CONTEXT, pairs + [(b, a) for a, b in pairs])  16 us
    pallas_call x1, Pallas kernels, large(): pl.pallas_call(body, in_specs=whole(len(inputs)) + whole(len(behind), pl....  9.14 us
    pallas_call x3, Pallas kernels, the_rest(): pl.pallas_call(kernel, grid=(count,), in_specs=whole(len(inputs)) + whole...  8.99 us
    ppermute x4, starting transfers between devices, edges(): return lax.ppermute(value, CONTEXT, pairs + [(b, a) for a, b in pairs])  5.44 us
    pallas_call x1, Pallas kernels, own_sums(): pl.pallas_call(own_kernel, in_specs=whole(1) + whole(4, pl.ANY), out_spec...  5.03 us
    ppermute x4, starting transfers between devices, across(): lax.ppermute(value, 'head', [(j, (j + subs) % size) for j in range(size)])  4.34 us
    ppermute x2, waiting for transfers between devices, around(): return lax.ppermute(value, 'head', pairs)  3.76 us
  transfers between devices with their start and end apart: 10, of which 7 were waited for; matrix products, arithmetic and copies ran while one was open for 0% of the time, Pallas kernels for 20%

profile of v2, /device:TPU:0, one launch (start us, length us, event | category | flops | bytes accessed | tf_op | source)
XLA Modules:
  0.0 75.7 jit_solution(3490694743859804011)
XLA Ops:
  0.7 0.1 pad_add_fusion.place
  0.7 0.0 copy-start
  0.7 1.5 %shard_map.104 = bf16[128,1024]{1,0:T(8,128)(2,1)S(1)} custom-call(s32[4]{0:T(128)S(1)} %pad_add_fusion.place, bf16[128,1024]{1,0:T(8,128)(2,1)} %keys.1, bf16[128,1024]{1,0:T(8,128)(2,1)} %values.1), custom_call_target="tpu_custom_call" | custom-call | tf_op jit(solution)/shard_map/pallas_call | solution.py:340
  2.2 3.0 %collective-permute-start = (bf16[128,1024]{1,0:T(8,128)(2,1)S(1)}, bf16[128,1024]{1,0:T(8,128)(2,1)S(1)}, u32[]{:S(2)}, u32[]{:S(2)}) collective-permute-start(bf16[128,1024]{1,0:T(8,128)(2,1)S(1)} %shard_map.104), channel_id=1, source_target_pairs={{0,16},{8,24},{16,0},{24,8},{1,17},{9,25},{17,1},{25,9},{2,18},{10... | collective-permute-start | bytes 786440 | tf_op jit(solution)/shard_map/ppermute | solution.py:321
  5.3 0.0 copy-done
  5.3 0.7 shard_map.101.flag.refs_0_
  6.0 0.0 copy-start.1
  6.0 0.6 copy-done.1
  6.6 0.8 %shard_map.102.bias_ref.refs_2_ = f32[384,128]{1,0:T(8,128)S(1)} custom-call(s32[6]{0:T(128)S(4)} %shard_map.101.flag.refs_0_, s32[32]{0:T(128)S(1)} %copy-done.1), custom_call_target="tpu_custom_call" | custom-call | tf_op jit(solution)/shard_map/pallas_call | solution.py:364
  7.4 5.0 %shard_map.103 = (bf16[128,8192]{1,0:T(8,128)(2,1)S(1)}, bf16[128,8192]{1,0:T(8,128)(2,1)S(1)}, bf16[128,1024]{1,0:T(8,128)(2,1)S(1)}, bf16[128,1024]{1,0:T(8,128)(2,1)S(1)}, f32[8,8,1024]{2,1,0:T(8,128)S(1)}) custom-call(f32[384,128]{1,0:T(8,128)S(1)} %shard_map.102.bias_ref.refs_2_, bf16[128,8192]{1,0:T(8,128)(2,1)} %refs_0_.1, bf16[128,8192]{1,0:T(8,128)(2,1)} %refs_1_.1, ...), custom_call_target="tpu_custom_call" | custom-call | flops 4294967296 | bytes 1 | tf_op jit(solution)/shard_map/pallas_call | solution.py:227
  12.4 0.0 collective-permute-done.refs_3_
  12.5 0.1 shard_map.105
  12.5 1.6 %collective-permute-start.1 = (bf16[128,1024]{1,0:T(8,128)(2,1)S(1)}, bf16[128,1024]{1,0:T(8,128)(2,1)S(1)}, u32[]{:S(2)}, u32[]{:S(2)}) collective-permute-start(bf16[128,1024]{1,0:T(8,128)(2,1)S(1)} %get-tuple-element.54), channel_id=1, source_target_pairs={{0,1},{2,3},{4,5},{6,7},{1,0},{3,2},{5,4},{7,6},{8,9},{10,11},{12,... | collective-permute-start | bytes 786440 | tf_op jit(solution)/shard_map/ppermute | solution.py:329
  14.1 0.7 collective-permute-start.2
  14.8 10.2 %collective-permute-done.1.refs_4_ = bf16[128,1024]{1,0:T(8,128)(2,1)S(1)} collective-permute-done((bf16[128,1024]{1,0:T(8,128)(2,1)S(1)}, bf16[128,1024]{1,0:T(8,128)(2,1)S(1)}, u32[]{:S(2)}, u32[]{:S(2)}) %collective-permute-start.1) | collective-permute-done | bytes 262176 | tf_op jit(solution)/shard_map/ppermute | solution.py:329
  25.0 0.0 collective-permute-done.2.refs_5_
  25.0 0.1 shard_map.106
  25.1 0.6 collective-permute-start.3
  25.6 6.3 %collective-permute-done.3.refs_4_ = bf16[128,1024]{1,0:T(8,128)(2,1)S(1)} collective-permute-done((bf16[128,1024]{1,0:T(8,128)(2,1)S(1)}, bf16[128,1024]{1,0:T(8,128)(2,1)S(1)}, u32[]{:S(2)}, u32[]{:S(2)}) %collective-permute-start.3) | collective-permute-done | bytes 262176 | tf_op jit(solution)/shard_map/ppermute | solution.py:321
  32.0 0.1 shard_map.107
  32.1 0.1 collective-permute-start.4
  32.1 1.9 %collective-permute-done.4.refs_5_ = bf16[128,2048]{1,0:T(8,128)(2,1)S(1)} collective-permute-done((bf16[128,2048]{1,0:T(8,128)(2,1)S(1)}, bf16[128,2048]{1,0:T(8,128)(2,1)S(1)}, u32[]{:S(2)}, u32[]{:S(2)}) %collective-permute-start.4) | collective-permute-done | bytes 524320 | tf_op jit(solution)/shard_map/ppermute | solution.py:325
  34.0 9.1 %shard_map.108 = (f32[8,8,128]{2,1,0:T(8,128)S(1)}, f32[8,8,1024]{2,1,0:T(8,128)S(1)}, bf16[8,256,1024]{2,1,0:T(8,128)(2,1)S(1)}, bf16[8,256,1024]{2,1,0:T(8,128...) custom-call(bf16[128,8192]{1,0:T(8,128)(2,1)S(1)} %get-tuple-element, ...), custom_call_target="tpu_custom_call" | custom-call | flops 17179869184 | bytes 1 | tf_op jit(solution)/shard_map/pallas_call | solution.py:210
  43.2 0.2 collective-permute-start.5
  43.4 1.9 %collective-permute-done.5.refs_4_ = bf16[144,2048]{1,0:T(8,128)(2,1)S(1)} collective-permute-done((bf16[144,2048]{1,0:T(8,128)(2,1)S(1)}, bf16[144,2048]{1,0:T(8,128)(2,1)S(1)}, u32[]{:S(2)}, u32[]{:S(2)}) %collective-permute-start.5) | collective-permute-done | bytes 589856 | tf_op jit(solution)/shard_map/ppermute | solution.py:325
  45.3 0.3 shard_map.110
  45.6 0.4 collective-permute-start.6
  45.9 2.4 %shard_map.111 = (bf16[128,8192]{1,0:T(8,128)(2,1)}, bf16[128,8192]{1,0:T(8,128)(2,1)}, f32[128,256]{1,0:T(8,128)S(1)}, f32[128,256]{1,0:T(8,128)S(1)}) custom-call(bf16[128,8192]{1,0:T(8,128)(2,1)S(1)} %get-tuple-element.49.refs_0_, bf16[128,8192]{1,0:T(8,128)(2,1)S(1)} %get-tuple-element.50.refs_1_, f32[384,128]{1,0:T(8,128)S(1)} %shard_map.102.bias_ref.refs_2_, ...), custom_call_target="tpu_custom_call" | custom-call | flops 5368709120 | bytes 1 | tf_op jit(solution)/shard_map/pallas_call | solution.py:267
  48.3 6.4 %collective-permute-done.6.refs_2_.refs_7_ = bf16[144,1024]{1,0:T(8,128)(2,1)S(1)} collective-permute-done((bf16[144,1024]{1,0:T(8,128)(2,1)S(1)}, bf16[144,1024]{1,0:T(8,128)(2,1)S(1)}, u32[]{:S(2)}, u32[]{:S(2)}) %collective-permute-start.6) | collective-permute-done | bytes 294944 | tf_op jit(solution)/shard_map/ppermute | solution.py:321
  54.7 2.6 %collective-permute-start.7 = (bf16[128,1024]{1,0:T(8,128)(2,1)S(1)}, bf16[128,1024]{1,0:T(8,128)(2,1)S(1)}, u32[]{:S(2)}, u32[]{:S(2)}) collective-permute-start(bf16[128,1024]{1,0:T(8,128)(2,1)S(1)} %get-tuple-element.79), channel_id=1, source_target_pairs={{0,1},{2,3},{4,5},{6,7},{1,0},{3,2},{5,4},{7,6},{8,9},{10,11},{12,... | collective-permute-start | bytes 786440 | tf_op jit(solution)/shard_map/ppermute | solution.py:329
  57.3 0.7 collective-permute-start.8
  58.0 4.2 %shard_map.112 = (bf16[128,8192]{1,0:T(8,128)(2,1)}, bf16[128,8192]{1,0:T(8,128)(2,1)}, f32[128,512]{1,0:T(8,128)S(1)}, f32[128,512]{1,0:T(8,128)S(1)}) custom-call(bf16[128,8192]{1,0:T(8,128)(2,1)S(1)} %get-tuple-element.49.refs_0_, bf16[128,8192]{1,0:T(8,128)(2,1)S(1)} %get-tuple-element.50.refs_1_, ...), custom_call_target="tpu_custom_call", output_to_operand_aliasing={{0}: (11, {}), {1}: (12, {})} | custom-call | flops 10737418240 | bytes 1 | tf_op jit(solution)/shard_map/pallas_call | solution.py:267
  62.2 5.8 %collective-permute-done.7.refs_3_ = bf16[128,1024]{1,0:T(8,128)(2,1)S(1)} collective-permute-done((bf16[128,1024]{1,0:T(8,128)(2,1)S(1)}, bf16[128,1024]{1,0:T(8,128)(2,1)S(1)}, u32[]{:S(2)}, u32[]{:S(2)}) %collective-permute-start.7) | collective-permute-done | bytes 262176 | tf_op jit(solution)/shard_map/ppermute | solution.py:329
  67.9 0.0 collective-permute-done.8.refs_4_
  67.9 0.1 shard_map.115
  68.0 0.4 collective-permute-start.9
  68.4 2.4 %shard_map.113 = (bf16[128,8192]{1,0:T(8,128)(2,1)}, bf16[128,8192]{1,0:T(8,128)(2,1)}, f32[128,256]{1,0:T(8,128)S(1)}, f32[128,256]{1,0:T(8,128)S(1)}) custom-call(bf16[128,8192]{1,0:T(8,128)(2,1)S(1)} %get-tuple-element.49.refs_0_, bf16[128,8192]{1,0:T(8,128)(2,1)S(1)} %get-tuple-element.50.refs_1_, ...), custom_call_target="tpu_custom_call", output_to_operand_aliasing={{0}: (11, {}), {1}: (12, {})} | custom-call | flops 5368709120 | bytes 1 | tf_op jit(solution)/shard_map/pallas_call | solution.py:267
  70.8 3.9 %collective-permute-done.9.other = bf16[128,1024]{1,0:T(8,128)(2,1)S(1)} collective-permute-done((bf16[128,1024]{1,0:T(8,128)(2,1)S(1)}, bf16[128,1024]{1,0:T(8,128)(2,1)S(1)}, u32[]{:S(2)}, u32[]{:S(2)}) %collective-permute-start.9) | collective-permute-done | bytes 262176 | tf_op jit(solution)/shard_map/ppermute | solution.py:321
  74.7 1.1 %shard_map.116 = (bf16[128,1024]{1,0:T(8,128)(2,1)}, bf16[128,1024]{1,0:T(8,128)(2,1)}, f32[16,512]{1,0:T(8,128)}) custom-call(s32[6]{0:T(128)S(4)} %shard_map.101.flag.refs_0_, f32[128,1024]{1,0:T(8,128)S(1)} %get-tuple-element.75.own_key, f32[128,1024]{1,0:T(8,128)S(1)} %get-tuple-element.76.own_value, bf16[128,1024]{1,0:T(8,128)(2,1)S(1)} %get-tuple-element.82.mine, ...), custom_call_target="tpu_custom_call" | custom-call | tf_op jit(solution)/shard_map/pallas_call | solution.py:536
  (2 shorter events, 0.1 us)
Async XLA Ops:
  0.7 4.6 %copy-start = (s32[4]{0:T(128)}, s32[4]{0:T(128)S(1)}, u32[]{:S(2)}) copy-start(s32[4]{0:T(128)S(1)} %pad_add_fusion.place) | copy-start | bytes 52
  2.2 10.2 %collective-permute-start = (bf16[128,1024]{1,0:T(8,128)(2,1)S(1)}, bf16[128,1024]{1,0:T(8,128)(2,1)S(1)}, u32[]{:S(2)}, u32[]{:S(2)}) collective-permute-start(bf16[128,1024]{1,0:T(8,128)(2,1)S(1)} %shard_map.104), channel_id=1, source_target_pairs={{0,16},{8,24},{16,0},{24,8},{1,17},{9,25},{17,1},{25,9},{2,18},{10... | collective-permute-start | bytes 786440 | tf_op jit(solution)/shard_map/ppermute | solution.py:321
  6.0 0.7 copy-start.1
  12.5 12.5 %collective-permute-start.1 = (bf16[128,1024]{1,0:T(8,128)(2,1)S(1)}, bf16[128,1024]{1,0:T(8,128)(2,1)S(1)}, u32[]{:S(2)}, u32[]{:S(2)}) collective-permute-start(bf16[128,1024]{1,0:T(8,128)(2,1)S(1)} %get-tuple-element.54), channel_id=1, source_target_pairs={{0,1},{2,3},{4,5},{6,7},{1,0},{3,2},{5,4},{7,6},{8,9},{10,11},{12,... | collective-permute-start | bytes 786440 | tf_op jit(solution)/shard_map/ppermute | solution.py:329
  14.1 10.9 %collective-permute-start.2 = (bf16[128,1024]{1,0:T(8,128)(2,1)S(1)}, bf16[128,1024]{1,0:T(8,128)(2,1)S(1)}, u32[]{:S(2)}, u32[]{:S(2)}) collective-permute-start(bf16[128,1024]{1,0:T(8,128)(2,1)S(1)} %get-tuple-element.55), channel_id=1, source_target_pairs={{1,2},{3,4},{5,6},{2,1},{4,3},{6,5},{9,10},{11,12},{13,14},{10,9},... | collective-permute-start | bytes 786440 | tf_op jit(solution)/shard_map/ppermute | solution.py:329
  25.1 6.9 %collective-permute-start.3 = (bf16[128,1024]{1,0:T(8,128)(2,1)S(1)}, bf16[128,1024]{1,0:T(8,128)(2,1)S(1)}, u32[]{:S(2)}, u32[]{:S(2)}) collective-permute-start(bf16[128,1024]{1,0:T(8,128)(2,1)S(1)} %get-tuple-element.57), channel_id=1, source_target_pairs={{0,16},{8,24},{16,0},{24,8},{1,17},{9,25},{17,1},{25,9},{2,18},{10... | collective-permute-start | bytes 786440 | tf_op jit(solution)/shard_map/ppermute | solution.py:321
  32.1 2.0 %collective-permute-start.4 = (bf16[128,2048]{1,0:T(8,128)(2,1)S(1)}, bf16[128,2048]{1,0:T(8,128)(2,1)S(1)}, u32[]{:S(2)}, u32[]{:S(2)}) collective-permute-start(bf16[128,2048]{1,0:T(8,128)(2,1)S(1)} %get-tuple-element.60), channel_id=1, source_target_pairs={{0,8},{8,0},{16,24},{24,16},{1,9},{9,1},{17,25},{25,17},{2,10},{10... | collective-permute-start | bytes 1572872 | tf_op jit(solution)/shard_map/ppermute | solution.py:325
  43.2 2.1 %collective-permute-start.5 = (bf16[144,2048]{1,0:T(8,128)(2,1)S(1)}, bf16[144,2048]{1,0:T(8,128)(2,1)S(1)}, u32[]{:S(2)}, u32[]{:S(2)}) collective-permute-start(bf16[144,2048]{1,0:T(8,128)(2,1)S(1)} %shard_map.109), channel_id=1, source_target_pairs={{0,8},{8,0},{16,24},{24,16},{1,9},{9,1},{17,25},{25,17},{2,10},{10... | collective-permute-start | bytes 1769480 | tf_op jit(solution)/shard_map/ppermute | solution.py:325
  45.6 9.1 %collective-permute-start.6 = (bf16[144,1024]{1,0:T(8,128)(2,1)S(1)}, bf16[144,1024]{1,0:T(8,128)(2,1)S(1)}, u32[]{:S(2)}, u32[]{:S(2)}) collective-permute-start(bf16[144,1024]{1,0:T(8,128)(2,1)S(1)} %get-tuple-element.69.refs_11_.refs_13_), channel_id=1, source_target_pairs={{0,16},{8,24},{16,0},{24,8},{1,17},{9,25},{17,1},{25,9},{2,18},{10... | collective-permute-start | bytes 884744 | tf_op jit(solution)/shard_map/ppermute | solution.py:321
  54.7 13.2 %collective-permute-start.7 = (bf16[128,1024]{1,0:T(8,128)(2,1)S(1)}, bf16[128,1024]{1,0:T(8,128)(2,1)S(1)}, u32[]{:S(2)}, u32[]{:S(2)}) collective-permute-start(bf16[128,1024]{1,0:T(8,128)(2,1)S(1)} %get-tuple-element.79), channel_id=1, source_target_pairs={{0,1},{2,3},{4,5},{6,7},{1,0},{3,2},{5,4},{7,6},{8,9},{10,11},{12,... | collective-permute-start | bytes 786440 | tf_op jit(solution)/shard_map/ppermute | solution.py:329
  57.3 10.7 %collective-permute-start.8 = (bf16[128,1024]{1,0:T(8,128)(2,1)S(1)}, bf16[128,1024]{1,0:T(8,128)(2,1)S(1)}, u32[]{:S(2)}, u32[]{:S(2)}) collective-permute-start(bf16[128,1024]{1,0:T(8,128)(2,1)S(1)} %get-tuple-element.80), channel_id=1, source_target_pairs={{1,2},{3,4},{5,6},{2,1},{4,3},{6,5},{9,10},{11,12},{13,14},{10,9},... | collective-permute-start | bytes 786440 | tf_op jit(solution)/shard_map/ppermute | solution.py:329
  68.0 6.7 %collective-permute-start.9 = (bf16[128,1024]{1,0:T(8,128)(2,1)S(1)}, bf16[128,1024]{1,0:T(8,128)(2,1)S(1)}, u32[]{:S(2)}, u32[]{:S(2)}) collective-permute-start(bf16[128,1024]{1,0:T(8,128)(2,1)S(1)} %get-tuple-element.83), channel_id=1, source_target_pairs={{0,16},{8,24},{16,0},{24,8},{1,17},{9,25},{17,1},{25,9},{2,18},{10... | collective-permute-start | bytes 786440 | tf_op jit(solution)/shard_map/ppermute | solution.py:321

commit v3 on v2

--- a/solution.py
+++ b/solution.py
@@ -15,10 +15,10 @@
 SCALE = 1.0 / math.sqrt(WIDTH)
 MASKED = -1e30
 CONTEXT = ("inner", "outer")
-CHUNKS = 1
+CHUNKS = 2
 UNROLL = 2
 EXTRA = 16
-BEHIND = (2, 4, 2)
+BEHIND = ((2, 2), (2, 2))
 LOG2E = math.log2(math.e)
 VMEM_SMALL = 8 * 2**20
 VMEM_LARGE = 16 * 2**20
@@ -44,13 +44,29 @@
     return jnp.concatenate([bias] * GROUP, axis=1)
 
 
-def own_kernel(bias_ref, *refs):
+def row_sums(g, at, q_ref, do_ref, k_ref, v_ref, bias, stat_ref):
+    s = dot(k_ref[:, lanes(g)], group_rows(q_ref, g), NT) + tiled(bias)
+    dp = dot(v_ref[:, lanes(g)], group_rows(do_ref, g), NT)
+    top = jnp.max(s, axis=0, keepdims=True)
+    t = (s - top) * (SCALE * LOG2E)
+    e = jnp.exp2(t)
+    stat_ref[at, 0:1, :] = top
+    stat_ref[at, 1:2, :] = jnp.sum(e, axis=0, keepdims=True)
+    stat_ref[at, 2:3, :] = jnp.sum(e * t, axis=0, keepdims=True)
+    stat_ref[at, 3:4, :] = jnp.sum(e * dp, axis=0, keepdims=True)
+
+
+def first_kernel(contexts, count, place, *refs):
     sources, refs = refs[:4], refs[4:]
-    loaded, (stat_ref, sems) = refs[:4], refs[4:]
+    spans_far, docs_far, refs = refs[0], refs[1], refs[2:]
+    loaded, (flag, bias_ref, stat_ref, sems, spans, docs) = refs[:4], refs[4:]
     q_ref, do_ref, k_ref, v_ref = loaded
     rows = q_ref.shape[0]
-    last = bias_ref.shape[0] - rows
     heads = k_ref.shape[1] // WIDTH
+    short = [
+        pltpu.make_async_copy(spans_far, spans, sems.at[2, 1]),
+        pltpu.make_async_copy(docs_far, docs, sems.at[3, 1]),
+    ]
     narrow = [pltpu.make_async_copy(sources[i], loaded[i], sems.at[i, 0]) for i in (2, 3)]
 
     def wide(g):
@@ -60,27 +76,56 @@
             for i in (0, 1)
         ]
 
-    copies = narrow + [copy for g in range(heads) for copy in wide(g)]
+    copies = short + narrow + [copy for g in range(heads) for copy in wide(g)]
     for copy in copies:
         copy.start()
+    for copy in short:
+        copy.wait()
+    span = spans[2 * place[0] + place[1]]
+    subs = bias_ref.shape[0] // rows - 1
+    first = (span * subs + place[2]) * rows
+    flag[0] = first
+    for index in (1, 2):
+        flag[index] = place[index]
+    flag[3] = (span == place[0]).astype(jnp.int32)
+    flag[4] = place[3]
+    flag[5] = (place[0] == contexts - 1).astype(jnp.int32)
+    q_pos = first + lax.broadcasted_iota(jnp.int32, (1, rows), 1)
+    at = jnp.int32(0)
+    start = jnp.zeros((1, rows), jnp.int32)
+
+    def later(index, carry):
+        at, start = carry
+        return at + docs[index], jnp.where(at <= q_pos, at, start)
+
+    _, start = lax.fori_loop(0, docs.shape[0], later, (at, start))
+    window = bias_ref.shape[0]
+    k_pos = first + rows - window + lax.broadcasted_iota(jnp.int32, (window, rows), 0)
+    bias = jnp.where((k_pos >= start) & (k_pos <= q_pos), 0.0, MASKED)
+    bias_ref[...] = bias
     for copy in narrow:
         copy.wait()
 
     def step(g, _):
         for copy in wide(g):
             copy.wait()
-        s = dot(k_ref[:, lanes(g)], group_rows(q_ref, g), NT) + tiled(bias_ref[last:, :])
-        dp = dot(v_ref[:, lanes(g)], group_rows(do_ref, g), NT)
-        top = jnp.max(s, axis=0, keepdims=True)
-        t = (s - top) * (SCALE * LOG2E)
-        e = jnp.exp2(t)
-        stat_ref[g, 0:1, :] = top
-        stat_ref[g, 1:2, :] = jnp.sum(e, axis=0, keepdims=True)
-        stat_ref[g, 2:3, :] = jnp.sum(e * t, axis=0, keepdims=True)
-        stat_ref[g, 3:4, :] = jnp.sum(e * dp, axis=0, keepdims=True)
+        row_sums(g, g, q_ref, do_ref, k_ref, v_ref, bias_ref[window - rows :, :], stat_ref)
         return 0
 
-    lax.fori_loop(0, heads, step, 0)
+    lax.fori_loop(0, count, step, 0)
+    for g in range(count, heads):
+        for copy in wide(g):
+            copy.wait()
+
+
+def sums_kernel(start, count, q_ref, do_ref, k_ref, v_ref, bias_ref, stat_ref):
+    last = bias_ref.shape[0] - q_ref.shape[0]
+
+    def step(at, _):
+        row_sums(start + at, at, q_ref, do_ref, k_ref, v_ref, bias_ref[last:, :], stat_ref)
+        return 0
+
+    lax.fori_loop(0, count, step, 0)
 
 
 def earlier_kernel(start, count, near, q_ref, do_ref, bias_ref, first_k, first_v, *refs):
@@ -102,7 +147,7 @@
         q_all, do_all = group_rows(q_ref, g), group_rows(do_ref, g)
         s = dot(k_rows, q_all, NT) + tiled(bias_ref[:window, :])
         dp = dot(v_rows, do_all, NT)
-        own_top, own_total = stat_ref[g, 0:1, :], stat_ref[g, 1:2, :]
+        own_top, own_total = stat_ref[at, 0:1, :], stat_ref[at, 1:2, :]
         top = jnp.maximum(jnp.max(s, axis=0, keepdims=True), own_top)
         t = (s - top) * (SCALE * LOG2E)
         e = jnp.exp2(t)
@@ -110,12 +155,12 @@
         ratio = jnp.exp2(shift)
         total = own_total * ratio + jnp.sum(e, axis=0, keepdims=True)
         inv = 1.0 / total
-        spread = (stat_ref[g, 2:3, :] + shift * own_total) * ratio
+        spread = (stat_ref[at, 2:3, :] + shift * own_total) * ratio
         spread = spread + jnp.sum(e * t, axis=0, keepdims=True)
         entropy = jnp.log(total) - spread * inv * math.log(2.0)
         for h in range(GROUP):
             ent_ref[at, h : h + 1, :] = entropy[:, h * rows : (h + 1) * rows]
-        delta = stat_ref[g, 3:4, :] * ratio + jnp.sum(e * dp, axis=0, keepdims=True)
+        delta = stat_ref[at, 3:4, :] * ratio + jnp.sum(e * dp, axis=0, keepdims=True)
         delta = delta * inv
         row_ref[at, 0:1, :] = top * (SCALE * LOG2E) + jnp.log2(total)
         row_ref[at, 1:2, :] = delta
@@ -221,19 +266,39 @@
     return pltpu.with_memory_space_constraint(value, pltpu.HBM)
 
 
-def own_sums(bias, *arrays):
+def first_step(contexts, subs, count, place, arrays, spans, docs, behind):
     rows = arrays[0].shape[0]
     heads = arrays[2].shape[1] // WIDTH
-    return pl.pallas_call(
-        own_kernel,
-        in_specs=whole(1) + whole(4, pl.ANY),
-        out_specs=whole(5),
+
+    def kernel(place, *refs):
+        first_kernel(contexts, count, place, *refs[:6], *refs[7:])
+
+    results = pl.pallas_call(
+        kernel,
+        in_specs=whole(1, pltpu.SMEM) + whole(7, pl.ANY),
+        out_specs=whole(4) + whole(1, pltpu.SMEM) + whole(2),
         out_shape=[pltpu.VMEM(array.shape, array.dtype) for array in arrays]
-        + [pltpu.VMEM((heads, 8, GROUP * rows), jnp.float32)],
-        scratch_shapes=[pltpu.SemaphoreType.DMA((4, heads))],
+        + [
+            pltpu.SMEM((6,), jnp.int32),
+            pltpu.VMEM(((subs + 1) * rows, rows), jnp.float32),
+            pltpu.VMEM((count, 8, GROUP * rows), jnp.float32),
+        ],
+        scratch_shapes=[
+            pltpu.SemaphoreType.DMA((4, heads)),
+            pltpu.SMEM(spans.shape, jnp.int32),
+            pltpu.SMEM(docs.shape, jnp.int32),
+        ],
         compiler_params=pltpu.CompilerParams(vmem_limit_bytes=VMEM_LARGE),
-        cost_estimate=cost(heads, rows, 2),
-    )(near_by(bias), *[far(array) for array in arrays])
+        cost_estimate=cost(count, rows, 3),
+    )(place, *[far(array) for array in (*arrays, spans, docs)], behind)
+    return results[4], results[:2], results[2:4], results[5], results[6]
+
+
+def more_sums(wide, own, bias, start, count, behind=()):
+    rows = wide[0].shape[0]
+    kernel = functools.partial(sums_kernel, start, count)
+    outs = [((count, 8, GROUP * rows), jnp.float32)]
+    return large(kernel, [*wide, *own, bias], outs, cost(count, rows, 2), behind)[0]
 
 
 def earlier_terms(queries, dout, bias, before, near, stats, start, behind=()):
@@ -299,21 +364,6 @@
     context = lax.axis_index(CONTEXT)
     place = jnp.stack([context, side, sub, context % 2]).astype(jnp.int32)
 
-    def place_flags(place, spans, flag):
-        span = spans[2 * place[0] + place[1]]
-        flag[0] = (span * subs + place[2]) * rows
-        for index in (1, 2):
-            flag[index] = place[index]
-        flag[3] = (span == place[0]).astype(jnp.int32)
-        flag[4] = place[3]
-        flag[5] = (place[0] == contexts - 1).astype(jnp.int32)
-
-    flags = pl.pallas_call(
-        place_flags,
-        in_specs=whole(2, pltpu.SMEM),
-        out_specs=whole(1, pltpu.SMEM)[0],
-        out_shape=pltpu.SMEM((6,), jnp.int32),
-    )(place, span_order)
     width = keys.shape[1] // CHUNKS
     half = ((rows, width), jnp.bfloat16)
 
@@ -328,62 +378,52 @@
         pairs = [(c, c + 1) for c in range(start, contexts - 1, 2)]
         return lax.ppermute(value, CONTEXT, pairs + [(b, a) for a, b in pairs])
 
+    def columns(chunk):
+        return slice(chunk * width, (chunk + 1) * width)
+
     def pick_in(place, keys, values, give, sem):
         for flag, source in ((0, values), (1, keys)):
 
             @pl.when(place[1] == flag)
             def _(source=source):
-                copy = pltpu.make_async_copy(source, give, sem)
+                copy = pltpu.make_async_copy(source.at[:, columns(0)], give, sem)
                 copy.start()
                 copy.wait()
 
-    give = pl.pallas_call(
+    first_give = pl.pallas_call(
         pick_in,
         in_specs=whole(1, pltpu.SMEM) + whole(2, pl.ANY),
         out_specs=whole(1)[0],
-        out_shape=pltpu.VMEM(keys.shape, keys.dtype),
+        out_shape=pltpu.VMEM(*half),
         scratch_shapes=[pltpu.SemaphoreType.DMA],
         compiler_params=pltpu.CompilerParams(vmem_limit_bytes=VMEM_SMALL),
     )(place, far(keys), far(values))
 
-    def mask(flag, doc_ref, bias_ref):
-        first = flag[0]
-        window = bias_ref.shape[0]
-        q_pos = first + lax.broadcasted_iota(jnp.int32, (1, rows), 1)
-
-        def step(index, carry):
-            at, start = carry
-            return at + doc_ref[index], jnp.where(at <= q_pos, at, start)
-
-        _, start = lax.fori_loop(
-            0, doc_ref.shape[0], step, (jnp.int32(0), jnp.zeros((1, rows), jnp.int32))
-        )
-        k_pos = first + rows - window + lax.broadcasted_iota(jnp.int32, (window, rows), 0)
-        bias_ref[...] = jnp.where((k_pos >= start) & (k_pos <= q_pos), 0.0, MASKED)
-
-    bias = pl.pallas_call(
-        mask,
-        in_specs=whole(2, pltpu.SMEM),
-        out_specs=whole(1)[0],
-        out_shape=pltpu.VMEM(((subs + 1) * rows, rows), jnp.float32),
-        compiler_params=pltpu.CompilerParams(vmem_limit_bytes=VMEM_SMALL),
-    )(in_scalars(flags), doc_lengths)
+    def later_give(own, chunk, behind):
+        def kernel(flag, key, value, give):
+            for which, source in ((0, value), (1, key)):
+
+                @pl.when(flag[1] == which)
+                def _(source=source):
+                    give[...] = source[:, columns(chunk)]
+
+        return small(kernel, flags, own, [half], behind)[0]
 
     def out_of_step(flag, backward):
         return (flag[3] + flag[4] + (1 if backward else 0)) % 2
 
-    def edge_parts(own, got, backward, behind=()):
+    def edge_parts(own, got, backward, cols=slice(None), behind=()):
         def kernel(flag, *refs):
             own, (got, even, odd) = refs[:-3], refs[-3:]
             for which, keep in enumerate(own):
 
                 @pl.when((flag[1] == which) | (len(own) == 1))
                 def _(keep=keep):
-                    route(out_of_step(flag, backward), keep, got.at[:rows], even, odd)
+                    route(out_of_step(flag, backward), keep.at[:, cols], got.at[:rows], even, odd)
 
         return small(kernel, flags, [*own, got], [half, half], behind)
 
-    def edge_done(own, got, even, odd, backward, behind=()):
+    def edge_done(own, got, even, odd, backward, cols=slice(None), behind=()):
         def kernel(flag, *refs):
             own, (got, even, odd, mine, theirs) = refs[:-5], refs[-5:]
             takes_odd = (flag[3] + flag[4]) % 2
@@ -399,7 +439,7 @@
 
                 @pl.when((flag[5] != 0) & (kept != 0) & ((flag[1] == which) | (len(own) == 1)))
                 def _(keep=keep):
-                    route(takes_odd, keep, even, mine, theirs)
+                    route(takes_odd, keep.at[:, cols], even, mine, theirs)
 
             @pl.when((flag[5] != 0) & (kept == 0))
             def _():
@@ -407,7 +447,7 @@
 
         return small(kernel, flags, [*own, got, even, odd], [half, half], behind)
 
-    def window_parts(own, mine, other, behind=()):
+    def window_parts(own, mine, other, cols, behind=()):
         def kernel(flag, own_key, own_value, mine, other, key, value, *sent):
             route(flag[1], other, mine, key, value)
             for index, out in enumerate(sent):
@@ -415,8 +455,8 @@
 
                 @pl.when(inside)
                 def _():
-                    out[:, :width] = own_key[...]
-                    out[:, width:] = own_value[...]
+                    out[:, :width] = own_key[:, cols]
+                    out[:, width:] = own_value[:, cols]
 
                 @pl.when(jnp.logical_not(inside))
                 def _():
@@ -436,32 +476,37 @@
             block = jnp.concatenate([block, fill], axis=0)
         high = block.astype(jnp.bfloat16)
         out[rows:, lo : lo + rows] = high
-        lo += WIDTH
+        lo += rows
         out[rows:, lo : lo + rows] = (block - high.astype(jnp.float32)).astype(jnp.bfloat16)
 
     def one_part(ref, lo):
-        high, low = ref[rows:, lo : lo + rows], ref[rows:, lo + WIDTH : lo + WIDTH + rows]
+        high, low = ref[rows:, lo : lo + rows], ref[rows:, lo + rows : lo + 2 * rows]
         return high.astype(jnp.float32) + low.astype(jnp.float32)
 
-    def near_terms(dk, dv, entropies):
-        def kernel(flag, ent, *refs):
+    def near_terms(dk, dv, entropies=(), behind=()):
+        extra = EXTRA if entropies else 0
+
+        def kernel(flag, *refs):
+            ents, refs = refs[: len(entropies)], refs[len(entropies) :]
             for index in range(subs - 1):
                 out = refs[2 * (subs - 1) + index]
                 out[:rows, :width] = refs[index][...]
                 out[:rows, width:] = refs[subs - 1 + index][...]
                 to = lax.rem(flag[2] + index + 1, subs)
-                for which in range(2):
-                    block = ent[pl.ds((which * subs + to) * per_device, per_device)]
-                    two_parts(out, 2 * which * WIDTH, block)
-
-        both = ((rows + EXTRA, 2 * width), jnp.bfloat16)
-        outs = small(kernel, flags, [entropies, *dk[1:], *dv[1:]], [both] * (subs - 1))
+                for which, ent in enumerate(ents):
+                    two_parts(out, 2 * which * rows, ent[pl.ds(to * per_device, per_device)])
+
+        both = ((rows + extra, 2 * width), jnp.bfloat16)
+        outs = small(kernel, flags, [*entropies, *dk[1:], *dv[1:]], [both] * (subs - 1), behind)
         return [around(out, index + 1 - subs) for index, out in enumerate(outs)]
 
-    def collect(dk, dv, entropies, arrived, behind=()):
-        def kernel(flag, dk, dv, ent, *refs):
+    def collect(dk, dv, arrived, entropies=(), behind=()):
+        extra = EXTRA if entropies else 0
+
+        def kernel(flag, dk, dv, *refs):
+            ents, refs = refs[: len(entropies)], refs[len(entropies) :]
             got = refs[: subs - 1]
-            keep, give, own_key, own_value, ent_out = refs[subs - 1 :]
+            keep, give, own_key, own_value = refs[subs - 1 : subs + 3]
             for which, term, own in ((0, dk, own_key), (1, dv, own_value)):
                 before = term[...].astype(jnp.float32)
                 mine = jnp.zeros_like(before)
@@ -481,52 +526,55 @@
                 def _():
                     give[:rows, :] = before
 
-            for which in range(2):
-                block = ent[pl.ds((which * subs + flag[2]) * per_device, per_device)]
+            for which, ent in enumerate(ents):
+                block = ent[pl.ds(flag[2] * per_device, per_device)]
                 blocks = [block.reshape(-1, rows)]
-                blocks += [one_part(ref, 2 * which * WIDTH)[: blocks[0].shape[0]] for ref in got]
+                blocks += [one_part(ref, 2 * which * rows)[: blocks[0].shape[0]] for ref in got]
 
                 @pl.when(flag[1] == which)
                 def _(blocks=blocks):
                     for index, block in enumerate(blocks):
-                        ent_out[index] = block
+                        refs[subs + 3][index] = block
 
                 @pl.when(flag[1] != which)
                 def _(blocks=blocks):
                     for index, block in enumerate(blocks):
-                        two_parts(give, 2 * index * WIDTH, block)
+                        two_parts(give, 2 * index * rows, block)
 
         full = ((rows, width), jnp.float32)
-        kept = ((subs, per_device * GROUP, rows), jnp.float32)
-        given = ((rows + EXTRA, width), jnp.bfloat16)
-        inputs = [dk[0], dv[0], entropies, *arrived]
-        return small(kernel, flags, inputs, [half, given, full, full, kept], behind)
-
-    def finish(own_key, own_value, pieces, mine, other, entropies, got):
-        spots = [0]
-        for dk, dv in pieces:
-            spots.append(spots[-1] + dk.shape[1])
-        local = [own_key, own_value, mine, other, *[term for piece in pieces for term in piece]]
-        local += [entropies, got]
+        outs = [half, ((rows + extra, width), jnp.bfloat16), full, full]
+        if entropies:
+            outs.append(((subs, per_device * GROUP, rows), jnp.float32))
+        return small(kernel, flags, [dk[0], dv[0], *entropies, *arrived], outs, behind)
+
+    def finish(chunks, entropies, got):
+        local, plans = [entropies, got], []
+        for chunk, (own_key, own_value, pieces, mine, other) in enumerate(chunks):
+            spot = 0
+            for dk, dv in pieces:
+                cols = slice(spot, spot + dk.shape[1])
+                plans.append((len(local), cols, slice(cols.start + chunk * width, cols.stop + chunk * width)))
+                local += [own_key, own_value, mine, other, dk, dv]
+                spot = cols.stop
         count = per_device * GROUP
 
-        def kernel(flag, own_key, own_value, mine, other, *refs):
-            terms, refs = refs[: 2 * len(pieces)], refs[2 * len(pieces) :]
-            ent, got, out_key, out_value, out_ent = refs
+        def kernel(flag, *refs):
+            ent, got = refs[:2]
+            out_key, out_value, out_ent = refs[-3:]
             is_key = flag[1] == 0
-            for index in range(len(pieces)):
-                cols = slice(spots[index], spots[index + 1])
+            for at, cols, to in plans:
+                own_key, own_value, mine, other, dk, dv = refs[at : at + 6]
                 here = mine[:, cols].astype(jnp.float32)
                 there = other[:, cols].astype(jnp.float32)
                 for out, own, term, back in (
-                    (out_key, own_key, terms[2 * index], jnp.where(is_key, here, there)),
-                    (out_value, own_value, terms[2 * index + 1], jnp.where(is_key, there, here)),
+                    (out_key, own_key, dk, jnp.where(is_key, here, there)),
+                    (out_value, own_value, dv, jnp.where(is_key, there, here)),
                 ):
-                    out[:, cols] = (own[:, cols] + term[...] + back).astype(jnp.bfloat16)
+                    out[:, to] = (own[:, cols] + term[...] + back).astype(jnp.bfloat16)
             for index in range(subs):
                 steps = 0 if index == 0 else subs - index
                 source = lax.rem(flag[2] + steps, subs)
-                for way, block in ((flag[1], ent[index]), (1 - flag[1], one_part(got, 2 * index * WIDTH))):
+                for way, block in ((flag[1], ent[index]), (1 - flag[1], one_part(got, 2 * index * rows))):
                     for spot in range(size):
 
                         @pl.when(way * subs + source == spot)
@@ -537,41 +585,73 @@
             kernel,
             grid=(1,),
             in_specs=whole(1, pltpu.SMEM) + whole(len(local)),
-            out_specs=[pl.BlockSpec((rows, width), lambda g: (0, 0))] * 2
+            out_specs=[pl.BlockSpec(keys.shape, lambda g: (0, 0))] * 2
             + [pl.BlockSpec((count, size * rows), lambda g: (0, 0))],
             out_shape=[jax.ShapeDtypeStruct(keys.shape, jnp.bfloat16)] * 2
             + [jax.ShapeDtypeStruct((count, size * rows), jnp.float32)],
             compiler_params=pltpu.CompilerParams(vmem_limit_bytes=VMEM_SMALL),
         )(in_scalars(flags), *[near_by(v) for v in local])
 
-    def travel(keep, got, backward, behind=()):
-        even, odd = edge_parts(keep, got, backward, behind)
-        return edges(even, 0), edges(odd, 1)
-
-    def land(keep, got, even, odd, backward, behind=()):
-        mine, theirs = edge_done(keep, got, even, odd, backward, behind)
-        return mine, across(theirs)
-
-    got = across(give)
-    q_near, do_near, *own, stats = own_sums(bias, queries, dout, keys, values)
-    even, odd = travel(own, got, False, [stats])
-    mine, other = land(own, got, even, odd, False)
-    before, near = window_parts(own, mine, other)
-    entropies, kept, dk, dv = earlier_terms(q_near, do_near, bias, before, near, stats, 0)
-    arrived = near_terms(dk, dv, entropies)
-    keep, give, own_key, own_value, entropies = collect(dk, dv, entropies, arrived)
-    got = across(give)
-    wide, pieces, done = [], [], 0
-    for count in BEHIND:
-        wide, piece = the_rest(
-            q_near, do_near, bias, before, near, own, kept, 0, done, count, wide, [give]
+    def over(parts):
+        odd = edges(parts[1], 1)
+        return edges(parts[0], 0), odd
+
+    per_chunk = KEY_VALUE_HEADS // CHUNKS
+    got = [across(first_give)]
+    flags, wide_near, own, bias, stats = first_step(
+        contexts, subs, per_chunk, place, (queries, dout, keys, values), span_order, doc_lengths, first_give
+    )
+    got.append(across(later_give(own, 1, got)))
+    cols = [columns(chunk) for chunk in range(CHUNKS)]
+    in0 = edge_parts(own, got[0], False, cols[0], [stats])
+    edge0 = over(in0)
+    in1 = edge_parts(own, got[1], False, cols[1])
+    edge1 = over(in1)
+    stats = [stats, more_sums(wide_near, own, bias, per_chunk, per_chunk, in1[:1])]
+    mine0, theirs0 = edge_done(own, got[0], *edge0, False, cols[0], stats[1:])
+    other0 = across(theirs0)
+    mine1, theirs1 = edge_done(own, got[1], *edge1, False, cols[1], [theirs0])
+    other1 = across(theirs1)
+    before0, near0 = window_parts(own, mine0, other0, cols[0], [theirs1])
+    ent0, kept0, dk0, dv0 = earlier_terms(*wide_near, bias, before0, near0, stats[0], 0)
+    before1, near1 = window_parts(own, mine1, other1, cols[1], [ent0])
+    keep0, give0, *own0 = collect(dk0, dv0, near_terms(dk0, dv0))
+    back0 = across(give0)
+    ent1, kept1, dk1, dv1 = earlier_terms(
+        *wide_near, bias, before1, near1, stats[1], per_chunk, [give0]
+    )
+    out0 = edge_parts([keep0], back0, True)
+    edge0 = over(out0)
+    ents = [ent0, ent1]
+    keep1, give1, *own1, entropies = collect(
+        dk1, dv1, near_terms(dk1, dv1, ents, out0[:1]), ents
+    )
+    back1 = across(give1)
+    wide, pieces = [], []
+
+    def rest(chunk, piece, behind):
+        nonlocal wide
+        before, near, kept = ((before0, near0, kept0), (before1, near1, kept1))[chunk]
+        skip, count = sum(BEHIND[chunk][:piece]), BEHIND[chunk][piece]
+        start = chunk * per_chunk
+        wide, terms = the_rest(
+            *wide_near, bias, before, near, own, kept, start, skip, count, wide, behind
         )
-        pieces.append(piece)
-        done += count
-    even, odd = travel([keep], got, True, pieces[0][:1])
-    mine, other = land([keep], got, even, odd, True, pieces[1][:1])
+        pieces.append(terms)
+        return terms[:1]
+
+    done = rest(0, 0, [give1])
+    out1 = edge_parts([keep1], back1, True, behind=done)
+    edge1 = over(out1)
+    done = rest(0, 1, out1[:1])
+    mine0, theirs0 = edge_done([keep0], back0, *edge0, True, behind=done)
+    other0 = across(theirs0)
+    done = rest(1, 0, [theirs0, *edge1])
+    mine1, theirs1 = edge_done([keep1], back1, *edge1, True, behind=done)
+    other1 = across(theirs1)
+    rest(1, 1, [theirs1])
     grad_key, grad_value, entropy = finish(
-        own_key, own_value, pieces, mine, other, entropies, got
+        [(*own0, pieces[:2], mine0, other0), (*own1, pieces[2:], mine1, other1)], entropies, back1
     )
     return wide[0], entropy.T, wide[1], grad_key, grad_value
 

time: 75.9 us -> 68.2 us (0.90)
  waiting for transfers between devices: 36.4 us -> 12.3 us
  starting transfers between devices: 10.1 us -> 27.2 us
    ppermute x4 -> x8, waiting for transfers between devices: 16 us -> 1.99 us  [edges(): return lax.ppermute(value, CONTEXT, pairs + [(b, a) for a, b in pairs])]
    ppermute x4 -> x8, starting transfers between devices: 5.44 us -> 15.5 us  [edges(): return lax.ppermute(value, CONTEXT, pairs + [(b, a) for a, b in pairs])]
    ppermute x4 -> x8, waiting for transfers between devices: 16.6 us -> 8.14 us  [across(): lax.ppermute(value, 'head', [(j, (j + subs) % size) for j in range(size)])]
    ppermute x4 -> x8, starting transfers between devices: 4.34 us -> 11 us  [across(): lax.ppermute(value, 'head', [(j, (j + subs) % size) for j in range(size)])]
    pallas_call x3 -> x1, Pallas kernels: 6.47 us -> 3.79 us  [first_step(): pl.pallas_call(kernel, in_specs=whole(1, pltpu.SMEM) + whole(7, pl.ANY),...]
    pallas_call x1 -> x3, Pallas kernels: 9.14 us -> 10.9 us  [large(): pl.pallas_call(body, in_specs=whole(len(inputs)) + whole(len(behind), pl....]
    ppermute x2 -> x4, waiting for transfers between devices: 3.76 us -> 2.16 us  [around(): return lax.ppermute(value, 'head', pairs)]
    pallas_call x3 -> x4, Pallas kernels: 8.99 us -> 9.63 us  [the_rest(): pl.pallas_call(kernel, grid=(count,), in_specs=whole(len(inputs)) + whole...]
  transfers between devices with their start and end apart: 10 -> 20, of which waited for: 7 -> 9; matrix products, arithmetic and copies ran while one was open for 0% -> 0% of each run, Pallas kernels for 20% -> 37%
where the time goes in v3:
time: 68.2 us; the launch traced here: 68 us
  Pallas kernels  27.5 us (40%)
  starting transfers between devices  27.2 us (40%)
  waiting for transfers between devices  12.3 us (18%)
  between operations  0.91 us (1%)
    ppermute x8, starting transfers between devices, edges(): return lax.ppermute(value, CONTEXT, pairs + [(b, a) for a, b in pairs])  15.5 us
    ppermute x8, starting transfers between devices, across(): lax.ppermute(value, 'head', [(j, (j + subs) % size) for j in range(size)])  11 us
    pallas_call x3, Pallas kernels, large(): pl.pallas_call(body, in_specs=whole(len(inputs)) + whole(len(behind), pl....  10.9 us
    pallas_call x4, Pallas kernels, the_rest(): pl.pallas_call(kernel, grid=(count,), in_specs=whole(len(inputs)) + whole...  9.63 us
    ppermute x8, waiting for transfers between devices, across(): lax.ppermute(value, 'head', [(j, (j + subs) % size) for j in range(size)])  8.14 us
    pallas_call x1, Pallas kernels, first_step(): pl.pallas_call(kernel, in_specs=whole(1, pltpu.SMEM) + whole(7, pl.ANY),...  3.79 us
    ppermute x4, waiting for transfers between devices, around(): return lax.ppermute(value, 'head', pairs)  2.16 us
    ppermute x8, waiting for transfers between devices, edges(): return lax.ppermute(value, CONTEXT, pairs + [(b, a) for a, b in pairs])  1.99 us
  transfers between devices with their start and end apart: 20, of which 9 were waited for; matrix products, arithmetic and copies ran while one was open for 0% of the time, Pallas kernels for 37%

profile of v3, /device:TPU:0, one launch (start us, length us, event | category | flops | bytes accessed | tf_op | source)
XLA Modules:
  0.0 68.0 jit_solution(14539095847093515182)
XLA Ops:
  0.7 0.1 pad_add_fusion.place
  0.7 1.5 %shard_map.101.refs_6_ = bf16[128,512]{1,0:T(8,128)(2,1)S(1)} custom-call(s32[4]{0:T(128)S(1)} %pad_add_fusion.place, bf16[128,1024]{1,0:T(8,128)(2,1)} %refs_2_.1, bf16[128,1024]{1,0:T(8,128)(2,1)} %refs_3_.1), custom_call_target="tpu_custom_call" | custom-call | tf_op jit(solution)/shard_map/pallas_call | solution.py:393
  2.2 3.0 %collective-permute-start = (bf16[128,512]{1,0:T(8,128)(2,1)S(1)}, bf16[128,512]{1,0:T(8,128)(2,1)S(1)}, u32[]{:S(2)}, u32[]{:S(2)}) collective-permute-start(bf16[128,512]{1,0:T(8,128)(2,1)S(1)} %shard_map.101.refs_6_), channel_id=1, source_target_pairs={{0,16},{8,24},{16,0},{24,8},{1,17},{9,25},{17,1},{25,9},{2,18},{10... | collective-permute-start | bytes 393224 | tf_op jit(solution)/shard_map/ppermute | solution.py:371
  5.2 3.8 %shard_map.102 = (bf16[128,8192]{1,0:T(8,128)(2,1)S(1)}, bf16[128,8192]{1,0:T(8,128)(2,1)S(1)}, bf16[128,1024]{1,0:T(8,128)(2,1)S(1)}, bf16[128,1024]{1,0:T(8,12...) custom-call(s32[4]{0:T(128)S(1)} %pad_add_fusion.place, bf16[128,8192]{1,0:T(8,128)(2,1)} %refs_0_.1, ...), custom_call_target="tpu_custom_call" | custom-call | flops 3221225472 | bytes 1 | tf_op jit(solution)/shard_map/pallas_call | solution.py:276
  9.0 0.0 collective-permute-done.refs_3_
  9.1 1.5 %collective-permute-start.1 = (bf16[128,512]{1,0:T(8,128)(2,1)S(1)}, bf16[128,512]{1,0:T(8,128)(2,1)S(1)}, u32[]{:S(2)}, u32[]{:S(2)}) collective-permute-start(bf16[128,512]{1,0:T(8,128)(2,1)S(1)} %shard_map.103), channel_id=1, source_target_pairs={{0,16},{8,24},{16,0},{24,8},{1,17},{9,25},{17,1},{25,9},{2,18},{10... | collective-permute-start | bytes 393224 | tf_op jit(solution)/shard_map/ppermute | solution.py:371
  10.6 1.6 %collective-permute-start.4 = (bf16[128,512]{1,0:T(8,128)(2,1)S(1)}, bf16[128,512]{1,0:T(8,128)(2,1)S(1)}, u32[]{:S(2)}, u32[]{:S(2)}) collective-permute-start(bf16[128,512]{1,0:T(8,128)(2,1)S(1)} %get-tuple-element.87), channel_id=1, source_target_pairs={{0,1},{2,3},{4,5},{6,7},{1,0},{3,2},{5,4},{7,6},{8,9},{10,11},{12,... | collective-permute-start | bytes 393224 | tf_op jit(solution)/shard_map/ppermute | solution.py:379
  12.1 0.7 collective-permute-start.5
  12.8 1.3 %collective-permute-done.1.refs_3_ = bf16[128,512]{1,0:T(8,128)(2,1)S(1)} collective-permute-done((bf16[128,512]{1,0:T(8,128)(2,1)S(1)}, bf16[128,512]{1,0:T(8,128)(2,1)S(1)}, u32[]{:S(2)}, u32[]{:S(2)}) %collective-permute-start.1) | collective-permute-done | bytes 131104 | tf_op jit(solution)/shard_map/ppermute | solution.py:371
  14.1 0.7 collective-permute-start.3
  14.8 4.7 %collective-permute-start.2 = (bf16[128,512]{1,0:T(8,128)(2,1)S(1)}, bf16[128,512]{1,0:T(8,128)(2,1)S(1)}, u32[]{:S(2)}, u32[]{:S(2)}) collective-permute-start(bf16[128,512]{1,0:T(8,128)(2,1)S(1)} %get-tuple-element.84.refs_5_), channel_id=1, source_target_pairs={{0,1},{2,3},{4,5},{6,7},{1,0},{3,2},{5,4},{7,6},{8,9},{10,11},{12,... | collective-permute-start | bytes 393224 | tf_op jit(solution)/shard_map/ppermute | solution.py:379
  19.6 1.7 %shard_map.106.refs_6_ = f32[4,8,1024]{2,1,0:T(8,128)S(1)} custom-call(bf16[128,8192]{1,0:T(8,128)(2,1)S(1)} %get-tuple-element.78.refs_0_, bf16[128,8192]{1,0:T(8,128)(2,1)S(1)} %get-tuple-element.79.refs_1_, bf16[128,1024]{1,0:T(8,128)(2,1)S(1)} %get-tuple-element.82.refs_1_.refs_2_.refs_6_, ...), custom_call_target="tpu_custom_call" | custom-call | flops 2147483648 | bytes 1 | tf_op jit(solution)/shard_map/pallas_call | solution.py:255
  21.3 0.1 shard_map.107
  21.4 1.1 %collective-permute-start.7 = (bf16[128,512]{1,0:T(8,128)(2,1)S(1)}, bf16[128,512]{1,0:T(8,128)(2,1)S(1)}, u32[]{:S(2)}, u32[]{:S(2)}) collective-permute-start(bf16[128,512]{1,0:T(8,128)(2,1)S(1)} %get-tuple-element.89.refs_6_), channel_id=1, source_target_pairs={{0,16},{8,24},{16,0},{24,8},{1,17},{9,25},{17,1},{25,9},{2,18},{10... | collective-permute-start | bytes 393224 | tf_op jit(solution)/shard_map/ppermute | solution.py:371
  22.5 1.1 %collective-permute-done.2.refs_4_ = bf16[128,512]{1,0:T(8,128)(2,1)S(1)} collective-permute-done((bf16[128,512]{1,0:T(8,128)(2,1)S(1)}, bf16[128,512]{1,0:T(8,128)(2,1)S(1)}, u32[]{:S(2)}, u32[]{:S(2)}) %collective-permute-start.2) | collective-permute-done | bytes 131104 | tf_op jit(solution)/shard_map/ppermute | solution.py:379
  23.6 2.8 %collective-permute-done.7.refs_4_ = bf16[128,512]{1,0:T(8,128)(2,1)S(1)} collective-permute-done((bf16[128,512]{1,0:T(8,128)(2,1)S(1)}, bf16[128,512]{1,0:T(8,128)(2,1)S(1)}, u32[]{:S(2)}, u32[]{:S(2)}) %collective-permute-start.7) | collective-permute-done | bytes 131104 | tf_op jit(solution)/shard_map/ppermute | solution.py:371
  26.5 0.1 collective-permute-start.8
  26.6 1.1 %collective-permute-start.6 = (bf16[128,512]{1,0:T(8,128)(2,1)S(1)}, bf16[128,512]{1,0:T(8,128)(2,1)S(1)}, u32[]{:S(2)}, u32[]{:S(2)}) collective-permute-start(bf16[128,512]{1,0:T(8,128)(2,1)S(1)} %get-tuple-element.91.refs_5_), channel_id=1, source_target_pairs={{0,16},{8,24},{16,0},{24,8},{1,17},{9,25},{17,1},{25,9},{2,18},{10... | collective-permute-start | bytes 393224 | tf_op jit(solution)/shard_map/ppermute | solution.py:371
  27.6 0.4 collective-permute-done.8.refs_5_
  28.1 4.5 %shard_map.110 = (f32[4,8,128]{2,1,0:T(8,128)S(1)}, f32[4,8,1024]{2,1,0:T(8,128)S(1)}, bf16[4,256,1024]{2,1,0:T(8,128)(2,1)S(1)}, bf16[4,256,1024]{2,1,0:T(8,128...) custom-call(bf16[128,8192]{1,0:T(8,128)(2,1)S(1)} %get-tuple-element, ...), custom_call_target="tpu_custom_call" | custom-call | flops 8589934592 | bytes 1 | tf_op jit(solution)/shard_map/pallas_call | solution.py:255
  32.6 0.2 collective-permute-start.10
  32.8 0.0 collective-permute-done.6.refs_4_
  32.9 0.4 collective-permute-start.9
  33.3 0.9 %collective-permute-done.10.refs_3_ = bf16[128,1024]{1,0:T(8,128)(2,1)S(1)} collective-permute-done((bf16[128,1024]{1,0:T(8,128)(2,1)S(1)}, bf16[128,1024]{1,0:T(8,128)(2,1)S(1)}, u32[]{:S(2)}, u32[]{:S(2)}) %collective-permute-start.10) | collective-permute-done | bytes 262176 | tf_op jit(solution)/shard_map/ppermute | solution.py:375
  34.2 0.1 shard_map.113
  34.4 1.1 %collective-permute-start.11 = (bf16[128,512]{1,0:T(8,128)(2,1)S(1)}, bf16[128,512]{1,0:T(8,128)(2,1)S(1)}, u32[]{:S(2)}, u32[]{:S(2)}) collective-permute-start(bf16[128,512]{1,0:T(8,128)(2,1)S(1)} %get-tuple-element.104.refs_7_), channel_id=1, source_target_pairs={{0,16},{8,24},{16,0},{24,8},{1,17},{9,25},{17,1},{25,9},{2,18},{10... | collective-permute-start | bytes 393224 | tf_op jit(solution)/shard_map/ppermute | solution.py:371
  35.4 0.0 collective-permute-done.9.refs_5_
  35.5 4.6 %shard_map.114 = (f32[4,8,128]{2,1,0:T(8,128)S(1)}, f32[4,8,1024]{2,1,0:T(8,128)S(1)}, bf16[4,256,1024]{2,1,0:T(8,128)(2,1)S(1)}, bf16[4,256,1024]{2,1,0:T(8,128...) custom-call(bf16[128,8192]{1,0:T(8,128)(2,1)S(1)} %get-tuple-element, ...), custom_call_target="tpu_custom_call" | custom-call | flops 8589934592 | bytes 1 | tf_op jit(solution)/shard_map/pallas_call | solution.py:255
  40.0 0.0 collective-permute-done.11.refs_2_
  40.1 0.1 collective-permute-start.12
  40.2 0.1 collective-permute-start.14
  40.3 0.7 collective-permute-start.15
  41.0 0.8 %collective-permute-done.12.refs_5_ = bf16[144,1024]{1,0:T(8,128)(2,1)S(1)} collective-permute-done((bf16[144,1024]{1,0:T(8,128)(2,1)S(1)}, bf16[144,1024]{1,0:T(8,128)(2,1)S(1)}, u32[]{:S(2)}, u32[]{:S(2)}) %collective-permute-start.12) | collective-permute-done | bytes 294944 | tf_op jit(solution)/shard_map/ppermute | solution.py:375
  41.8 0.1 shard_map.117
  41.9 1.1 %collective-permute-start.13 = (bf16[144,512]{1,0:T(8,128)(2,1)S(1)}, bf16[144,512]{1,0:T(8,128)(2,1)S(1)}, u32[]{:S(2)}, u32[]{:S(2)}) collective-permute-start(bf16[144,512]{1,0:T(8,128)(2,1)S(1)} %get-tuple-element.118.refs_11_), channel_id=1, source_target_pairs={{0,16},{8,24},{16,0},{24,8},{1,17},{9,25},{17,1},{25,9},{2,18},{10... | collective-permute-start | bytes 442376 | tf_op jit(solution)/shard_map/ppermute | solution.py:371
  43.0 2.4 %shard_map.118 = (bf16[128,8192]{1,0:T(8,128)(2,1)}, bf16[128,8192]{1,0:T(8,128)(2,1)}, f32[128,256]{1,0:T(8,128)S(1)}, f32[128,256]{1,0:T(8,128)S(1)}) custom-call(bf16[128,8192]{1,0:T(8,128)(2,1)S(1)} %get-tuple-element.78.refs_0_, bf16[128,8192]{1,0:T(8,128)(2,1)S(1)} %get-tuple-element.79.refs_1_, f32[384,128]{1,0:T(8,128)S(1)} %get-tuple-element.80.refs_4_.refs_2_, ...), custom_call_target="tpu_custom_call" | custom-call | flops 5368709120 | bytes 1 | tf_op jit(solution)/shard_map/pallas_call | solution.py:332
  45.4 2.5 %collective-permute-done.13.refs_2_.refs_1_ = bf16[144,512]{1,0:T(8,128)(2,1)S(1)} collective-permute-done((bf16[144,512]{1,0:T(8,128)(2,1)S(1)}, bf16[144,512]{1,0:T(8,128)(2,1)S(1)}, u32[]{:S(2)}, u32[]{:S(2)}) %collective-permute-start.13) | collective-permute-done | bytes 147488 | tf_op jit(solution)/shard_map/ppermute | solution.py:371
  47.9 0.7 collective-permute-start.17
  48.6 6.4 %collective-permute-start.16 = (bf16[128,512]{1,0:T(8,128)(2,1)S(1)}, bf16[128,512]{1,0:T(8,128)(2,1)S(1)}, u32[]{:S(2)}, u32[]{:S(2)}) collective-permute-start(bf16[128,512]{1,0:T(8,128)(2,1)S(1)} %get-tuple-element.123.refs_13_), channel_id=1, source_target_pairs={{0,1},{2,3},{4,5},{6,7},{1,0},{3,2},{5,4},{7,6},{8,9},{10,11},{12,... | collective-permute-start | bytes 393224 | tf_op jit(solution)/shard_map/ppermute | solution.py:379
  55.0 2.4 %shard_map.120 = (bf16[128,8192]{1,0:T(8,128)(2,1)}, bf16[128,8192]{1,0:T(8,128)(2,1)}, f32[128,256]{1,0:T(8,128)S(1)}, f32[128,256]{1,0:T(8,128)S(1)}) custom-call(bf16[128,8192]{1,0:T(8,128)(2,1)S(1)} %get-tuple-element.78.refs_0_, bf16[128,8192]{1,0:T(8,128)(2,1)S(1)} %get-tuple-element.79.refs_1_, ...), custom_call_target="tpu_custom_call", output_to_operand_aliasing={{0}: (11, {}), {1}: (12, {})} | custom-call | flops 5368709120 | bytes 1 | tf_op jit(solution)/shard_map/pallas_call | solution.py:332
  57.4 0.1 shard_map.121
  57.5 1.1 %collective-permute-start.18 = (bf16[128,512]{1,0:T(8,128)(2,1)S(1)}, bf16[128,512]{1,0:T(8,128)(2,1)S(1)}, u32[]{:S(2)}, u32[]{:S(2)}) collective-permute-start(bf16[128,512]{1,0:T(8,128)(2,1)S(1)} %get-tuple-element.128.refs_13_), channel_id=1, source_target_pairs={{0,16},{8,24},{16,0},{24,8},{1,17},{9,25},{17,1},{25,9},{2,18},{10... | collective-permute-start | bytes 393224 | tf_op jit(solution)/shard_map/ppermute | solution.py:371
  58.6 0.9 %collective-permute-done.16.refs_14_.refs_3_ = bf16[128,512]{1,0:T(8,128)(2,1)S(1)} collective-permute-done((bf16[128,512]{1,0:T(8,128)(2,1)S(1)}, bf16[128,512]{1,0:T(8,128)(2,1)S(1)}, u32[]{:S(2)}, u32[]{:S(2)}) %collective-permute-start.16) | collective-permute-done | bytes 131104 | tf_op jit(solution)/shard_map/ppermute | solution.py:379
  59.5 2.4 %shard_map.122 = (bf16[128,8192]{1,0:T(8,128)(2,1)}, bf16[128,8192]{1,0:T(8,128)(2,1)}, f32[128,256]{1,0:T(8,128)S(1)}, f32[128,256]{1,0:T(8,128)S(1)}) custom-call(bf16[128,8192]{1,0:T(8,128)(2,1)S(1)} %get-tuple-element.78.refs_0_, bf16[128,8192]{1,0:T(8,128)(2,1)S(1)} %get-tuple-element.79.refs_1_, ...), custom_call_target="tpu_custom_call", output_to_operand_aliasing={{0}: (11, {}), {1}: (12, {})} | custom-call | flops 5368709120 | bytes 1 | tf_op jit(solution)/shard_map/pallas_call | solution.py:332
  61.9 1.1 %collective-permute-start.19 = (bf16[128,512]{1,0:T(8,128)(2,1)S(1)}, bf16[128,512]{1,0:T(8,128)(2,1)S(1)}, u32[]{:S(2)}, u32[]{:S(2)}) collective-permute-start(bf16[128,512]{1,0:T(8,128)(2,1)S(1)} %get-tuple-element.133.refs_13_), channel_id=1, source_target_pairs={{0,16},{8,24},{16,0},{24,8},{1,17},{9,25},{17,1},{25,9},{2,18},{10... | collective-permute-start | bytes 393224 | tf_op jit(solution)/shard_map/ppermute | solution.py:371
  63.0 2.4 %shard_map.124 = (bf16[128,8192]{1,0:T(8,128)(2,1)}, bf16[128,8192]{1,0:T(8,128)(2,1)}, f32[128,256]{1,0:T(8,128)S(1)}, f32[128,256]{1,0:T(8,128)S(1)}) custom-call(bf16[128,8192]{1,0:T(8,128)(2,1)S(1)} %get-tuple-element.78.refs_0_, bf16[128,8192]{1,0:T(8,128)(2,1)S(1)} %get-tuple-element.79.refs_1_, ...), custom_call_target="tpu_custom_call", output_to_operand_aliasing={{0}: (11, {}), {1}: (12, {})} | custom-call | flops 5368709120 | bytes 1 | tf_op jit(solution)/shard_map/pallas_call | solution.py:332
  65.4 1.5 %collective-permute-done.19.refs_17_.refs_23_ = bf16[128,512]{1,0:T(8,128)(2,1)S(1)} collective-permute-done((bf16[128,512]{1,0:T(8,128)(2,1)S(1)}, bf16[128,512]{1,0:T(8,128)(2,1)S(1)}, u32[]{:S(2)}, u32[]{:S(2)}) %collective-permute-start.19) | collective-permute-done | bytes 131104 | tf_op jit(solution)/shard_map/ppermute | solution.py:371
  67.0 1.0 %shard_map.125 = (bf16[128,1024]{1,0:T(8,128)(2,1)}, bf16[128,1024]{1,0:T(8,128)(2,1)}, f32[16,512]{1,0:T(8,128)}) custom-call(s32[6]{0:T(128)S(4)} %get-tuple-element.81.refs_0_.flag, f32[2,16,128]{2,1,0:T(8,128)S(1)} %get-tuple-element.135.refs_0_, bf16[144,512]{1,0:T(8,128)(2,1)S(1)} %collective-permute-done.13.refs_2_.refs_1_, ...), custom_call_target="tpu_custom_call" | custom-call | tf_op jit(solution)/shard_map/pallas_call | solution.py:584
  (18 shorter events, 0.4 us)
Async XLA Ops:
  2.2 6.8 %collective-permute-start = (bf16[128,512]{1,0:T(8,128)(2,1)S(1)}, bf16[128,512]{1,0:T(8,128)(2,1)S(1)}, u32[]{:S(2)}, u32[]{:S(2)}) collective-permute-start(bf16[128,512]{1,0:T(8,128)(2,1)S(1)} %shard_map.101.refs_6_), channel_id=1, source_target_pairs={{0,16},{8,24},{16,0},{24,8},{1,17},{9,25},{17,1},{25,9},{2,18},{10... | collective-permute-start | bytes 393224 | tf_op jit(solution)/shard_map/ppermute | solution.py:371
  9.1 5.0 %collective-permute-start.1 = (bf16[128,512]{1,0:T(8,128)(2,1)S(1)}, bf16[128,512]{1,0:T(8,128)(2,1)S(1)}, u32[]{:S(2)}, u32[]{:S(2)}) collective-permute-start(bf16[128,512]{1,0:T(8,128)(2,1)S(1)} %shard_map.103), channel_id=1, source_target_pairs={{0,16},{8,24},{16,0},{24,8},{1,17},{9,25},{17,1},{25,9},{2,18},{10... | collective-permute-start | bytes 393224 | tf_op jit(solution)/shard_map/ppermute | solution.py:371
  10.6 10.7 %collective-permute-start.4 = (bf16[128,512]{1,0:T(8,128)(2,1)S(1)}, bf16[128,512]{1,0:T(8,128)(2,1)S(1)}, u32[]{:S(2)}, u32[]{:S(2)}) collective-permute-start(bf16[128,512]{1,0:T(8,128)(2,1)S(1)} %get-tuple-element.87), channel_id=1, source_target_pairs={{0,1},{2,3},{4,5},{6,7},{1,0},{3,2},{5,4},{7,6},{8,9},{10,11},{12,... | collective-permute-start | bytes 393224 | tf_op jit(solution)/shard_map/ppermute | solution.py:379
  12.1 9.2 %collective-permute-start.5 = (bf16[128,512]{1,0:T(8,128)(2,1)S(1)}, bf16[128,512]{1,0:T(8,128)(2,1)S(1)}, u32[]{:S(2)}, u32[]{:S(2)}) collective-permute-start(bf16[128,512]{1,0:T(8,128)(2,1)S(1)} %get-tuple-element.88), channel_id=1, source_target_pairs={{1,2},{3,4},{5,6},{2,1},{4,3},{6,5},{9,10},{11,12},{13,14},{10,9},... | collective-permute-start | bytes 393224 | tf_op jit(solution)/shard_map/ppermute | solution.py:379
  14.1 8.3 %collective-permute-start.3 = (bf16[128,512]{1,0:T(8,128)(2,1)S(1)}, bf16[128,512]{1,0:T(8,128)(2,1)S(1)}, u32[]{:S(2)}, u32[]{:S(2)}) collective-permute-start(bf16[128,512]{1,0:T(8,128)(2,1)S(1)} %get-tuple-element.85), channel_id=1, source_target_pairs={{1,2},{3,4},{5,6},{2,1},{4,3},{6,5},{9,10},{11,12},{13,14},{10,9},... | collective-permute-start | bytes 393224 | tf_op jit(solution)/shard_map/ppermute | solution.py:379
  14.8 8.7 %collective-permute-start.2 = (bf16[128,512]{1,0:T(8,128)(2,1)S(1)}, bf16[128,512]{1,0:T(8,128)(2,1)S(1)}, u32[]{:S(2)}, u32[]{:S(2)}) collective-permute-start(bf16[128,512]{1,0:T(8,128)(2,1)S(1)} %get-tuple-element.84.refs_5_), channel_id=1, source_target_pairs={{0,1},{2,3},{4,5},{6,7},{1,0},{3,2},{5,4},{7,6},{8,9},{10,11},{12,... | collective-permute-start | bytes 393224 | tf_op jit(solution)/shard_map/ppermute | solution.py:379
  21.4 5.0 %collective-permute-start.7 = (bf16[128,512]{1,0:T(8,128)(2,1)S(1)}, bf16[128,512]{1,0:T(8,128)(2,1)S(1)}, u32[]{:S(2)}, u32[]{:S(2)}) collective-permute-start(bf16[128,512]{1,0:T(8,128)(2,1)S(1)} %get-tuple-element.89.refs_6_), channel_id=1, source_target_pairs={{0,16},{8,24},{16,0},{24,8},{1,17},{9,25},{17,1},{25,9},{2,18},{10... | collective-permute-start | bytes 393224 | tf_op jit(solution)/shard_map/ppermute | solution.py:371
  26.5 1.6 %collective-permute-start.8 = (bf16[128,1024]{1,0:T(8,128)(2,1)S(1)}, bf16[128,1024]{1,0:T(8,128)(2,1)S(1)}, u32[]{:S(2)}, u32[]{:S(2)}) collective-permute-start(bf16[128,1024]{1,0:T(8,128)(2,1)S(1)} %get-tuple-element.95), channel_id=1, source_target_pairs={{0,8},{8,0},{16,24},{24,16},{1,9},{9,1},{17,25},{25,17},{2,10},{10... | collective-permute-start | bytes 786440 | tf_op jit(solution)/shard_map/ppermute | solution.py:375
  26.6 6.3 %collective-permute-start.6 = (bf16[128,512]{1,0:T(8,128)(2,1)S(1)}, bf16[128,512]{1,0:T(8,128)(2,1)S(1)}, u32[]{:S(2)}, u32[]{:S(2)}) collective-permute-start(bf16[128,512]{1,0:T(8,128)(2,1)S(1)} %get-tuple-element.91.refs_5_), channel_id=1, source_target_pairs={{0,16},{8,24},{16,0},{24,8},{1,17},{9,25},{17,1},{25,9},{2,18},{10... | collective-permute-start | bytes 393224 | tf_op jit(solution)/shard_map/ppermute | solution.py:371
  32.6 1.6 %collective-permute-start.10 = (bf16[128,1024]{1,0:T(8,128)(2,1)S(1)}, bf16[128,1024]{1,0:T(8,128)(2,1)S(1)}, u32[]{:S(2)}, u32[]{:S(2)}) collective-permute-start(bf16[128,1024]{1,0:T(8,128)(2,1)S(1)} %shard_map.112), channel_id=1, source_target_pairs={{0,8},{8,0},{16,24},{24,16},{1,9},{9,1},{17,25},{25,17},{2,10},{10... | collective-permute-start | bytes 786440 | tf_op jit(solution)/shard_map/ppermute | solution.py:375
  32.9 2.6 %collective-permute-start.9 = (bf16[128,1024]{1,0:T(8,128)(2,1)S(1)}, bf16[128,1024]{1,0:T(8,128)(2,1)S(1)}, u32[]{:S(2)}, u32[]{:S(2)}) collective-permute-start(bf16[128,1024]{1,0:T(8,128)(2,1)S(1)} %get-tuple-element.99), channel_id=1, source_target_pairs={{0,8},{8,0},{16,24},{24,16},{1,9},{9,1},{17,25},{25,17},{2,10},{10... | collective-permute-start | bytes 786440 | tf_op jit(solution)/shard_map/ppermute | solution.py:375
  34.4 5.7 %collective-permute-start.11 = (bf16[128,512]{1,0:T(8,128)(2,1)S(1)}, bf16[128,512]{1,0:T(8,128)(2,1)S(1)}, u32[]{:S(2)}, u32[]{:S(2)}) collective-permute-start(bf16[128,512]{1,0:T(8,128)(2,1)S(1)} %get-tuple-element.104.refs_7_), channel_id=1, source_target_pairs={{0,16},{8,24},{16,0},{24,8},{1,17},{9,25},{17,1},{25,9},{2,18},{10... | collective-permute-start | bytes 393224 | tf_op jit(solution)/shard_map/ppermute | solution.py:371
  40.1 1.6 %collective-permute-start.12 = (bf16[144,1024]{1,0:T(8,128)(2,1)S(1)}, bf16[144,1024]{1,0:T(8,128)(2,1)S(1)}, u32[]{:S(2)}, u32[]{:S(2)}) collective-permute-start(bf16[144,1024]{1,0:T(8,128)(2,1)S(1)} %shard_map.116), channel_id=1, source_target_pairs={{0,8},{8,0},{16,24},{24,16},{1,9},{9,1},{17,25},{25,17},{2,10},{10... | collective-permute-start | bytes 884744 | tf_op jit(solution)/shard_map/ppermute | solution.py:375
  40.2 17.2 %collective-permute-start.14 = (bf16[128,512]{1,0:T(8,128)(2,1)S(1)}, bf16[128,512]{1,0:T(8,128)(2,1)S(1)}, u32[]{:S(2)}, u32[]{:S(2)}) collective-permute-start(bf16[128,512]{1,0:T(8,128)(2,1)S(1)} %get-tuple-element.117.refs_5_), channel_id=1, source_target_pairs={{0,1},{2,3},{4,5},{6,7},{1,0},{3,2},{5,4},{7,6},{8,9},{10,11},{12,... | collective-permute-start | bytes 393224 | tf_op jit(solution)/shard_map/ppermute | solution.py:379
  40.3 17.1 %collective-permute-start.15 = (bf16[128,512]{1,0:T(8,128)(2,1)S(1)}, bf16[128,512]{1,0:T(8,128)(2,1)S(1)}, u32[]{:S(2)}, u32[]{:S(2)}) collective-permute-start(bf16[128,512]{1,0:T(8,128)(2,1)S(1)} %get-tuple-element.126), channel_id=1, source_target_pairs={{1,2},{3,4},{5,6},{2,1},{4,3},{6,5},{9,10},{11,12},{13,14},{10,9},... | collective-permute-start | bytes 393224 | tf_op jit(solution)/shard_map/ppermute | solution.py:379
  41.9 6.0 %collective-permute-start.13 = (bf16[144,512]{1,0:T(8,128)(2,1)S(1)}, bf16[144,512]{1,0:T(8,128)(2,1)S(1)}, u32[]{:S(2)}, u32[]{:S(2)}) collective-permute-start(bf16[144,512]{1,0:T(8,128)(2,1)S(1)} %get-tuple-element.118.refs_11_), channel_id=1, source_target_pairs={{0,16},{8,24},{16,0},{24,8},{1,17},{9,25},{17,1},{25,9},{2,18},{10... | collective-permute-start | bytes 442376 | tf_op jit(solution)/shard_map/ppermute | solution.py:371
  47.9 10.7 %collective-permute-start.17 = (bf16[128,512]{1,0:T(8,128)(2,1)S(1)}, bf16[128,512]{1,0:T(8,128)(2,1)S(1)}, u32[]{:S(2)}, u32[]{:S(2)}) collective-permute-start(bf16[128,512]{1,0:T(8,128)(2,1)S(1)} %get-tuple-element.129), channel_id=1, source_target_pairs={{1,2},{3,4},{5,6},{2,1},{4,3},{6,5},{9,10},{11,12},{13,14},{10,9},... | collective-permute-start | bytes 393224 | tf_op jit(solution)/shard_map/ppermute | solution.py:379
  48.6 10.9 %collective-permute-start.16 = (bf16[128,512]{1,0:T(8,128)(2,1)S(1)}, bf16[128,512]{1,0:T(8,128)(2,1)S(1)}, u32[]{:S(2)}, u32[]{:S(2)}) collective-permute-start(bf16[128,512]{1,0:T(8,128)(2,1)S(1)} %get-tuple-element.123.refs_13_), channel_id=1, source_target_pairs={{0,1},{2,3},{4,5},{6,7},{1,0},{3,2},{5,4},{7,6},{8,9},{10,11},{12,... | collective-permute-start | bytes 393224 | tf_op jit(solution)/shard_map/ppermute | solution.py:379
  57.5 7.9 %collective-permute-start.18 = (bf16[128,512]{1,0:T(8,128)(2,1)S(1)}, bf16[128,512]{1,0:T(8,128)(2,1)S(1)}, u32[]{:S(2)}, u32[]{:S(2)}) collective-permute-start(bf16[128,512]{1,0:T(8,128)(2,1)S(1)} %get-tuple-element.128.refs_13_), channel_id=1, source_target_pairs={{0,16},{8,24},{16,0},{24,8},{1,17},{9,25},{17,1},{25,9},{2,18},{10... | collective-permute-start | bytes 393224 | tf_op jit(solution)/shard_map/ppermute | solution.py:371
  61.9 5.0 %collective-permute-start.19 = (bf16[128,512]{1,0:T(8,128)(2,1)S(1)}, bf16[128,512]{1,0:T(8,128)(2,1)S(1)}, u32[]{:S(2)}, u32[]{:S(2)}) collective-permute-start(bf16[128,512]{1,0:T(8,128)(2,1)S(1)} %get-tuple-element.133.refs_13_), channel_id=1, source_target_pairs={{0,16},{8,24},{16,0},{24,8},{1,17},{9,25},{17,1},{25,9},{2,18},{10... | collective-permute-start | bytes 393224 | tf_op jit(solution)/shard_map/ppermute | solution.py:371

commit v4 on v3

--- a/solution.py
+++ b/solution.py
@@ -18,7 +18,7 @@
 CHUNKS = 2
 UNROLL = 2
 EXTRA = 16
-BEHIND = ((2, 2), (2, 2))
+BEHIND = ((1, 1, 2), (2, 2))
 LOG2E = math.log2(math.e)
 VMEM_SMALL = 8 * 2**20
 VMEM_LARGE = 16 * 2**20
@@ -56,7 +56,7 @@
     stat_ref[at, 3:4, :] = jnp.sum(e * dp, axis=0, keepdims=True)
 
 
-def first_kernel(contexts, count, place, *refs):
+def first_kernel(contexts, count, *refs):
     sources, refs = refs[:4], refs[4:]
     spans_far, docs_far, refs = refs[0], refs[1], refs[2:]
     loaded, (flag, bias_ref, stat_ref, sems, spans, docs) = refs[:4], refs[4:]
@@ -81,15 +81,17 @@
         copy.start()
     for copy in short:
         copy.wait()
-    span = spans[2 * place[0] + place[1]]
     subs = bias_ref.shape[0] // rows - 1
-    first = (span * subs + place[2]) * rows
+    here, context = lax.axis_index("head"), lax.axis_index(CONTEXT)
+    side, sub = here // subs, lax.rem(here, subs)
+    span = spans[2 * context + side]
+    first = (span * subs + sub) * rows
     flag[0] = first
-    for index in (1, 2):
-        flag[index] = place[index]
-    flag[3] = (span == place[0]).astype(jnp.int32)
-    flag[4] = place[3]
-    flag[5] = (place[0] == contexts - 1).astype(jnp.int32)
+    flag[1] = side
+    flag[2] = sub
+    flag[3] = (span == context).astype(jnp.int32)
+    flag[4] = lax.rem(context, 2)
+    flag[5] = (context == contexts - 1).astype(jnp.int32)
     q_pos = first + lax.broadcasted_iota(jnp.int32, (1, rows), 1)
     at = jnp.int32(0)
     start = jnp.zeros((1, rows), jnp.int32)
@@ -242,7 +244,7 @@
 
 def cost(count, rows, products):
     return pl.CostEstimate(
-        flops=16 * products * count * rows * GROUP * rows * WIDTH,
+        flops=4 * products * count * rows * GROUP * rows * WIDTH,
         bytes_accessed=1,
         transcendentals=0,
     )
@@ -266,16 +268,16 @@
     return pltpu.with_memory_space_constraint(value, pltpu.HBM)
 
 
-def first_step(contexts, subs, count, place, arrays, spans, docs, behind):
+def first_step(contexts, subs, count, arrays, spans, docs, behind):
     rows = arrays[0].shape[0]
     heads = arrays[2].shape[1] // WIDTH
 
-    def kernel(place, *refs):
-        first_kernel(contexts, count, place, *refs[:6], *refs[7:])
+    def kernel(*refs):
+        first_kernel(contexts, count, *refs[:6], *refs[7:])
 
     results = pl.pallas_call(
         kernel,
-        in_specs=whole(1, pltpu.SMEM) + whole(7, pl.ANY),
+        in_specs=whole(7, pl.ANY),
         out_specs=whole(4) + whole(1, pltpu.SMEM) + whole(2),
         out_shape=[pltpu.VMEM(array.shape, array.dtype) for array in arrays]
         + [
@@ -290,7 +292,7 @@
         ],
         compiler_params=pltpu.CompilerParams(vmem_limit_bytes=VMEM_LARGE),
         cost_estimate=cost(count, rows, 3),
-    )(place, *[far(array) for array in (*arrays, spans, docs)], behind)
+    )(*[far(array) for array in (*arrays, spans, docs)], behind)
     return results[4], results[:2], results[2:4], results[5], results[6]
 
 
@@ -358,12 +360,7 @@
     rows = queries.shape[0]
     size = lax.axis_size("head")
     subs = size // 2
-    here = lax.axis_index("head")
-    side, sub = here // subs, here % subs
     contexts = lax.axis_size(CONTEXT)
-    context = lax.axis_index(CONTEXT)
-    place = jnp.stack([context, side, sub, context % 2]).astype(jnp.int32)
-
     width = keys.shape[1] // CHUNKS
     half = ((rows, width), jnp.bfloat16)
 
@@ -381,10 +378,10 @@
     def columns(chunk):
         return slice(chunk * width, (chunk + 1) * width)
 
-    def pick_in(place, keys, values, give, sem):
+    def pick_in(keys, values, give, sem):
         for flag, source in ((0, values), (1, keys)):
 
-            @pl.when(place[1] == flag)
+            @pl.when(lax.axis_index("head") // subs == flag)
             def _(source=source):
                 copy = pltpu.make_async_copy(source.at[:, columns(0)], give, sem)
                 copy.start()
@@ -392,12 +389,12 @@
 
     first_give = pl.pallas_call(
         pick_in,
-        in_specs=whole(1, pltpu.SMEM) + whole(2, pl.ANY),
+        in_specs=whole(2, pl.ANY),
         out_specs=whole(1)[0],
         out_shape=pltpu.VMEM(*half),
         scratch_shapes=[pltpu.SemaphoreType.DMA],
         compiler_params=pltpu.CompilerParams(vmem_limit_bytes=VMEM_SMALL),
-    )(place, far(keys), far(values))
+    )(far(keys), far(values))
 
     def later_give(own, chunk, behind):
         def kernel(flag, key, value, give):
@@ -412,16 +409,21 @@
     def out_of_step(flag, backward):
         return (flag[3] + flag[4] + (1 if backward else 0)) % 2
 
-    def edge_parts(own, got, backward, cols=slice(None), behind=()):
+    def edge_part(own, got, backward, odd, cols=slice(None), behind=()):
         def kernel(flag, *refs):
-            own, (got, even, odd) = refs[:-3], refs[-3:]
+            own, (got, out) = refs[:-2], refs[-2:]
+            keeps = out_of_step(flag, backward) != odd
             for which, keep in enumerate(own):
 
-                @pl.when((flag[1] == which) | (len(own) == 1))
+                @pl.when(keeps & ((flag[1] == which) | (len(own) == 1)))
                 def _(keep=keep):
-                    route(out_of_step(flag, backward), keep.at[:, cols], got.at[:rows], even, odd)
-
-        return small(kernel, flags, [*own, got], [half, half], behind)
+                    out[...] = keep[:, cols]
+
+            @pl.when(jnp.logical_not(keeps))
+            def _():
+                out[...] = got[:rows, :]
+
+        return small(kernel, flags, [*own, got], [half], behind)[0]
 
     def edge_done(own, got, even, odd, backward, cols=slice(None), behind=()):
         def kernel(flag, *refs):
@@ -498,7 +500,7 @@
 
         both = ((rows + extra, 2 * width), jnp.bfloat16)
         outs = small(kernel, flags, [*entropies, *dk[1:], *dv[1:]], [both] * (subs - 1), behind)
-        return [around(out, index + 1 - subs) for index, out in enumerate(outs)]
+        return [around(out, index + 1 - subs) for index, out in enumerate(outs)], outs
 
     def collect(dk, dv, arrived, entropies=(), behind=()):
         extra = EXTRA if entropies else 0
@@ -592,46 +594,30 @@
             compiler_params=pltpu.CompilerParams(vmem_limit_bytes=VMEM_SMALL),
         )(in_scalars(flags), *[near_by(v) for v in local])
 
-    def over(parts):
-        odd = edges(parts[1], 1)
-        return edges(parts[0], 0), odd
-
     per_chunk = KEY_VALUE_HEADS // CHUNKS
     got = [across(first_give)]
     flags, wide_near, own, bias, stats = first_step(
-        contexts, subs, per_chunk, place, (queries, dout, keys, values), span_order, doc_lengths, first_give
+        contexts, subs, per_chunk, (queries, dout, keys, values), span_order, doc_lengths, first_give
     )
     got.append(across(later_give(own, 1, got)))
     cols = [columns(chunk) for chunk in range(CHUNKS)]
-    in0 = edge_parts(own, got[0], False, cols[0], [stats])
-    edge0 = over(in0)
-    in1 = edge_parts(own, got[1], False, cols[1])
-    edge1 = over(in1)
-    stats = [stats, more_sums(wide_near, own, bias, per_chunk, per_chunk, in1[:1])]
-    mine0, theirs0 = edge_done(own, got[0], *edge0, False, cols[0], stats[1:])
+    in0 = [edge_part(own, got[0], False, odd, cols[0], [stats]) for odd in range(2)]
+    edge0 = [edges(part, odd) for odd, part in enumerate(in0)]
+    in1 = [edge_part(own, got[1], False, odd, cols[1]) for odd in range(2)]
+    edge1 = [edges(part, odd) for odd, part in enumerate(in1)]
+    mine0, theirs0 = edge_done(own, got[0], *edge0, False, cols[0])
     other0 = across(theirs0)
+    stats = [stats, more_sums(wide_near, own, bias, per_chunk, per_chunk, [theirs0])]
     mine1, theirs1 = edge_done(own, got[1], *edge1, False, cols[1], [theirs0])
     other1 = across(theirs1)
-    before0, near0 = window_parts(own, mine0, other0, cols[0], [theirs1])
+    before0, near0 = window_parts(own, mine0, other0, cols[0], [theirs1, stats[1]])
     ent0, kept0, dk0, dv0 = earlier_terms(*wide_near, bias, before0, near0, stats[0], 0)
     before1, near1 = window_parts(own, mine1, other1, cols[1], [ent0])
-    keep0, give0, *own0 = collect(dk0, dv0, near_terms(dk0, dv0))
-    back0 = across(give0)
-    ent1, kept1, dk1, dv1 = earlier_terms(
-        *wide_near, bias, before1, near1, stats[1], per_chunk, [give0]
-    )
-    out0 = edge_parts([keep0], back0, True)
-    edge0 = over(out0)
-    ents = [ent0, ent1]
-    keep1, give1, *own1, entropies = collect(
-        dk1, dv1, near_terms(dk1, dv1, ents, out0[:1]), ents
-    )
-    back1 = across(give1)
     wide, pieces = [], []
 
     def rest(chunk, piece, behind):
         nonlocal wide
-        before, near, kept = ((before0, near0, kept0), (before1, near1, kept1))[chunk]
+        before, near, kept = held[chunk]
         skip, count = sum(BEHIND[chunk][:piece]), BEHIND[chunk][piece]
         start = chunk * per_chunk
         wide, terms = the_rest(
@@ -640,18 +626,34 @@
         pieces.append(terms)
         return terms[:1]
 
-    done = rest(0, 0, [give1])
-    out1 = edge_parts([keep1], back1, True, behind=done)
-    edge1 = over(out1)
-    done = rest(0, 1, out1[:1])
-    mine0, theirs0 = edge_done([keep0], back0, *edge0, True, behind=done)
+    held = [(before0, near0, kept0), (before1, near1, None)]
+    arrived, sent = near_terms(dk0, dv0)
+    done = rest(0, 0, sent[:1])
+    keep0, give0, *own0 = collect(dk0, dv0, arrived)
+    back0 = across(give0)
+    ent1, kept1, dk1, dv1 = earlier_terms(
+        *wide_near, bias, before1, near1, stats[1], per_chunk, [give0, *done]
+    )
+    held[1] = (before1, near1, kept1)
+    out0 = edge_part([keep0], back0, True, 0)
+    edge0 = [edges(out0, 0)]
+    ents = [ent0, ent1]
+    arrived, sent = near_terms(dk1, dv1, ents, [out0])
+    keep1, give1, *own1, entropies = collect(dk1, dv1, arrived, ents)
+    back1 = across(give1)
+    edge0.append(edges(edge_part([keep0], back0, True, 1, behind=[give1]), 1))
+    done = rest(0, 1, [give1])
+    out1 = [edge_part([keep1], back1, True, odd, behind=done) for odd in range(2)]
+    edge1 = [edges(part, odd) for odd, part in enumerate(out1)]
+    mine0, theirs0 = edge_done([keep0], back0, *edge0, True, behind=out1[:1])
     other0 = across(theirs0)
-    done = rest(1, 0, [theirs0, *edge1])
+    done = rest(0, 2, [theirs0])
+    done = rest(1, 0, done)
     mine1, theirs1 = edge_done([keep1], back1, *edge1, True, behind=done)
     other1 = across(theirs1)
     rest(1, 1, [theirs1])
     grad_key, grad_value, entropy = finish(
-        [(*own0, pieces[:2], mine0, other0), (*own1, pieces[2:], mine1, other1)], entropies, back1
+        [(*own0, pieces[:3], mine0, other0), (*own1, pieces[3:], mine1, other1)], entropies, back1
     )
     return wide[0], entropy.T, wide[1], grad_key, grad_value
 

time: 68.2 us -> 64.6 us (0.947)
  waiting for transfers between devices: 12.3 us -> 8.32 us
  starting transfers between devices: 27.2 us -> 28.1 us
    ppermute x8, waiting for transfers between devices: 8.14 us -> 3.03 us  [across(): lax.ppermute(value, 'head', [(j, (j + subs) % size) for j in range(size)])]
    ppermute x8, starting transfers between devices: 15.5 us -> 17.4 us  [edges(): return lax.ppermute(value, CONTEXT, pairs + [(b, a) for a, b in pairs])]
    pallas_call x2, Pallas kernels: 5.25 us -> 4.18 us  [the longest x1 3.25 us: first_step(): pl.pallas_call(kernel, in_specs=whole(7, pl.ANY), out_specs=whole(4) + wh...]
    ppermute x8, starting transfers between devices: 11 us -> 9.95 us  [across(): lax.ppermute(value, 'head', [(j, (j + subs) % size) for j in range(size)])]
    ppermute x8, waiting for transfers between devices: 1.99 us -> 2.76 us  [edges(): return lax.ppermute(value, CONTEXT, pairs + [(b, a) for a, b in pairs])]
    pallas_call x4 -> x5, Pallas kernels: 9.63 us -> 10.2 us  [the_rest(): pl.pallas_call(kernel, grid=(count,), in_specs=whole(len(inputs)) + whole...]
  transfers between devices with their start and end apart: 20 -> 20, of which waited for: 9 -> 7; matrix products, arithmetic and copies ran while one was open for 0% -> 0% of each run, Pallas kernels for 37% -> 39%
where the time goes in v4:
time: 64.6 us; the launch traced here: 64.4 us
  starting transfers between devices  28.1 us (43%)
  Pallas kernels  27.1 us (42%)
  waiting for transfers between devices  8.32 us (13%)
  between operations  0.9 us (1%)
    ppermute x8, starting transfers between devices, edges(): return lax.ppermute(value, CONTEXT, pairs + [(b, a) for a, b in pairs])  17.4 us
    pallas_call x3, Pallas kernels, large(): pl.pallas_call(body, in_specs=whole(len(inputs)) + whole(len(behind), pl....  10.9 us
    pallas_call x5, Pallas kernels, the_rest(): pl.pallas_call(kernel, grid=(count,), in_specs=whole(len(inputs)) + whole...  10.2 us
    ppermute x8, starting transfers between devices, across(): lax.ppermute(value, 'head', [(j, (j + subs) % size) for j in range(size)])  9.95 us
    pallas_call x1, Pallas kernels, first_step(): pl.pallas_call(kernel, in_specs=whole(7, pl.ANY), out_specs=whole(4) + wh...  3.25 us
    ppermute x8, waiting for transfers between devices, across(): lax.ppermute(value, 'head', [(j, (j + subs) % size) for j in range(size)])  3.03 us
    ppermute x8, waiting for transfers between devices, edges(): return lax.ppermute(value, CONTEXT, pairs + [(b, a) for a, b in pairs])  2.76 us
    ppermute x4, waiting for transfers between devices, around(): return lax.ppermute(value, 'head', pairs)  2.54 us
  transfers between devices with their start and end apart: 20, of which 7 were waited for; matrix products, arithmetic and copies ran while one was open for 0% of the time, Pallas kernels for 39%

profile of v4, /device:TPU:0, one launch (start us, length us, event | category | flops | bytes accessed | tf_op | source)
XLA Modules:
  0.0 64.4 jit_solution(14758443950488540076)
XLA Ops:
  0.6 0.9 %shard_map.101.refs_6_ = bf16[128,512]{1,0:T(8,128)(2,1)S(1)} custom-call(bf16[128,1024]{1,0:T(8,128)(2,1)} %refs_2_.1, bf16[128,1024]{1,0:T(8,128)(2,1)} %refs_3_.1), custom_call_target="tpu_custom_call" | custom-call | tf_op jit(solution)/shard_map/pallas_call | solution.py:390
  1.6 3.0 %collective-permute-start = (bf16[128,512]{1,0:T(8,128)(2,1)S(1)}, bf16[128,512]{1,0:T(8,128)(2,1)S(1)}, u32[]{:S(2)}, u32[]{:S(2)}) collective-permute-start(bf16[128,512]{1,0:T(8,128)(2,1)S(1)} %shard_map.101.refs_6_), channel_id=1, source_target_pairs={{0,16},{8,24},{16,0},{24,8},{1,17},{9,25},{17,1},{25,9},{2,18},{10... | collective-permute-start | bytes 393224 | tf_op jit(solution)/shard_map/ppermute | solution.py:368
  4.6 3.2 %shard_map.102 = (bf16[128,8192]{1,0:T(8,128)(2,1)S(1)}, bf16[128,8192]{1,0:T(8,128)(2,1)S(1)}, bf16[128,1024]{1,0:T(8,128)(2,1)S(1)}, bf16[128,1024]{1,0:T(8,12...) custom-call(bf16[128,8192]{1,0:T(8,128)(2,1)} %refs_0_.1, ...), custom_call_target="tpu_custom_call" | custom-call | flops 805306368 | bytes 1 | tf_op jit(solution)/shard_map/pallas_call | solution.py:278
  7.9 0.2 collective-permute-done.refs_3_
  8.1 1.8 %collective-permute-start.1 = (bf16[128,512]{1,0:T(8,128)(2,1)S(1)}, bf16[128,512]{1,0:T(8,128)(2,1)S(1)}, u32[]{:S(2)}, u32[]{:S(2)}) collective-permute-start(bf16[128,512]{1,0:T(8,128)(2,1)S(1)} %shard_map.103), channel_id=1, source_target_pairs={{0,16},{8,24},{16,0},{24,8},{1,17},{9,25},{17,1},{25,9},{2,18},{10... | collective-permute-start | bytes 393224 | tf_op jit(solution)/shard_map/ppermute | solution.py:368
  9.9 1.6 %collective-permute-start.4 = (bf16[128,512]{1,0:T(8,128)(2,1)S(1)}, bf16[128,512]{1,0:T(8,128)(2,1)S(1)}, u32[]{:S(2)}, u32[]{:S(2)}) collective-permute-start(bf16[128,512]{1,0:T(8,128)(2,1)S(1)} %shard_map.106), channel_id=1, source_target_pairs={{0,1},{2,3},{4,5},{6,7},{1,0},{3,2},{5,4},{7,6},{8,9},{10,11},{12,... | collective-permute-start | bytes 393224 | tf_op jit(solution)/shard_map/ppermute | solution.py:376
  11.5 0.7 %collective-permute-start.5 = (bf16[128,512]{1,0:T(8,128)(2,1)S(1)}, bf16[128,512]{1,0:T(8,128)(2,1)S(1)}, u32[]{:S(2)}, u32[]{:S(2)}) collective-permute-start(bf16[128,512]{1,0:T(8,128)(2,1)S(1)} %shard_map.107), channel_id=1, source_target_pairs={{1,2},{3,4},{5,6},{2,1},{4,3},{6,5},{9,10},{11,12},{13,14},{10,9},... | collective-permute-start | bytes 393224 | tf_op jit(solution)/shard_map/ppermute | solution.py:376
  12.2 1.0 %collective-permute-done.1.refs_3_ = bf16[128,512]{1,0:T(8,128)(2,1)S(1)} collective-permute-done((bf16[128,512]{1,0:T(8,128)(2,1)S(1)}, bf16[128,512]{1,0:T(8,128)(2,1)S(1)}, u32[]{:S(2)}, u32[]{:S(2)}) %collective-permute-start.1) | collective-permute-done | bytes 131104 | tf_op jit(solution)/shard_map/ppermute | solution.py:368
  13.2 3.4 %collective-permute-start.2 = (bf16[128,512]{1,0:T(8,128)(2,1)S(1)}, bf16[128,512]{1,0:T(8,128)(2,1)S(1)}, u32[]{:S(2)}, u32[]{:S(2)}) collective-permute-start(bf16[128,512]{1,0:T(8,128)(2,1)S(1)} %shard_map.104), channel_id=1, source_target_pairs={{0,1},{2,3},{4,5},{6,7},{1,0},{3,2},{5,4},{7,6},{8,9},{10,11},{12,... | collective-permute-start | bytes 393224 | tf_op jit(solution)/shard_map/ppermute | solution.py:376
  16.6 0.7 %collective-permute-start.3 = (bf16[128,512]{1,0:T(8,128)(2,1)S(1)}, bf16[128,512]{1,0:T(8,128)(2,1)S(1)}, u32[]{:S(2)}, u32[]{:S(2)}) collective-permute-start(bf16[128,512]{1,0:T(8,128)(2,1)S(1)} %shard_map.105), channel_id=1, source_target_pairs={{1,2},{3,4},{5,6},{2,1},{4,3},{6,5},{9,10},{11,12},{13,14},{10,9},... | collective-permute-start | bytes 393224 | tf_op jit(solution)/shard_map/ppermute | solution.py:376
  17.3 0.0 collective-permute-done.4.refs_4_
  17.3 0.1 shard_map.108
  17.4 0.6 collective-permute-start.7
  18.0 1.7 %shard_map.110.refs_6_ = f32[4,8,1024]{2,1,0:T(8,128)S(1)} custom-call(bf16[128,8192]{1,0:T(8,128)(2,1)S(1)} %get-tuple-element.74.refs_0_, bf16[128,8192]{1,0:T(8,128)(2,1)S(1)} %get-tuple-element.75.refs_1_, bf16[128,1024]{1,0:T(8,128)(2,1)S(1)} %get-tuple-element.78.refs_1_.refs_2_.refs_6_, ...), custom_call_target="tpu_custom_call" | custom-call | flops 536870912 | bytes 1 | tf_op jit(solution)/shard_map/pallas_call | solution.py:257
  19.7 2.7 %collective-permute-done.2.refs_4_ = bf16[128,512]{1,0:T(8,128)(2,1)S(1)} collective-permute-done((bf16[128,512]{1,0:T(8,128)(2,1)S(1)}, bf16[128,512]{1,0:T(8,128)(2,1)S(1)}, u32[]{:S(2)}, u32[]{:S(2)}) %collective-permute-start.2) | collective-permute-done | bytes 131104 | tf_op jit(solution)/shard_map/ppermute | solution.py:376
  22.4 0.1 shard_map.109
  22.5 0.0 collective-permute-done.7.refs_4_
  22.5 0.1 shard_map.111
  22.6 0.1 collective-permute-start.8
  22.7 0.6 collective-permute-start.6
  23.2 1.0 %collective-permute-done.8.refs_5_ = bf16[128,1024]{1,0:T(8,128)(2,1)S(1)} collective-permute-done((bf16[128,1024]{1,0:T(8,128)(2,1)S(1)}, bf16[128,1024]{1,0:T(8,128)(2,1)S(1)}, u32[]{:S(2)}, u32[]{:S(2)}) %collective-permute-start.8) | collective-permute-done | bytes 262176 | tf_op jit(solution)/shard_map/ppermute | solution.py:372
  24.2 4.5 %shard_map.112 = (f32[4,8,128]{2,1,0:T(8,128)S(1)}, f32[4,8,1024]{2,1,0:T(8,128)S(1)}, bf16[4,256,1024]{2,1,0:T(8,128)(2,1)S(1)}, bf16[4,256,1024]{2,1,0:T(8,128...) custom-call(bf16[128,8192]{1,0:T(8,128)(2,1)S(1)} %get-tuple-element, ...), custom_call_target="tpu_custom_call" | custom-call | flops 2147483648 | bytes 1 | tf_op jit(solution)/shard_map/pallas_call | solution.py:257
  28.7 0.2 collective-permute-start.10
  29.0 0.4 collective-permute-start.9
  29.4 1.5 %shard_map.116 = (bf16[128,8192]{1,0:T(8,128)(2,1)}, bf16[128,8192]{1,0:T(8,128)(2,1)}, f32[128,128]{1,0:T(8,128)S(1)}, f32[128,128]{1,0:T(8,128)S(1)}) custom-call(bf16[128,8192]{1,0:T(8,128)(2,1)S(1)} %get-tuple-element.74.refs_0_, bf16[128,8192]{1,0:T(8,128)(2,1)S(1)} %get-tuple-element.75.refs_1_, f32[384,128]{1,0:T(8,128)S(1)} %get-tuple-element.76.refs_4_.refs_2_, ...), custom_call_target="tpu_custom_call" | custom-call | flops 671088640 | bytes 1 | tf_op jit(solution)/shard_map/pallas_call | solution.py:334
  30.9 0.0 collective-permute-done.10.refs_3_
  31.0 0.1 shard_map.115
  31.1 0.6 collective-permute-start.11
  31.7 0.0 collective-permute-done.9.refs_5_
  31.7 4.6 %shard_map.117 = (f32[4,8,128]{2,1,0:T(8,128)S(1)}, f32[4,8,1024]{2,1,0:T(8,128)S(1)}, bf16[4,256,1024]{2,1,0:T(8,128)(2,1)S(1)}, bf16[4,256,1024]{2,1,0:T(8,128...) custom-call(bf16[128,8192]{1,0:T(8,128)(2,1)S(1)} %get-tuple-element, ...), custom_call_target="tpu_custom_call" | custom-call | flops 2147483648 | bytes 1 | tf_op jit(solution)/shard_map/pallas_call | solution.py:257
  36.3 0.4 collective-permute-done.11.refs_2_
  36.7 0.1 collective-permute-start.12
  36.8 1.6 %collective-permute-done.12.refs_5_ = bf16[144,1024]{1,0:T(8,128)(2,1)S(1)} collective-permute-done((bf16[144,1024]{1,0:T(8,128)(2,1)S(1)}, bf16[144,1024]{1,0:T(8,128)(2,1)S(1)}, u32[]{:S(2)}, u32[]{:S(2)}) %collective-permute-start.12) | collective-permute-done | bytes 294944 | tf_op jit(solution)/shard_map/ppermute | solution.py:372
  38.4 0.1 shard_map.120
  38.5 1.2 %collective-permute-start.15 = (bf16[144,512]{1,0:T(8,128)(2,1)S(1)}, bf16[144,512]{1,0:T(8,128)(2,1)S(1)}, u32[]{:S(2)}, u32[]{:S(2)}) collective-permute-start(bf16[144,512]{1,0:T(8,128)(2,1)S(1)} %get-tuple-element.112.refs_13_.refs_3_), channel_id=1, source_target_pairs={{0,16},{8,24},{16,0},{24,8},{1,17},{9,25},{17,1},{25,9},{2,18},{10... | collective-permute-start | bytes 442376 | tf_op jit(solution)/shard_map/ppermute | solution.py:368
  39.7 4.2 %collective-permute-start.13 = (bf16[128,512]{1,0:T(8,128)(2,1)S(1)}, bf16[128,512]{1,0:T(8,128)(2,1)S(1)}, u32[]{:S(2)}, u32[]{:S(2)}) collective-permute-start(bf16[128,512]{1,0:T(8,128)(2,1)S(1)} %shard_map.118.refs_5_), channel_id=1, source_target_pairs={{0,1},{2,3},{4,5},{6,7},{1,0},{3,2},{5,4},{7,6},{8,9},{10,11},{12,... | collective-permute-start | bytes 393224 | tf_op jit(solution)/shard_map/ppermute | solution.py:376
  43.9 0.7 %collective-permute-start.14 = (bf16[128,512]{1,0:T(8,128)(2,1)S(1)}, bf16[128,512]{1,0:T(8,128)(2,1)S(1)}, u32[]{:S(2)}, u32[]{:S(2)}) collective-permute-start(bf16[128,512]{1,0:T(8,128)(2,1)S(1)} %shard_map.122), channel_id=1, source_target_pairs={{1,2},{3,4},{5,6},{2,1},{4,3},{6,5},{9,10},{11,12},{13,14},{10,9},... | collective-permute-start | bytes 393224 | tf_op jit(solution)/shard_map/ppermute | solution.py:376
  44.6 1.5 %shard_map.121 = (bf16[128,8192]{1,0:T(8,128)(2,1)}, bf16[128,8192]{1,0:T(8,128)(2,1)}, f32[128,128]{1,0:T(8,128)S(1)}, f32[128,128]{1,0:T(8,128)S(1)}) custom-call(bf16[128,8192]{1,0:T(8,128)(2,1)S(1)} %get-tuple-element.74.refs_0_, bf16[128,8192]{1,0:T(8,128)(2,1)S(1)} %get-tuple-element.75.refs_1_, ...), custom_call_target="tpu_custom_call", output_to_operand_aliasing={{0}: (11, {}), {1}: (12, {})} | custom-call | flops 671088640 | bytes 1 | tf_op jit(solution)/shard_map/pallas_call | solution.py:334
  46.1 0.7 %collective-permute-start.17 = (bf16[128,512]{1,0:T(8,128)(2,1)S(1)}, bf16[128,512]{1,0:T(8,128)(2,1)S(1)}, u32[]{:S(2)}, u32[]{:S(2)}) collective-permute-start(bf16[128,512]{1,0:T(8,128)(2,1)S(1)} %shard_map.127), channel_id=1, source_target_pairs={{1,2},{3,4},{5,6},{2,1},{4,3},{6,5},{9,10},{11,12},{13,14},{10,9},... | collective-permute-start | bytes 393224 | tf_op jit(solution)/shard_map/ppermute | solution.py:376
  46.8 5.6 %collective-permute-start.16 = (bf16[128,512]{1,0:T(8,128)(2,1)S(1)}, bf16[128,512]{1,0:T(8,128)(2,1)S(1)}, u32[]{:S(2)}, u32[]{:S(2)}) collective-permute-start(bf16[128,512]{1,0:T(8,128)(2,1)S(1)} %shard_map.123.refs_5_), channel_id=1, source_target_pairs={{0,1},{2,3},{4,5},{6,7},{1,0},{3,2},{5,4},{7,6},{8,9},{10,11},{12,... | collective-permute-start | bytes 393224 | tf_op jit(solution)/shard_map/ppermute | solution.py:376
  52.5 1.0 %collective-permute-start.18 = (bf16[128,512]{1,0:T(8,128)(2,1)S(1)}, bf16[128,512]{1,0:T(8,128)(2,1)S(1)}, u32[]{:S(2)}, u32[]{:S(2)}) collective-permute-start(bf16[128,512]{1,0:T(8,128)(2,1)S(1)} %get-tuple-element.117.refs_13_), channel_id=1, source_target_pairs={{0,16},{8,24},{16,0},{24,8},{1,17},{9,25},{17,1},{25,9},{2,18},{10... | collective-permute-start | bytes 393224 | tf_op jit(solution)/shard_map/ppermute | solution.py:368
  53.4 2.4 %shard_map.125 = (bf16[128,8192]{1,0:T(8,128)(2,1)}, bf16[128,8192]{1,0:T(8,128)(2,1)}, f32[128,256]{1,0:T(8,128)S(1)}, f32[128,256]{1,0:T(8,128)S(1)}) custom-call(bf16[128,8192]{1,0:T(8,128)(2,1)S(1)} %get-tuple-element.74.refs_0_, bf16[128,8192]{1,0:T(8,128)(2,1)S(1)} %get-tuple-element.75.refs_1_, ...), custom_call_target="tpu_custom_call", output_to_operand_aliasing={{0}: (11, {}), {1}: (12, {})} | custom-call | flops 1342177280 | bytes 1 | tf_op jit(solution)/shard_map/pallas_call | solution.py:334
  55.9 2.4 %shard_map.126 = (bf16[128,8192]{1,0:T(8,128)(2,1)}, bf16[128,8192]{1,0:T(8,128)(2,1)}, f32[128,256]{1,0:T(8,128)S(1)}, f32[128,256]{1,0:T(8,128)S(1)}) custom-call(bf16[128,8192]{1,0:T(8,128)(2,1)S(1)} %get-tuple-element.74.refs_0_, bf16[128,8192]{1,0:T(8,128)(2,1)S(1)} %get-tuple-element.75.refs_1_, ...), custom_call_target="tpu_custom_call", output_to_operand_aliasing={{0}: (11, {}), {1}: (12, {})} | custom-call | flops 1342177280 | bytes 1 | tf_op jit(solution)/shard_map/pallas_call | solution.py:334
  58.3 0.1 shard_map.128
  58.3 1.2 %collective-permute-start.19 = (bf16[128,512]{1,0:T(8,128)(2,1)S(1)}, bf16[128,512]{1,0:T(8,128)(2,1)S(1)}, u32[]{:S(2)}, u32[]{:S(2)}) collective-permute-start(bf16[128,512]{1,0:T(8,128)(2,1)S(1)} %get-tuple-element.124.refs_13_), channel_id=1, source_target_pairs={{0,16},{8,24},{16,0},{24,8},{1,17},{9,25},{17,1},{25,9},{2,18},{10... | collective-permute-start | bytes 393224 | tf_op jit(solution)/shard_map/ppermute | solution.py:368
  59.5 2.4 %shard_map.129 = (bf16[128,8192]{1,0:T(8,128)(2,1)}, bf16[128,8192]{1,0:T(8,128)(2,1)}, f32[128,256]{1,0:T(8,128)S(1)}, f32[128,256]{1,0:T(8,128)S(1)}) custom-call(bf16[128,8192]{1,0:T(8,128)(2,1)S(1)} %get-tuple-element.74.refs_0_, bf16[128,8192]{1,0:T(8,128)(2,1)S(1)} %get-tuple-element.75.refs_1_, ...), custom_call_target="tpu_custom_call", output_to_operand_aliasing={{0}: (11, {}), {1}: (12, {})} | custom-call | flops 1342177280 | bytes 1 | tf_op jit(solution)/shard_map/pallas_call | solution.py:334
  61.9 1.4 %collective-permute-done.19.refs_23_.refs_29_ = bf16[128,512]{1,0:T(8,128)(2,1)S(1)} collective-permute-done((bf16[128,512]{1,0:T(8,128)(2,1)S(1)}, bf16[128,512]{1,0:T(8,128)(2,1)S(1)}, u32[]{:S(2)}, u32[]{:S(2)}) %collective-permute-start.19) | collective-permute-done | bytes 131104 | tf_op jit(solution)/shard_map/ppermute | solution.py:368
  63.4 1.1 %shard_map.130 = (bf16[128,1024]{1,0:T(8,128)(2,1)}, bf16[128,1024]{1,0:T(8,128)(2,1)}, f32[16,512]{1,0:T(8,128)}) custom-call(s32[6]{0:T(128)S(4)} %get-tuple-element.77.refs_0_.flag, f32[2,16,128]{2,1,0:T(8,128)S(1)} %get-tuple-element.126.refs_0_, bf16[144,512]{1,0:T(8,128)(2,1)S(1)} %collective-permute-done.15.refs_2_.refs_1_, ...), custom_call_target="tpu_custom_call" | custom-call | tf_op jit(solution)/shard_map/pallas_call | solution.py:586
  (22 shorter events, 0.3 us)
Async XLA Ops:
  1.6 6.5 %collective-permute-start = (bf16[128,512]{1,0:T(8,128)(2,1)S(1)}, bf16[128,512]{1,0:T(8,128)(2,1)S(1)}, u32[]{:S(2)}, u32[]{:S(2)}) collective-permute-start(bf16[128,512]{1,0:T(8,128)(2,1)S(1)} %shard_map.101.refs_6_), channel_id=1, source_target_pairs={{0,16},{8,24},{16,0},{24,8},{1,17},{9,25},{17,1},{25,9},{2,18},{10... | collective-permute-start | bytes 393224 | tf_op jit(solution)/shard_map/ppermute | solution.py:368
  8.1 5.0 %collective-permute-start.1 = (bf16[128,512]{1,0:T(8,128)(2,1)S(1)}, bf16[128,512]{1,0:T(8,128)(2,1)S(1)}, u32[]{:S(2)}, u32[]{:S(2)}) collective-permute-start(bf16[128,512]{1,0:T(8,128)(2,1)S(1)} %shard_map.103), channel_id=1, source_target_pairs={{0,16},{8,24},{16,0},{24,8},{1,17},{9,25},{17,1},{25,9},{2,18},{10... | collective-permute-start | bytes 393224 | tf_op jit(solution)/shard_map/ppermute | solution.py:368
  9.9 7.3 %collective-permute-start.4 = (bf16[128,512]{1,0:T(8,128)(2,1)S(1)}, bf16[128,512]{1,0:T(8,128)(2,1)S(1)}, u32[]{:S(2)}, u32[]{:S(2)}) collective-permute-start(bf16[128,512]{1,0:T(8,128)(2,1)S(1)} %shard_map.106), channel_id=1, source_target_pairs={{0,1},{2,3},{4,5},{6,7},{1,0},{3,2},{5,4},{7,6},{8,9},{10,11},{12,... | collective-permute-start | bytes 393224 | tf_op jit(solution)/shard_map/ppermute | solution.py:376
  11.5 5.8 %collective-permute-start.5 = (bf16[128,512]{1,0:T(8,128)(2,1)S(1)}, bf16[128,512]{1,0:T(8,128)(2,1)S(1)}, u32[]{:S(2)}, u32[]{:S(2)}) collective-permute-start(bf16[128,512]{1,0:T(8,128)(2,1)S(1)} %shard_map.107), channel_id=1, source_target_pairs={{1,2},{3,4},{5,6},{2,1},{4,3},{6,5},{9,10},{11,12},{13,14},{10,9},... | collective-permute-start | bytes 393224 | tf_op jit(solution)/shard_map/ppermute | solution.py:376
  13.2 9.3 %collective-permute-start.2 = (bf16[128,512]{1,0:T(8,128)(2,1)S(1)}, bf16[128,512]{1,0:T(8,128)(2,1)S(1)}, u32[]{:S(2)}, u32[]{:S(2)}) collective-permute-start(bf16[128,512]{1,0:T(8,128)(2,1)S(1)} %shard_map.104), channel_id=1, source_target_pairs={{0,1},{2,3},{4,5},{6,7},{1,0},{3,2},{5,4},{7,6},{8,9},{10,11},{12,... | collective-permute-start | bytes 393224 | tf_op jit(solution)/shard_map/ppermute | solution.py:376
  16.6 5.9 %collective-permute-start.3 = (bf16[128,512]{1,0:T(8,128)(2,1)S(1)}, bf16[128,512]{1,0:T(8,128)(2,1)S(1)}, u32[]{:S(2)}, u32[]{:S(2)}) collective-permute-start(bf16[128,512]{1,0:T(8,128)(2,1)S(1)} %shard_map.105), channel_id=1, source_target_pairs={{1,2},{3,4},{5,6},{2,1},{4,3},{6,5},{9,10},{11,12},{13,14},{10,9},... | collective-permute-start | bytes 393224 | tf_op jit(solution)/shard_map/ppermute | solution.py:376
  17.4 5.2 %collective-permute-start.7 = (bf16[128,512]{1,0:T(8,128)(2,1)S(1)}, bf16[128,512]{1,0:T(8,128)(2,1)S(1)}, u32[]{:S(2)}, u32[]{:S(2)}) collective-permute-start(bf16[128,512]{1,0:T(8,128)(2,1)S(1)} %get-tuple-element.81.refs_6_.refs_5_), channel_id=1, source_target_pairs={{0,16},{8,24},{16,0},{24,8},{1,17},{9,25},{17,1},{25,9},{2,18},{10... | collective-permute-start | bytes 393224 | tf_op jit(solution)/shard_map/ppermute | solution.py:368
  22.6 1.6 %collective-permute-start.8 = (bf16[128,1024]{1,0:T(8,128)(2,1)S(1)}, bf16[128,1024]{1,0:T(8,128)(2,1)S(1)}, u32[]{:S(2)}, u32[]{:S(2)}) collective-permute-start(bf16[128,1024]{1,0:T(8,128)(2,1)S(1)} %get-tuple-element.87), channel_id=1, source_target_pairs={{0,8},{8,0},{16,24},{24,16},{1,9},{9,1},{17,25},{25,17},{2,10},{10... | collective-permute-start | bytes 786440 | tf_op jit(solution)/shard_map/ppermute | solution.py:372
  22.7 6.3 %collective-permute-start.6 = (bf16[128,512]{1,0:T(8,128)(2,1)S(1)}, bf16[128,512]{1,0:T(8,128)(2,1)S(1)}, u32[]{:S(2)}, u32[]{:S(2)}) collective-permute-start(bf16[128,512]{1,0:T(8,128)(2,1)S(1)} %get-tuple-element.83.refs_5_), channel_id=1, source_target_pairs={{0,16},{8,24},{16,0},{24,8},{1,17},{9,25},{17,1},{25,9},{2,18},{10... | collective-permute-start | bytes 393224 | tf_op jit(solution)/shard_map/ppermute | solution.py:368
  28.7 2.2 %collective-permute-start.10 = (bf16[128,1024]{1,0:T(8,128)(2,1)S(1)}, bf16[128,1024]{1,0:T(8,128)(2,1)S(1)}, u32[]{:S(2)}, u32[]{:S(2)}) collective-permute-start(bf16[128,1024]{1,0:T(8,128)(2,1)S(1)} %shard_map.114.refs_11_), channel_id=1, source_target_pairs={{0,8},{8,0},{16,24},{24,16},{1,9},{9,1},{17,25},{25,17},{2,10},{10... | collective-permute-start | bytes 786440 | tf_op jit(solution)/shard_map/ppermute | solution.py:372
  29.0 2.7 %collective-permute-start.9 = (bf16[128,1024]{1,0:T(8,128)(2,1)S(1)}, bf16[128,1024]{1,0:T(8,128)(2,1)S(1)}, u32[]{:S(2)}, u32[]{:S(2)}) collective-permute-start(bf16[128,1024]{1,0:T(8,128)(2,1)S(1)} %get-tuple-element.91), channel_id=1, source_target_pairs={{0,8},{8,0},{16,24},{24,16},{1,9},{9,1},{17,25},{25,17},{2,10},{10... | collective-permute-start | bytes 786440 | tf_op jit(solution)/shard_map/ppermute | solution.py:372
  31.1 5.6 %collective-permute-start.11 = (bf16[128,512]{1,0:T(8,128)(2,1)S(1)}, bf16[128,512]{1,0:T(8,128)(2,1)S(1)}, u32[]{:S(2)}, u32[]{:S(2)}) collective-permute-start(bf16[128,512]{1,0:T(8,128)(2,1)S(1)} %get-tuple-element.96.refs_7_), channel_id=1, source_target_pairs={{0,16},{8,24},{16,0},{24,8},{1,17},{9,25},{17,1},{25,9},{2,18},{10... | collective-permute-start | bytes 393224 | tf_op jit(solution)/shard_map/ppermute | solution.py:368
  36.7 1.6 %collective-permute-start.12 = (bf16[144,1024]{1,0:T(8,128)(2,1)S(1)}, bf16[144,1024]{1,0:T(8,128)(2,1)S(1)}, u32[]{:S(2)}, u32[]{:S(2)}) collective-permute-start(bf16[144,1024]{1,0:T(8,128)(2,1)S(1)} %shard_map.119), channel_id=1, source_target_pairs={{0,8},{8,0},{16,24},{24,16},{1,9},{9,1},{17,25},{25,17},{2,10},{10... | collective-permute-start | bytes 884744 | tf_op jit(solution)/shard_map/ppermute | solution.py:372
  38.5 7.5 %collective-permute-start.15 = (bf16[144,512]{1,0:T(8,128)(2,1)S(1)}, bf16[144,512]{1,0:T(8,128)(2,1)S(1)}, u32[]{:S(2)}, u32[]{:S(2)}) collective-permute-start(bf16[144,512]{1,0:T(8,128)(2,1)S(1)} %get-tuple-element.112.refs_13_.refs_3_), channel_id=1, source_target_pairs={{0,16},{8,24},{16,0},{24,8},{1,17},{9,25},{17,1},{25,9},{2,18},{10... | collective-permute-start | bytes 442376 | tf_op jit(solution)/shard_map/ppermute | solution.py:368
  39.7 12.7 %collective-permute-start.13 = (bf16[128,512]{1,0:T(8,128)(2,1)S(1)}, bf16[128,512]{1,0:T(8,128)(2,1)S(1)}, u32[]{:S(2)}, u32[]{:S(2)}) collective-permute-start(bf16[128,512]{1,0:T(8,128)(2,1)S(1)} %shard_map.118.refs_5_), channel_id=1, source_target_pairs={{0,1},{2,3},{4,5},{6,7},{1,0},{3,2},{5,4},{7,6},{8,9},{10,11},{12,... | collective-permute-start | bytes 393224 | tf_op jit(solution)/shard_map/ppermute | solution.py:376
  43.9 8.5 %collective-permute-start.14 = (bf16[128,512]{1,0:T(8,128)(2,1)S(1)}, bf16[128,512]{1,0:T(8,128)(2,1)S(1)}, u32[]{:S(2)}, u32[]{:S(2)}) collective-permute-start(bf16[128,512]{1,0:T(8,128)(2,1)S(1)} %shard_map.122), channel_id=1, source_target_pairs={{1,2},{3,4},{5,6},{2,1},{4,3},{6,5},{9,10},{11,12},{13,14},{10,9},... | collective-permute-start | bytes 393224 | tf_op jit(solution)/shard_map/ppermute | solution.py:376
  46.1 12.1 %collective-permute-start.17 = (bf16[128,512]{1,0:T(8,128)(2,1)S(1)}, bf16[128,512]{1,0:T(8,128)(2,1)S(1)}, u32[]{:S(2)}, u32[]{:S(2)}) collective-permute-start(bf16[128,512]{1,0:T(8,128)(2,1)S(1)} %shard_map.127), channel_id=1, source_target_pairs={{1,2},{3,4},{5,6},{2,1},{4,3},{6,5},{9,10},{11,12},{13,14},{10,9},... | collective-permute-start | bytes 393224 | tf_op jit(solution)/shard_map/ppermute | solution.py:376
  46.8 11.4 %collective-permute-start.16 = (bf16[128,512]{1,0:T(8,128)(2,1)S(1)}, bf16[128,512]{1,0:T(8,128)(2,1)S(1)}, u32[]{:S(2)}, u32[]{:S(2)}) collective-permute-start(bf16[128,512]{1,0:T(8,128)(2,1)S(1)} %shard_map.123.refs_5_), channel_id=1, source_target_pairs={{0,1},{2,3},{4,5},{6,7},{1,0},{3,2},{5,4},{7,6},{8,9},{10,11},{12,... | collective-permute-start | bytes 393224 | tf_op jit(solution)/shard_map/ppermute | solution.py:376
  52.5 9.4 %collective-permute-start.18 = (bf16[128,512]{1,0:T(8,128)(2,1)S(1)}, bf16[128,512]{1,0:T(8,128)(2,1)S(1)}, u32[]{:S(2)}, u32[]{:S(2)}) collective-permute-start(bf16[128,512]{1,0:T(8,128)(2,1)S(1)} %get-tuple-element.117.refs_13_), channel_id=1, source_target_pairs={{0,16},{8,24},{16,0},{24,8},{1,17},{9,25},{17,1},{25,9},{2,18},{10... | collective-permute-start | bytes 393224 | tf_op jit(solution)/shard_map/ppermute | solution.py:368
  58.3 5.0 %collective-permute-start.19 = (bf16[128,512]{1,0:T(8,128)(2,1)S(1)}, bf16[128,512]{1,0:T(8,128)(2,1)S(1)}, u32[]{:S(2)}, u32[]{:S(2)}) collective-permute-start(bf16[128,512]{1,0:T(8,128)(2,1)S(1)} %get-tuple-element.124.refs_13_), channel_id=1, source_target_pairs={{0,16},{8,24},{16,0},{24,8},{1,17},{9,25},{17,1},{25,9},{2,18},{10... | collective-permute-start | bytes 393224 | tf_op jit(solution)/shard_map/ppermute | solution.py:368

commit v5 on v4

--- a/solution.py
+++ b/solution.py
@@ -18,7 +18,7 @@
 CHUNKS = 2
 UNROLL = 2
 EXTRA = 16
-BEHIND = ((1, 1, 2), (2, 2))
+BEHIND = ((1, 1, 2), (1, 3))
 LOG2E = math.log2(math.e)
 VMEM_SMALL = 8 * 2**20
 VMEM_LARGE = 16 * 2**20
@@ -639,11 +639,11 @@
     edge0 = [edges(out0, 0)]
     ents = [ent0, ent1]
     arrived, sent = near_terms(dk1, dv1, ents, [out0])
-    keep1, give1, *own1, entropies = collect(dk1, dv1, arrived, ents)
+    done = rest(0, 1, sent[:1])
+    keep1, give1, *own1, entropies = collect(dk1, dv1, arrived, ents, done)
     back1 = across(give1)
     edge0.append(edges(edge_part([keep0], back0, True, 1, behind=[give1]), 1))
-    done = rest(0, 1, [give1])
-    out1 = [edge_part([keep1], back1, True, odd, behind=done) for odd in range(2)]
+    out1 = [edge_part([keep1], back1, True, odd) for odd in range(2)]
     edge1 = [edges(part, odd) for odd, part in enumerate(out1)]
     mine0, theirs0 = edge_done([keep0], back0, *edge0, True, behind=out1[:1])
     other0 = across(theirs0)

time: 64.6 us -> 63.5 us (0.983)
  waiting for transfers between devices: 8.32 us -> 6.34 us
  starting transfers between devices: 28.1 us -> 29 us
    ppermute x4, waiting for transfers between devices: 2.54 us -> 0.98 us  [around(): return lax.ppermute(value, 'head', pairs)]
    ppermute x8, starting transfers between devices: 17.4 us -> 18.1 us  [edges(): return lax.ppermute(value, CONTEXT, pairs + [(b, a) for a, b in pairs])]
where the time goes in v5:
time: 63.5 us; the launch traced here: 63.3 us
  starting transfers between devices  29 us (46%)
  Pallas kernels  27.1 us (43%)
  waiting for transfers between devices  6.34 us (10%)
  between operations  0.89 us (1%)
    ppermute x8, starting transfers between devices, edges(): return lax.ppermute(value, CONTEXT, pairs + [(b, a) for a, b in pairs])  18.1 us
    pallas_call x3, Pallas kernels, large(): pl.pallas_call(body, in_specs=whole(len(inputs)) + whole(len(behind), pl....  10.9 us
    pallas_call x5, Pallas kernels, the_rest(): pl.pallas_call(kernel, grid=(count,), in_specs=whole(len(inputs)) + whole...  10.2 us
    ppermute x8, starting transfers between devices, across(): lax.ppermute(value, 'head', [(j, (j + subs) % size) for j in range(size)])  10.1 us
    pallas_call x1, Pallas kernels, first_step(): pl.pallas_call(kernel, in_specs=whole(7, pl.ANY), out_specs=whole(4) + wh...  3.25 us
    ppermute x8, waiting for transfers between devices, edges(): return lax.ppermute(value, CONTEXT, pairs + [(b, a) for a, b in pairs])  2.76 us
    ppermute x8, waiting for transfers between devices, across(): lax.ppermute(value, 'head', [(j, (j + subs) % size) for j in range(size)])  2.59 us
  transfers between devices with their start and end apart: 20, of which 7 were waited for; matrix products, arithmetic and copies ran while one was open for 0% of the time, Pallas kernels for 39%

profile of v5, /device:TPU:0, one launch (start us, length us, event | category | flops | bytes accessed | tf_op | source)
XLA Modules:
  0.0 63.3 jit_solution(13716796675087008517)
XLA Ops:
  0.6 0.9 %shard_map.101.refs_6_ = bf16[128,512]{1,0:T(8,128)(2,1)S(1)} custom-call(bf16[128,1024]{1,0:T(8,128)(2,1)} %refs_2_.1, bf16[128,1024]{1,0:T(8,128)(2,1)} %refs_3_.1), custom_call_target="tpu_custom_call" | custom-call | tf_op jit(solution)/shard_map/pallas_call | solution.py:390
  1.6 3.0 %collective-permute-start = (bf16[128,512]{1,0:T(8,128)(2,1)S(1)}, bf16[128,512]{1,0:T(8,128)(2,1)S(1)}, u32[]{:S(2)}, u32[]{:S(2)}) collective-permute-start(bf16[128,512]{1,0:T(8,128)(2,1)S(1)} %shard_map.101.refs_6_), channel_id=1, source_target_pairs={{0,16},{8,24},{16,0},{24,8},{1,17},{9,25},{17,1},{25,9},{2,18},{10... | collective-permute-start | bytes 393224 | tf_op jit(solution)/shard_map/ppermute | solution.py:368
  4.6 3.2 %shard_map.102 = (bf16[128,8192]{1,0:T(8,128)(2,1)S(1)}, bf16[128,8192]{1,0:T(8,128)(2,1)S(1)}, bf16[128,1024]{1,0:T(8,128)(2,1)S(1)}, bf16[128,1024]{1,0:T(8,12...) custom-call(bf16[128,8192]{1,0:T(8,128)(2,1)} %refs_0_.1, ...), custom_call_target="tpu_custom_call" | custom-call | flops 805306368 | bytes 1 | tf_op jit(solution)/shard_map/pallas_call | solution.py:278
  7.9 0.2 collective-permute-done.refs_3_
  8.1 1.8 %collective-permute-start.1 = (bf16[128,512]{1,0:T(8,128)(2,1)S(1)}, bf16[128,512]{1,0:T(8,128)(2,1)S(1)}, u32[]{:S(2)}, u32[]{:S(2)}) collective-permute-start(bf16[128,512]{1,0:T(8,128)(2,1)S(1)} %shard_map.103), channel_id=1, source_target_pairs={{0,16},{8,24},{16,0},{24,8},{1,17},{9,25},{17,1},{25,9},{2,18},{10... | collective-permute-start | bytes 393224 | tf_op jit(solution)/shard_map/ppermute | solution.py:368
  9.9 1.6 %collective-permute-start.4 = (bf16[128,512]{1,0:T(8,128)(2,1)S(1)}, bf16[128,512]{1,0:T(8,128)(2,1)S(1)}, u32[]{:S(2)}, u32[]{:S(2)}) collective-permute-start(bf16[128,512]{1,0:T(8,128)(2,1)S(1)} %shard_map.106), channel_id=1, source_target_pairs={{0,1},{2,3},{4,5},{6,7},{1,0},{3,2},{5,4},{7,6},{8,9},{10,11},{12,... | collective-permute-start | bytes 393224 | tf_op jit(solution)/shard_map/ppermute | solution.py:376
  11.5 0.7 %collective-permute-start.5 = (bf16[128,512]{1,0:T(8,128)(2,1)S(1)}, bf16[128,512]{1,0:T(8,128)(2,1)S(1)}, u32[]{:S(2)}, u32[]{:S(2)}) collective-permute-start(bf16[128,512]{1,0:T(8,128)(2,1)S(1)} %shard_map.107), channel_id=1, source_target_pairs={{1,2},{3,4},{5,6},{2,1},{4,3},{6,5},{9,10},{11,12},{13,14},{10,9},... | collective-permute-start | bytes 393224 | tf_op jit(solution)/shard_map/ppermute | solution.py:376
  12.2 1.0 %collective-permute-done.1.refs_3_ = bf16[128,512]{1,0:T(8,128)(2,1)S(1)} collective-permute-done((bf16[128,512]{1,0:T(8,128)(2,1)S(1)}, bf16[128,512]{1,0:T(8,128)(2,1)S(1)}, u32[]{:S(2)}, u32[]{:S(2)}) %collective-permute-start.1) | collective-permute-done | bytes 131104 | tf_op jit(solution)/shard_map/ppermute | solution.py:368
  13.2 3.4 %collective-permute-start.2 = (bf16[128,512]{1,0:T(8,128)(2,1)S(1)}, bf16[128,512]{1,0:T(8,128)(2,1)S(1)}, u32[]{:S(2)}, u32[]{:S(2)}) collective-permute-start(bf16[128,512]{1,0:T(8,128)(2,1)S(1)} %shard_map.104), channel_id=1, source_target_pairs={{0,1},{2,3},{4,5},{6,7},{1,0},{3,2},{5,4},{7,6},{8,9},{10,11},{12,... | collective-permute-start | bytes 393224 | tf_op jit(solution)/shard_map/ppermute | solution.py:376
  16.6 0.7 %collective-permute-start.3 = (bf16[128,512]{1,0:T(8,128)(2,1)S(1)}, bf16[128,512]{1,0:T(8,128)(2,1)S(1)}, u32[]{:S(2)}, u32[]{:S(2)}) collective-permute-start(bf16[128,512]{1,0:T(8,128)(2,1)S(1)} %shard_map.105), channel_id=1, source_target_pairs={{1,2},{3,4},{5,6},{2,1},{4,3},{6,5},{9,10},{11,12},{13,14},{10,9},... | collective-permute-start | bytes 393224 | tf_op jit(solution)/shard_map/ppermute | solution.py:376
  17.3 0.0 collective-permute-done.4.refs_4_
  17.3 0.0 collective-permute-done.5.refs_5_
  17.3 0.1 shard_map.108
  17.4 0.5 collective-permute-start.7
  17.9 1.7 %shard_map.110.refs_6_ = f32[4,8,1024]{2,1,0:T(8,128)S(1)} custom-call(bf16[128,8192]{1,0:T(8,128)(2,1)S(1)} %get-tuple-element.74.refs_0_, bf16[128,8192]{1,0:T(8,128)(2,1)S(1)} %get-tuple-element.75.refs_1_, bf16[128,1024]{1,0:T(8,128)(2,1)S(1)} %get-tuple-element.78.refs_1_.refs_2_.refs_6_, ...), custom_call_target="tpu_custom_call" | custom-call | flops 536870912 | bytes 1 | tf_op jit(solution)/shard_map/pallas_call | solution.py:257
  19.7 2.7 %collective-permute-done.2.refs_4_ = bf16[128,512]{1,0:T(8,128)(2,1)S(1)} collective-permute-done((bf16[128,512]{1,0:T(8,128)(2,1)S(1)}, bf16[128,512]{1,0:T(8,128)(2,1)S(1)}, u32[]{:S(2)}, u32[]{:S(2)}) %collective-permute-start.2) | collective-permute-done | bytes 131104 | tf_op jit(solution)/shard_map/ppermute | solution.py:376
  22.5 0.0 collective-permute-done.7.refs_4_
  22.5 0.1 shard_map.111
  22.6 0.1 collective-permute-start.8
  22.6 0.6 collective-permute-start.6
  23.2 0.9 %collective-permute-done.8.refs_5_ = bf16[128,1024]{1,0:T(8,128)(2,1)S(1)} collective-permute-done((bf16[128,1024]{1,0:T(8,128)(2,1)S(1)}, bf16[128,1024]{1,0:T(8,128)(2,1)S(1)}, u32[]{:S(2)}, u32[]{:S(2)}) %collective-permute-start.8) | collective-permute-done | bytes 262176 | tf_op jit(solution)/shard_map/ppermute | solution.py:372
  24.2 4.5 %shard_map.112 = (f32[4,8,128]{2,1,0:T(8,128)S(1)}, f32[4,8,1024]{2,1,0:T(8,128)S(1)}, bf16[4,256,1024]{2,1,0:T(8,128)(2,1)S(1)}, bf16[4,256,1024]{2,1,0:T(8,128...) custom-call(bf16[128,8192]{1,0:T(8,128)(2,1)S(1)} %get-tuple-element, ...), custom_call_target="tpu_custom_call" | custom-call | flops 2147483648 | bytes 1 | tf_op jit(solution)/shard_map/pallas_call | solution.py:257
  28.7 0.2 collective-permute-start.10
  29.0 0.4 collective-permute-start.9
  29.4 1.5 %shard_map.116 = (bf16[128,8192]{1,0:T(8,128)(2,1)}, bf16[128,8192]{1,0:T(8,128)(2,1)}, f32[128,128]{1,0:T(8,128)S(1)}, f32[128,128]{1,0:T(8,128)S(1)}) custom-call(bf16[128,8192]{1,0:T(8,128)(2,1)S(1)} %get-tuple-element.74.refs_0_, bf16[128,8192]{1,0:T(8,128)(2,1)S(1)} %get-tuple-element.75.refs_1_, f32[384,128]{1,0:T(8,128)S(1)} %get-tuple-element.76.refs_4_.refs_2_, ...), custom_call_target="tpu_custom_call" | custom-call | flops 671088640 | bytes 1 | tf_op jit(solution)/shard_map/pallas_call | solution.py:334
  30.9 0.1 shard_map.115
  31.1 0.6 %collective-permute-start.11 = (bf16[128,512]{1,0:T(8,128)(2,1)S(1)}, bf16[128,512]{1,0:T(8,128)(2,1)S(1)}, u32[]{:S(2)}, u32[]{:S(2)}) collective-permute-start(bf16[128,512]{1,0:T(8,128)(2,1)S(1)} %get-tuple-element.96.refs_7_), channel_id=1, source_target_pairs={{0,16},{8,24},{16,0},{24,8},{1,17},{9,25},{17,1},{25,9},{2,18},{10... | collective-permute-start | bytes 393224 | tf_op jit(solution)/shard_map/ppermute | solution.py:368
  31.7 4.6 %shard_map.117 = (f32[4,8,128]{2,1,0:T(8,128)S(1)}, f32[4,8,1024]{2,1,0:T(8,128)S(1)}, bf16[4,256,1024]{2,1,0:T(8,128)(2,1)S(1)}, bf16[4,256,1024]{2,1,0:T(8,128...) custom-call(bf16[128,8192]{1,0:T(8,128)(2,1)S(1)} %get-tuple-element, ...), custom_call_target="tpu_custom_call" | custom-call | flops 2147483648 | bytes 1 | tf_op jit(solution)/shard_map/pallas_call | solution.py:257
  36.3 0.4 collective-permute-done.11.refs_2_
  36.7 0.1 collective-permute-start.13
  36.8 1.5 %shard_map.120 = (bf16[128,8192]{1,0:T(8,128)(2,1)}, bf16[128,8192]{1,0:T(8,128)(2,1)}, f32[128,128]{1,0:T(8,128)S(1)}, f32[128,128]{1,0:T(8,128)S(1)}) custom-call(bf16[128,8192]{1,0:T(8,128)(2,1)S(1)} %get-tuple-element.74.refs_0_, bf16[128,8192]{1,0:T(8,128)(2,1)S(1)} %get-tuple-element.75.refs_1_, ...), custom_call_target="tpu_custom_call", output_to_operand_aliasing={{0}: (11, {}), {1}: (12, {})} | custom-call | flops 671088640 | bytes 1 | tf_op jit(solution)/shard_map/pallas_call | solution.py:334
  38.3 0.0 collective-permute-done.13.refs_5_
  38.4 0.1 shard_map.121
  38.5 1.2 %collective-permute-start.15 = (bf16[144,512]{1,0:T(8,128)(2,1)S(1)}, bf16[144,512]{1,0:T(8,128)(2,1)S(1)}, u32[]{:S(2)}, u32[]{:S(2)}) collective-permute-start(bf16[144,512]{1,0:T(8,128)(2,1)S(1)} %get-tuple-element.115.refs_3_), channel_id=1, source_target_pairs={{0,16},{8,24},{16,0},{24,8},{1,17},{9,25},{17,1},{25,9},{2,18},{10... | collective-permute-start | bytes 442376 | tf_op jit(solution)/shard_map/ppermute | solution.py:368
  39.7 4.2 %collective-permute-start.12 = (bf16[128,512]{1,0:T(8,128)(2,1)S(1)}, bf16[128,512]{1,0:T(8,128)(2,1)S(1)}, u32[]{:S(2)}, u32[]{:S(2)}) collective-permute-start(bf16[128,512]{1,0:T(8,128)(2,1)S(1)} %shard_map.118.refs_5_), channel_id=1, source_target_pairs={{0,1},{2,3},{4,5},{6,7},{1,0},{3,2},{5,4},{7,6},{8,9},{10,11},{12,... | collective-permute-start | bytes 393224 | tf_op jit(solution)/shard_map/ppermute | solution.py:376
  43.9 0.7 %collective-permute-start.14 = (bf16[128,512]{1,0:T(8,128)(2,1)S(1)}, bf16[128,512]{1,0:T(8,128)(2,1)S(1)}, u32[]{:S(2)}, u32[]{:S(2)}) collective-permute-start(bf16[128,512]{1,0:T(8,128)(2,1)S(1)} %shard_map.122), channel_id=1, source_target_pairs={{1,2},{3,4},{5,6},{2,1},{4,3},{6,5},{9,10},{11,12},{13,14},{10,9},... | collective-permute-start | bytes 393224 | tf_op jit(solution)/shard_map/ppermute | solution.py:376
  44.6 0.2 collective-permute-done.15.refs_2_.refs_1_
  44.8 0.7 %collective-permute-start.17 = (bf16[128,512]{1,0:T(8,128)(2,1)S(1)}, bf16[128,512]{1,0:T(8,128)(2,1)S(1)}, u32[]{:S(2)}, u32[]{:S(2)}) collective-permute-start(bf16[128,512]{1,0:T(8,128)(2,1)S(1)} %shard_map.127), channel_id=1, source_target_pairs={{1,2},{3,4},{5,6},{2,1},{4,3},{6,5},{9,10},{11,12},{13,14},{10,9},... | collective-permute-start | bytes 393224 | tf_op jit(solution)/shard_map/ppermute | solution.py:376
  45.5 6.3 %collective-permute-start.16 = (bf16[128,512]{1,0:T(8,128)(2,1)S(1)}, bf16[128,512]{1,0:T(8,128)(2,1)S(1)}, u32[]{:S(2)}, u32[]{:S(2)}) collective-permute-start(bf16[128,512]{1,0:T(8,128)(2,1)S(1)} %shard_map.123.refs_5_), channel_id=1, source_target_pairs={{0,1},{2,3},{4,5},{6,7},{1,0},{3,2},{5,4},{7,6},{8,9},{10,11},{12,... | collective-permute-start | bytes 393224 | tf_op jit(solution)/shard_map/ppermute | solution.py:376
  51.9 1.2 %collective-permute-start.18 = (bf16[128,512]{1,0:T(8,128)(2,1)S(1)}, bf16[128,512]{1,0:T(8,128)(2,1)S(1)}, u32[]{:S(2)}, u32[]{:S(2)}) collective-permute-start(bf16[128,512]{1,0:T(8,128)(2,1)S(1)} %get-tuple-element.117.refs_13_), channel_id=1, source_target_pairs={{0,16},{8,24},{16,0},{24,8},{1,17},{9,25},{17,1},{25,9},{2,18},{10... | collective-permute-start | bytes 393224 | tf_op jit(solution)/shard_map/ppermute | solution.py:368
  53.0 2.4 %shard_map.125 = (bf16[128,8192]{1,0:T(8,128)(2,1)}, bf16[128,8192]{1,0:T(8,128)(2,1)}, f32[128,256]{1,0:T(8,128)S(1)}, f32[128,256]{1,0:T(8,128)S(1)}) custom-call(bf16[128,8192]{1,0:T(8,128)(2,1)S(1)} %get-tuple-element.74.refs_0_, bf16[128,8192]{1,0:T(8,128)(2,1)S(1)} %get-tuple-element.75.refs_1_, ...), custom_call_target="tpu_custom_call", output_to_operand_aliasing={{0}: (11, {}), {1}: (12, {})} | custom-call | flops 1342177280 | bytes 1 | tf_op jit(solution)/shard_map/pallas_call | solution.py:334
  55.5 1.5 %shard_map.126 = (bf16[128,8192]{1,0:T(8,128)(2,1)}, bf16[128,8192]{1,0:T(8,128)(2,1)}, f32[128,128]{1,0:T(8,128)S(1)}, f32[128,128]{1,0:T(8,128)S(1)}) custom-call(bf16[128,8192]{1,0:T(8,128)(2,1)S(1)} %get-tuple-element.74.refs_0_, bf16[128,8192]{1,0:T(8,128)(2,1)S(1)} %get-tuple-element.75.refs_1_, ...), custom_call_target="tpu_custom_call", output_to_operand_aliasing={{0}: (11, {}), {1}: (12, {})} | custom-call | flops 671088640 | bytes 1 | tf_op jit(solution)/shard_map/pallas_call | solution.py:334
  57.0 0.0 collective-permute-done.17.refs_4_
  57.0 0.0 collective-permute-done.16.refs_3_
  57.0 1.1 %collective-permute-start.19 = (bf16[128,512]{1,0:T(8,128)(2,1)S(1)}, bf16[128,512]{1,0:T(8,128)(2,1)S(1)}, u32[]{:S(2)}, u32[]{:S(2)}) collective-permute-start(bf16[128,512]{1,0:T(8,128)(2,1)S(1)} %get-tuple-element.124.refs_13_), channel_id=1, source_target_pairs={{0,16},{8,24},{16,0},{24,8},{1,17},{9,25},{17,1},{25,9},{2,18},{10... | collective-permute-start | bytes 393224 | tf_op jit(solution)/shard_map/ppermute | solution.py:368
  58.1 3.3 %shard_map.129 = (bf16[128,8192]{1,0:T(8,128)(2,1)}, bf16[128,8192]{1,0:T(8,128)(2,1)}, f32[128,384]{1,0:T(8,128)S(1)}, f32[128,384]{1,0:T(8,128)S(1)}) custom-call(bf16[128,8192]{1,0:T(8,128)(2,1)S(1)} %get-tuple-element.74.refs_0_, bf16[128,8192]{1,0:T(8,128)(2,1)S(1)} %get-tuple-element.75.refs_1_, ...), custom_call_target="tpu_custom_call", output_to_operand_aliasing={{0}: (11, {}), {1}: (12, {})} | custom-call | flops 2013265920 | bytes 1 | tf_op jit(solution)/shard_map/pallas_call | solution.py:334
  61.4 0.8 %collective-permute-done.19.refs_23_.refs_29_ = bf16[128,512]{1,0:T(8,128)(2,1)S(1)} collective-permute-done((bf16[128,512]{1,0:T(8,128)(2,1)S(1)}, bf16[128,512]{1,0:T(8,128)(2,1)S(1)}, u32[]{:S(2)}, u32[]{:S(2)}) %collective-permute-start.19) | collective-permute-done | bytes 131104 | tf_op jit(solution)/shard_map/ppermute | solution.py:368
  62.2 1.1 %shard_map.130 = (bf16[128,1024]{1,0:T(8,128)(2,1)}, bf16[128,1024]{1,0:T(8,128)(2,1)}, f32[16,512]{1,0:T(8,128)}) custom-call(s32[6]{0:T(128)S(4)} %get-tuple-element.77.refs_0_.flag, f32[2,16,128]{2,1,0:T(8,128)S(1)} %get-tuple-element.126.refs_0_, bf16[144,512]{1,0:T(8,128)(2,1)S(1)} %collective-permute-done.15.refs_2_.refs_1_, ...), custom_call_target="tpu_custom_call" | custom-call | tf_op jit(solution)/shard_map/pallas_call | solution.py:586
  (22 shorter events, 0.4 us)
Async XLA Ops:
  1.6 6.5 %collective-permute-start = (bf16[128,512]{1,0:T(8,128)(2,1)S(1)}, bf16[128,512]{1,0:T(8,128)(2,1)S(1)}, u32[]{:S(2)}, u32[]{:S(2)}) collective-permute-start(bf16[128,512]{1,0:T(8,128)(2,1)S(1)} %shard_map.101.refs_6_), channel_id=1, source_target_pairs={{0,16},{8,24},{16,0},{24,8},{1,17},{9,25},{17,1},{25,9},{2,18},{10... | collective-permute-start | bytes 393224 | tf_op jit(solution)/shard_map/ppermute | solution.py:368
  8.1 5.0 %collective-permute-start.1 = (bf16[128,512]{1,0:T(8,128)(2,1)S(1)}, bf16[128,512]{1,0:T(8,128)(2,1)S(1)}, u32[]{:S(2)}, u32[]{:S(2)}) collective-permute-start(bf16[128,512]{1,0:T(8,128)(2,1)S(1)} %shard_map.103), channel_id=1, source_target_pairs={{0,16},{8,24},{16,0},{24,8},{1,17},{9,25},{17,1},{25,9},{2,18},{10... | collective-permute-start | bytes 393224 | tf_op jit(solution)/shard_map/ppermute | solution.py:368
  9.9 7.4 %collective-permute-start.4 = (bf16[128,512]{1,0:T(8,128)(2,1)S(1)}, bf16[128,512]{1,0:T(8,128)(2,1)S(1)}, u32[]{:S(2)}, u32[]{:S(2)}) collective-permute-start(bf16[128,512]{1,0:T(8,128)(2,1)S(1)} %shard_map.106), channel_id=1, source_target_pairs={{0,1},{2,3},{4,5},{6,7},{1,0},{3,2},{5,4},{7,6},{8,9},{10,11},{12,... | collective-permute-start | bytes 393224 | tf_op jit(solution)/shard_map/ppermute | solution.py:376
  11.5 5.8 %collective-permute-start.5 = (bf16[128,512]{1,0:T(8,128)(2,1)S(1)}, bf16[128,512]{1,0:T(8,128)(2,1)S(1)}, u32[]{:S(2)}, u32[]{:S(2)}) collective-permute-start(bf16[128,512]{1,0:T(8,128)(2,1)S(1)} %shard_map.107), channel_id=1, source_target_pairs={{1,2},{3,4},{5,6},{2,1},{4,3},{6,5},{9,10},{11,12},{13,14},{10,9},... | collective-permute-start | bytes 393224 | tf_op jit(solution)/shard_map/ppermute | solution.py:376
  13.2 9.3 %collective-permute-start.2 = (bf16[128,512]{1,0:T(8,128)(2,1)S(1)}, bf16[128,512]{1,0:T(8,128)(2,1)S(1)}, u32[]{:S(2)}, u32[]{:S(2)}) collective-permute-start(bf16[128,512]{1,0:T(8,128)(2,1)S(1)} %shard_map.104), channel_id=1, source_target_pairs={{0,1},{2,3},{4,5},{6,7},{1,0},{3,2},{5,4},{7,6},{8,9},{10,11},{12,... | collective-permute-start | bytes 393224 | tf_op jit(solution)/shard_map/ppermute | solution.py:376
  16.6 5.8 %collective-permute-start.3 = (bf16[128,512]{1,0:T(8,128)(2,1)S(1)}, bf16[128,512]{1,0:T(8,128)(2,1)S(1)}, u32[]{:S(2)}, u32[]{:S(2)}) collective-permute-start(bf16[128,512]{1,0:T(8,128)(2,1)S(1)} %shard_map.105), channel_id=1, source_target_pairs={{1,2},{3,4},{5,6},{2,1},{4,3},{6,5},{9,10},{11,12},{13,14},{10,9},... | collective-permute-start | bytes 393224 | tf_op jit(solution)/shard_map/ppermute | solution.py:376
  17.4 5.1 %collective-permute-start.7 = (bf16[128,512]{1,0:T(8,128)(2,1)S(1)}, bf16[128,512]{1,0:T(8,128)(2,1)S(1)}, u32[]{:S(2)}, u32[]{:S(2)}) collective-permute-start(bf16[128,512]{1,0:T(8,128)(2,1)S(1)} %get-tuple-element.81.refs_6_.refs_5_), channel_id=1, source_target_pairs={{0,16},{8,24},{16,0},{24,8},{1,17},{9,25},{17,1},{25,9},{2,18},{10... | collective-permute-start | bytes 393224 | tf_op jit(solution)/shard_map/ppermute | solution.py:368
  22.6 1.6 %collective-permute-start.8 = (bf16[128,1024]{1,0:T(8,128)(2,1)S(1)}, bf16[128,1024]{1,0:T(8,128)(2,1)S(1)}, u32[]{:S(2)}, u32[]{:S(2)}) collective-permute-start(bf16[128,1024]{1,0:T(8,128)(2,1)S(1)} %get-tuple-element.87), channel_id=1, source_target_pairs={{0,8},{8,0},{16,24},{24,16},{1,9},{9,1},{17,25},{25,17},{2,10},{10... | collective-permute-start | bytes 786440 | tf_op jit(solution)/shard_map/ppermute | solution.py:372
  22.6 6.3 %collective-permute-start.6 = (bf16[128,512]{1,0:T(8,128)(2,1)S(1)}, bf16[128,512]{1,0:T(8,128)(2,1)S(1)}, u32[]{:S(2)}, u32[]{:S(2)}) collective-permute-start(bf16[128,512]{1,0:T(8,128)(2,1)S(1)} %get-tuple-element.83.refs_5_), channel_id=1, source_target_pairs={{0,16},{8,24},{16,0},{24,8},{1,17},{9,25},{17,1},{25,9},{2,18},{10... | collective-permute-start | bytes 393224 | tf_op jit(solution)/shard_map/ppermute | solution.py:368
  28.7 2.2 %collective-permute-start.10 = (bf16[128,1024]{1,0:T(8,128)(2,1)S(1)}, bf16[128,1024]{1,0:T(8,128)(2,1)S(1)}, u32[]{:S(2)}, u32[]{:S(2)}) collective-permute-start(bf16[128,1024]{1,0:T(8,128)(2,1)S(1)} %shard_map.114.refs_11_), channel_id=1, source_target_pairs={{0,8},{8,0},{16,24},{24,16},{1,9},{9,1},{17,25},{25,17},{2,10},{10... | collective-permute-start | bytes 786440 | tf_op jit(solution)/shard_map/ppermute | solution.py:372
  29.0 2.7 %collective-permute-start.9 = (bf16[128,1024]{1,0:T(8,128)(2,1)S(1)}, bf16[128,1024]{1,0:T(8,128)(2,1)S(1)}, u32[]{:S(2)}, u32[]{:S(2)}) collective-permute-start(bf16[128,1024]{1,0:T(8,128)(2,1)S(1)} %get-tuple-element.91), channel_id=1, source_target_pairs={{0,8},{8,0},{16,24},{24,16},{1,9},{9,1},{17,25},{25,17},{2,10},{10... | collective-permute-start | bytes 786440 | tf_op jit(solution)/shard_map/ppermute | solution.py:372
  31.1 5.6 %collective-permute-start.11 = (bf16[128,512]{1,0:T(8,128)(2,1)S(1)}, bf16[128,512]{1,0:T(8,128)(2,1)S(1)}, u32[]{:S(2)}, u32[]{:S(2)}) collective-permute-start(bf16[128,512]{1,0:T(8,128)(2,1)S(1)} %get-tuple-element.96.refs_7_), channel_id=1, source_target_pairs={{0,16},{8,24},{16,0},{24,8},{1,17},{9,25},{17,1},{25,9},{2,18},{10... | collective-permute-start | bytes 393224 | tf_op jit(solution)/shard_map/ppermute | solution.py:368
  36.7 1.6 %collective-permute-start.13 = (bf16[144,1024]{1,0:T(8,128)(2,1)S(1)}, bf16[144,1024]{1,0:T(8,128)(2,1)S(1)}, u32[]{:S(2)}, u32[]{:S(2)}) collective-permute-start(bf16[144,1024]{1,0:T(8,128)(2,1)S(1)} %shard_map.119.refs_13_), channel_id=1, source_target_pairs={{0,8},{8,0},{16,24},{24,16},{1,9},{9,1},{17,25},{25,17},{2,10},{10... | collective-permute-start | bytes 884744 | tf_op jit(solution)/shard_map/ppermute | solution.py:372
  38.5 6.3 %collective-permute-start.15 = (bf16[144,512]{1,0:T(8,128)(2,1)S(1)}, bf16[144,512]{1,0:T(8,128)(2,1)S(1)}, u32[]{:S(2)}, u32[]{:S(2)}) collective-permute-start(bf16[144,512]{1,0:T(8,128)(2,1)S(1)} %get-tuple-element.115.refs_3_), channel_id=1, source_target_pairs={{0,16},{8,24},{16,0},{24,8},{1,17},{9,25},{17,1},{25,9},{2,18},{10... | collective-permute-start | bytes 442376 | tf_op jit(solution)/shard_map/ppermute | solution.py:368
  39.7 12.1 %collective-permute-start.12 = (bf16[128,512]{1,0:T(8,128)(2,1)S(1)}, bf16[128,512]{1,0:T(8,128)(2,1)S(1)}, u32[]{:S(2)}, u32[]{:S(2)}) collective-permute-start(bf16[128,512]{1,0:T(8,128)(2,1)S(1)} %shard_map.118.refs_5_), channel_id=1, source_target_pairs={{0,1},{2,3},{4,5},{6,7},{1,0},{3,2},{5,4},{7,6},{8,9},{10,11},{12,... | collective-permute-start | bytes 393224 | tf_op jit(solution)/shard_map/ppermute | solution.py:376
  43.9 7.9 %collective-permute-start.14 = (bf16[128,512]{1,0:T(8,128)(2,1)S(1)}, bf16[128,512]{1,0:T(8,128)(2,1)S(1)}, u32[]{:S(2)}, u32[]{:S(2)}) collective-permute-start(bf16[128,512]{1,0:T(8,128)(2,1)S(1)} %shard_map.122), channel_id=1, source_target_pairs={{1,2},{3,4},{5,6},{2,1},{4,3},{6,5},{9,10},{11,12},{13,14},{10,9},... | collective-permute-start | bytes 393224 | tf_op jit(solution)/shard_map/ppermute | solution.py:376
  44.8 12.2 %collective-permute-start.17 = (bf16[128,512]{1,0:T(8,128)(2,1)S(1)}, bf16[128,512]{1,0:T(8,128)(2,1)S(1)}, u32[]{:S(2)}, u32[]{:S(2)}) collective-permute-start(bf16[128,512]{1,0:T(8,128)(2,1)S(1)} %shard_map.127), channel_id=1, source_target_pairs={{1,2},{3,4},{5,6},{2,1},{4,3},{6,5},{9,10},{11,12},{13,14},{10,9},... | collective-permute-start | bytes 393224 | tf_op jit(solution)/shard_map/ppermute | solution.py:376
  45.5 11.5 %collective-permute-start.16 = (bf16[128,512]{1,0:T(8,128)(2,1)S(1)}, bf16[128,512]{1,0:T(8,128)(2,1)S(1)}, u32[]{:S(2)}, u32[]{:S(2)}) collective-permute-start(bf16[128,512]{1,0:T(8,128)(2,1)S(1)} %shard_map.123.refs_5_), channel_id=1, source_target_pairs={{0,1},{2,3},{4,5},{6,7},{1,0},{3,2},{5,4},{7,6},{8,9},{10,11},{12,... | collective-permute-start | bytes 393224 | tf_op jit(solution)/shard_map/ppermute | solution.py:376
  51.9 9.5 %collective-permute-start.18 = (bf16[128,512]{1,0:T(8,128)(2,1)S(1)}, bf16[128,512]{1,0:T(8,128)(2,1)S(1)}, u32[]{:S(2)}, u32[]{:S(2)}) collective-permute-start(bf16[128,512]{1,0:T(8,128)(2,1)S(1)} %get-tuple-element.117.refs_13_), channel_id=1, source_target_pairs={{0,16},{8,24},{16,0},{24,8},{1,17},{9,25},{17,1},{25,9},{2,18},{10... | collective-permute-start | bytes 393224 | tf_op jit(solution)/shard_map/ppermute | solution.py:368
  57.0 5.2 %collective-permute-start.19 = (bf16[128,512]{1,0:T(8,128)(2,1)S(1)}, bf16[128,512]{1,0:T(8,128)(2,1)S(1)}, u32[]{:S(2)}, u32[]{:S(2)}) collective-permute-start(bf16[128,512]{1,0:T(8,128)(2,1)S(1)} %get-tuple-element.124.refs_13_), channel_id=1, source_target_pairs={{0,16},{8,24},{16,0},{24,8},{1,17},{9,25},{17,1},{25,9},{2,18},{10... | collective-permute-start | bytes 393224 | tf_op jit(solution)/shard_map/ppermute | solution.py:368

commit v6 on v5

--- a/solution.py
+++ b/solution.py
@@ -18,7 +18,7 @@
 CHUNKS = 2
 UNROLL = 2
 EXTRA = 16
-BEHIND = ((1, 1, 2), (1, 3))
+BEHIND = ((1, 3), (4,))
 LOG2E = math.log2(math.e)
 VMEM_SMALL = 8 * 2**20
 VMEM_LARGE = 16 * 2**20
@@ -229,7 +229,7 @@
     return pltpu.with_memory_space_constraint(value, pltpu.SMEM)
 
 
-def small(kernel, flags, inputs, outs, behind=()):
+def small(kernel, flags, inputs, outs, behind=(), price=None):
     def body(*refs):
         kernel(*refs[: 1 + len(inputs)], *refs[1 + len(inputs) + len(behind) :])
 
@@ -239,6 +239,7 @@
         out_specs=whole(len(outs)),
         out_shape=[pltpu.VMEM(shape, dtype) for shape, dtype in outs],
         compiler_params=pltpu.CompilerParams(vmem_limit_bytes=VMEM_SMALL),
+        cost_estimate=price,
     )(in_scalars(flags), *[near_by(value) for value in inputs], *behind)
 
 
@@ -409,7 +410,7 @@
     def out_of_step(flag, backward):
         return (flag[3] + flag[4] + (1 if backward else 0)) % 2
 
-    def edge_part(own, got, backward, odd, cols=slice(None), behind=()):
+    def edge_part(own, got, backward, odd, cols=slice(None), behind=(), price=None):
         def kernel(flag, *refs):
             own, (got, out) = refs[:-2], refs[-2:]
             keeps = out_of_step(flag, backward) != odd
@@ -423,7 +424,7 @@
             def _():
                 out[...] = got[:rows, :]
 
-        return small(kernel, flags, [*own, got], [half], behind)[0]
+        return small(kernel, flags, [*own, got], [half], behind, price)[0]
 
     def edge_done(own, got, even, odd, backward, cols=slice(None), behind=()):
         def kernel(flag, *refs):
@@ -593,6 +594,12 @@
             + [jax.ShapeDtypeStruct((count, size * rows), jnp.float32)],
             compiler_params=pltpu.CompilerParams(vmem_limit_bytes=VMEM_SMALL),
         )(in_scalars(flags), *[near_by(v) for v in local])
+
+    def taken(value, behind=(), price=None):
+        def kernel(flag, value, out):
+            out[...] = value[...]
+
+        return small(kernel, flags, [value], [half], behind, price)[0]
 
     per_chunk = KEY_VALUE_HEADS // CHUNKS
     got = [across(first_give)]
@@ -639,21 +646,20 @@
     edge0 = [edges(out0, 0)]
     ents = [ent0, ent1]
     arrived, sent = near_terms(dk1, dv1, ents, [out0])
-    done = rest(0, 1, sent[:1])
-    keep1, give1, *own1, entropies = collect(dk1, dv1, arrived, ents, done)
+    keep1, give1, *own1, entropies = collect(dk1, dv1, arrived, ents)
     back1 = across(give1)
-    edge0.append(edges(edge_part([keep0], back0, True, 1, behind=[give1]), 1))
+    edge0.append(edges(edge_part([keep0], back0, True, 1, behind=[give1], price=cost(4, rows, 10)), 1))
     out1 = [edge_part([keep1], back1, True, odd) for odd in range(2)]
     edge1 = [edges(part, odd) for odd, part in enumerate(out1)]
     mine0, theirs0 = edge_done([keep0], back0, *edge0, True, behind=out1[:1])
     other0 = across(theirs0)
-    done = rest(0, 2, [theirs0])
-    done = rest(1, 0, done)
+    done = rest(0, 1, [theirs0])
+    edge1[0] = taken(taken(edge1[0], done), price=cost(4, rows, 10))
     mine1, theirs1 = edge_done([keep1], back1, *edge1, True, behind=done)
     other1 = across(theirs1)
-    rest(1, 1, [theirs1])
+    rest(1, 0, [theirs1])
     grad_key, grad_value, entropy = finish(
-        [(*own0, pieces[:3], mine0, other0), (*own1, pieces[3:], mine1, other1)], entropies, back1
+        [(*own0, pieces[:2], mine0, other0), (*own1, pieces[2:], mine1, other1)], entropies, back1
     )
     return wide[0], entropy.T, wide[1], grad_key, grad_value
 

time: 63.5 us -> 63.2 us (level)
  waiting for transfers between devices: 6.34 us -> 9.42 us
  starting transfers between devices: 29 us -> 26.9 us
  Pallas kernels: 27.1 us -> 25.8 us
    ppermute x8, waiting for transfers between devices: 2.59 us -> 5.69 us  [across(): lax.ppermute(value, 'head', [(j, (j + subs) % size) for j in range(size)])]
    ppermute x8, starting transfers between devices: 18.1 us -> 16.2 us  [edges(): return lax.ppermute(value, CONTEXT, pairs + [(b, a) for a, b in pairs])]
    pallas_call x5 -> x3, Pallas kernels: 10.2 us -> 8.91 us  [the_rest(): pl.pallas_call(kernel, grid=(count,), in_specs=whole(len(inputs)) + whole...]
  transfers between devices with their start and end apart: 20 -> 20, of which waited for: 7 -> 6; matrix products, arithmetic and copies ran while one was open for 0% -> 0% of each run, Pallas kernels for 39% -> 38%
where the time goes in v6:
time: 63.2 us; the launch traced here: 63 us
  starting transfers between devices  26.9 us (43%)
  Pallas kernels  25.8 us (41%)
  waiting for transfers between devices  9.42 us (15%)
  between operations  0.91 us (1%)
    ppermute x8, starting transfers between devices, edges(): return lax.ppermute(value, CONTEXT, pairs + [(b, a) for a, b in pairs])  16.2 us
    pallas_call x3, Pallas kernels, large(): pl.pallas_call(body, in_specs=whole(len(inputs)) + whole(len(behind), pl....  10.9 us
    ppermute x8, starting transfers between devices, across(): lax.ppermute(value, 'head', [(j, (j + subs) % size) for j in range(size)])  9.94 us
    pallas_call x3, Pallas kernels, the_rest(): pl.pallas_call(kernel, grid=(count,), in_specs=whole(len(inputs)) + whole...  8.91 us
    ppermute x8, waiting for transfers between devices, across(): lax.ppermute(value, 'head', [(j, (j + subs) % size) for j in range(size)])  5.69 us
    pallas_call x1, Pallas kernels, first_step(): pl.pallas_call(kernel, in_specs=whole(7, pl.ANY), out_specs=whole(4) + wh...  3.25 us
    ppermute x8, waiting for transfers between devices, edges(): return lax.ppermute(value, CONTEXT, pairs + [(b, a) for a, b in pairs])  2.76 us
  transfers between devices with their start and end apart: 20, of which 6 were waited for; matrix products, arithmetic and copies ran while one was open for 0% of the time, Pallas kernels for 38%

profile of v6, /device:TPU:0, one launch (start us, length us, event | category | flops | bytes accessed | tf_op | source)
XLA Modules:
  0.0 63.0 jit_solution(281475596854357380)
XLA Ops:
  0.6 0.9 %shard_map.101.refs_6_ = bf16[128,512]{1,0:T(8,128)(2,1)S(1)} custom-call(bf16[128,1024]{1,0:T(8,128)(2,1)} %refs_2_.1, bf16[128,1024]{1,0:T(8,128)(2,1)} %refs_3_.1), custom_call_target="tpu_custom_call" | custom-call | tf_op jit(solution)/shard_map/pallas_call | solution.py:391
  1.6 3.0 %collective-permute-start = (bf16[128,512]{1,0:T(8,128)(2,1)S(1)}, bf16[128,512]{1,0:T(8,128)(2,1)S(1)}, u32[]{:S(2)}, u32[]{:S(2)}) collective-permute-start(bf16[128,512]{1,0:T(8,128)(2,1)S(1)} %shard_map.101.refs_6_), channel_id=1, source_target_pairs={{0,16},{8,24},{16,0},{24,8},{1,17},{9,25},{17,1},{25,9},{2,18},{10... | collective-permute-start | bytes 393224 | tf_op jit(solution)/shard_map/ppermute | solution.py:369
  4.6 3.2 %shard_map.102 = (bf16[128,8192]{1,0:T(8,128)(2,1)S(1)}, bf16[128,8192]{1,0:T(8,128)(2,1)S(1)}, bf16[128,1024]{1,0:T(8,128)(2,1)S(1)}, bf16[128,1024]{1,0:T(8,12...) custom-call(bf16[128,8192]{1,0:T(8,128)(2,1)} %refs_0_.1, ...), custom_call_target="tpu_custom_call" | custom-call | flops 805306368 | bytes 1 | tf_op jit(solution)/shard_map/pallas_call | solution.py:279
  7.9 0.2 collective-permute-done.refs_3_
  8.1 1.8 %collective-permute-start.1 = (bf16[128,512]{1,0:T(8,128)(2,1)S(1)}, bf16[128,512]{1,0:T(8,128)(2,1)S(1)}, u32[]{:S(2)}, u32[]{:S(2)}) collective-permute-start(bf16[128,512]{1,0:T(8,128)(2,1)S(1)} %shard_map.103), channel_id=1, source_target_pairs={{0,16},{8,24},{16,0},{24,8},{1,17},{9,25},{17,1},{25,9},{2,18},{10... | collective-permute-start | bytes 393224 | tf_op jit(solution)/shard_map/ppermute | solution.py:369
  9.9 1.6 %collective-permute-start.4 = (bf16[128,512]{1,0:T(8,128)(2,1)S(1)}, bf16[128,512]{1,0:T(8,128)(2,1)S(1)}, u32[]{:S(2)}, u32[]{:S(2)}) collective-permute-start(bf16[128,512]{1,0:T(8,128)(2,1)S(1)} %shard_map.106), channel_id=1, source_target_pairs={{0,1},{2,3},{4,5},{6,7},{1,0},{3,2},{5,4},{7,6},{8,9},{10,11},{12,... | collective-permute-start | bytes 393224 | tf_op jit(solution)/shard_map/ppermute | solution.py:377
  11.5 0.7 %collective-permute-start.5 = (bf16[128,512]{1,0:T(8,128)(2,1)S(1)}, bf16[128,512]{1,0:T(8,128)(2,1)S(1)}, u32[]{:S(2)}, u32[]{:S(2)}) collective-permute-start(bf16[128,512]{1,0:T(8,128)(2,1)S(1)} %shard_map.107), channel_id=1, source_target_pairs={{1,2},{3,4},{5,6},{2,1},{4,3},{6,5},{9,10},{11,12},{13,14},{10,9},... | collective-permute-start | bytes 393224 | tf_op jit(solution)/shard_map/ppermute | solution.py:377
  12.2 1.0 %collective-permute-done.1.refs_3_ = bf16[128,512]{1,0:T(8,128)(2,1)S(1)} collective-permute-done((bf16[128,512]{1,0:T(8,128)(2,1)S(1)}, bf16[128,512]{1,0:T(8,128)(2,1)S(1)}, u32[]{:S(2)}, u32[]{:S(2)}) %collective-permute-start.1) | collective-permute-done | bytes 131104 | tf_op jit(solution)/shard_map/ppermute | solution.py:369
  13.2 3.4 %collective-permute-start.2 = (bf16[128,512]{1,0:T(8,128)(2,1)S(1)}, bf16[128,512]{1,0:T(8,128)(2,1)S(1)}, u32[]{:S(2)}, u32[]{:S(2)}) collective-permute-start(bf16[128,512]{1,0:T(8,128)(2,1)S(1)} %shard_map.104), channel_id=1, source_target_pairs={{0,1},{2,3},{4,5},{6,7},{1,0},{3,2},{5,4},{7,6},{8,9},{10,11},{12,... | collective-permute-start | bytes 393224 | tf_op jit(solution)/shard_map/ppermute | solution.py:377
  16.6 0.7 %collective-permute-start.3 = (bf16[128,512]{1,0:T(8,128)(2,1)S(1)}, bf16[128,512]{1,0:T(8,128)(2,1)S(1)}, u32[]{:S(2)}, u32[]{:S(2)}) collective-permute-start(bf16[128,512]{1,0:T(8,128)(2,1)S(1)} %shard_map.105), channel_id=1, source_target_pairs={{1,2},{3,4},{5,6},{2,1},{4,3},{6,5},{9,10},{11,12},{13,14},{10,9},... | collective-permute-start | bytes 393224 | tf_op jit(solution)/shard_map/ppermute | solution.py:377
  17.3 0.0 collective-permute-done.4.refs_4_
  17.3 0.1 shard_map.108
  17.4 0.6 collective-permute-start.7
  17.9 1.7 %shard_map.110.refs_6_ = f32[4,8,1024]{2,1,0:T(8,128)S(1)} custom-call(bf16[128,8192]{1,0:T(8,128)(2,1)S(1)} %get-tuple-element.66.refs_0_, bf16[128,8192]{1,0:T(8,128)(2,1)S(1)} %get-tuple-element.67.refs_1_, bf16[128,1024]{1,0:T(8,128)(2,1)S(1)} %get-tuple-element.70.refs_1_.refs_2_.refs_6_, ...), custom_call_target="tpu_custom_call" | custom-call | flops 536870912 | bytes 1 | tf_op jit(solution)/shard_map/pallas_call | solution.py:258
  19.7 2.7 %collective-permute-done.2.refs_4_ = bf16[128,512]{1,0:T(8,128)(2,1)S(1)} collective-permute-done((bf16[128,512]{1,0:T(8,128)(2,1)S(1)}, bf16[128,512]{1,0:T(8,128)(2,1)S(1)}, u32[]{:S(2)}, u32[]{:S(2)}) %collective-permute-start.2) | collective-permute-done | bytes 131104 | tf_op jit(solution)/shard_map/ppermute | solution.py:377
  22.4 0.0 collective-permute-done.3.refs_5_
  22.4 0.1 shard_map.109
  22.5 0.1 shard_map.111
  22.6 0.1 collective-permute-start.8
  22.7 0.6 collective-permute-start.6
  23.2 1.0 %collective-permute-done.8.refs_5_ = bf16[128,1024]{1,0:T(8,128)(2,1)S(1)} collective-permute-done((bf16[128,1024]{1,0:T(8,128)(2,1)S(1)}, bf16[128,1024]{1,0:T(8,128)(2,1)S(1)}, u32[]{:S(2)}, u32[]{:S(2)}) %collective-permute-start.8) | collective-permute-done | bytes 262176 | tf_op jit(solution)/shard_map/ppermute | solution.py:373
  24.2 4.5 %shard_map.112 = (f32[4,8,128]{2,1,0:T(8,128)S(1)}, f32[4,8,1024]{2,1,0:T(8,128)S(1)}, bf16[4,256,1024]{2,1,0:T(8,128)(2,1)S(1)}, bf16[4,256,1024]{2,1,0:T(8,128...) custom-call(bf16[128,8192]{1,0:T(8,128)(2,1)S(1)} %get-tuple-element, ...), custom_call_target="tpu_custom_call" | custom-call | flops 2147483648 | bytes 1 | tf_op jit(solution)/shard_map/pallas_call | solution.py:258
  28.7 0.2 collective-permute-start.10
  28.9 0.0 collective-permute-done.6.refs_4_
  29.0 0.4 collective-permute-start.9
  29.4 1.5 %shard_map.116 = (bf16[128,8192]{1,0:T(8,128)(2,1)}, bf16[128,8192]{1,0:T(8,128)(2,1)}, f32[128,128]{1,0:T(8,128)S(1)}, f32[128,128]{1,0:T(8,128)S(1)}) custom-call(bf16[128,8192]{1,0:T(8,128)(2,1)S(1)} %get-tuple-element.66.refs_0_, bf16[128,8192]{1,0:T(8,128)(2,1)S(1)} %get-tuple-element.67.refs_1_, f32[384,128]{1,0:T(8,128)S(1)} %get-tuple-element.68.refs_4_.refs_2_, ...), custom_call_target="tpu_custom_call" | custom-call | flops 671088640 | bytes 1 | tf_op jit(solution)/shard_map/pallas_call | solution.py:335
  30.9 0.0 collective-permute-done.10.refs_3_
  31.0 0.1 shard_map.115
  31.1 0.6 %collective-permute-start.11 = (bf16[128,512]{1,0:T(8,128)(2,1)S(1)}, bf16[128,512]{1,0:T(8,128)(2,1)S(1)}, u32[]{:S(2)}, u32[]{:S(2)}) collective-permute-start(bf16[128,512]{1,0:T(8,128)(2,1)S(1)} %get-tuple-element.88.refs_7_), channel_id=1, source_target_pairs={{0,16},{8,24},{16,0},{24,8},{1,17},{9,25},{17,1},{25,9},{2,18},{10... | collective-permute-start | bytes 393224 | tf_op jit(solution)/shard_map/ppermute | solution.py:369
  31.7 0.0 collective-permute-done.9.refs_5_
  31.7 4.6 %shard_map.117 = (f32[4,8,128]{2,1,0:T(8,128)S(1)}, f32[4,8,1024]{2,1,0:T(8,128)S(1)}, bf16[4,256,1024]{2,1,0:T(8,128)(2,1)S(1)}, bf16[4,256,1024]{2,1,0:T(8,128...) custom-call(bf16[128,8192]{1,0:T(8,128)(2,1)S(1)} %get-tuple-element, ...), custom_call_target="tpu_custom_call" | custom-call | flops 2147483648 | bytes 1 | tf_op jit(solution)/shard_map/pallas_call | solution.py:258
  36.3 0.4 collective-permute-done.11.refs_2_
  36.7 0.1 collective-permute-start.13
  36.8 4.2 %collective-permute-start.12 = (bf16[128,512]{1,0:T(8,128)(2,1)S(1)}, bf16[128,512]{1,0:T(8,128)(2,1)S(1)}, u32[]{:S(2)}, u32[]{:S(2)}) collective-permute-start(bf16[128,512]{1,0:T(8,128)(2,1)S(1)} %shard_map.118.refs_5_), channel_id=1, source_target_pairs={{0,1},{2,3},{4,5},{6,7},{1,0},{3,2},{5,4},{7,6},{8,9},{10,11},{12,... | collective-permute-start | bytes 393224 | tf_op jit(solution)/shard_map/ppermute | solution.py:377
  41.0 0.1 shard_map.120
  41.2 1.2 %collective-permute-start.15 = (bf16[144,512]{1,0:T(8,128)(2,1)S(1)}, bf16[144,512]{1,0:T(8,128)(2,1)S(1)}, u32[]{:S(2)}, u32[]{:S(2)}) collective-permute-start(bf16[144,512]{1,0:T(8,128)(2,1)S(1)} %get-tuple-element.104.refs_3_), channel_id=1, source_target_pairs={{0,16},{8,24},{16,0},{24,8},{1,17},{9,25},{17,1},{25,9},{2,18},{10... | collective-permute-start | bytes 442376 | tf_op jit(solution)/shard_map/ppermute | solution.py:369
  42.4 0.7 %collective-permute-start.14 = (bf16[128,512]{1,0:T(8,128)(2,1)S(1)}, bf16[128,512]{1,0:T(8,128)(2,1)S(1)}, u32[]{:S(2)}, u32[]{:S(2)}) collective-permute-start(bf16[128,512]{1,0:T(8,128)(2,1)S(1)} %shard_map.121), channel_id=1, source_target_pairs={{1,2},{3,4},{5,6},{2,1},{4,3},{6,5},{9,10},{11,12},{13,14},{10,9},... | collective-permute-start | bytes 393224 | tf_op jit(solution)/shard_map/ppermute | solution.py:377
  43.1 4.1 %collective-permute-done.15.refs_2_.refs_1_ = bf16[144,512]{1,0:T(8,128)(2,1)S(1)} collective-permute-done((bf16[144,512]{1,0:T(8,128)(2,1)S(1)}, bf16[144,512]{1,0:T(8,128)(2,1)S(1)}, u32[]{:S(2)}, u32[]{:S(2)}) %collective-permute-start.15) | collective-permute-done | bytes 147488 | tf_op jit(solution)/shard_map/ppermute | solution.py:369
  47.2 0.7 %collective-permute-start.17 = (bf16[128,512]{1,0:T(8,128)(2,1)S(1)}, bf16[128,512]{1,0:T(8,128)(2,1)S(1)}, u32[]{:S(2)}, u32[]{:S(2)}) collective-permute-start(bf16[128,512]{1,0:T(8,128)(2,1)S(1)} %shard_map.127), channel_id=1, source_target_pairs={{1,2},{3,4},{5,6},{2,1},{4,3},{6,5},{9,10},{11,12},{13,14},{10,9},... | collective-permute-start | bytes 393224 | tf_op jit(solution)/shard_map/ppermute | solution.py:377
  47.9 4.3 %collective-permute-start.16 = (bf16[128,512]{1,0:T(8,128)(2,1)S(1)}, bf16[128,512]{1,0:T(8,128)(2,1)S(1)}, u32[]{:S(2)}, u32[]{:S(2)}) collective-permute-start(bf16[128,512]{1,0:T(8,128)(2,1)S(1)} %shard_map.122.refs_5_), channel_id=1, source_target_pairs={{0,1},{2,3},{4,5},{6,7},{1,0},{3,2},{5,4},{7,6},{8,9},{10,11},{12,... | collective-permute-start | bytes 393224 | tf_op jit(solution)/shard_map/ppermute | solution.py:377
  52.2 0.0 collective-permute-done.12.refs_3_
  52.2 0.0 collective-permute-done.14.refs_4_
  52.3 1.2 %collective-permute-start.18 = (bf16[128,512]{1,0:T(8,128)(2,1)S(1)}, bf16[128,512]{1,0:T(8,128)(2,1)S(1)}, u32[]{:S(2)}, u32[]{:S(2)}) collective-permute-start(bf16[128,512]{1,0:T(8,128)(2,1)S(1)} %get-tuple-element.106.refs_13_), channel_id=1, source_target_pairs={{0,16},{8,24},{16,0},{24,8},{1,17},{9,25},{17,1},{25,9},{2,18},{10... | collective-permute-start | bytes 393224 | tf_op jit(solution)/shard_map/ppermute | solution.py:369
  53.5 3.3 %shard_map.124 = (bf16[128,8192]{1,0:T(8,128)(2,1)}, bf16[128,8192]{1,0:T(8,128)(2,1)}, f32[128,384]{1,0:T(8,128)S(1)}, f32[128,384]{1,0:T(8,128)S(1)}) custom-call(bf16[128,8192]{1,0:T(8,128)(2,1)S(1)} %get-tuple-element.66.refs_0_, bf16[128,8192]{1,0:T(8,128)(2,1)S(1)} %get-tuple-element.67.refs_1_, ...), custom_call_target="tpu_custom_call", output_to_operand_aliasing={{0}: (11, {}), {1}: (12, {})} | custom-call | flops 2013265920 | bytes 1 | tf_op jit(solution)/shard_map/pallas_call | solution.py:335
  56.8 0.1 shard_map.128
  56.9 1.0 %collective-permute-start.19 = (bf16[128,512]{1,0:T(8,128)(2,1)S(1)}, bf16[128,512]{1,0:T(8,128)(2,1)S(1)}, u32[]{:S(2)}, u32[]{:S(2)}) collective-permute-start(bf16[128,512]{1,0:T(8,128)(2,1)S(1)} %get-tuple-element.110.refs_13_), channel_id=1, source_target_pairs={{0,16},{8,24},{16,0},{24,8},{1,17},{9,25},{17,1},{25,9},{2,18},{10... | collective-permute-start | bytes 393224 | tf_op jit(solution)/shard_map/ppermute | solution.py:369
  57.8 4.1 %shard_map.129 = (bf16[128,8192]{1,0:T(8,128)(2,1)}, bf16[128,8192]{1,0:T(8,128)(2,1)}, f32[128,512]{1,0:T(8,128)S(1)}, f32[128,512]{1,0:T(8,128)S(1)}) custom-call(bf16[128,8192]{1,0:T(8,128)(2,1)S(1)} %get-tuple-element.66.refs_0_, bf16[128,8192]{1,0:T(8,128)(2,1)S(1)} %get-tuple-element.67.refs_1_, ...), custom_call_target="tpu_custom_call", output_to_operand_aliasing={{0}: (11, {}), {1}: (12, {})} | custom-call | flops 2684354560 | bytes 1 | tf_op jit(solution)/shard_map/pallas_call | solution.py:335
  62.0 1.1 %shard_map.130 = (bf16[128,1024]{1,0:T(8,128)(2,1)}, bf16[128,1024]{1,0:T(8,128)(2,1)}, f32[16,512]{1,0:T(8,128)}) custom-call(s32[6]{0:T(128)S(4)} %get-tuple-element.69.refs_0_.flag, f32[2,16,128]{2,1,0:T(8,128)S(1)} %get-tuple-element.112.refs_0_, bf16[144,512]{1,0:T(8,128)(2,1)S(1)} %collective-permute-done.15.refs_2_.refs_1_, ...), custom_call_target="tpu_custom_call" | custom-call | tf_op jit(solution)/shard_map/pallas_call | solution.py:587
  (22 shorter events, 0.3 us)
Async XLA Ops:
  1.6 6.5 %collective-permute-start = (bf16[128,512]{1,0:T(8,128)(2,1)S(1)}, bf16[128,512]{1,0:T(8,128)(2,1)S(1)}, u32[]{:S(2)}, u32[]{:S(2)}) collective-permute-start(bf16[128,512]{1,0:T(8,128)(2,1)S(1)} %shard_map.101.refs_6_), channel_id=1, source_target_pairs={{0,16},{8,24},{16,0},{24,8},{1,17},{9,25},{17,1},{25,9},{2,18},{10... | collective-permute-start | bytes 393224 | tf_op jit(solution)/shard_map/ppermute | solution.py:369
  8.1 5.0 %collective-permute-start.1 = (bf16[128,512]{1,0:T(8,128)(2,1)S(1)}, bf16[128,512]{1,0:T(8,128)(2,1)S(1)}, u32[]{:S(2)}, u32[]{:S(2)}) collective-permute-start(bf16[128,512]{1,0:T(8,128)(2,1)S(1)} %shard_map.103), channel_id=1, source_target_pairs={{0,16},{8,24},{16,0},{24,8},{1,17},{9,25},{17,1},{25,9},{2,18},{10... | collective-permute-start | bytes 393224 | tf_op jit(solution)/shard_map/ppermute | solution.py:369
  9.9 7.3 %collective-permute-start.4 = (bf16[128,512]{1,0:T(8,128)(2,1)S(1)}, bf16[128,512]{1,0:T(8,128)(2,1)S(1)}, u32[]{:S(2)}, u32[]{:S(2)}) collective-permute-start(bf16[128,512]{1,0:T(8,128)(2,1)S(1)} %shard_map.106), channel_id=1, source_target_pairs={{0,1},{2,3},{4,5},{6,7},{1,0},{3,2},{5,4},{7,6},{8,9},{10,11},{12,... | collective-permute-start | bytes 393224 | tf_op jit(solution)/shard_map/ppermute | solution.py:377
  11.5 5.8 %collective-permute-start.5 = (bf16[128,512]{1,0:T(8,128)(2,1)S(1)}, bf16[128,512]{1,0:T(8,128)(2,1)S(1)}, u32[]{:S(2)}, u32[]{:S(2)}) collective-permute-start(bf16[128,512]{1,0:T(8,128)(2,1)S(1)} %shard_map.107), channel_id=1, source_target_pairs={{1,2},{3,4},{5,6},{2,1},{4,3},{6,5},{9,10},{11,12},{13,14},{10,9},... | collective-permute-start | bytes 393224 | tf_op jit(solution)/shard_map/ppermute | solution.py:377
  13.2 9.3 %collective-permute-start.2 = (bf16[128,512]{1,0:T(8,128)(2,1)S(1)}, bf16[128,512]{1,0:T(8,128)(2,1)S(1)}, u32[]{:S(2)}, u32[]{:S(2)}) collective-permute-start(bf16[128,512]{1,0:T(8,128)(2,1)S(1)} %shard_map.104), channel_id=1, source_target_pairs={{0,1},{2,3},{4,5},{6,7},{1,0},{3,2},{5,4},{7,6},{8,9},{10,11},{12,... | collective-permute-start | bytes 393224 | tf_op jit(solution)/shard_map/ppermute | solution.py:377
  16.6 5.8 %collective-permute-start.3 = (bf16[128,512]{1,0:T(8,128)(2,1)S(1)}, bf16[128,512]{1,0:T(8,128)(2,1)S(1)}, u32[]{:S(2)}, u32[]{:S(2)}) collective-permute-start(bf16[128,512]{1,0:T(8,128)(2,1)S(1)} %shard_map.105), channel_id=1, source_target_pairs={{1,2},{3,4},{5,6},{2,1},{4,3},{6,5},{9,10},{11,12},{13,14},{10,9},... | collective-permute-start | bytes 393224 | tf_op jit(solution)/shard_map/ppermute | solution.py:377
  17.4 5.1 %collective-permute-start.7 = (bf16[128,512]{1,0:T(8,128)(2,1)S(1)}, bf16[128,512]{1,0:T(8,128)(2,1)S(1)}, u32[]{:S(2)}, u32[]{:S(2)}) collective-permute-start(bf16[128,512]{1,0:T(8,128)(2,1)S(1)} %get-tuple-element.73.refs_6_.refs_5_), channel_id=1, source_target_pairs={{0,16},{8,24},{16,0},{24,8},{1,17},{9,25},{17,1},{25,9},{2,18},{10... | collective-permute-start | bytes 393224 | tf_op jit(solution)/shard_map/ppermute | solution.py:369
  22.6 1.6 %collective-permute-start.8 = (bf16[128,1024]{1,0:T(8,128)(2,1)S(1)}, bf16[128,1024]{1,0:T(8,128)(2,1)S(1)}, u32[]{:S(2)}, u32[]{:S(2)}) collective-permute-start(bf16[128,1024]{1,0:T(8,128)(2,1)S(1)} %get-tuple-element.79), channel_id=1, source_target_pairs={{0,8},{8,0},{16,24},{24,16},{1,9},{9,1},{17,25},{25,17},{2,10},{10... | collective-permute-start | bytes 786440 | tf_op jit(solution)/shard_map/ppermute | solution.py:373
  22.7 6.3 %collective-permute-start.6 = (bf16[128,512]{1,0:T(8,128)(2,1)S(1)}, bf16[128,512]{1,0:T(8,128)(2,1)S(1)}, u32[]{:S(2)}, u32[]{:S(2)}) collective-permute-start(bf16[128,512]{1,0:T(8,128)(2,1)S(1)} %get-tuple-element.75.refs_5_), channel_id=1, source_target_pairs={{0,16},{8,24},{16,0},{24,8},{1,17},{9,25},{17,1},{25,9},{2,18},{10... | collective-permute-start | bytes 393224 | tf_op jit(solution)/shard_map/ppermute | solution.py:369
  28.7 2.2 %collective-permute-start.10 = (bf16[128,1024]{1,0:T(8,128)(2,1)S(1)}, bf16[128,1024]{1,0:T(8,128)(2,1)S(1)}, u32[]{:S(2)}, u32[]{:S(2)}) collective-permute-start(bf16[128,1024]{1,0:T(8,128)(2,1)S(1)} %shard_map.114.refs_11_), channel_id=1, source_target_pairs={{0,8},{8,0},{16,24},{24,16},{1,9},{9,1},{17,25},{25,17},{2,10},{10... | collective-permute-start | bytes 786440 | tf_op jit(solution)/shard_map/ppermute | solution.py:373
  29.0 2.7 %collective-permute-start.9 = (bf16[128,1024]{1,0:T(8,128)(2,1)S(1)}, bf16[128,1024]{1,0:T(8,128)(2,1)S(1)}, u32[]{:S(2)}, u32[]{:S(2)}) collective-permute-start(bf16[128,1024]{1,0:T(8,128)(2,1)S(1)} %get-tuple-element.83), channel_id=1, source_target_pairs={{0,8},{8,0},{16,24},{24,16},{1,9},{9,1},{17,25},{25,17},{2,10},{10... | collective-permute-start | bytes 786440 | tf_op jit(solution)/shard_map/ppermute | solution.py:373
  31.1 5.6 %collective-permute-start.11 = (bf16[128,512]{1,0:T(8,128)(2,1)S(1)}, bf16[128,512]{1,0:T(8,128)(2,1)S(1)}, u32[]{:S(2)}, u32[]{:S(2)}) collective-permute-start(bf16[128,512]{1,0:T(8,128)(2,1)S(1)} %get-tuple-element.88.refs_7_), channel_id=1, source_target_pairs={{0,16},{8,24},{16,0},{24,8},{1,17},{9,25},{17,1},{25,9},{2,18},{10... | collective-permute-start | bytes 393224 | tf_op jit(solution)/shard_map/ppermute | solution.py:369
  36.7 4.3 %collective-permute-start.13 = (bf16[144,1024]{1,0:T(8,128)(2,1)S(1)}, bf16[144,1024]{1,0:T(8,128)(2,1)S(1)}, u32[]{:S(2)}, u32[]{:S(2)}) collective-permute-start(bf16[144,1024]{1,0:T(8,128)(2,1)S(1)} %shard_map.119), channel_id=1, source_target_pairs={{0,8},{8,0},{16,24},{24,16},{1,9},{9,1},{17,25},{25,17},{2,10},{10... | collective-permute-start | bytes 884744 | tf_op jit(solution)/shard_map/ppermute | solution.py:373
  36.8 15.4 %collective-permute-start.12 = (bf16[128,512]{1,0:T(8,128)(2,1)S(1)}, bf16[128,512]{1,0:T(8,128)(2,1)S(1)}, u32[]{:S(2)}, u32[]{:S(2)}) collective-permute-start(bf16[128,512]{1,0:T(8,128)(2,1)S(1)} %shard_map.118.refs_5_), channel_id=1, source_target_pairs={{0,1},{2,3},{4,5},{6,7},{1,0},{3,2},{5,4},{7,6},{8,9},{10,11},{12,... | collective-permute-start | bytes 393224 | tf_op jit(solution)/shard_map/ppermute | solution.py:377
  41.2 6.0 %collective-permute-start.15 = (bf16[144,512]{1,0:T(8,128)(2,1)S(1)}, bf16[144,512]{1,0:T(8,128)(2,1)S(1)}, u32[]{:S(2)}, u32[]{:S(2)}) collective-permute-start(bf16[144,512]{1,0:T(8,128)(2,1)S(1)} %get-tuple-element.104.refs_3_), channel_id=1, source_target_pairs={{0,16},{8,24},{16,0},{24,8},{1,17},{9,25},{17,1},{25,9},{2,18},{10... | collective-permute-start | bytes 442376 | tf_op jit(solution)/shard_map/ppermute | solution.py:369
  42.4 9.8 %collective-permute-start.14 = (bf16[128,512]{1,0:T(8,128)(2,1)S(1)}, bf16[128,512]{1,0:T(8,128)(2,1)S(1)}, u32[]{:S(2)}, u32[]{:S(2)}) collective-permute-start(bf16[128,512]{1,0:T(8,128)(2,1)S(1)} %shard_map.121), channel_id=1, source_target_pairs={{1,2},{3,4},{5,6},{2,1},{4,3},{6,5},{9,10},{11,12},{13,14},{10,9},... | collective-permute-start | bytes 393224 | tf_op jit(solution)/shard_map/ppermute | solution.py:377
  47.2 9.6 %collective-permute-start.17 = (bf16[128,512]{1,0:T(8,128)(2,1)S(1)}, bf16[128,512]{1,0:T(8,128)(2,1)S(1)}, u32[]{:S(2)}, u32[]{:S(2)}) collective-permute-start(bf16[128,512]{1,0:T(8,128)(2,1)S(1)} %shard_map.127), channel_id=1, source_target_pairs={{1,2},{3,4},{5,6},{2,1},{4,3},{6,5},{9,10},{11,12},{13,14},{10,9},... | collective-permute-start | bytes 393224 | tf_op jit(solution)/shard_map/ppermute | solution.py:377
  47.9 8.8 %collective-permute-start.16 = (bf16[128,512]{1,0:T(8,128)(2,1)S(1)}, bf16[128,512]{1,0:T(8,128)(2,1)S(1)}, u32[]{:S(2)}, u32[]{:S(2)}) collective-permute-start(bf16[128,512]{1,0:T(8,128)(2,1)S(1)} %shard_map.122.refs_5_), channel_id=1, source_target_pairs={{0,1},{2,3},{4,5},{6,7},{1,0},{3,2},{5,4},{7,6},{8,9},{10,11},{12,... | collective-permute-start | bytes 393224 | tf_op jit(solution)/shard_map/ppermute | solution.py:377
  52.3 9.7 %collective-permute-start.18 = (bf16[128,512]{1,0:T(8,128)(2,1)S(1)}, bf16[128,512]{1,0:T(8,128)(2,1)S(1)}, u32[]{:S(2)}, u32[]{:S(2)}) collective-permute-start(bf16[128,512]{1,0:T(8,128)(2,1)S(1)} %get-tuple-element.106.refs_13_), channel_id=1, source_target_pairs={{0,16},{8,24},{16,0},{24,8},{1,17},{9,25},{17,1},{25,9},{2,18},{10... | collective-permute-start | bytes 393224 | tf_op jit(solution)/shard_map/ppermute | solution.py:369
  56.9 5.1 %collective-permute-start.19 = (bf16[128,512]{1,0:T(8,128)(2,1)S(1)}, bf16[128,512]{1,0:T(8,128)(2,1)S(1)}, u32[]{:S(2)}, u32[]{:S(2)}) collective-permute-start(bf16[128,512]{1,0:T(8,128)(2,1)S(1)} %get-tuple-element.110.refs_13_), channel_id=1, source_target_pairs={{0,16},{8,24},{16,0},{24,8},{1,17},{9,25},{17,1},{25,9},{2,18},{10... | collective-permute-start | bytes 393224 | tf_op jit(solution)/shard_map/ppermute | solution.py:369

commit v7 on v6

--- a/solution.py
+++ b/solution.py
@@ -340,7 +340,7 @@
         out_shape=[wide, wide] + [pltpu.VMEM((rows, count * WIDTH), jnp.float32)] * 2,
         input_output_aliases={len(inputs): 0, len(inputs) + 1: 1} if earlier else {},
         compiler_params=pltpu.CompilerParams(vmem_limit_bytes=VMEM_LARGE),
-        cost_estimate=cost(count, rows, 10),
+        cost_estimate=cost(count, rows, 5),
     )(*inputs, *extra)
     return results[:2], results[2:]
 

time: 63.2 us -> 61.8 us (0.978)
  starting transfers between devices: 26.9 us -> 24.1 us
  waiting for transfers between devices: 9.42 us -> 10.6 us
    ppermute x8, starting transfers between devices: 16.2 us -> 13.4 us  [edges(): return lax.ppermute(value, CONTEXT, pairs + [(b, a) for a, b in pairs])]
    ppermute x8, waiting for transfers between devices: 2.76 us -> 3.9 us  [edges(): return lax.ppermute(value, CONTEXT, pairs + [(b, a) for a, b in pairs])]
  transfers between devices with their start and end apart: 20 -> 20, of which waited for: 6 -> 7; matrix products, arithmetic and copies ran while one was open for 0% -> 0% of each run, Pallas kernels for 38% -> 39%
where the time goes in v7:
time: 61.8 us; the launch traced here: 61.4 us
  Pallas kernels  25.8 us (42%)
  starting transfers between devices  24.1 us (39%)
  waiting for transfers between devices  10.6 us (17%)
  between operations  0.92 us (1%)
    ppermute x8, starting transfers between devices, edges(): return lax.ppermute(value, CONTEXT, pairs + [(b, a) for a, b in pairs])  13.4 us
    pallas_call x3, Pallas kernels, large(): pl.pallas_call(body, in_specs=whole(len(inputs)) + whole(len(behind), pl....  10.9 us
    ppermute x8, starting transfers between devices, across(): lax.ppermute(value, 'head', [(j, (j + subs) % size) for j in range(size)])  9.95 us
    pallas_call x3, Pallas kernels, the_rest(): pl.pallas_call(kernel, grid=(count,), in_specs=whole(len(inputs)) + whole...  8.9 us
    ppermute x8, waiting for transfers between devices, across(): lax.ppermute(value, 'head', [(j, (j + subs) % size) for j in range(size)])  5.7 us
    ppermute x8, waiting for transfers between devices, edges(): return lax.ppermute(value, CONTEXT, pairs + [(b, a) for a, b in pairs])  3.9 us
    pallas_call x1, Pallas kernels, first_step(): pl.pallas_call(kernel, in_specs=whole(7, pl.ANY), out_specs=whole(4) + wh...  3.25 us
  transfers between devices with their start and end apart: 20, of which 7 were waited for; matrix products, arithmetic and copies ran while one was open for 0% of the time, Pallas kernels for 39%

profile of v7, /device:TPU:0, one launch (start us, length us, event | category | flops | bytes accessed | tf_op | source)
XLA Modules:
  0.0 61.4 jit_solution(538607149333528059)
XLA Ops:
  0.6 0.9 %shard_map.101.refs_6_ = bf16[128,512]{1,0:T(8,128)(2,1)S(1)} custom-call(bf16[128,1024]{1,0:T(8,128)(2,1)} %refs_2_.1, bf16[128,1024]{1,0:T(8,128)(2,1)} %refs_3_.1), custom_call_target="tpu_custom_call" | custom-call | tf_op jit(solution)/shard_map/pallas_call | solution.py:391
  1.6 3.0 %collective-permute-start = (bf16[128,512]{1,0:T(8,128)(2,1)S(1)}, bf16[128,512]{1,0:T(8,128)(2,1)S(1)}, u32[]{:S(2)}, u32[]{:S(2)}) collective-permute-start(bf16[128,512]{1,0:T(8,128)(2,1)S(1)} %shard_map.101.refs_6_), channel_id=1, source_target_pairs={{0,16},{8,24},{16,0},{24,8},{1,17},{9,25},{17,1},{25,9},{2,18},{10... | collective-permute-start | bytes 393224 | tf_op jit(solution)/shard_map/ppermute | solution.py:369
  4.6 3.2 %shard_map.102 = (bf16[128,8192]{1,0:T(8,128)(2,1)S(1)}, bf16[128,8192]{1,0:T(8,128)(2,1)S(1)}, bf16[128,1024]{1,0:T(8,128)(2,1)S(1)}, bf16[128,1024]{1,0:T(8,12...) custom-call(bf16[128,8192]{1,0:T(8,128)(2,1)} %refs_0_.1, ...), custom_call_target="tpu_custom_call" | custom-call | flops 805306368 | bytes 1 | tf_op jit(solution)/shard_map/pallas_call | solution.py:279
  7.9 0.2 collective-permute-done.refs_3_
  8.1 1.8 %collective-permute-start.1 = (bf16[128,512]{1,0:T(8,128)(2,1)S(1)}, bf16[128,512]{1,0:T(8,128)(2,1)S(1)}, u32[]{:S(2)}, u32[]{:S(2)}) collective-permute-start(bf16[128,512]{1,0:T(8,128)(2,1)S(1)} %shard_map.103), channel_id=1, source_target_pairs={{0,16},{8,24},{16,0},{24,8},{1,17},{9,25},{17,1},{25,9},{2,18},{10... | collective-permute-start | bytes 393224 | tf_op jit(solution)/shard_map/ppermute | solution.py:369
  9.9 1.5 %collective-permute-start.4 = (bf16[128,512]{1,0:T(8,128)(2,1)S(1)}, bf16[128,512]{1,0:T(8,128)(2,1)S(1)}, u32[]{:S(2)}, u32[]{:S(2)}) collective-permute-start(bf16[128,512]{1,0:T(8,128)(2,1)S(1)} %shard_map.106), channel_id=1, source_target_pairs={{0,1},{2,3},{4,5},{6,7},{1,0},{3,2},{5,4},{7,6},{8,9},{10,11},{12,... | collective-permute-start | bytes 393224 | tf_op jit(solution)/shard_map/ppermute | solution.py:377
  11.5 0.7 %collective-permute-start.5 = (bf16[128,512]{1,0:T(8,128)(2,1)S(1)}, bf16[128,512]{1,0:T(8,128)(2,1)S(1)}, u32[]{:S(2)}, u32[]{:S(2)}) collective-permute-start(bf16[128,512]{1,0:T(8,128)(2,1)S(1)} %shard_map.107), channel_id=1, source_target_pairs={{1,2},{3,4},{5,6},{2,1},{4,3},{6,5},{9,10},{11,12},{13,14},{10,9},... | collective-permute-start | bytes 393224 | tf_op jit(solution)/shard_map/ppermute | solution.py:377
  12.2 1.0 %collective-permute-done.1.refs_3_ = bf16[128,512]{1,0:T(8,128)(2,1)S(1)} collective-permute-done((bf16[128,512]{1,0:T(8,128)(2,1)S(1)}, bf16[128,512]{1,0:T(8,128)(2,1)S(1)}, u32[]{:S(2)}, u32[]{:S(2)}) %collective-permute-start.1) | collective-permute-done | bytes 131104 | tf_op jit(solution)/shard_map/ppermute | solution.py:369
  13.2 3.4 %collective-permute-start.2 = (bf16[128,512]{1,0:T(8,128)(2,1)S(1)}, bf16[128,512]{1,0:T(8,128)(2,1)S(1)}, u32[]{:S(2)}, u32[]{:S(2)}) collective-permute-start(bf16[128,512]{1,0:T(8,128)(2,1)S(1)} %shard_map.104), channel_id=1, source_target_pairs={{0,1},{2,3},{4,5},{6,7},{1,0},{3,2},{5,4},{7,6},{8,9},{10,11},{12,... | collective-permute-start | bytes 393224 | tf_op jit(solution)/shard_map/ppermute | solution.py:377
  16.6 0.7 %collective-permute-start.3 = (bf16[128,512]{1,0:T(8,128)(2,1)S(1)}, bf16[128,512]{1,0:T(8,128)(2,1)S(1)}, u32[]{:S(2)}, u32[]{:S(2)}) collective-permute-start(bf16[128,512]{1,0:T(8,128)(2,1)S(1)} %shard_map.105), channel_id=1, source_target_pairs={{1,2},{3,4},{5,6},{2,1},{4,3},{6,5},{9,10},{11,12},{13,14},{10,9},... | collective-permute-start | bytes 393224 | tf_op jit(solution)/shard_map/ppermute | solution.py:377
  17.3 0.0 collective-permute-done.4.refs_4_
  17.3 0.1 shard_map.108
  17.4 0.6 collective-permute-start.7
  18.0 1.7 %shard_map.110.refs_6_ = f32[4,8,1024]{2,1,0:T(8,128)S(1)} custom-call(bf16[128,8192]{1,0:T(8,128)(2,1)S(1)} %get-tuple-element.66.refs_0_, bf16[128,8192]{1,0:T(8,128)(2,1)S(1)} %get-tuple-element.67.refs_1_, bf16[128,1024]{1,0:T(8,128)(2,1)S(1)} %get-tuple-element.70.refs_1_.refs_2_.refs_6_, ...), custom_call_target="tpu_custom_call" | custom-call | flops 536870912 | bytes 1 | tf_op jit(solution)/shard_map/pallas_call | solution.py:258
  19.7 2.7 %collective-permute-done.2.refs_4_ = bf16[128,512]{1,0:T(8,128)(2,1)S(1)} collective-permute-done((bf16[128,512]{1,0:T(8,128)(2,1)S(1)}, bf16[128,512]{1,0:T(8,128)(2,1)S(1)}, u32[]{:S(2)}, u32[]{:S(2)}) %collective-permute-start.2) | collective-permute-done | bytes 131104 | tf_op jit(solution)/shard_map/ppermute | solution.py:377
  22.4 0.0 collective-permute-done.3.refs_5_
  22.4 0.1 shard_map.109
  22.5 0.1 shard_map.111
  22.6 0.1 collective-permute-start.8
  22.7 0.6 collective-permute-start.6
  23.2 0.9 %collective-permute-done.8.refs_5_ = bf16[128,1024]{1,0:T(8,128)(2,1)S(1)} collective-permute-done((bf16[128,1024]{1,0:T(8,128)(2,1)S(1)}, bf16[128,1024]{1,0:T(8,128)(2,1)S(1)}, u32[]{:S(2)}, u32[]{:S(2)}) %collective-permute-start.8) | collective-permute-done | bytes 262176 | tf_op jit(solution)/shard_map/ppermute | solution.py:373
  24.2 4.5 %shard_map.112 = (f32[4,8,128]{2,1,0:T(8,128)S(1)}, f32[4,8,1024]{2,1,0:T(8,128)S(1)}, bf16[4,256,1024]{2,1,0:T(8,128)(2,1)S(1)}, bf16[4,256,1024]{2,1,0:T(8,128...) custom-call(bf16[128,8192]{1,0:T(8,128)(2,1)S(1)} %get-tuple-element, ...), custom_call_target="tpu_custom_call" | custom-call | flops 2147483648 | bytes 1 | tf_op jit(solution)/shard_map/pallas_call | solution.py:258
  28.7 0.2 collective-permute-start.10
  28.9 0.0 collective-permute-done.6.refs_4_
  29.0 0.4 collective-permute-start.9
  29.4 1.5 %shard_map.116 = (bf16[128,8192]{1,0:T(8,128)(2,1)}, bf16[128,8192]{1,0:T(8,128)(2,1)}, f32[128,128]{1,0:T(8,128)S(1)}, f32[128,128]{1,0:T(8,128)S(1)}) custom-call(bf16[128,8192]{1,0:T(8,128)(2,1)S(1)} %get-tuple-element.66.refs_0_, bf16[128,8192]{1,0:T(8,128)(2,1)S(1)} %get-tuple-element.67.refs_1_, f32[384,128]{1,0:T(8,128)S(1)} %get-tuple-element.68.refs_4_.refs_2_, ...), custom_call_target="tpu_custom_call" | custom-call | flops 335544320 | bytes 1 | tf_op jit(solution)/shard_map/pallas_call | solution.py:335
  30.9 0.0 collective-permute-done.10.refs_3_
  30.9 0.1 shard_map.115
  31.1 0.6 %collective-permute-start.11 = (bf16[128,512]{1,0:T(8,128)(2,1)S(1)}, bf16[128,512]{1,0:T(8,128)(2,1)S(1)}, u32[]{:S(2)}, u32[]{:S(2)}) collective-permute-start(bf16[128,512]{1,0:T(8,128)(2,1)S(1)} %get-tuple-element.88.refs_7_), channel_id=1, source_target_pairs={{0,16},{8,24},{16,0},{24,8},{1,17},{9,25},{17,1},{25,9},{2,18},{10... | collective-permute-start | bytes 393224 | tf_op jit(solution)/shard_map/ppermute | solution.py:369
  31.7 0.0 collective-permute-done.9.refs_5_
  31.7 4.6 %shard_map.117 = (f32[4,8,128]{2,1,0:T(8,128)S(1)}, f32[4,8,1024]{2,1,0:T(8,128)S(1)}, bf16[4,256,1024]{2,1,0:T(8,128)(2,1)S(1)}, bf16[4,256,1024]{2,1,0:T(8,128...) custom-call(bf16[128,8192]{1,0:T(8,128)(2,1)S(1)} %get-tuple-element, ...), custom_call_target="tpu_custom_call" | custom-call | flops 2147483648 | bytes 1 | tf_op jit(solution)/shard_map/pallas_call | solution.py:258
  36.3 0.4 collective-permute-done.11.refs_2_
  36.7 0.1 collective-permute-start.13
  36.8 4.2 %collective-permute-start.12 = (bf16[128,512]{1,0:T(8,128)(2,1)S(1)}, bf16[128,512]{1,0:T(8,128)(2,1)S(1)}, u32[]{:S(2)}, u32[]{:S(2)}) collective-permute-start(bf16[128,512]{1,0:T(8,128)(2,1)S(1)} %shard_map.118.refs_5_), channel_id=1, source_target_pairs={{0,1},{2,3},{4,5},{6,7},{1,0},{3,2},{5,4},{7,6},{8,9},{10,11},{12,... | collective-permute-start | bytes 393224 | tf_op jit(solution)/shard_map/ppermute | solution.py:377
  41.0 0.1 shard_map.120
  41.2 1.2 %collective-permute-start.15 = (bf16[144,512]{1,0:T(8,128)(2,1)S(1)}, bf16[144,512]{1,0:T(8,128)(2,1)S(1)}, u32[]{:S(2)}, u32[]{:S(2)}) collective-permute-start(bf16[144,512]{1,0:T(8,128)(2,1)S(1)} %get-tuple-element.104.refs_3_), channel_id=1, source_target_pairs={{0,16},{8,24},{16,0},{24,8},{1,17},{9,25},{17,1},{25,9},{2,18},{10... | collective-permute-start | bytes 442376 | tf_op jit(solution)/shard_map/ppermute | solution.py:369
  42.4 0.7 %collective-permute-start.14 = (bf16[128,512]{1,0:T(8,128)(2,1)S(1)}, bf16[128,512]{1,0:T(8,128)(2,1)S(1)}, u32[]{:S(2)}, u32[]{:S(2)}) collective-permute-start(bf16[128,512]{1,0:T(8,128)(2,1)S(1)} %shard_map.121), channel_id=1, source_target_pairs={{1,2},{3,4},{5,6},{2,1},{4,3},{6,5},{9,10},{11,12},{13,14},{10,9},... | collective-permute-start | bytes 393224 | tf_op jit(solution)/shard_map/ppermute | solution.py:377
  43.0 4.1 %collective-permute-done.15.refs_2_.refs_1_ = bf16[144,512]{1,0:T(8,128)(2,1)S(1)} collective-permute-done((bf16[144,512]{1,0:T(8,128)(2,1)S(1)}, bf16[144,512]{1,0:T(8,128)(2,1)S(1)}, u32[]{:S(2)}, u32[]{:S(2)}) %collective-permute-start.15) | collective-permute-done | bytes 147488 | tf_op jit(solution)/shard_map/ppermute | solution.py:369
  47.2 1.5 %collective-permute-start.16 = (bf16[128,512]{1,0:T(8,128)(2,1)S(1)}, bf16[128,512]{1,0:T(8,128)(2,1)S(1)}, u32[]{:S(2)}, u32[]{:S(2)}) collective-permute-start(bf16[128,512]{1,0:T(8,128)(2,1)S(1)} %shard_map.122.refs_5_), channel_id=1, source_target_pairs={{0,1},{2,3},{4,5},{6,7},{1,0},{3,2},{5,4},{7,6},{8,9},{10,11},{12,... | collective-permute-start | bytes 393224 | tf_op jit(solution)/shard_map/ppermute | solution.py:377
  48.7 0.7 %collective-permute-start.17 = (bf16[128,512]{1,0:T(8,128)(2,1)S(1)}, bf16[128,512]{1,0:T(8,128)(2,1)S(1)}, u32[]{:S(2)}, u32[]{:S(2)}) collective-permute-start(bf16[128,512]{1,0:T(8,128)(2,1)S(1)} %shard_map.127), channel_id=1, source_target_pairs={{1,2},{3,4},{5,6},{2,1},{4,3},{6,5},{9,10},{11,12},{13,14},{10,9},... | collective-permute-start | bytes 393224 | tf_op jit(solution)/shard_map/ppermute | solution.py:377
  49.4 0.1 shard_map.123
  49.5 1.2 %collective-permute-start.18 = (bf16[128,512]{1,0:T(8,128)(2,1)S(1)}, bf16[128,512]{1,0:T(8,128)(2,1)S(1)}, u32[]{:S(2)}, u32[]{:S(2)}) collective-permute-start(bf16[128,512]{1,0:T(8,128)(2,1)S(1)} %get-tuple-element.106.refs_13_), channel_id=1, source_target_pairs={{0,16},{8,24},{16,0},{24,8},{1,17},{9,25},{17,1},{25,9},{2,18},{10... | collective-permute-start | bytes 393224 | tf_op jit(solution)/shard_map/ppermute | solution.py:369
  50.7 3.3 %shard_map.124 = (bf16[128,8192]{1,0:T(8,128)(2,1)}, bf16[128,8192]{1,0:T(8,128)(2,1)}, f32[128,384]{1,0:T(8,128)S(1)}, f32[128,384]{1,0:T(8,128)S(1)}) custom-call(bf16[128,8192]{1,0:T(8,128)(2,1)S(1)} %get-tuple-element.66.refs_0_, bf16[128,8192]{1,0:T(8,128)(2,1)S(1)} %get-tuple-element.67.refs_1_, ...), custom_call_target="tpu_custom_call", output_to_operand_aliasing={{0}: (11, {}), {1}: (12, {})} | custom-call | flops 1006632960 | bytes 1 | tf_op jit(solution)/shard_map/pallas_call | solution.py:335
  53.9 1.2 %collective-permute-done.16.refs_1_ = bf16[128,512]{1,0:T(8,128)(2,1)S(1)} collective-permute-done((bf16[128,512]{1,0:T(8,128)(2,1)S(1)}, bf16[128,512]{1,0:T(8,128)(2,1)S(1)}, u32[]{:S(2)}, u32[]{:S(2)}) %collective-permute-start.16) | collective-permute-done | bytes 131104 | tf_op jit(solution)/shard_map/ppermute | solution.py:377
  55.1 0.1 shard_map.128
  55.2 1.0 %collective-permute-start.19 = (bf16[128,512]{1,0:T(8,128)(2,1)S(1)}, bf16[128,512]{1,0:T(8,128)(2,1)S(1)}, u32[]{:S(2)}, u32[]{:S(2)}) collective-permute-start(bf16[128,512]{1,0:T(8,128)(2,1)S(1)} %get-tuple-element.110.refs_13_), channel_id=1, source_target_pairs={{0,16},{8,24},{16,0},{24,8},{1,17},{9,25},{17,1},{25,9},{2,18},{10... | collective-permute-start | bytes 393224 | tf_op jit(solution)/shard_map/ppermute | solution.py:369
  56.2 4.1 %shard_map.129 = (bf16[128,8192]{1,0:T(8,128)(2,1)}, bf16[128,8192]{1,0:T(8,128)(2,1)}, f32[128,512]{1,0:T(8,128)S(1)}, f32[128,512]{1,0:T(8,128)S(1)}) custom-call(bf16[128,8192]{1,0:T(8,128)(2,1)S(1)} %get-tuple-element.66.refs_0_, bf16[128,8192]{1,0:T(8,128)(2,1)S(1)} %get-tuple-element.67.refs_1_, ...), custom_call_target="tpu_custom_call", output_to_operand_aliasing={{0}: (11, {}), {1}: (12, {})} | custom-call | flops 1342177280 | bytes 1 | tf_op jit(solution)/shard_map/pallas_call | solution.py:335
  60.3 1.1 %shard_map.130 = (bf16[128,1024]{1,0:T(8,128)(2,1)}, bf16[128,1024]{1,0:T(8,128)(2,1)}, f32[16,512]{1,0:T(8,128)}) custom-call(s32[6]{0:T(128)S(4)} %get-tuple-element.69.refs_0_.flag, f32[2,16,128]{2,1,0:T(8,128)S(1)} %get-tuple-element.112.refs_0_, bf16[144,512]{1,0:T(8,128)(2,1)S(1)} %collective-permute-done.15.refs_2_.refs_1_, ...), custom_call_target="tpu_custom_call" | custom-call | tf_op jit(solution)/shard_map/pallas_call | solution.py:587
  (22 shorter events, 0.2 us)
Async XLA Ops:
  1.6 6.5 %collective-permute-start = (bf16[128,512]{1,0:T(8,128)(2,1)S(1)}, bf16[128,512]{1,0:T(8,128)(2,1)S(1)}, u32[]{:S(2)}, u32[]{:S(2)}) collective-permute-start(bf16[128,512]{1,0:T(8,128)(2,1)S(1)} %shard_map.101.refs_6_), channel_id=1, source_target_pairs={{0,16},{8,24},{16,0},{24,8},{1,17},{9,25},{17,1},{25,9},{2,18},{10... | collective-permute-start | bytes 393224 | tf_op jit(solution)/shard_map/ppermute | solution.py:369
  8.1 5.0 %collective-permute-start.1 = (bf16[128,512]{1,0:T(8,128)(2,1)S(1)}, bf16[128,512]{1,0:T(8,128)(2,1)S(1)}, u32[]{:S(2)}, u32[]{:S(2)}) collective-permute-start(bf16[128,512]{1,0:T(8,128)(2,1)S(1)} %shard_map.103), channel_id=1, source_target_pairs={{0,16},{8,24},{16,0},{24,8},{1,17},{9,25},{17,1},{25,9},{2,18},{10... | collective-permute-start | bytes 393224 | tf_op jit(solution)/shard_map/ppermute | solution.py:369
  9.9 7.3 %collective-permute-start.4 = (bf16[128,512]{1,0:T(8,128)(2,1)S(1)}, bf16[128,512]{1,0:T(8,128)(2,1)S(1)}, u32[]{:S(2)}, u32[]{:S(2)}) collective-permute-start(bf16[128,512]{1,0:T(8,128)(2,1)S(1)} %shard_map.106), channel_id=1, source_target_pairs={{0,1},{2,3},{4,5},{6,7},{1,0},{3,2},{5,4},{7,6},{8,9},{10,11},{12,... | collective-permute-start | bytes 393224 | tf_op jit(solution)/shard_map/ppermute | solution.py:377
  11.5 5.8 %collective-permute-start.5 = (bf16[128,512]{1,0:T(8,128)(2,1)S(1)}, bf16[128,512]{1,0:T(8,128)(2,1)S(1)}, u32[]{:S(2)}, u32[]{:S(2)}) collective-permute-start(bf16[128,512]{1,0:T(8,128)(2,1)S(1)} %shard_map.107), channel_id=1, source_target_pairs={{1,2},{3,4},{5,6},{2,1},{4,3},{6,5},{9,10},{11,12},{13,14},{10,9},... | collective-permute-start | bytes 393224 | tf_op jit(solution)/shard_map/ppermute | solution.py:377
  13.2 9.3 %collective-permute-start.2 = (bf16[128,512]{1,0:T(8,128)(2,1)S(1)}, bf16[128,512]{1,0:T(8,128)(2,1)S(1)}, u32[]{:S(2)}, u32[]{:S(2)}) collective-permute-start(bf16[128,512]{1,0:T(8,128)(2,1)S(1)} %shard_map.104), channel_id=1, source_target_pairs={{0,1},{2,3},{4,5},{6,7},{1,0},{3,2},{5,4},{7,6},{8,9},{10,11},{12,... | collective-permute-start | bytes 393224 | tf_op jit(solution)/shard_map/ppermute | solution.py:377
  16.6 5.8 %collective-permute-start.3 = (bf16[128,512]{1,0:T(8,128)(2,1)S(1)}, bf16[128,512]{1,0:T(8,128)(2,1)S(1)}, u32[]{:S(2)}, u32[]{:S(2)}) collective-permute-start(bf16[128,512]{1,0:T(8,128)(2,1)S(1)} %shard_map.105), channel_id=1, source_target_pairs={{1,2},{3,4},{5,6},{2,1},{4,3},{6,5},{9,10},{11,12},{13,14},{10,9},... | collective-permute-start | bytes 393224 | tf_op jit(solution)/shard_map/ppermute | solution.py:377
  17.4 5.1 %collective-permute-start.7 = (bf16[128,512]{1,0:T(8,128)(2,1)S(1)}, bf16[128,512]{1,0:T(8,128)(2,1)S(1)}, u32[]{:S(2)}, u32[]{:S(2)}) collective-permute-start(bf16[128,512]{1,0:T(8,128)(2,1)S(1)} %get-tuple-element.73.refs_6_.refs_5_), channel_id=1, source_target_pairs={{0,16},{8,24},{16,0},{24,8},{1,17},{9,25},{17,1},{25,9},{2,18},{10... | collective-permute-start | bytes 393224 | tf_op jit(solution)/shard_map/ppermute | solution.py:369
  22.6 1.6 %collective-permute-start.8 = (bf16[128,1024]{1,0:T(8,128)(2,1)S(1)}, bf16[128,1024]{1,0:T(8,128)(2,1)S(1)}, u32[]{:S(2)}, u32[]{:S(2)}) collective-permute-start(bf16[128,1024]{1,0:T(8,128)(2,1)S(1)} %get-tuple-element.79), channel_id=1, source_target_pairs={{0,8},{8,0},{16,24},{24,16},{1,9},{9,1},{17,25},{25,17},{2,10},{10... | collective-permute-start | bytes 786440 | tf_op jit(solution)/shard_map/ppermute | solution.py:373
  22.7 6.3 %collective-permute-start.6 = (bf16[128,512]{1,0:T(8,128)(2,1)S(1)}, bf16[128,512]{1,0:T(8,128)(2,1)S(1)}, u32[]{:S(2)}, u32[]{:S(2)}) collective-permute-start(bf16[128,512]{1,0:T(8,128)(2,1)S(1)} %get-tuple-element.75.refs_5_), channel_id=1, source_target_pairs={{0,16},{8,24},{16,0},{24,8},{1,17},{9,25},{17,1},{25,9},{2,18},{10... | collective-permute-start | bytes 393224 | tf_op jit(solution)/shard_map/ppermute | solution.py:369
  28.7 2.2 %collective-permute-start.10 = (bf16[128,1024]{1,0:T(8,128)(2,1)S(1)}, bf16[128,1024]{1,0:T(8,128)(2,1)S(1)}, u32[]{:S(2)}, u32[]{:S(2)}) collective-permute-start(bf16[128,1024]{1,0:T(8,128)(2,1)S(1)} %shard_map.114.refs_11_), channel_id=1, source_target_pairs={{0,8},{8,0},{16,24},{24,16},{1,9},{9,1},{17,25},{25,17},{2,10},{10... | collective-permute-start | bytes 786440 | tf_op jit(solution)/shard_map/ppermute | solution.py:373
  29.0 2.7 %collective-permute-start.9 = (bf16[128,1024]{1,0:T(8,128)(2,1)S(1)}, bf16[128,1024]{1,0:T(8,128)(2,1)S(1)}, u32[]{:S(2)}, u32[]{:S(2)}) collective-permute-start(bf16[128,1024]{1,0:T(8,128)(2,1)S(1)} %get-tuple-element.83), channel_id=1, source_target_pairs={{0,8},{8,0},{16,24},{24,16},{1,9},{9,1},{17,25},{25,17},{2,10},{10... | collective-permute-start | bytes 786440 | tf_op jit(solution)/shard_map/ppermute | solution.py:373
  31.1 5.6 %collective-permute-start.11 = (bf16[128,512]{1,0:T(8,128)(2,1)S(1)}, bf16[128,512]{1,0:T(8,128)(2,1)S(1)}, u32[]{:S(2)}, u32[]{:S(2)}) collective-permute-start(bf16[128,512]{1,0:T(8,128)(2,1)S(1)} %get-tuple-element.88.refs_7_), channel_id=1, source_target_pairs={{0,16},{8,24},{16,0},{24,8},{1,17},{9,25},{17,1},{25,9},{2,18},{10... | collective-permute-start | bytes 393224 | tf_op jit(solution)/shard_map/ppermute | solution.py:369
  36.7 4.3 %collective-permute-start.13 = (bf16[144,1024]{1,0:T(8,128)(2,1)S(1)}, bf16[144,1024]{1,0:T(8,128)(2,1)S(1)}, u32[]{:S(2)}, u32[]{:S(2)}) collective-permute-start(bf16[144,1024]{1,0:T(8,128)(2,1)S(1)} %shard_map.119), channel_id=1, source_target_pairs={{0,8},{8,0},{16,24},{24,16},{1,9},{9,1},{17,25},{25,17},{2,10},{10... | collective-permute-start | bytes 884744 | tf_op jit(solution)/shard_map/ppermute | solution.py:373
  36.8 12.6 %collective-permute-start.12 = (bf16[128,512]{1,0:T(8,128)(2,1)S(1)}, bf16[128,512]{1,0:T(8,128)(2,1)S(1)}, u32[]{:S(2)}, u32[]{:S(2)}) collective-permute-start(bf16[128,512]{1,0:T(8,128)(2,1)S(1)} %shard_map.118.refs_5_), channel_id=1, source_target_pairs={{0,1},{2,3},{4,5},{6,7},{1,0},{3,2},{5,4},{7,6},{8,9},{10,11},{12,... | collective-permute-start | bytes 393224 | tf_op jit(solution)/shard_map/ppermute | solution.py:377
  41.2 6.0 %collective-permute-start.15 = (bf16[144,512]{1,0:T(8,128)(2,1)S(1)}, bf16[144,512]{1,0:T(8,128)(2,1)S(1)}, u32[]{:S(2)}, u32[]{:S(2)}) collective-permute-start(bf16[144,512]{1,0:T(8,128)(2,1)S(1)} %get-tuple-element.104.refs_3_), channel_id=1, source_target_pairs={{0,16},{8,24},{16,0},{24,8},{1,17},{9,25},{17,1},{25,9},{2,18},{10... | collective-permute-start | bytes 442376 | tf_op jit(solution)/shard_map/ppermute | solution.py:369
  42.4 7.1 %collective-permute-start.14 = (bf16[128,512]{1,0:T(8,128)(2,1)S(1)}, bf16[128,512]{1,0:T(8,128)(2,1)S(1)}, u32[]{:S(2)}, u32[]{:S(2)}) collective-permute-start(bf16[128,512]{1,0:T(8,128)(2,1)S(1)} %shard_map.121), channel_id=1, source_target_pairs={{1,2},{3,4},{5,6},{2,1},{4,3},{6,5},{9,10},{11,12},{13,14},{10,9},... | collective-permute-start | bytes 393224 | tf_op jit(solution)/shard_map/ppermute | solution.py:377
  47.2 7.9 %collective-permute-start.16 = (bf16[128,512]{1,0:T(8,128)(2,1)S(1)}, bf16[128,512]{1,0:T(8,128)(2,1)S(1)}, u32[]{:S(2)}, u32[]{:S(2)}) collective-permute-start(bf16[128,512]{1,0:T(8,128)(2,1)S(1)} %shard_map.122.refs_5_), channel_id=1, source_target_pairs={{0,1},{2,3},{4,5},{6,7},{1,0},{3,2},{5,4},{7,6},{8,9},{10,11},{12,... | collective-permute-start | bytes 393224 | tf_op jit(solution)/shard_map/ppermute | solution.py:377
  48.7 6.4 %collective-permute-start.17 = (bf16[128,512]{1,0:T(8,128)(2,1)S(1)}, bf16[128,512]{1,0:T(8,128)(2,1)S(1)}, u32[]{:S(2)}, u32[]{:S(2)}) collective-permute-start(bf16[128,512]{1,0:T(8,128)(2,1)S(1)} %shard_map.127), channel_id=1, source_target_pairs={{1,2},{3,4},{5,6},{2,1},{4,3},{6,5},{9,10},{11,12},{13,14},{10,9},... | collective-permute-start | bytes 393224 | tf_op jit(solution)/shard_map/ppermute | solution.py:377
  49.5 10.8 %collective-permute-start.18 = (bf16[128,512]{1,0:T(8,128)(2,1)S(1)}, bf16[128,512]{1,0:T(8,128)(2,1)S(1)}, u32[]{:S(2)}, u32[]{:S(2)}) collective-permute-start(bf16[128,512]{1,0:T(8,128)(2,1)S(1)} %get-tuple-element.106.refs_13_), channel_id=1, source_target_pairs={{0,16},{8,24},{16,0},{24,8},{1,17},{9,25},{17,1},{25,9},{2,18},{10... | collective-permute-start | bytes 393224 | tf_op jit(solution)/shard_map/ppermute | solution.py:369
  55.2 5.1 %collective-permute-start.19 = (bf16[128,512]{1,0:T(8,128)(2,1)S(1)}, bf16[128,512]{1,0:T(8,128)(2,1)S(1)}, u32[]{:S(2)}, u32[]{:S(2)}) collective-permute-start(bf16[128,512]{1,0:T(8,128)(2,1)S(1)} %get-tuple-element.110.refs_13_), channel_id=1, source_target_pairs={{0,16},{8,24},{16,0},{24,8},{1,17},{9,25},{17,1},{25,9},{2,18},{10... | collective-permute-start | bytes 393224 | tf_op jit(solution)/shard_map/ppermute | solution.py:369

commit v8 on v7

--- a/solution.py
+++ b/solution.py
@@ -18,7 +18,7 @@
 CHUNKS = 2
 UNROLL = 2
 EXTRA = 16
-BEHIND = ((1, 3), (4,))
+BEHIND = (((3, 1, 1), (0, 3, 1)), ((0, 4, 2),))
 LOG2E = math.log2(math.e)
 VMEM_SMALL = 8 * 2**20
 VMEM_LARGE = 16 * 2**20
@@ -183,38 +183,39 @@
     lax.fori_loop(0, count, head, 0, unroll=UNROLL)
 
 
-def rest_kernel(start, skip, near, q_ref, do_ref, bias_ref, first_k, first_v, *refs):
+def rest_kernel(start, skip, per, near, q_ref, do_ref, bias_ref, first_k, first_v, *refs):
     near_refs, (own_k, own_v), refs = refs[:near], refs[near : near + 2], refs[near + 2 :]
     row_ref, p_ref, ds_ref, att_ref, dq_ref, dk_ref, dv_ref = refs
     rows = q_ref.shape[0]
     width = first_k.shape[1] // WIDTH
     last = bias_ref.shape[0] - rows
-    index = pl.program_id(0)
-    at, g = skip + index, start + skip + index
-    own_keys, own_values = own_k[:, lanes(g)], own_v[:, lanes(g)]
-    k_rows = jnp.concatenate(
-        [first_k[:, lanes(at)], *[ref[:, lanes(at)] for ref in near_refs], own_keys], axis=0
-    )
-    v_rows = jnp.concatenate(
-        [first_v[:, lanes(at)], *[ref[:, lanes(at + width)] for ref in near_refs], own_values],
-        axis=0,
-    )
-    q_all, do_all = group_rows(q_ref, g), group_rows(do_ref, g)
-    s = dot(own_keys, q_all, NT) + tiled(bias_ref[last:, :])
-    dp = dot(own_values, do_all, NT)
-    p = jnp.exp2(s * (SCALE * LOG2E) - row_ref[at, 0:1, :])
-    pb = p.astype(jnp.bfloat16)
-    ds = (p * (dp - row_ref[at, 1:2, :])).astype(jnp.bfloat16)
-    dv_ref[:, lanes(index)] = dot(pb, do_all, NN)
-    dk_ref[:, lanes(index)] = dot(ds, q_all, NN) * SCALE
-    p_all = jnp.concatenate([p_ref[at], pb], axis=0)
-    ds_all = jnp.concatenate([ds_ref[at], ds], axis=0)
-    out = dot(v_rows.T, p_all, NN).astype(jnp.bfloat16).T
-    dq = (dot(k_rows.T, ds_all, NN) * SCALE).astype(jnp.bfloat16).T
-    for h in range(GROUP):
-        spot = slice(h * rows, (h + 1) * rows)
-        att_ref[:, lanes(h)] = out[spot, :]
-        dq_ref[:, lanes(h)] = dq[spot, :]
+    for step in range(per):
+        index = pl.program_id(0) * per + step
+        at, g = skip + index, start + skip + index
+        own_keys, own_values = own_k[:, lanes(g)], own_v[:, lanes(g)]
+        k_rows = jnp.concatenate(
+            [first_k[:, lanes(at)], *[ref[:, lanes(at)] for ref in near_refs], own_keys], axis=0
+        )
+        v_rows = jnp.concatenate(
+            [first_v[:, lanes(at)], *[ref[:, lanes(at + width)] for ref in near_refs], own_values],
+            axis=0,
+        )
+        q_all, do_all = group_rows(q_ref, g), group_rows(do_ref, g)
+        s = dot(own_keys, q_all, NT) + tiled(bias_ref[last:, :])
+        dp = dot(own_values, do_all, NT)
+        p = jnp.exp2(s * (SCALE * LOG2E) - row_ref[at, 0:1, :])
+        pb = p.astype(jnp.bfloat16)
+        ds = (p * (dp - row_ref[at, 1:2, :])).astype(jnp.bfloat16)
+        dv_ref[:, lanes(index)] = dot(pb, do_all, NN)
+        dk_ref[:, lanes(index)] = dot(ds, q_all, NN) * SCALE
+        p_all = jnp.concatenate([p_ref[at], pb], axis=0)
+        ds_all = jnp.concatenate([ds_ref[at], ds], axis=0)
+        out = dot(v_rows.T, p_all, NN).T.astype(jnp.bfloat16)
+        dq = (dot(k_rows.T, ds_all, NN) * SCALE).T.astype(jnp.bfloat16)
+        for h in range(GROUP):
+            spot = slice(h * rows, (h + 1) * rows)
+            att_ref[:, lanes(step * GROUP + h)] = out[spot, :]
+            dq_ref[:, lanes(step * GROUP + h)] = dq[spot, :]
 
 
 def whole(count, space=pltpu.VMEM):
@@ -321,20 +322,21 @@
     return results[0], results[1:4], results[4 : 4 + units], results[4 + units :]
 
 
-def the_rest(queries, dout, bias, before, near, own, kept, start, skip, count, earlier, behind=()):
+def the_rest(queries, dout, bias, before, near, own, kept, start, spots, earlier, behind=()):
     rows = queries.shape[0]
-    block = pl.BlockSpec((rows, GROUP * WIDTH), lambda g: (0, start + skip + g))
+    skip, count, per = spots
+    block = pl.BlockSpec((rows, per * GROUP * WIDTH), lambda g: (0, (start + skip) // per + g))
     inputs = [near_by(v) for v in (queries, dout, bias, *before, *near, *own, *kept)]
     extra = [*earlier, *behind]
 
     def kernel(*refs):
         refs = refs[: len(inputs)] + refs[len(inputs) + len(extra) :]
-        rest_kernel(start, skip, len(near), *refs)
+        rest_kernel(start, skip, per, len(near), *refs)
 
     wide = jax.ShapeDtypeStruct(queries.shape, jnp.bfloat16)
     results = pl.pallas_call(
         kernel,
-        grid=(count,),
+        grid=(count // per,),
         in_specs=whole(len(inputs)) + whole(len(extra), pl.ANY),
         out_specs=[block, block] + whole(2),
         out_shape=[wide, wide] + [pltpu.VMEM((rows, count * WIDTH), jnp.float32)] * 2,
@@ -615,6 +617,7 @@
     mine0, theirs0 = edge_done(own, got[0], *edge0, False, cols[0])
     other0 = across(theirs0)
     stats = [stats, more_sums(wide_near, own, bias, per_chunk, per_chunk, [theirs0])]
+    edge1[1] = taken(taken(edge1[1], [theirs0]), price=cost(4, rows, 10))
     mine1, theirs1 = edge_done(own, got[1], *edge1, False, cols[1], [theirs0])
     other1 = across(theirs1)
     before0, near0 = window_parts(own, mine0, other0, cols[0], [theirs1, stats[1]])
@@ -625,10 +628,9 @@
     def rest(chunk, piece, behind):
         nonlocal wide
         before, near, kept = held[chunk]
-        skip, count = sum(BEHIND[chunk][:piece]), BEHIND[chunk][piece]
         start = chunk * per_chunk
         wide, terms = the_rest(
-            *wide_near, bias, before, near, own, kept, start, skip, count, wide, behind
+            *wide_near, bias, before, near, own, kept, start, BEHIND[chunk][piece], wide, behind
         )
         pieces.append(terms)
         return terms[:1]
@@ -659,7 +661,7 @@
     other1 = across(theirs1)
     rest(1, 0, [theirs1])
     grad_key, grad_value, entropy = finish(
-        [(*own0, pieces[:2], mine0, other0), (*own1, pieces[2:], mine1, other1)], entropies, back1
+        [(*own0, pieces[1::-1], mine0, other0), (*own1, pieces[2:], mine1, other1)], entropies, back1
     )
     return wide[0], entropy.T, wide[1], grad_key, grad_value
 

time: 61.8 us -> 61.4 us (level)
    ppermute x8, waiting for transfers between devices: 3.9 us -> 2.51 us  [edges(): return lax.ppermute(value, CONTEXT, pairs + [(b, a) for a, b in pairs])]
    ppermute x8, waiting for transfers between devices: 5.7 us -> 7.02 us  [across(): lax.ppermute(value, 'head', [(j, (j + subs) % size) for j in range(size)])]
    ppermute x8, starting transfers between devices: 9.95 us -> 11.2 us  [across(): lax.ppermute(value, 'head', [(j, (j + subs) % size) for j in range(size)])]
    ppermute x8, starting transfers between devices: 13.4 us -> 12.3 us  [edges(): return lax.ppermute(value, CONTEXT, pairs + [(b, a) for a, b in pairs])]
  transfers between devices with their start and end apart: 20 -> 20, of which waited for: 7 -> 9; matrix products, arithmetic and copies ran while one was open for 0% -> 0% of each run, Pallas kernels for 39% -> 38%
where the time goes in v8:
time: 61.4 us; the launch traced here: 60.6 us
  Pallas kernels  25.3 us (41%)
  starting transfers between devices  24.3 us (40%)
  waiting for transfers between devices  10.1 us (16%)
  between operations  0.94 us (2%)
    ppermute x8, starting transfers between devices, edges(): return lax.ppermute(value, CONTEXT, pairs + [(b, a) for a, b in pairs])  12.3 us
    ppermute x8, starting transfers between devices, across(): lax.ppermute(value, 'head', [(j, (j + subs) % size) for j in range(size)])  11.2 us
    pallas_call x3, Pallas kernels, large(): pl.pallas_call(body, in_specs=whole(len(inputs)) + whole(len(behind), pl....  10.9 us
    pallas_call x3, Pallas kernels, the_rest(): pl.pallas_call(kernel, grid=(count // per,), in_specs=whole(len(inputs))...  8.4 us
    ppermute x8, waiting for transfers between devices, across(): lax.ppermute(value, 'head', [(j, (j + subs) % size) for j in range(size)])  7.02 us
    pallas_call x1, Pallas kernels, first_step(): pl.pallas_call(kernel, in_specs=whole(7, pl.ANY), out_specs=whole(4) + wh...  3.25 us
    ppermute x8, waiting for transfers between devices, edges(): return lax.ppermute(value, CONTEXT, pairs + [(b, a) for a, b in pairs])  2.51 us
  transfers between devices with their start and end apart: 20, of which 9 were waited for; matrix products, arithmetic and copies ran while one was open for 0% of the time, Pallas kernels for 38%

profile of v8, /device:TPU:0, one launch (start us, length us, event | category | flops | bytes accessed | tf_op | source)
XLA Modules:
  0.0 60.6 jit_solution(8655030843729234067)
XLA Ops:
  0.6 0.9 %shard_map.101.refs_6_ = bf16[128,512]{1,0:T(8,128)(2,1)S(1)} custom-call(bf16[128,1024]{1,0:T(8,128)(2,1)} %refs_2_.1, bf16[128,1024]{1,0:T(8,128)(2,1)} %refs_3_.1), custom_call_target="tpu_custom_call" | custom-call | tf_op jit(solution)/shard_map/pallas_call | solution.py:393
  1.6 3.0 %collective-permute-start = (bf16[128,512]{1,0:T(8,128)(2,1)S(1)}, bf16[128,512]{1,0:T(8,128)(2,1)S(1)}, u32[]{:S(2)}, u32[]{:S(2)}) collective-permute-start(bf16[128,512]{1,0:T(8,128)(2,1)S(1)} %shard_map.101.refs_6_), channel_id=1, source_target_pairs={{0,16},{8,24},{16,0},{24,8},{1,17},{9,25},{17,1},{25,9},{2,18},{10... | collective-permute-start | bytes 393224 | tf_op jit(solution)/shard_map/ppermute | solution.py:371
  4.6 3.2 %shard_map.102 = (bf16[128,8192]{1,0:T(8,128)(2,1)S(1)}, bf16[128,8192]{1,0:T(8,128)(2,1)S(1)}, bf16[128,1024]{1,0:T(8,128)(2,1)S(1)}, bf16[128,1024]{1,0:T(8,12...) custom-call(bf16[128,8192]{1,0:T(8,128)(2,1)} %refs_0_.1, ...), custom_call_target="tpu_custom_call" | custom-call | flops 805306368 | bytes 1 | tf_op jit(solution)/shard_map/pallas_call | solution.py:280
  7.9 0.2 collective-permute-done.refs_3_
  8.1 1.8 %collective-permute-start.1 = (bf16[128,512]{1,0:T(8,128)(2,1)S(1)}, bf16[128,512]{1,0:T(8,128)(2,1)S(1)}, u32[]{:S(2)}, u32[]{:S(2)}) collective-permute-start(bf16[128,512]{1,0:T(8,128)(2,1)S(1)} %shard_map.103), channel_id=1, source_target_pairs={{0,16},{8,24},{16,0},{24,8},{1,17},{9,25},{17,1},{25,9},{2,18},{10... | collective-permute-start | bytes 393224 | tf_op jit(solution)/shard_map/ppermute | solution.py:371
  9.9 1.6 %collective-permute-start.4 = (bf16[128,512]{1,0:T(8,128)(2,1)S(1)}, bf16[128,512]{1,0:T(8,128)(2,1)S(1)}, u32[]{:S(2)}, u32[]{:S(2)}) collective-permute-start(bf16[128,512]{1,0:T(8,128)(2,1)S(1)} %shard_map.106), channel_id=1, source_target_pairs={{0,1},{2,3},{4,5},{6,7},{1,0},{3,2},{5,4},{7,6},{8,9},{10,11},{12,... | collective-permute-start | bytes 393224 | tf_op jit(solution)/shard_map/ppermute | solution.py:379
  11.5 0.7 %collective-permute-start.5 = (bf16[128,512]{1,0:T(8,128)(2,1)S(1)}, bf16[128,512]{1,0:T(8,128)(2,1)S(1)}, u32[]{:S(2)}, u32[]{:S(2)}) collective-permute-start(bf16[128,512]{1,0:T(8,128)(2,1)S(1)} %shard_map.107), channel_id=1, source_target_pairs={{1,2},{3,4},{5,6},{2,1},{4,3},{6,5},{9,10},{11,12},{13,14},{10,9},... | collective-permute-start | bytes 393224 | tf_op jit(solution)/shard_map/ppermute | solution.py:379
  12.2 1.0 %collective-permute-done.1.refs_3_ = bf16[128,512]{1,0:T(8,128)(2,1)S(1)} collective-permute-done((bf16[128,512]{1,0:T(8,128)(2,1)S(1)}, bf16[128,512]{1,0:T(8,128)(2,1)S(1)}, u32[]{:S(2)}, u32[]{:S(2)}) %collective-permute-start.1) | collective-permute-done | bytes 131104 | tf_op jit(solution)/shard_map/ppermute | solution.py:371
  13.2 0.7 %collective-permute-start.3 = (bf16[128,512]{1,0:T(8,128)(2,1)S(1)}, bf16[128,512]{1,0:T(8,128)(2,1)S(1)}, u32[]{:S(2)}, u32[]{:S(2)}) collective-permute-start(bf16[128,512]{1,0:T(8,128)(2,1)S(1)} %shard_map.105), channel_id=1, source_target_pairs={{1,2},{3,4},{5,6},{2,1},{4,3},{6,5},{9,10},{11,12},{13,14},{10,9},... | collective-permute-start | bytes 393224 | tf_op jit(solution)/shard_map/ppermute | solution.py:379
  13.9 5.1 %collective-permute-start.2 = (bf16[128,512]{1,0:T(8,128)(2,1)S(1)}, bf16[128,512]{1,0:T(8,128)(2,1)S(1)}, u32[]{:S(2)}, u32[]{:S(2)}) collective-permute-start(bf16[128,512]{1,0:T(8,128)(2,1)S(1)} %shard_map.104), channel_id=1, source_target_pairs={{0,1},{2,3},{4,5},{6,7},{1,0},{3,2},{5,4},{7,6},{8,9},{10,11},{12,... | collective-permute-start | bytes 393224 | tf_op jit(solution)/shard_map/ppermute | solution.py:379
  19.0 0.0 collective-permute-done.4.refs_4_
  19.0 0.0 collective-permute-done.5.refs_5_
  19.0 0.1 shard_map.108
  19.0 1.1 %collective-permute-start.7 = (bf16[128,512]{1,0:T(8,128)(2,1)S(1)}, bf16[128,512]{1,0:T(8,128)(2,1)S(1)}, u32[]{:S(2)}, u32[]{:S(2)}) collective-permute-start(bf16[128,512]{1,0:T(8,128)(2,1)S(1)} %get-tuple-element.73.refs_2_.refs_6_.refs_5_), channel_id=1, source_target_pairs={{0,16},{8,24},{16,0},{24,8},{1,17},{9,25},{17,1},{25,9},{2,18},{10... | collective-permute-start | bytes 393224 | tf_op jit(solution)/shard_map/ppermute | solution.py:371
  20.1 1.8 %shard_map.112.refs_6_ = f32[4,8,1024]{2,1,0:T(8,128)S(1)} custom-call(bf16[128,8192]{1,0:T(8,128)(2,1)S(1)} %get-tuple-element.66.refs_0_, bf16[128,8192]{1,0:T(8,128)(2,1)S(1)} %get-tuple-element.67.refs_1_, bf16[128,1024]{1,0:T(8,128)(2,1)S(1)} %get-tuple-element.70.refs_1_.refs_2_.refs_6_, ...), custom_call_target="tpu_custom_call" | custom-call | flops 536870912 | bytes 1 | tf_op jit(solution)/shard_map/pallas_call | solution.py:259
  21.9 1.0 %collective-permute-done.2.refs_4_ = bf16[128,512]{1,0:T(8,128)(2,1)S(1)} collective-permute-done((bf16[128,512]{1,0:T(8,128)(2,1)S(1)}, bf16[128,512]{1,0:T(8,128)(2,1)S(1)}, u32[]{:S(2)}, u32[]{:S(2)}) %collective-permute-start.2) | collective-permute-done | bytes 131104 | tf_op jit(solution)/shard_map/ppermute | solution.py:379
  22.9 0.1 shard_map.111
  23.0 1.1 %collective-permute-done.7.refs_4_ = bf16[128,512]{1,0:T(8,128)(2,1)S(1)} collective-permute-done((bf16[128,512]{1,0:T(8,128)(2,1)S(1)}, bf16[128,512]{1,0:T(8,128)(2,1)S(1)}, u32[]{:S(2)}, u32[]{:S(2)}) %collective-permute-start.7) | collective-permute-done | bytes 131104 | tf_op jit(solution)/shard_map/ppermute | solution.py:371
  24.1 0.1 collective-permute-start.8
  24.2 1.1 %collective-permute-start.6 = (bf16[128,512]{1,0:T(8,128)(2,1)S(1)}, bf16[128,512]{1,0:T(8,128)(2,1)S(1)}, u32[]{:S(2)}, u32[]{:S(2)}) collective-permute-start(bf16[128,512]{1,0:T(8,128)(2,1)S(1)} %get-tuple-element.75.refs_5_), channel_id=1, source_target_pairs={{0,16},{8,24},{16,0},{24,8},{1,17},{9,25},{17,1},{25,9},{2,18},{10... | collective-permute-start | bytes 393224 | tf_op jit(solution)/shard_map/ppermute | solution.py:371
  25.3 0.5 collective-permute-done.8.refs_5_
  25.7 4.5 %shard_map.114 = (f32[4,8,128]{2,1,0:T(8,128)S(1)}, f32[4,8,1024]{2,1,0:T(8,128)S(1)}, bf16[4,256,1024]{2,1,0:T(8,128)(2,1)S(1)}, bf16[4,256,1024]{2,1,0:T(8,128...) custom-call(bf16[128,8192]{1,0:T(8,128)(2,1)S(1)} %get-tuple-element, ...), custom_call_target="tpu_custom_call" | custom-call | flops 2147483648 | bytes 1 | tf_op jit(solution)/shard_map/pallas_call | solution.py:259
  30.3 0.2 collective-permute-start.10
  30.5 0.4 collective-permute-start.9
  31.0 1.5 %shard_map.118 = (bf16[128,8192]{1,0:T(8,128)(2,1)}, bf16[128,8192]{1,0:T(8,128)(2,1)}, f32[128,128]{1,0:T(8,128)S(1)}, f32[128,128]{1,0:T(8,128)S(1)}) custom-call(bf16[128,8192]{1,0:T(8,128)(2,1)S(1)} %get-tuple-element.66.refs_0_, bf16[128,8192]{1,0:T(8,128)(2,1)S(1)} %get-tuple-element.67.refs_1_, f32[384,128]{1,0:T(8,128)S(1)} %get-tuple-element.68.refs_4_.refs_2_, ...), custom_call_target="tpu_custom_call" | custom-call | flops 335544320 | bytes 1 | tf_op jit(solution)/shard_map/pallas_call | solution.py:337
  32.5 0.1 shard_map.117
  32.6 1.1 %collective-permute-start.11 = (bf16[128,512]{1,0:T(8,128)(2,1)S(1)}, bf16[128,512]{1,0:T(8,128)(2,1)S(1)}, u32[]{:S(2)}, u32[]{:S(2)}) collective-permute-start(bf16[128,512]{1,0:T(8,128)(2,1)S(1)} %get-tuple-element.88.refs_7_), channel_id=1, source_target_pairs={{0,16},{8,24},{16,0},{24,8},{1,17},{9,25},{17,1},{25,9},{2,18},{10... | collective-permute-start | bytes 393224 | tf_op jit(solution)/shard_map/ppermute | solution.py:371
  33.7 0.0 collective-permute-done.9.refs_5_
  33.7 4.6 %shard_map.119 = (f32[4,8,128]{2,1,0:T(8,128)S(1)}, f32[4,8,1024]{2,1,0:T(8,128)S(1)}, bf16[4,256,1024]{2,1,0:T(8,128)(2,1)S(1)}, bf16[4,256,1024]{2,1,0:T(8,128...) custom-call(bf16[128,8192]{1,0:T(8,128)(2,1)S(1)} %get-tuple-element, ...), custom_call_target="tpu_custom_call" | custom-call | flops 2147483648 | bytes 1 | tf_op jit(solution)/shard_map/pallas_call | solution.py:259
  38.3 0.0 collective-permute-done.11.refs_2_
  38.3 0.1 collective-permute-start.13
  38.4 1.4 %collective-permute-start.12 = (bf16[128,512]{1,0:T(8,128)(2,1)S(1)}, bf16[128,512]{1,0:T(8,128)(2,1)S(1)}, u32[]{:S(2)}, u32[]{:S(2)}) collective-permute-start(bf16[128,512]{1,0:T(8,128)(2,1)S(1)} %shard_map.120.refs_5_), channel_id=1, source_target_pairs={{0,1},{2,3},{4,5},{6,7},{1,0},{3,2},{5,4},{7,6},{8,9},{10,11},{12,... | collective-permute-start | bytes 393224 | tf_op jit(solution)/shard_map/ppermute | solution.py:379
  39.9 0.1 collective-permute-done.13.refs_5_
  40.0 0.1 shard_map.122
  40.1 1.1 %collective-permute-start.15 = (bf16[144,512]{1,0:T(8,128)(2,1)S(1)}, bf16[144,512]{1,0:T(8,128)(2,1)S(1)}, u32[]{:S(2)}, u32[]{:S(2)}) collective-permute-start(bf16[144,512]{1,0:T(8,128)(2,1)S(1)} %get-tuple-element.104.refs_3_), channel_id=1, source_target_pairs={{0,16},{8,24},{16,0},{24,8},{1,17},{9,25},{17,1},{25,9},{2,18},{10... | collective-permute-start | bytes 442376 | tf_op jit(solution)/shard_map/ppermute | solution.py:371
  41.3 0.7 %collective-permute-start.14 = (bf16[128,512]{1,0:T(8,128)(2,1)S(1)}, bf16[128,512]{1,0:T(8,128)(2,1)S(1)}, u32[]{:S(2)}, u32[]{:S(2)}) collective-permute-start(bf16[128,512]{1,0:T(8,128)(2,1)S(1)} %shard_map.123), channel_id=1, source_target_pairs={{1,2},{3,4},{5,6},{2,1},{4,3},{6,5},{9,10},{11,12},{13,14},{10,9},... | collective-permute-start | bytes 393224 | tf_op jit(solution)/shard_map/ppermute | solution.py:379
  41.9 4.2 %collective-permute-done.15.refs_2_.refs_1_ = bf16[144,512]{1,0:T(8,128)(2,1)S(1)} collective-permute-done((bf16[144,512]{1,0:T(8,128)(2,1)S(1)}, bf16[144,512]{1,0:T(8,128)(2,1)S(1)}, u32[]{:S(2)}, u32[]{:S(2)}) %collective-permute-start.15) | collective-permute-done | bytes 147488 | tf_op jit(solution)/shard_map/ppermute | solution.py:371
  46.1 1.6 %collective-permute-start.16 = (bf16[128,512]{1,0:T(8,128)(2,1)S(1)}, bf16[128,512]{1,0:T(8,128)(2,1)S(1)}, u32[]{:S(2)}, u32[]{:S(2)}) collective-permute-start(bf16[128,512]{1,0:T(8,128)(2,1)S(1)} %shard_map.124.refs_5_), channel_id=1, source_target_pairs={{0,1},{2,3},{4,5},{6,7},{1,0},{3,2},{5,4},{7,6},{8,9},{10,11},{12,... | collective-permute-start | bytes 393224 | tf_op jit(solution)/shard_map/ppermute | solution.py:379
  47.7 0.7 %collective-permute-start.17 = (bf16[128,512]{1,0:T(8,128)(2,1)S(1)}, bf16[128,512]{1,0:T(8,128)(2,1)S(1)}, u32[]{:S(2)}, u32[]{:S(2)}) collective-permute-start(bf16[128,512]{1,0:T(8,128)(2,1)S(1)} %shard_map.129), channel_id=1, source_target_pairs={{1,2},{3,4},{5,6},{2,1},{4,3},{6,5},{9,10},{11,12},{13,14},{10,9},... | collective-permute-start | bytes 393224 | tf_op jit(solution)/shard_map/ppermute | solution.py:379
  48.4 0.1 shard_map.125
  48.4 1.1 %collective-permute-start.18 = (bf16[128,512]{1,0:T(8,128)(2,1)S(1)}, bf16[128,512]{1,0:T(8,128)(2,1)S(1)}, u32[]{:S(2)}, u32[]{:S(2)}) collective-permute-start(bf16[128,512]{1,0:T(8,128)(2,1)S(1)} %get-tuple-element.106.refs_13_), channel_id=1, source_target_pairs={{0,16},{8,24},{16,0},{24,8},{1,17},{9,25},{17,1},{25,9},{2,18},{10... | collective-permute-start | bytes 393224 | tf_op jit(solution)/shard_map/ppermute | solution.py:371
  49.5 3.2 %shard_map.126 = (bf16[128,8192]{1,0:T(8,128)(2,1)}, bf16[128,8192]{1,0:T(8,128)(2,1)}, f32[128,384]{1,0:T(8,128)S(1)}, f32[128,384]{1,0:T(8,128)S(1)}) custom-call(bf16[128,8192]{1,0:T(8,128)(2,1)S(1)} %get-tuple-element.66.refs_0_, bf16[128,8192]{1,0:T(8,128)(2,1)S(1)} %get-tuple-element.67.refs_1_, ...), custom_call_target="tpu_custom_call", output_to_operand_aliasing={{0}: (11, {}), {1}: (12, {})} | custom-call | flops 1006632960 | bytes 1 | tf_op jit(solution)/shard_map/pallas_call | solution.py:337
  52.7 1.5 %collective-permute-done.16.refs_1_ = bf16[128,512]{1,0:T(8,128)(2,1)S(1)} collective-permute-done((bf16[128,512]{1,0:T(8,128)(2,1)S(1)}, bf16[128,512]{1,0:T(8,128)(2,1)S(1)}, u32[]{:S(2)}, u32[]{:S(2)}) %collective-permute-start.16) | collective-permute-done | bytes 131104 | tf_op jit(solution)/shard_map/ppermute | solution.py:379
  54.2 0.1 shard_map.130
  54.3 1.0 %collective-permute-start.19 = (bf16[128,512]{1,0:T(8,128)(2,1)S(1)}, bf16[128,512]{1,0:T(8,128)(2,1)S(1)}, u32[]{:S(2)}, u32[]{:S(2)}) collective-permute-start(bf16[128,512]{1,0:T(8,128)(2,1)S(1)} %get-tuple-element.110.refs_13_), channel_id=1, source_target_pairs={{0,16},{8,24},{16,0},{24,8},{1,17},{9,25},{17,1},{25,9},{2,18},{10... | collective-permute-start | bytes 393224 | tf_op jit(solution)/shard_map/ppermute | solution.py:371
  55.3 3.7 %shard_map.131 = (bf16[128,8192]{1,0:T(8,128)(2,1)}, bf16[128,8192]{1,0:T(8,128)(2,1)}, f32[128,512]{1,0:T(8,128)S(1)}, f32[128,512]{1,0:T(8,128)S(1)}) custom-call(bf16[128,8192]{1,0:T(8,128)(2,1)S(1)} %get-tuple-element.66.refs_0_, bf16[128,8192]{1,0:T(8,128)(2,1)S(1)} %get-tuple-element.67.refs_1_, ...), custom_call_target="tpu_custom_call", output_to_operand_aliasing={{0}: (11, {}), {1}: (12, {})} | custom-call | flops 1342177280 | bytes 1 | tf_op jit(solution)/shard_map/pallas_call | solution.py:337
  59.0 0.6 collective-permute-done.19.refs_17_
  59.6 1.1 %shard_map.132 = (bf16[128,1024]{1,0:T(8,128)(2,1)}, bf16[128,1024]{1,0:T(8,128)(2,1)}, f32[16,512]{1,0:T(8,128)}) custom-call(s32[6]{0:T(128)S(4)} %get-tuple-element.69.refs_0_.flag, f32[2,16,128]{2,1,0:T(8,128)S(1)} %get-tuple-element.112.refs_0_, bf16[144,512]{1,0:T(8,128)(2,1)S(1)} %collective-permute-done.15.refs_2_.refs_1_, ...), custom_call_target="tpu_custom_call" | custom-call | tf_op jit(solution)/shard_map/pallas_call | solution.py:589
  (24 shorter events, 0.3 us)
Async XLA Ops:
  1.6 6.5 %collective-permute-start = (bf16[128,512]{1,0:T(8,128)(2,1)S(1)}, bf16[128,512]{1,0:T(8,128)(2,1)S(1)}, u32[]{:S(2)}, u32[]{:S(2)}) collective-permute-start(bf16[128,512]{1,0:T(8,128)(2,1)S(1)} %shard_map.101.refs_6_), channel_id=1, source_target_pairs={{0,16},{8,24},{16,0},{24,8},{1,17},{9,25},{17,1},{25,9},{2,18},{10... | collective-permute-start | bytes 393224 | tf_op jit(solution)/shard_map/ppermute | solution.py:371
  8.1 5.0 %collective-permute-start.1 = (bf16[128,512]{1,0:T(8,128)(2,1)S(1)}, bf16[128,512]{1,0:T(8,128)(2,1)S(1)}, u32[]{:S(2)}, u32[]{:S(2)}) collective-permute-start(bf16[128,512]{1,0:T(8,128)(2,1)S(1)} %shard_map.103), channel_id=1, source_target_pairs={{0,16},{8,24},{16,0},{24,8},{1,17},{9,25},{17,1},{25,9},{2,18},{10... | collective-permute-start | bytes 393224 | tf_op jit(solution)/shard_map/ppermute | solution.py:371
  9.9 9.0 %collective-permute-start.4 = (bf16[128,512]{1,0:T(8,128)(2,1)S(1)}, bf16[128,512]{1,0:T(8,128)(2,1)S(1)}, u32[]{:S(2)}, u32[]{:S(2)}) collective-permute-start(bf16[128,512]{1,0:T(8,128)(2,1)S(1)} %shard_map.106), channel_id=1, source_target_pairs={{0,1},{2,3},{4,5},{6,7},{1,0},{3,2},{5,4},{7,6},{8,9},{10,11},{12,... | collective-permute-start | bytes 393224 | tf_op jit(solution)/shard_map/ppermute | solution.py:379
  11.5 7.5 %collective-permute-start.5 = (bf16[128,512]{1,0:T(8,128)(2,1)S(1)}, bf16[128,512]{1,0:T(8,128)(2,1)S(1)}, u32[]{:S(2)}, u32[]{:S(2)}) collective-permute-start(bf16[128,512]{1,0:T(8,128)(2,1)S(1)} %shard_map.107), channel_id=1, source_target_pairs={{1,2},{3,4},{5,6},{2,1},{4,3},{6,5},{9,10},{11,12},{13,14},{10,9},... | collective-permute-start | bytes 393224 | tf_op jit(solution)/shard_map/ppermute | solution.py:379
  13.2 8.7 %collective-permute-start.3 = (bf16[128,512]{1,0:T(8,128)(2,1)S(1)}, bf16[128,512]{1,0:T(8,128)(2,1)S(1)}, u32[]{:S(2)}, u32[]{:S(2)}) collective-permute-start(bf16[128,512]{1,0:T(8,128)(2,1)S(1)} %shard_map.105), channel_id=1, source_target_pairs={{1,2},{3,4},{5,6},{2,1},{4,3},{6,5},{9,10},{11,12},{13,14},{10,9},... | collective-permute-start | bytes 393224 | tf_op jit(solution)/shard_map/ppermute | solution.py:379
  13.9 9.1 %collective-permute-start.2 = (bf16[128,512]{1,0:T(8,128)(2,1)S(1)}, bf16[128,512]{1,0:T(8,128)(2,1)S(1)}, u32[]{:S(2)}, u32[]{:S(2)}) collective-permute-start(bf16[128,512]{1,0:T(8,128)(2,1)S(1)} %shard_map.104), channel_id=1, source_target_pairs={{0,1},{2,3},{4,5},{6,7},{1,0},{3,2},{5,4},{7,6},{8,9},{10,11},{12,... | collective-permute-start | bytes 393224 | tf_op jit(solution)/shard_map/ppermute | solution.py:379
  19.0 5.0 %collective-permute-start.7 = (bf16[128,512]{1,0:T(8,128)(2,1)S(1)}, bf16[128,512]{1,0:T(8,128)(2,1)S(1)}, u32[]{:S(2)}, u32[]{:S(2)}) collective-permute-start(bf16[128,512]{1,0:T(8,128)(2,1)S(1)} %get-tuple-element.73.refs_2_.refs_6_.refs_5_), channel_id=1, source_target_pairs={{0,16},{8,24},{16,0},{24,8},{1,17},{9,25},{17,1},{25,9},{2,18},{10... | collective-permute-start | bytes 393224 | tf_op jit(solution)/shard_map/ppermute | solution.py:371
  24.1 1.6 %collective-permute-start.8 = (bf16[128,1024]{1,0:T(8,128)(2,1)S(1)}, bf16[128,1024]{1,0:T(8,128)(2,1)S(1)}, u32[]{:S(2)}, u32[]{:S(2)}) collective-permute-start(bf16[128,1024]{1,0:T(8,128)(2,1)S(1)} %get-tuple-element.79), channel_id=1, source_target_pairs={{0,8},{8,0},{16,24},{24,16},{1,9},{9,1},{17,25},{25,17},{2,10},{10... | collective-permute-start | bytes 786440 | tf_op jit(solution)/shard_map/ppermute | solution.py:375
  24.2 6.3 %collective-permute-start.6 = (bf16[128,512]{1,0:T(8,128)(2,1)S(1)}, bf16[128,512]{1,0:T(8,128)(2,1)S(1)}, u32[]{:S(2)}, u32[]{:S(2)}) collective-permute-start(bf16[128,512]{1,0:T(8,128)(2,1)S(1)} %get-tuple-element.75.refs_5_), channel_id=1, source_target_pairs={{0,16},{8,24},{16,0},{24,8},{1,17},{9,25},{17,1},{25,9},{2,18},{10... | collective-permute-start | bytes 393224 | tf_op jit(solution)/shard_map/ppermute | solution.py:371
  30.3 2.2 %collective-permute-start.10 = (bf16[128,1024]{1,0:T(8,128)(2,1)S(1)}, bf16[128,1024]{1,0:T(8,128)(2,1)S(1)}, u32[]{:S(2)}, u32[]{:S(2)}) collective-permute-start(bf16[128,1024]{1,0:T(8,128)(2,1)S(1)} %shard_map.116.refs_11_), channel_id=1, source_target_pairs={{0,8},{8,0},{16,24},{24,16},{1,9},{9,1},{17,25},{25,17},{2,10},{10... | collective-permute-start | bytes 786440 | tf_op jit(solution)/shard_map/ppermute | solution.py:375
  30.5 3.1 %collective-permute-start.9 = (bf16[128,1024]{1,0:T(8,128)(2,1)S(1)}, bf16[128,1024]{1,0:T(8,128)(2,1)S(1)}, u32[]{:S(2)}, u32[]{:S(2)}) collective-permute-start(bf16[128,1024]{1,0:T(8,128)(2,1)S(1)} %get-tuple-element.83), channel_id=1, source_target_pairs={{0,8},{8,0},{16,24},{24,16},{1,9},{9,1},{17,25},{25,17},{2,10},{10... | collective-permute-start | bytes 786440 | tf_op jit(solution)/shard_map/ppermute | solution.py:375
  32.6 5.7 %collective-permute-start.11 = (bf16[128,512]{1,0:T(8,128)(2,1)S(1)}, bf16[128,512]{1,0:T(8,128)(2,1)S(1)}, u32[]{:S(2)}, u32[]{:S(2)}) collective-permute-start(bf16[128,512]{1,0:T(8,128)(2,1)S(1)} %get-tuple-element.88.refs_7_), channel_id=1, source_target_pairs={{0,16},{8,24},{16,0},{24,8},{1,17},{9,25},{17,1},{25,9},{2,18},{10... | collective-permute-start | bytes 393224 | tf_op jit(solution)/shard_map/ppermute | solution.py:371
  38.3 1.6 %collective-permute-start.13 = (bf16[144,1024]{1,0:T(8,128)(2,1)S(1)}, bf16[144,1024]{1,0:T(8,128)(2,1)S(1)}, u32[]{:S(2)}, u32[]{:S(2)}) collective-permute-start(bf16[144,1024]{1,0:T(8,128)(2,1)S(1)} %shard_map.121), channel_id=1, source_target_pairs={{0,8},{8,0},{16,24},{24,16},{1,9},{9,1},{17,25},{25,17},{2,10},{10... | collective-permute-start | bytes 884744 | tf_op jit(solution)/shard_map/ppermute | solution.py:375
  38.4 10.0 %collective-permute-start.12 = (bf16[128,512]{1,0:T(8,128)(2,1)S(1)}, bf16[128,512]{1,0:T(8,128)(2,1)S(1)}, u32[]{:S(2)}, u32[]{:S(2)}) collective-permute-start(bf16[128,512]{1,0:T(8,128)(2,1)S(1)} %shard_map.120.refs_5_), channel_id=1, source_target_pairs={{0,1},{2,3},{4,5},{6,7},{1,0},{3,2},{5,4},{7,6},{8,9},{10,11},{12,... | collective-permute-start | bytes 393224 | tf_op jit(solution)/shard_map/ppermute | solution.py:379
  40.1 6.0 %collective-permute-start.15 = (bf16[144,512]{1,0:T(8,128)(2,1)S(1)}, bf16[144,512]{1,0:T(8,128)(2,1)S(1)}, u32[]{:S(2)}, u32[]{:S(2)}) collective-permute-start(bf16[144,512]{1,0:T(8,128)(2,1)S(1)} %get-tuple-element.104.refs_3_), channel_id=1, source_target_pairs={{0,16},{8,24},{16,0},{24,8},{1,17},{9,25},{17,1},{25,9},{2,18},{10... | collective-permute-start | bytes 442376 | tf_op jit(solution)/shard_map/ppermute | solution.py:371
  41.3 7.1 %collective-permute-start.14 = (bf16[128,512]{1,0:T(8,128)(2,1)S(1)}, bf16[128,512]{1,0:T(8,128)(2,1)S(1)}, u32[]{:S(2)}, u32[]{:S(2)}) collective-permute-start(bf16[128,512]{1,0:T(8,128)(2,1)S(1)} %shard_map.123), channel_id=1, source_target_pairs={{1,2},{3,4},{5,6},{2,1},{4,3},{6,5},{9,10},{11,12},{13,14},{10,9},... | collective-permute-start | bytes 393224 | tf_op jit(solution)/shard_map/ppermute | solution.py:379
  46.1 8.1 %collective-permute-start.16 = (bf16[128,512]{1,0:T(8,128)(2,1)S(1)}, bf16[128,512]{1,0:T(8,128)(2,1)S(1)}, u32[]{:S(2)}, u32[]{:S(2)}) collective-permute-start(bf16[128,512]{1,0:T(8,128)(2,1)S(1)} %shard_map.124.refs_5_), channel_id=1, source_target_pairs={{0,1},{2,3},{4,5},{6,7},{1,0},{3,2},{5,4},{7,6},{8,9},{10,11},{12,... | collective-permute-start | bytes 393224 | tf_op jit(solution)/shard_map/ppermute | solution.py:379
  47.7 6.5 %collective-permute-start.17 = (bf16[128,512]{1,0:T(8,128)(2,1)S(1)}, bf16[128,512]{1,0:T(8,128)(2,1)S(1)}, u32[]{:S(2)}, u32[]{:S(2)}) collective-permute-start(bf16[128,512]{1,0:T(8,128)(2,1)S(1)} %shard_map.129), channel_id=1, source_target_pairs={{1,2},{3,4},{5,6},{2,1},{4,3},{6,5},{9,10},{11,12},{13,14},{10,9},... | collective-permute-start | bytes 393224 | tf_op jit(solution)/shard_map/ppermute | solution.py:379
  48.4 10.5 %collective-permute-start.18 = (bf16[128,512]{1,0:T(8,128)(2,1)S(1)}, bf16[128,512]{1,0:T(8,128)(2,1)S(1)}, u32[]{:S(2)}, u32[]{:S(2)}) collective-permute-start(bf16[128,512]{1,0:T(8,128)(2,1)S(1)} %get-tuple-element.106.refs_13_), channel_id=1, source_target_pairs={{0,16},{8,24},{16,0},{24,8},{1,17},{9,25},{17,1},{25,9},{2,18},{10... | collective-permute-start | bytes 393224 | tf_op jit(solution)/shard_map/ppermute | solution.py:371
  54.3 5.3 %collective-permute-start.19 = (bf16[128,512]{1,0:T(8,128)(2,1)S(1)}, bf16[128,512]{1,0:T(8,128)(2,1)S(1)}, u32[]{:S(2)}, u32[]{:S(2)}) collective-permute-start(bf16[128,512]{1,0:T(8,128)(2,1)S(1)} %get-tuple-element.110.refs_13_), channel_id=1, source_target_pairs={{0,16},{8,24},{16,0},{24,8},{1,17},{9,25},{17,1},{25,9},{2,18},{10... | collective-permute-start | bytes 393224 | tf_op jit(solution)/shard_map/ppermute | solution.py:371

commit v9 on v8

--- a/solution.py
+++ b/solution.py
@@ -16,9 +16,9 @@
 MASKED = -1e30
 CONTEXT = ("inner", "outer")
 CHUNKS = 2
-UNROLL = 2
+UNROLL = 4
 EXTRA = 16
-BEHIND = (((3, 1, 1), (0, 3, 1)), ((0, 4, 2),))
+BEHIND = (((0, 4, 2),), ((0, 4, 2),))
 LOG2E = math.log2(math.e)
 VMEM_SMALL = 8 * 2**20
 VMEM_LARGE = 16 * 2**20
@@ -637,11 +637,10 @@
 
     held = [(before0, near0, kept0), (before1, near1, None)]
     arrived, sent = near_terms(dk0, dv0)
-    done = rest(0, 0, sent[:1])
     keep0, give0, *own0 = collect(dk0, dv0, arrived)
     back0 = across(give0)
     ent1, kept1, dk1, dv1 = earlier_terms(
-        *wide_near, bias, before1, near1, stats[1], per_chunk, [give0, *done]
+        *wide_near, bias, before1, near1, stats[1], per_chunk, [give0]
     )
     held[1] = (before1, near1, kept1)
     out0 = edge_part([keep0], back0, True, 0)
@@ -655,13 +654,13 @@
     edge1 = [edges(part, odd) for odd, part in enumerate(out1)]
     mine0, theirs0 = edge_done([keep0], back0, *edge0, True, behind=out1[:1])
     other0 = across(theirs0)
-    done = rest(0, 1, [theirs0])
+    done = rest(0, 0, [theirs0])
     edge1[0] = taken(taken(edge1[0], done), price=cost(4, rows, 10))
     mine1, theirs1 = edge_done([keep1], back1, *edge1, True, behind=done)
     other1 = across(theirs1)
     rest(1, 0, [theirs1])
     grad_key, grad_value, entropy = finish(
-        [(*own0, pieces[1::-1], mine0, other0), (*own1, pieces[2:], mine1, other1)], entropies, back1
+        [(*own0, pieces[:1], mine0, other0), (*own1, pieces[1:], mine1, other1)], entropies, back1
     )
     return wide[0], entropy.T, wide[1], grad_key, grad_value
 

time: 61.4 us -> 60.7 us (0.989)
  Pallas kernels: 25.3 us -> 24.1 us
    pallas_call x3 -> x2, Pallas kernels: 8.4 us -> 7.3 us  [the_rest(): pl.pallas_call(kernel, grid=(count // per,), in_specs=whole(len(inputs))...]
    ppermute x4, waiting for transfers between devices: 0.59 us -> 1.41 us  [around(): return lax.ppermute(value, 'head', pairs)]
  transfers between devices with their start and end apart: 20 -> 20, of which waited for: 9 -> 11; matrix products, arithmetic and copies ran while one was open for 0% -> 0% of each run, Pallas kernels for 38% -> 37%
where the time goes in v9:
time: 60.7 us; the launch traced here: 59.7 us
  starting transfers between devices  24.4 us (40%)
  Pallas kernels  24.1 us (40%)
  waiting for transfers between devices  10.3 us (17%)
  between operations  0.92 us (2%)
    ppermute x8, starting transfers between devices, edges(): return lax.ppermute(value, CONTEXT, pairs + [(b, a) for a, b in pairs])  12.3 us
    ppermute x8, starting transfers between devices, across(): lax.ppermute(value, 'head', [(j, (j + subs) % size) for j in range(size)])  11.3 us
    pallas_call x3, Pallas kernels, large(): pl.pallas_call(body, in_specs=whole(len(inputs)) + whole(len(behind), pl....  10.6 us
    pallas_call x2, Pallas kernels, the_rest(): pl.pallas_call(kernel, grid=(count // per,), in_specs=whole(len(inputs))...  7.3 us
    ppermute x8, waiting for transfers between devices, across(): lax.ppermute(value, 'head', [(j, (j + subs) % size) for j in range(size)])  6.82 us
    pallas_call x1, Pallas kernels, first_step(): pl.pallas_call(kernel, in_specs=whole(7, pl.ANY), out_specs=whole(4) + wh...  3.25 us
    ppermute x8, waiting for transfers between devices, edges(): return lax.ppermute(value, CONTEXT, pairs + [(b, a) for a, b in pairs])  2.05 us
    ppermute x4, waiting for transfers between devices, around(): return lax.ppermute(value, 'head', pairs)  1.41 us
  transfers between devices with their start and end apart: 20, of which 11 were waited for; matrix products, arithmetic and copies ran while one was open for 0% of the time, Pallas kernels for 37%

profile of v9, /device:TPU:0, one launch (start us, length us, event | category | flops | bytes accessed | tf_op | source)
XLA Modules:
  0.0 59.7 jit_solution(205558513800985574)
XLA Ops:
  0.6 0.9 %shard_map.101.refs_6_ = bf16[128,512]{1,0:T(8,128)(2,1)S(1)} custom-call(bf16[128,1024]{1,0:T(8,128)(2,1)} %refs_2_.1, bf16[128,1024]{1,0:T(8,128)(2,1)} %refs_3_.1), custom_call_target="tpu_custom_call" | custom-call | tf_op jit(solution)/shard_map/pallas_call | solution.py:393
  1.6 3.0 %collective-permute-start = (bf16[128,512]{1,0:T(8,128)(2,1)S(1)}, bf16[128,512]{1,0:T(8,128)(2,1)S(1)}, u32[]{:S(2)}, u32[]{:S(2)}) collective-permute-start(bf16[128,512]{1,0:T(8,128)(2,1)S(1)} %shard_map.101.refs_6_), channel_id=1, source_target_pairs={{0,16},{8,24},{16,0},{24,8},{1,17},{9,25},{17,1},{25,9},{2,18},{10... | collective-permute-start | bytes 393224 | tf_op jit(solution)/shard_map/ppermute | solution.py:371
  4.6 3.2 %shard_map.102 = (bf16[128,8192]{1,0:T(8,128)(2,1)S(1)}, bf16[128,8192]{1,0:T(8,128)(2,1)S(1)}, bf16[128,1024]{1,0:T(8,128)(2,1)S(1)}, bf16[128,1024]{1,0:T(8,12...) custom-call(bf16[128,8192]{1,0:T(8,128)(2,1)} %refs_0_.1, ...), custom_call_target="tpu_custom_call" | custom-call | flops 805306368 | bytes 1 | tf_op jit(solution)/shard_map/pallas_call | solution.py:280
  7.9 0.2 collective-permute-done.refs_3_
  8.1 1.8 %collective-permute-start.1 = (bf16[128,512]{1,0:T(8,128)(2,1)S(1)}, bf16[128,512]{1,0:T(8,128)(2,1)S(1)}, u32[]{:S(2)}, u32[]{:S(2)}) collective-permute-start(bf16[128,512]{1,0:T(8,128)(2,1)S(1)} %shard_map.103), channel_id=1, source_target_pairs={{0,16},{8,24},{16,0},{24,8},{1,17},{9,25},{17,1},{25,9},{2,18},{10... | collective-permute-start | bytes 393224 | tf_op jit(solution)/shard_map/ppermute | solution.py:371
  9.9 1.6 %collective-permute-start.4 = (bf16[128,512]{1,0:T(8,128)(2,1)S(1)}, bf16[128,512]{1,0:T(8,128)(2,1)S(1)}, u32[]{:S(2)}, u32[]{:S(2)}) collective-permute-start(bf16[128,512]{1,0:T(8,128)(2,1)S(1)} %shard_map.106), channel_id=1, source_target_pairs={{0,1},{2,3},{4,5},{6,7},{1,0},{3,2},{5,4},{7,6},{8,9},{10,11},{12,... | collective-permute-start | bytes 393224 | tf_op jit(solution)/shard_map/ppermute | solution.py:379
  11.5 0.7 %collective-permute-start.5 = (bf16[128,512]{1,0:T(8,128)(2,1)S(1)}, bf16[128,512]{1,0:T(8,128)(2,1)S(1)}, u32[]{:S(2)}, u32[]{:S(2)}) collective-permute-start(bf16[128,512]{1,0:T(8,128)(2,1)S(1)} %shard_map.107), channel_id=1, source_target_pairs={{1,2},{3,4},{5,6},{2,1},{4,3},{6,5},{9,10},{11,12},{13,14},{10,9},... | collective-permute-start | bytes 393224 | tf_op jit(solution)/shard_map/ppermute | solution.py:379
  12.2 1.0 %collective-permute-done.1.refs_3_ = bf16[128,512]{1,0:T(8,128)(2,1)S(1)} collective-permute-done((bf16[128,512]{1,0:T(8,128)(2,1)S(1)}, bf16[128,512]{1,0:T(8,128)(2,1)S(1)}, u32[]{:S(2)}, u32[]{:S(2)}) %collective-permute-start.1) | collective-permute-done | bytes 131104 | tf_op jit(solution)/shard_map/ppermute | solution.py:371
  13.2 0.7 %collective-permute-start.3 = (bf16[128,512]{1,0:T(8,128)(2,1)S(1)}, bf16[128,512]{1,0:T(8,128)(2,1)S(1)}, u32[]{:S(2)}, u32[]{:S(2)}) collective-permute-start(bf16[128,512]{1,0:T(8,128)(2,1)S(1)} %shard_map.105), channel_id=1, source_target_pairs={{1,2},{3,4},{5,6},{2,1},{4,3},{6,5},{9,10},{11,12},{13,14},{10,9},... | collective-permute-start | bytes 393224 | tf_op jit(solution)/shard_map/ppermute | solution.py:379
  13.9 5.1 %collective-permute-start.2 = (bf16[128,512]{1,0:T(8,128)(2,1)S(1)}, bf16[128,512]{1,0:T(8,128)(2,1)S(1)}, u32[]{:S(2)}, u32[]{:S(2)}) collective-permute-start(bf16[128,512]{1,0:T(8,128)(2,1)S(1)} %shard_map.104), channel_id=1, source_target_pairs={{0,1},{2,3},{4,5},{6,7},{1,0},{3,2},{5,4},{7,6},{8,9},{10,11},{12,... | collective-permute-start | bytes 393224 | tf_op jit(solution)/shard_map/ppermute | solution.py:379
  19.0 0.0 collective-permute-done.4.refs_4_
  19.0 1.1 %collective-permute-start.7 = (bf16[128,512]{1,0:T(8,128)(2,1)S(1)}, bf16[128,512]{1,0:T(8,128)(2,1)S(1)}, u32[]{:S(2)}, u32[]{:S(2)}) collective-permute-start(bf16[128,512]{1,0:T(8,128)(2,1)S(1)} %get-tuple-element.69.refs_2_.refs_6_.refs_5_), channel_id=1, source_target_pairs={{0,16},{8,24},{16,0},{24,8},{1,17},{9,25},{17,1},{25,9},{2,18},{10... | collective-permute-start | bytes 393224 | tf_op jit(solution)/shard_map/ppermute | solution.py:371
  20.1 1.7 %shard_map.112.refs_6_ = f32[4,8,1024]{2,1,0:T(8,128)S(1)} custom-call(bf16[128,8192]{1,0:T(8,128)(2,1)S(1)} %get-tuple-element.62.refs_0_, bf16[128,8192]{1,0:T(8,128)(2,1)S(1)} %get-tuple-element.63.refs_1_, bf16[128,1024]{1,0:T(8,128)(2,1)S(1)} %get-tuple-element.66.refs_1_.refs_2_.refs_6_, ...), custom_call_target="tpu_custom_call" | custom-call | flops 536870912 | bytes 1 | tf_op jit(solution)/shard_map/pallas_call | solution.py:259
  21.9 0.0 collective-permute-done.3.refs_1_
  21.9 1.0 %collective-permute-done.2.refs_4_ = bf16[128,512]{1,0:T(8,128)(2,1)S(1)} collective-permute-done((bf16[128,512]{1,0:T(8,128)(2,1)S(1)}, bf16[128,512]{1,0:T(8,128)(2,1)S(1)}, u32[]{:S(2)}, u32[]{:S(2)}) %collective-permute-start.2) | collective-permute-done | bytes 131104 | tf_op jit(solution)/shard_map/ppermute | solution.py:379
  23.0 1.1 %collective-permute-done.7.refs_4_ = bf16[128,512]{1,0:T(8,128)(2,1)S(1)} collective-permute-done((bf16[128,512]{1,0:T(8,128)(2,1)S(1)}, bf16[128,512]{1,0:T(8,128)(2,1)S(1)}, u32[]{:S(2)}, u32[]{:S(2)}) %collective-permute-start.7) | collective-permute-done | bytes 131104 | tf_op jit(solution)/shard_map/ppermute | solution.py:371
  24.1 0.1 collective-permute-start.8
  24.2 1.1 %collective-permute-start.6 = (bf16[128,512]{1,0:T(8,128)(2,1)S(1)}, bf16[128,512]{1,0:T(8,128)(2,1)S(1)}, u32[]{:S(2)}, u32[]{:S(2)}) collective-permute-start(bf16[128,512]{1,0:T(8,128)(2,1)S(1)} %get-tuple-element.71.refs_5_), channel_id=1, source_target_pairs={{0,16},{8,24},{16,0},{24,8},{1,17},{9,25},{17,1},{25,9},{2,18},{10... | collective-permute-start | bytes 393224 | tf_op jit(solution)/shard_map/ppermute | solution.py:371
  25.3 0.4 collective-permute-done.8.refs_5_
  25.7 4.4 %shard_map.114 = (f32[4,8,128]{2,1,0:T(8,128)S(1)}, f32[4,8,1024]{2,1,0:T(8,128)S(1)}, bf16[4,256,1024]{2,1,0:T(8,128)(2,1)S(1)}, bf16[4,256,1024]{2,1,0:T(8,128...) custom-call(bf16[128,8192]{1,0:T(8,128)(2,1)S(1)} %get-tuple-element, ...), custom_call_target="tpu_custom_call" | custom-call | flops 2147483648 | bytes 1 | tf_op jit(solution)/shard_map/pallas_call | solution.py:259
  30.2 0.2 collective-permute-start.10
  30.4 0.4 collective-permute-start.9
  30.9 0.9 %collective-permute-done.10.refs_3_ = bf16[128,1024]{1,0:T(8,128)(2,1)S(1)} collective-permute-done((bf16[128,1024]{1,0:T(8,128)(2,1)S(1)}, bf16[128,1024]{1,0:T(8,128)(2,1)S(1)}, u32[]{:S(2)}, u32[]{:S(2)}) %collective-permute-start.10) | collective-permute-done | bytes 262176 | tf_op jit(solution)/shard_map/ppermute | solution.py:375
  31.8 0.1 shard_map.117
  31.9 1.1 %collective-permute-start.11 = (bf16[128,512]{1,0:T(8,128)(2,1)S(1)}, bf16[128,512]{1,0:T(8,128)(2,1)S(1)}, u32[]{:S(2)}, u32[]{:S(2)}) collective-permute-start(bf16[128,512]{1,0:T(8,128)(2,1)S(1)} %get-tuple-element.84.refs_7_), channel_id=1, source_target_pairs={{0,16},{8,24},{16,0},{24,8},{1,17},{9,25},{17,1},{25,9},{2,18},{10... | collective-permute-start | bytes 393224 | tf_op jit(solution)/shard_map/ppermute | solution.py:371
  33.0 4.4 %shard_map.118 = (f32[4,8,128]{2,1,0:T(8,128)S(1)}, f32[4,8,1024]{2,1,0:T(8,128)S(1)}, bf16[4,256,1024]{2,1,0:T(8,128)(2,1)S(1)}, bf16[4,256,1024]{2,1,0:T(8,128...) custom-call(bf16[128,8192]{1,0:T(8,128)(2,1)S(1)} %get-tuple-element, ...), custom_call_target="tpu_custom_call" | custom-call | flops 2147483648 | bytes 1 | tf_op jit(solution)/shard_map/pallas_call | solution.py:259
  37.4 0.1 collective-permute-done.11.refs_2_
  37.6 0.1 collective-permute-start.13
  37.6 1.5 %collective-permute-start.12 = (bf16[128,512]{1,0:T(8,128)(2,1)S(1)}, bf16[128,512]{1,0:T(8,128)(2,1)S(1)}, u32[]{:S(2)}, u32[]{:S(2)}) collective-permute-start(bf16[128,512]{1,0:T(8,128)(2,1)S(1)} %shard_map.119.refs_5_), channel_id=1, source_target_pairs={{0,1},{2,3},{4,5},{6,7},{1,0},{3,2},{5,4},{7,6},{8,9},{10,11},{12,... | collective-permute-start | bytes 393224 | tf_op jit(solution)/shard_map/ppermute | solution.py:379
  39.2 0.1 collective-permute-done.13.refs_5_
  39.2 0.3 shard_map.121
  39.5 1.1 %collective-permute-start.15 = (bf16[144,512]{1,0:T(8,128)(2,1)S(1)}, bf16[144,512]{1,0:T(8,128)(2,1)S(1)}, u32[]{:S(2)}, u32[]{:S(2)}) collective-permute-start(bf16[144,512]{1,0:T(8,128)(2,1)S(1)} %get-tuple-element.97.refs_3_), channel_id=1, source_target_pairs={{0,16},{8,24},{16,0},{24,8},{1,17},{9,25},{17,1},{25,9},{2,18},{10... | collective-permute-start | bytes 442376 | tf_op jit(solution)/shard_map/ppermute | solution.py:371
  40.6 0.7 %collective-permute-start.14 = (bf16[128,512]{1,0:T(8,128)(2,1)S(1)}, bf16[128,512]{1,0:T(8,128)(2,1)S(1)}, u32[]{:S(2)}, u32[]{:S(2)}) collective-permute-start(bf16[128,512]{1,0:T(8,128)(2,1)S(1)} %shard_map.122), channel_id=1, source_target_pairs={{1,2},{3,4},{5,6},{2,1},{4,3},{6,5},{9,10},{11,12},{13,14},{10,9},... | collective-permute-start | bytes 393224 | tf_op jit(solution)/shard_map/ppermute | solution.py:379
  41.3 4.2 %collective-permute-done.15.refs_2_.refs_1_ = bf16[144,512]{1,0:T(8,128)(2,1)S(1)} collective-permute-done((bf16[144,512]{1,0:T(8,128)(2,1)S(1)}, bf16[144,512]{1,0:T(8,128)(2,1)S(1)}, u32[]{:S(2)}, u32[]{:S(2)}) %collective-permute-start.15) | collective-permute-done | bytes 147488 | tf_op jit(solution)/shard_map/ppermute | solution.py:371
  45.5 1.5 %collective-permute-start.16 = (bf16[128,512]{1,0:T(8,128)(2,1)S(1)}, bf16[128,512]{1,0:T(8,128)(2,1)S(1)}, u32[]{:S(2)}, u32[]{:S(2)}) collective-permute-start(bf16[128,512]{1,0:T(8,128)(2,1)S(1)} %shard_map.123.refs_5_), channel_id=1, source_target_pairs={{0,1},{2,3},{4,5},{6,7},{1,0},{3,2},{5,4},{7,6},{8,9},{10,11},{12,... | collective-permute-start | bytes 393224 | tf_op jit(solution)/shard_map/ppermute | solution.py:379
  47.0 0.7 %collective-permute-start.17 = (bf16[128,512]{1,0:T(8,128)(2,1)S(1)}, bf16[128,512]{1,0:T(8,128)(2,1)S(1)}, u32[]{:S(2)}, u32[]{:S(2)}) collective-permute-start(bf16[128,512]{1,0:T(8,128)(2,1)S(1)} %shard_map.128), channel_id=1, source_target_pairs={{1,2},{3,4},{5,6},{2,1},{4,3},{6,5},{9,10},{11,12},{13,14},{10,9},... | collective-permute-start | bytes 393224 | tf_op jit(solution)/shard_map/ppermute | solution.py:379
  47.7 0.0 collective-permute-done.12.refs_3_
  47.7 0.0 collective-permute-done.14.refs_4_
  47.7 0.1 shard_map.124
  47.8 1.1 %collective-permute-start.18 = (bf16[128,512]{1,0:T(8,128)(2,1)S(1)}, bf16[128,512]{1,0:T(8,128)(2,1)S(1)}, u32[]{:S(2)}, u32[]{:S(2)}) collective-permute-start(bf16[128,512]{1,0:T(8,128)(2,1)S(1)} %get-tuple-element.99.refs_11_), channel_id=1, source_target_pairs={{0,16},{8,24},{16,0},{24,8},{1,17},{9,25},{17,1},{25,9},{2,18},{10... | collective-permute-start | bytes 393224 | tf_op jit(solution)/shard_map/ppermute | solution.py:371
  48.9 3.6 %shard_map.125 = (bf16[128,8192]{1,0:T(8,128)(2,1)}, bf16[128,8192]{1,0:T(8,128)(2,1)}, f32[128,512]{1,0:T(8,128)S(1)}, f32[128,512]{1,0:T(8,128)S(1)}) custom-call(bf16[128,8192]{1,0:T(8,128)(2,1)S(1)} %get-tuple-element.62.refs_0_, bf16[128,8192]{1,0:T(8,128)(2,1)S(1)} %get-tuple-element.63.refs_1_, f32[384,128]{1,0:T(8,128)S(1)} %get-tuple-element.64.refs_4_.refs_2_, ...), custom_call_target="tpu_custom_call" | custom-call | flops 1342177280 | bytes 1 | tf_op jit(solution)/shard_map/pallas_call | solution.py:337
  52.5 1.0 %collective-permute-done.16.refs_1_ = bf16[128,512]{1,0:T(8,128)(2,1)S(1)} collective-permute-done((bf16[128,512]{1,0:T(8,128)(2,1)S(1)}, bf16[128,512]{1,0:T(8,128)(2,1)S(1)}, u32[]{:S(2)}, u32[]{:S(2)}) %collective-permute-start.16) | collective-permute-done | bytes 131104 | tf_op jit(solution)/shard_map/ppermute | solution.py:379
  53.6 0.1 shard_map.129
  53.6 1.1 %collective-permute-start.19 = (bf16[128,512]{1,0:T(8,128)(2,1)S(1)}, bf16[128,512]{1,0:T(8,128)(2,1)S(1)}, u32[]{:S(2)}, u32[]{:S(2)}) collective-permute-start(bf16[128,512]{1,0:T(8,128)(2,1)S(1)} %get-tuple-element.103.refs_13_), channel_id=1, source_target_pairs={{0,16},{8,24},{16,0},{24,8},{1,17},{9,25},{17,1},{25,9},{2,18},{10... | collective-permute-start | bytes 393224 | tf_op jit(solution)/shard_map/ppermute | solution.py:371
  54.8 3.7 %shard_map.130 = (bf16[128,8192]{1,0:T(8,128)(2,1)}, bf16[128,8192]{1,0:T(8,128)(2,1)}, f32[128,512]{1,0:T(8,128)S(1)}, f32[128,512]{1,0:T(8,128)S(1)}) custom-call(bf16[128,8192]{1,0:T(8,128)(2,1)S(1)} %get-tuple-element.62.refs_0_, bf16[128,8192]{1,0:T(8,128)(2,1)S(1)} %get-tuple-element.63.refs_1_, ...), custom_call_target="tpu_custom_call", output_to_operand_aliasing={{0}: (11, {}), {1}: (12, {})} | custom-call | flops 1342177280 | bytes 1 | tf_op jit(solution)/shard_map/pallas_call | solution.py:337
  58.4 0.0 collective-permute-done.18.refs_5_
  58.4 0.3 collective-permute-done.19.refs_11_
  58.7 1.1 %shard_map.131 = (bf16[128,1024]{1,0:T(8,128)(2,1)}, bf16[128,1024]{1,0:T(8,128)(2,1)}, f32[16,512]{1,0:T(8,128)}) custom-call(s32[6]{0:T(128)S(4)} %get-tuple-element.65.refs_0_.flag, f32[2,16,128]{2,1,0:T(8,128)S(1)} %get-tuple-element.105.refs_0_, bf16[144,512]{1,0:T(8,128)(2,1)S(1)} %collective-permute-done.15.refs_2_.refs_1_, ...), custom_call_target="tpu_custom_call" | custom-call | tf_op jit(solution)/shard_map/pallas_call | solution.py:589
  (23 shorter events, 0.4 us)
Async XLA Ops:
  1.6 6.5 %collective-permute-start = (bf16[128,512]{1,0:T(8,128)(2,1)S(1)}, bf16[128,512]{1,0:T(8,128)(2,1)S(1)}, u32[]{:S(2)}, u32[]{:S(2)}) collective-permute-start(bf16[128,512]{1,0:T(8,128)(2,1)S(1)} %shard_map.101.refs_6_), channel_id=1, source_target_pairs={{0,16},{8,24},{16,0},{24,8},{1,17},{9,25},{17,1},{25,9},{2,18},{10... | collective-permute-start | bytes 393224 | tf_op jit(solution)/shard_map/ppermute | solution.py:371
  8.1 5.0 %collective-permute-start.1 = (bf16[128,512]{1,0:T(8,128)(2,1)S(1)}, bf16[128,512]{1,0:T(8,128)(2,1)S(1)}, u32[]{:S(2)}, u32[]{:S(2)}) collective-permute-start(bf16[128,512]{1,0:T(8,128)(2,1)S(1)} %shard_map.103), channel_id=1, source_target_pairs={{0,16},{8,24},{16,0},{24,8},{1,17},{9,25},{17,1},{25,9},{2,18},{10... | collective-permute-start | bytes 393224 | tf_op jit(solution)/shard_map/ppermute | solution.py:371
  9.9 9.0 %collective-permute-start.4 = (bf16[128,512]{1,0:T(8,128)(2,1)S(1)}, bf16[128,512]{1,0:T(8,128)(2,1)S(1)}, u32[]{:S(2)}, u32[]{:S(2)}) collective-permute-start(bf16[128,512]{1,0:T(8,128)(2,1)S(1)} %shard_map.106), channel_id=1, source_target_pairs={{0,1},{2,3},{4,5},{6,7},{1,0},{3,2},{5,4},{7,6},{8,9},{10,11},{12,... | collective-permute-start | bytes 393224 | tf_op jit(solution)/shard_map/ppermute | solution.py:379
  11.5 7.5 %collective-permute-start.5 = (bf16[128,512]{1,0:T(8,128)(2,1)S(1)}, bf16[128,512]{1,0:T(8,128)(2,1)S(1)}, u32[]{:S(2)}, u32[]{:S(2)}) collective-permute-start(bf16[128,512]{1,0:T(8,128)(2,1)S(1)} %shard_map.107), channel_id=1, source_target_pairs={{1,2},{3,4},{5,6},{2,1},{4,3},{6,5},{9,10},{11,12},{13,14},{10,9},... | collective-permute-start | bytes 393224 | tf_op jit(solution)/shard_map/ppermute | solution.py:379
  13.2 8.7 %collective-permute-start.3 = (bf16[128,512]{1,0:T(8,128)(2,1)S(1)}, bf16[128,512]{1,0:T(8,128)(2,1)S(1)}, u32[]{:S(2)}, u32[]{:S(2)}) collective-permute-start(bf16[128,512]{1,0:T(8,128)(2,1)S(1)} %shard_map.105), channel_id=1, source_target_pairs={{1,2},{3,4},{5,6},{2,1},{4,3},{6,5},{9,10},{11,12},{13,14},{10,9},... | collective-permute-start | bytes 393224 | tf_op jit(solution)/shard_map/ppermute | solution.py:379
  13.9 9.0 %collective-permute-start.2 = (bf16[128,512]{1,0:T(8,128)(2,1)S(1)}, bf16[128,512]{1,0:T(8,128)(2,1)S(1)}, u32[]{:S(2)}, u32[]{:S(2)}) collective-permute-start(bf16[128,512]{1,0:T(8,128)(2,1)S(1)} %shard_map.104), channel_id=1, source_target_pairs={{0,1},{2,3},{4,5},{6,7},{1,0},{3,2},{5,4},{7,6},{8,9},{10,11},{12,... | collective-permute-start | bytes 393224 | tf_op jit(solution)/shard_map/ppermute | solution.py:379
  19.0 5.0 %collective-permute-start.7 = (bf16[128,512]{1,0:T(8,128)(2,1)S(1)}, bf16[128,512]{1,0:T(8,128)(2,1)S(1)}, u32[]{:S(2)}, u32[]{:S(2)}) collective-permute-start(bf16[128,512]{1,0:T(8,128)(2,1)S(1)} %get-tuple-element.69.refs_2_.refs_6_.refs_5_), channel_id=1, source_target_pairs={{0,16},{8,24},{16,0},{24,8},{1,17},{9,25},{17,1},{25,9},{2,18},{10... | collective-permute-start | bytes 393224 | tf_op jit(solution)/shard_map/ppermute | solution.py:371
  24.1 1.6 %collective-permute-start.8 = (bf16[128,1024]{1,0:T(8,128)(2,1)S(1)}, bf16[128,1024]{1,0:T(8,128)(2,1)S(1)}, u32[]{:S(2)}, u32[]{:S(2)}) collective-permute-start(bf16[128,1024]{1,0:T(8,128)(2,1)S(1)} %get-tuple-element.75), channel_id=1, source_target_pairs={{0,8},{8,0},{16,24},{24,16},{1,9},{9,1},{17,25},{25,17},{2,10},{10... | collective-permute-start | bytes 786440 | tf_op jit(solution)/shard_map/ppermute | solution.py:375
  24.2 6.2 %collective-permute-start.6 = (bf16[128,512]{1,0:T(8,128)(2,1)S(1)}, bf16[128,512]{1,0:T(8,128)(2,1)S(1)}, u32[]{:S(2)}, u32[]{:S(2)}) collective-permute-start(bf16[128,512]{1,0:T(8,128)(2,1)S(1)} %get-tuple-element.71.refs_5_), channel_id=1, source_target_pairs={{0,16},{8,24},{16,0},{24,8},{1,17},{9,25},{17,1},{25,9},{2,18},{10... | collective-permute-start | bytes 393224 | tf_op jit(solution)/shard_map/ppermute | solution.py:371
  30.2 1.6 %collective-permute-start.10 = (bf16[128,1024]{1,0:T(8,128)(2,1)S(1)}, bf16[128,1024]{1,0:T(8,128)(2,1)S(1)}, u32[]{:S(2)}, u32[]{:S(2)}) collective-permute-start(bf16[128,1024]{1,0:T(8,128)(2,1)S(1)} %shard_map.116), channel_id=1, source_target_pairs={{0,8},{8,0},{16,24},{24,16},{1,9},{9,1},{17,25},{25,17},{2,10},{10... | collective-permute-start | bytes 786440 | tf_op jit(solution)/shard_map/ppermute | solution.py:375
  30.4 2.5 %collective-permute-start.9 = (bf16[128,1024]{1,0:T(8,128)(2,1)S(1)}, bf16[128,1024]{1,0:T(8,128)(2,1)S(1)}, u32[]{:S(2)}, u32[]{:S(2)}) collective-permute-start(bf16[128,1024]{1,0:T(8,128)(2,1)S(1)} %get-tuple-element.79), channel_id=1, source_target_pairs={{0,8},{8,0},{16,24},{24,16},{1,9},{9,1},{17,25},{25,17},{2,10},{10... | collective-permute-start | bytes 786440 | tf_op jit(solution)/shard_map/ppermute | solution.py:375
  31.9 5.6 %collective-permute-start.11 = (bf16[128,512]{1,0:T(8,128)(2,1)S(1)}, bf16[128,512]{1,0:T(8,128)(2,1)S(1)}, u32[]{:S(2)}, u32[]{:S(2)}) collective-permute-start(bf16[128,512]{1,0:T(8,128)(2,1)S(1)} %get-tuple-element.84.refs_7_), channel_id=1, source_target_pairs={{0,16},{8,24},{16,0},{24,8},{1,17},{9,25},{17,1},{25,9},{2,18},{10... | collective-permute-start | bytes 393224 | tf_op jit(solution)/shard_map/ppermute | solution.py:371
  37.6 1.6 %collective-permute-start.13 = (bf16[144,1024]{1,0:T(8,128)(2,1)S(1)}, bf16[144,1024]{1,0:T(8,128)(2,1)S(1)}, u32[]{:S(2)}, u32[]{:S(2)}) collective-permute-start(bf16[144,1024]{1,0:T(8,128)(2,1)S(1)} %shard_map.120), channel_id=1, source_target_pairs={{0,8},{8,0},{16,24},{24,16},{1,9},{9,1},{17,25},{25,17},{2,10},{10... | collective-permute-start | bytes 884744 | tf_op jit(solution)/shard_map/ppermute | solution.py:375
  37.6 10.1 %collective-permute-start.12 = (bf16[128,512]{1,0:T(8,128)(2,1)S(1)}, bf16[128,512]{1,0:T(8,128)(2,1)S(1)}, u32[]{:S(2)}, u32[]{:S(2)}) collective-permute-start(bf16[128,512]{1,0:T(8,128)(2,1)S(1)} %shard_map.119.refs_5_), channel_id=1, source_target_pairs={{0,1},{2,3},{4,5},{6,7},{1,0},{3,2},{5,4},{7,6},{8,9},{10,11},{12,... | collective-permute-start | bytes 393224 | tf_op jit(solution)/shard_map/ppermute | solution.py:379
  39.5 6.0 %collective-permute-start.15 = (bf16[144,512]{1,0:T(8,128)(2,1)S(1)}, bf16[144,512]{1,0:T(8,128)(2,1)S(1)}, u32[]{:S(2)}, u32[]{:S(2)}) collective-permute-start(bf16[144,512]{1,0:T(8,128)(2,1)S(1)} %get-tuple-element.97.refs_3_), channel_id=1, source_target_pairs={{0,16},{8,24},{16,0},{24,8},{1,17},{9,25},{17,1},{25,9},{2,18},{10... | collective-permute-start | bytes 442376 | tf_op jit(solution)/shard_map/ppermute | solution.py:371
  40.6 7.1 %collective-permute-start.14 = (bf16[128,512]{1,0:T(8,128)(2,1)S(1)}, bf16[128,512]{1,0:T(8,128)(2,1)S(1)}, u32[]{:S(2)}, u32[]{:S(2)}) collective-permute-start(bf16[128,512]{1,0:T(8,128)(2,1)S(1)} %shard_map.122), channel_id=1, source_target_pairs={{1,2},{3,4},{5,6},{2,1},{4,3},{6,5},{9,10},{11,12},{13,14},{10,9},... | collective-permute-start | bytes 393224 | tf_op jit(solution)/shard_map/ppermute | solution.py:379
  45.5 8.0 %collective-permute-start.16 = (bf16[128,512]{1,0:T(8,128)(2,1)S(1)}, bf16[128,512]{1,0:T(8,128)(2,1)S(1)}, u32[]{:S(2)}, u32[]{:S(2)}) collective-permute-start(bf16[128,512]{1,0:T(8,128)(2,1)S(1)} %shard_map.123.refs_5_), channel_id=1, source_target_pairs={{0,1},{2,3},{4,5},{6,7},{1,0},{3,2},{5,4},{7,6},{8,9},{10,11},{12,... | collective-permute-start | bytes 393224 | tf_op jit(solution)/shard_map/ppermute | solution.py:379
  47.0 6.5 %collective-permute-start.17 = (bf16[128,512]{1,0:T(8,128)(2,1)S(1)}, bf16[128,512]{1,0:T(8,128)(2,1)S(1)}, u32[]{:S(2)}, u32[]{:S(2)}) collective-permute-start(bf16[128,512]{1,0:T(8,128)(2,1)S(1)} %shard_map.128), channel_id=1, source_target_pairs={{1,2},{3,4},{5,6},{2,1},{4,3},{6,5},{9,10},{11,12},{13,14},{10,9},... | collective-permute-start | bytes 393224 | tf_op jit(solution)/shard_map/ppermute | solution.py:379
  47.8 10.6 %collective-permute-start.18 = (bf16[128,512]{1,0:T(8,128)(2,1)S(1)}, bf16[128,512]{1,0:T(8,128)(2,1)S(1)}, u32[]{:S(2)}, u32[]{:S(2)}) collective-permute-start(bf16[128,512]{1,0:T(8,128)(2,1)S(1)} %get-tuple-element.99.refs_11_), channel_id=1, source_target_pairs={{0,16},{8,24},{16,0},{24,8},{1,17},{9,25},{17,1},{25,9},{2,18},{10... | collective-permute-start | bytes 393224 | tf_op jit(solution)/shard_map/ppermute | solution.py:371
  53.6 5.0 %collective-permute-start.19 = (bf16[128,512]{1,0:T(8,128)(2,1)S(1)}, bf16[128,512]{1,0:T(8,128)(2,1)S(1)}, u32[]{:S(2)}, u32[]{:S(2)}) collective-permute-start(bf16[128,512]{1,0:T(8,128)(2,1)S(1)} %get-tuple-element.103.refs_13_), channel_id=1, source_target_pairs={{0,16},{8,24},{16,0},{24,8},{1,17},{9,25},{17,1},{25,9},{2,18},{10... | collective-permute-start | bytes 393224 | tf_op jit(solution)/shard_map/ppermute | solution.py:371

commit v10 on v9

--- a/solution.py
+++ b/solution.py
@@ -18,10 +18,10 @@
 CHUNKS = 2
 UNROLL = 4
 EXTRA = 16
-BEHIND = (((0, 4, 2),), ((0, 4, 2),))
+BEHIND = (((0, 4, 4),), ((0, 4, 2),))
 LOG2E = math.log2(math.e)
 VMEM_SMALL = 8 * 2**20
-VMEM_LARGE = 16 * 2**20
+VMEM_LARGE = 24 * 2**20
 NT = (((1,), (1,)), ((), ()))
 NN = (((1,), (0,)), ((), ()))
 
@@ -114,7 +114,7 @@
         row_sums(g, g, q_ref, do_ref, k_ref, v_ref, bias_ref[window - rows :, :], stat_ref)
         return 0
 
-    lax.fori_loop(0, count, step, 0)
+    lax.fori_loop(0, count, step, 0, unroll=2)
     for g in range(count, heads):
         for copy in wide(g):
             copy.wait()
@@ -127,7 +127,7 @@
         row_sums(start + at, at, q_ref, do_ref, k_ref, v_ref, bias_ref[last:, :], stat_ref)
         return 0
 
-    lax.fori_loop(0, count, step, 0)
+    lax.fori_loop(0, count, step, 0, unroll=2)
 
 
 def earlier_kernel(start, count, near, q_ref, do_ref, bias_ref, first_k, first_v, *refs):

time: 60.7 us -> 60.7 us (level)
  no operation moved by 1% of the time
where the time goes in v10:
time: 60.7 us; the launch traced here: 59.7 us
  starting transfers between devices  24.4 us (40%)
  Pallas kernels  23.9 us (39%)
  waiting for transfers between devices  10.5 us (17%)
  between operations  0.92 us (2%)
    ppermute x8, starting transfers between devices, edges(): return lax.ppermute(value, CONTEXT, pairs + [(b, a) for a, b in pairs])  12.3 us
    ppermute x8, starting transfers between devices, across(): lax.ppermute(value, 'head', [(j, (j + subs) % size) for j in range(size)])  11.3 us
    pallas_call x3, Pallas kernels, large(): pl.pallas_call(body, in_specs=whole(len(inputs)) + whole(len(behind), pl....  10.4 us
    pallas_call x2, Pallas kernels, the_rest(): pl.pallas_call(kernel, grid=(count // per,), in_specs=whole(len(inputs))...  7.32 us
    ppermute x8, waiting for transfers between devices, across(): lax.ppermute(value, 'head', [(j, (j + subs) % size) for j in range(size)])  6.83 us
    pallas_call x1, Pallas kernels, first_step(): pl.pallas_call(kernel, in_specs=whole(7, pl.ANY), out_specs=whole(4) + wh...  3.25 us
    ppermute x8, waiting for transfers between devices, edges(): return lax.ppermute(value, CONTEXT, pairs + [(b, a) for a, b in pairs])  2.26 us
    ppermute x4, waiting for transfers between devices, around(): return lax.ppermute(value, 'head', pairs)  1.42 us
  transfers between devices with their start and end apart: 20, of which 11 were waited for; matrix products, arithmetic and copies ran while one was open for 0% of the time, Pallas kernels for 37%

profile of v10, /device:TPU:0, one launch (start us, length us, event | category | flops | bytes accessed | tf_op | source)
XLA Modules:
  0.0 59.7 jit_solution(10534480494409865306)
XLA Ops:
  0.6 0.9 %shard_map.101.refs_6_ = bf16[128,512]{1,0:T(8,128)(2,1)S(1)} custom-call(bf16[128,1024]{1,0:T(8,128)(2,1)} %refs_2_.1, bf16[128,1024]{1,0:T(8,128)(2,1)} %refs_3_.1), custom_call_target="tpu_custom_call" | custom-call | tf_op jit(solution)/shard_map/pallas_call | solution.py:393
  1.6 3.0 %collective-permute-start = (bf16[128,512]{1,0:T(8,128)(2,1)S(1)}, bf16[128,512]{1,0:T(8,128)(2,1)S(1)}, u32[]{:S(2)}, u32[]{:S(2)}) collective-permute-start(bf16[128,512]{1,0:T(8,128)(2,1)S(1)} %shard_map.101.refs_6_), channel_id=1, source_target_pairs={{0,16},{8,24},{16,0},{24,8},{1,17},{9,25},{17,1},{25,9},{2,18},{10... | collective-permute-start | bytes 393224 | tf_op jit(solution)/shard_map/ppermute | solution.py:371
  4.6 3.3 %shard_map.102 = (bf16[128,8192]{1,0:T(8,128)(2,1)S(1)}, bf16[128,8192]{1,0:T(8,128)(2,1)S(1)}, bf16[128,1024]{1,0:T(8,128)(2,1)S(1)}, bf16[128,1024]{1,0:T(8,12...) custom-call(bf16[128,8192]{1,0:T(8,128)(2,1)} %refs_0_.1, ...), custom_call_target="tpu_custom_call" | custom-call | flops 805306368 | bytes 1 | tf_op jit(solution)/shard_map/pallas_call | solution.py:280
  7.9 0.2 collective-permute-done.refs_3_
  8.1 1.8 %collective-permute-start.1 = (bf16[128,512]{1,0:T(8,128)(2,1)S(1)}, bf16[128,512]{1,0:T(8,128)(2,1)S(1)}, u32[]{:S(2)}, u32[]{:S(2)}) collective-permute-start(bf16[128,512]{1,0:T(8,128)(2,1)S(1)} %shard_map.103), channel_id=1, source_target_pairs={{0,16},{8,24},{16,0},{24,8},{1,17},{9,25},{17,1},{25,9},{2,18},{10... | collective-permute-start | bytes 393224 | tf_op jit(solution)/shard_map/ppermute | solution.py:371
  9.9 1.6 %collective-permute-start.4 = (bf16[128,512]{1,0:T(8,128)(2,1)S(1)}, bf16[128,512]{1,0:T(8,128)(2,1)S(1)}, u32[]{:S(2)}, u32[]{:S(2)}) collective-permute-start(bf16[128,512]{1,0:T(8,128)(2,1)S(1)} %shard_map.106), channel_id=1, source_target_pairs={{0,1},{2,3},{4,5},{6,7},{1,0},{3,2},{5,4},{7,6},{8,9},{10,11},{12,... | collective-permute-start | bytes 393224 | tf_op jit(solution)/shard_map/ppermute | solution.py:379
  11.5 0.7 %collective-permute-start.5 = (bf16[128,512]{1,0:T(8,128)(2,1)S(1)}, bf16[128,512]{1,0:T(8,128)(2,1)S(1)}, u32[]{:S(2)}, u32[]{:S(2)}) collective-permute-start(bf16[128,512]{1,0:T(8,128)(2,1)S(1)} %shard_map.107), channel_id=1, source_target_pairs={{1,2},{3,4},{5,6},{2,1},{4,3},{6,5},{9,10},{11,12},{13,14},{10,9},... | collective-permute-start | bytes 393224 | tf_op jit(solution)/shard_map/ppermute | solution.py:379
  12.2 1.0 %collective-permute-done.1.refs_3_ = bf16[128,512]{1,0:T(8,128)(2,1)S(1)} collective-permute-done((bf16[128,512]{1,0:T(8,128)(2,1)S(1)}, bf16[128,512]{1,0:T(8,128)(2,1)S(1)}, u32[]{:S(2)}, u32[]{:S(2)}) %collective-permute-start.1) | collective-permute-done | bytes 131104 | tf_op jit(solution)/shard_map/ppermute | solution.py:371
  13.2 0.7 %collective-permute-start.3 = (bf16[128,512]{1,0:T(8,128)(2,1)S(1)}, bf16[128,512]{1,0:T(8,128)(2,1)S(1)}, u32[]{:S(2)}, u32[]{:S(2)}) collective-permute-start(bf16[128,512]{1,0:T(8,128)(2,1)S(1)} %shard_map.105), channel_id=1, source_target_pairs={{1,2},{3,4},{5,6},{2,1},{4,3},{6,5},{9,10},{11,12},{13,14},{10,9},... | collective-permute-start | bytes 393224 | tf_op jit(solution)/shard_map/ppermute | solution.py:379
  13.9 5.1 %collective-permute-start.2 = (bf16[128,512]{1,0:T(8,128)(2,1)S(1)}, bf16[128,512]{1,0:T(8,128)(2,1)S(1)}, u32[]{:S(2)}, u32[]{:S(2)}) collective-permute-start(bf16[128,512]{1,0:T(8,128)(2,1)S(1)} %shard_map.104), channel_id=1, source_target_pairs={{0,1},{2,3},{4,5},{6,7},{1,0},{3,2},{5,4},{7,6},{8,9},{10,11},{12,... | collective-permute-start | bytes 393224 | tf_op jit(solution)/shard_map/ppermute | solution.py:379
  19.0 0.0 collective-permute-done.4.refs_4_
  19.0 0.0 collective-permute-done.5.refs_5_
  19.0 1.1 %collective-permute-start.7 = (bf16[128,512]{1,0:T(8,128)(2,1)S(1)}, bf16[128,512]{1,0:T(8,128)(2,1)S(1)}, u32[]{:S(2)}, u32[]{:S(2)}) collective-permute-start(bf16[128,512]{1,0:T(8,128)(2,1)S(1)} %get-tuple-element.69.refs_2_.refs_6_.refs_5_), channel_id=1, source_target_pairs={{0,16},{8,24},{16,0},{24,8},{1,17},{9,25},{17,1},{25,9},{2,18},{10... | collective-permute-start | bytes 393224 | tf_op jit(solution)/shard_map/ppermute | solution.py:371
  20.1 1.5 %shard_map.112.refs_6_ = f32[4,8,1024]{2,1,0:T(8,128)S(1)} custom-call(bf16[128,8192]{1,0:T(8,128)(2,1)S(1)} %get-tuple-element.62.refs_0_, bf16[128,8192]{1,0:T(8,128)(2,1)S(1)} %get-tuple-element.63.refs_1_, bf16[128,1024]{1,0:T(8,128)(2,1)S(1)} %get-tuple-element.66.refs_1_.refs_2_.refs_6_, ...), custom_call_target="tpu_custom_call" | custom-call | flops 536870912 | bytes 1 | tf_op jit(solution)/shard_map/pallas_call | solution.py:259
  21.7 1.3 %collective-permute-done.2.refs_4_ = bf16[128,512]{1,0:T(8,128)(2,1)S(1)} collective-permute-done((bf16[128,512]{1,0:T(8,128)(2,1)S(1)}, bf16[128,512]{1,0:T(8,128)(2,1)S(1)}, u32[]{:S(2)}, u32[]{:S(2)}) %collective-permute-start.2) | collective-permute-done | bytes 131104 | tf_op jit(solution)/shard_map/ppermute | solution.py:379
  23.0 1.1 %collective-permute-done.7.refs_4_ = bf16[128,512]{1,0:T(8,128)(2,1)S(1)} collective-permute-done((bf16[128,512]{1,0:T(8,128)(2,1)S(1)}, bf16[128,512]{1,0:T(8,128)(2,1)S(1)}, u32[]{:S(2)}, u32[]{:S(2)}) %collective-permute-start.7) | collective-permute-done | bytes 131104 | tf_op jit(solution)/shard_map/ppermute | solution.py:371
  24.1 0.1 collective-permute-start.8
  24.2 1.1 %collective-permute-start.6 = (bf16[128,512]{1,0:T(8,128)(2,1)S(1)}, bf16[128,512]{1,0:T(8,128)(2,1)S(1)}, u32[]{:S(2)}, u32[]{:S(2)}) collective-permute-start(bf16[128,512]{1,0:T(8,128)(2,1)S(1)} %get-tuple-element.71.refs_5_), channel_id=1, source_target_pairs={{0,16},{8,24},{16,0},{24,8},{1,17},{9,25},{17,1},{25,9},{2,18},{10... | collective-permute-start | bytes 393224 | tf_op jit(solution)/shard_map/ppermute | solution.py:371
  25.3 0.5 collective-permute-done.8.refs_5_
  25.7 4.4 %shard_map.114 = (f32[4,8,128]{2,1,0:T(8,128)S(1)}, f32[4,8,1024]{2,1,0:T(8,128)S(1)}, bf16[4,256,1024]{2,1,0:T(8,128)(2,1)S(1)}, bf16[4,256,1024]{2,1,0:T(8,128...) custom-call(bf16[128,8192]{1,0:T(8,128)(2,1)S(1)} %get-tuple-element, ...), custom_call_target="tpu_custom_call" | custom-call | flops 2147483648 | bytes 1 | tf_op jit(solution)/shard_map/pallas_call | solution.py:259
  30.2 0.2 collective-permute-start.10
  30.4 0.0 collective-permute-done.6.refs_4_
  30.4 0.4 collective-permute-start.9
  30.9 0.9 %collective-permute-done.10.refs_3_ = bf16[128,1024]{1,0:T(8,128)(2,1)S(1)} collective-permute-done((bf16[128,1024]{1,0:T(8,128)(2,1)S(1)}, bf16[128,1024]{1,0:T(8,128)(2,1)S(1)}, u32[]{:S(2)}, u32[]{:S(2)}) %collective-permute-start.10) | collective-permute-done | bytes 262176 | tf_op jit(solution)/shard_map/ppermute | solution.py:375
  31.8 0.3 shard_map.117
  32.1 1.1 %collective-permute-start.11 = (bf16[128,512]{1,0:T(8,128)(2,1)S(1)}, bf16[128,512]{1,0:T(8,128)(2,1)S(1)}, u32[]{:S(2)}, u32[]{:S(2)}) collective-permute-start(bf16[128,512]{1,0:T(8,128)(2,1)S(1)} %get-tuple-element.84.refs_7_), channel_id=1, source_target_pairs={{0,16},{8,24},{16,0},{24,8},{1,17},{9,25},{17,1},{25,9},{2,18},{10... | collective-permute-start | bytes 393224 | tf_op jit(solution)/shard_map/ppermute | solution.py:371
  33.1 4.4 %shard_map.118 = (f32[4,8,128]{2,1,0:T(8,128)S(1)}, f32[4,8,1024]{2,1,0:T(8,128)S(1)}, bf16[4,256,1024]{2,1,0:T(8,128)(2,1)S(1)}, bf16[4,256,1024]{2,1,0:T(8,128...) custom-call(bf16[128,8192]{1,0:T(8,128)(2,1)S(1)} %get-tuple-element, ...), custom_call_target="tpu_custom_call" | custom-call | flops 2147483648 | bytes 1 | tf_op jit(solution)/shard_map/pallas_call | solution.py:259
  37.6 0.1 collective-permute-done.11.refs_2_
  37.7 0.1 collective-permute-start.13
  37.8 1.5 %collective-permute-start.12 = (bf16[128,512]{1,0:T(8,128)(2,1)S(1)}, bf16[128,512]{1,0:T(8,128)(2,1)S(1)}, u32[]{:S(2)}, u32[]{:S(2)}) collective-permute-start(bf16[128,512]{1,0:T(8,128)(2,1)S(1)} %shard_map.119.refs_5_), channel_id=1, source_target_pairs={{0,1},{2,3},{4,5},{6,7},{1,0},{3,2},{5,4},{7,6},{8,9},{10,11},{12,... | collective-permute-start | bytes 393224 | tf_op jit(solution)/shard_map/ppermute | solution.py:379
  39.3 0.1 collective-permute-done.13.refs_5_
  39.4 0.1 shard_map.121
  39.5 1.1 %collective-permute-start.15 = (bf16[144,512]{1,0:T(8,128)(2,1)S(1)}, bf16[144,512]{1,0:T(8,128)(2,1)S(1)}, u32[]{:S(2)}, u32[]{:S(2)}) collective-permute-start(bf16[144,512]{1,0:T(8,128)(2,1)S(1)} %get-tuple-element.97.refs_3_), channel_id=1, source_target_pairs={{0,16},{8,24},{16,0},{24,8},{1,17},{9,25},{17,1},{25,9},{2,18},{10... | collective-permute-start | bytes 442376 | tf_op jit(solution)/shard_map/ppermute | solution.py:371
  40.6 0.7 %collective-permute-start.14 = (bf16[128,512]{1,0:T(8,128)(2,1)S(1)}, bf16[128,512]{1,0:T(8,128)(2,1)S(1)}, u32[]{:S(2)}, u32[]{:S(2)}) collective-permute-start(bf16[128,512]{1,0:T(8,128)(2,1)S(1)} %shard_map.122), channel_id=1, source_target_pairs={{1,2},{3,4},{5,6},{2,1},{4,3},{6,5},{9,10},{11,12},{13,14},{10,9},... | collective-permute-start | bytes 393224 | tf_op jit(solution)/shard_map/ppermute | solution.py:379
  41.3 4.2 %collective-permute-done.15.refs_2_.refs_1_ = bf16[144,512]{1,0:T(8,128)(2,1)S(1)} collective-permute-done((bf16[144,512]{1,0:T(8,128)(2,1)S(1)}, bf16[144,512]{1,0:T(8,128)(2,1)S(1)}, u32[]{:S(2)}, u32[]{:S(2)}) %collective-permute-start.15) | collective-permute-done | bytes 147488 | tf_op jit(solution)/shard_map/ppermute | solution.py:371
  45.5 1.5 %collective-permute-start.16 = (bf16[128,512]{1,0:T(8,128)(2,1)S(1)}, bf16[128,512]{1,0:T(8,128)(2,1)S(1)}, u32[]{:S(2)}, u32[]{:S(2)}) collective-permute-start(bf16[128,512]{1,0:T(8,128)(2,1)S(1)} %shard_map.123.refs_5_), channel_id=1, source_target_pairs={{0,1},{2,3},{4,5},{6,7},{1,0},{3,2},{5,4},{7,6},{8,9},{10,11},{12,... | collective-permute-start | bytes 393224 | tf_op jit(solution)/shard_map/ppermute | solution.py:379
  47.0 0.7 %collective-permute-start.17 = (bf16[128,512]{1,0:T(8,128)(2,1)S(1)}, bf16[128,512]{1,0:T(8,128)(2,1)S(1)}, u32[]{:S(2)}, u32[]{:S(2)}) collective-permute-start(bf16[128,512]{1,0:T(8,128)(2,1)S(1)} %shard_map.128), channel_id=1, source_target_pairs={{1,2},{3,4},{5,6},{2,1},{4,3},{6,5},{9,10},{11,12},{13,14},{10,9},... | collective-permute-start | bytes 393224 | tf_op jit(solution)/shard_map/ppermute | solution.py:379
  47.7 0.0 collective-permute-done.12.refs_3_
  47.7 0.0 collective-permute-done.14.refs_4_
  47.7 0.1 shard_map.124
  47.8 1.1 %collective-permute-start.18 = (bf16[128,512]{1,0:T(8,128)(2,1)S(1)}, bf16[128,512]{1,0:T(8,128)(2,1)S(1)}, u32[]{:S(2)}, u32[]{:S(2)}) collective-permute-start(bf16[128,512]{1,0:T(8,128)(2,1)S(1)} %get-tuple-element.99.refs_11_), channel_id=1, source_target_pairs={{0,16},{8,24},{16,0},{24,8},{1,17},{9,25},{17,1},{25,9},{2,18},{10... | collective-permute-start | bytes 393224 | tf_op jit(solution)/shard_map/ppermute | solution.py:371
  48.9 3.7 %shard_map.125 = (bf16[128,8192]{1,0:T(8,128)(2,1)}, bf16[128,8192]{1,0:T(8,128)(2,1)}, f32[128,512]{1,0:T(8,128)S(1)}, f32[128,512]{1,0:T(8,128)S(1)}) custom-call(bf16[128,8192]{1,0:T(8,128)(2,1)S(1)} %get-tuple-element.62.refs_0_, bf16[128,8192]{1,0:T(8,128)(2,1)S(1)} %get-tuple-element.63.refs_1_, f32[384,128]{1,0:T(8,128)S(1)} %get-tuple-element.64.refs_4_.refs_2_, ...), custom_call_target="tpu_custom_call" | custom-call | flops 1342177280 | bytes 1 | tf_op jit(solution)/shard_map/pallas_call | solution.py:337
  52.6 1.0 %collective-permute-done.16.refs_1_ = bf16[128,512]{1,0:T(8,128)(2,1)S(1)} collective-permute-done((bf16[128,512]{1,0:T(8,128)(2,1)S(1)}, bf16[128,512]{1,0:T(8,128)(2,1)S(1)}, u32[]{:S(2)}, u32[]{:S(2)}) %collective-permute-start.16) | collective-permute-done | bytes 131104 | tf_op jit(solution)/shard_map/ppermute | solution.py:379
  53.6 0.1 shard_map.129
  53.6 1.1 %collective-permute-start.19 = (bf16[128,512]{1,0:T(8,128)(2,1)S(1)}, bf16[128,512]{1,0:T(8,128)(2,1)S(1)}, u32[]{:S(2)}, u32[]{:S(2)}) collective-permute-start(bf16[128,512]{1,0:T(8,128)(2,1)S(1)} %get-tuple-element.103.refs_13_), channel_id=1, source_target_pairs={{0,16},{8,24},{16,0},{24,8},{1,17},{9,25},{17,1},{25,9},{2,18},{10... | collective-permute-start | bytes 393224 | tf_op jit(solution)/shard_map/ppermute | solution.py:371
  54.8 3.7 %shard_map.130 = (bf16[128,8192]{1,0:T(8,128)(2,1)}, bf16[128,8192]{1,0:T(8,128)(2,1)}, f32[128,512]{1,0:T(8,128)S(1)}, f32[128,512]{1,0:T(8,128)S(1)}) custom-call(bf16[128,8192]{1,0:T(8,128)(2,1)S(1)} %get-tuple-element.62.refs_0_, bf16[128,8192]{1,0:T(8,128)(2,1)S(1)} %get-tuple-element.63.refs_1_, ...), custom_call_target="tpu_custom_call", output_to_operand_aliasing={{0}: (11, {}), {1}: (12, {})} | custom-call | flops 1342177280 | bytes 1 | tf_op jit(solution)/shard_map/pallas_call | solution.py:337
  58.4 0.3 collective-permute-done.19.refs_11_
  58.7 1.1 %shard_map.131 = (bf16[128,1024]{1,0:T(8,128)(2,1)}, bf16[128,1024]{1,0:T(8,128)(2,1)}, f32[16,512]{1,0:T(8,128)}) custom-call(s32[6]{0:T(128)S(4)} %get-tuple-element.65.refs_0_.flag, f32[2,16,128]{2,1,0:T(8,128)S(1)} %get-tuple-element.105.refs_0_, bf16[144,512]{1,0:T(8,128)(2,1)S(1)} %collective-permute-done.15.refs_2_.refs_1_, ...), custom_call_target="tpu_custom_call" | custom-call | tf_op jit(solution)/shard_map/pallas_call | solution.py:589
  (23 shorter events, 0.4 us)
Async XLA Ops:
  1.6 6.5 %collective-permute-start = (bf16[128,512]{1,0:T(8,128)(2,1)S(1)}, bf16[128,512]{1,0:T(8,128)(2,1)S(1)}, u32[]{:S(2)}, u32[]{:S(2)}) collective-permute-start(bf16[128,512]{1,0:T(8,128)(2,1)S(1)} %shard_map.101.refs_6_), channel_id=1, source_target_pairs={{0,16},{8,24},{16,0},{24,8},{1,17},{9,25},{17,1},{25,9},{2,18},{10... | collective-permute-start | bytes 393224 | tf_op jit(solution)/shard_map/ppermute | solution.py:371
  8.1 5.0 %collective-permute-start.1 = (bf16[128,512]{1,0:T(8,128)(2,1)S(1)}, bf16[128,512]{1,0:T(8,128)(2,1)S(1)}, u32[]{:S(2)}, u32[]{:S(2)}) collective-permute-start(bf16[128,512]{1,0:T(8,128)(2,1)S(1)} %shard_map.103), channel_id=1, source_target_pairs={{0,16},{8,24},{16,0},{24,8},{1,17},{9,25},{17,1},{25,9},{2,18},{10... | collective-permute-start | bytes 393224 | tf_op jit(solution)/shard_map/ppermute | solution.py:371
  9.9 9.0 %collective-permute-start.4 = (bf16[128,512]{1,0:T(8,128)(2,1)S(1)}, bf16[128,512]{1,0:T(8,128)(2,1)S(1)}, u32[]{:S(2)}, u32[]{:S(2)}) collective-permute-start(bf16[128,512]{1,0:T(8,128)(2,1)S(1)} %shard_map.106), channel_id=1, source_target_pairs={{0,1},{2,3},{4,5},{6,7},{1,0},{3,2},{5,4},{7,6},{8,9},{10,11},{12,... | collective-permute-start | bytes 393224 | tf_op jit(solution)/shard_map/ppermute | solution.py:379
  11.5 7.5 %collective-permute-start.5 = (bf16[128,512]{1,0:T(8,128)(2,1)S(1)}, bf16[128,512]{1,0:T(8,128)(2,1)S(1)}, u32[]{:S(2)}, u32[]{:S(2)}) collective-permute-start(bf16[128,512]{1,0:T(8,128)(2,1)S(1)} %shard_map.107), channel_id=1, source_target_pairs={{1,2},{3,4},{5,6},{2,1},{4,3},{6,5},{9,10},{11,12},{13,14},{10,9},... | collective-permute-start | bytes 393224 | tf_op jit(solution)/shard_map/ppermute | solution.py:379
  13.2 8.4 %collective-permute-start.3 = (bf16[128,512]{1,0:T(8,128)(2,1)S(1)}, bf16[128,512]{1,0:T(8,128)(2,1)S(1)}, u32[]{:S(2)}, u32[]{:S(2)}) collective-permute-start(bf16[128,512]{1,0:T(8,128)(2,1)S(1)} %shard_map.105), channel_id=1, source_target_pairs={{1,2},{3,4},{5,6},{2,1},{4,3},{6,5},{9,10},{11,12},{13,14},{10,9},... | collective-permute-start | bytes 393224 | tf_op jit(solution)/shard_map/ppermute | solution.py:379
  13.9 9.0 %collective-permute-start.2 = (bf16[128,512]{1,0:T(8,128)(2,1)S(1)}, bf16[128,512]{1,0:T(8,128)(2,1)S(1)}, u32[]{:S(2)}, u32[]{:S(2)}) collective-permute-start(bf16[128,512]{1,0:T(8,128)(2,1)S(1)} %shard_map.104), channel_id=1, source_target_pairs={{0,1},{2,3},{4,5},{6,7},{1,0},{3,2},{5,4},{7,6},{8,9},{10,11},{12,... | collective-permute-start | bytes 393224 | tf_op jit(solution)/shard_map/ppermute | solution.py:379
  19.0 5.0 %collective-permute-start.7 = (bf16[128,512]{1,0:T(8,128)(2,1)S(1)}, bf16[128,512]{1,0:T(8,128)(2,1)S(1)}, u32[]{:S(2)}, u32[]{:S(2)}) collective-permute-start(bf16[128,512]{1,0:T(8,128)(2,1)S(1)} %get-tuple-element.69.refs_2_.refs_6_.refs_5_), channel_id=1, source_target_pairs={{0,16},{8,24},{16,0},{24,8},{1,17},{9,25},{17,1},{25,9},{2,18},{10... | collective-permute-start | bytes 393224 | tf_op jit(solution)/shard_map/ppermute | solution.py:371
  24.1 1.6 %collective-permute-start.8 = (bf16[128,1024]{1,0:T(8,128)(2,1)S(1)}, bf16[128,1024]{1,0:T(8,128)(2,1)S(1)}, u32[]{:S(2)}, u32[]{:S(2)}) collective-permute-start(bf16[128,1024]{1,0:T(8,128)(2,1)S(1)} %get-tuple-element.75), channel_id=1, source_target_pairs={{0,8},{8,0},{16,24},{24,16},{1,9},{9,1},{17,25},{25,17},{2,10},{10... | collective-permute-start | bytes 786440 | tf_op jit(solution)/shard_map/ppermute | solution.py:375
  24.2 6.2 %collective-permute-start.6 = (bf16[128,512]{1,0:T(8,128)(2,1)S(1)}, bf16[128,512]{1,0:T(8,128)(2,1)S(1)}, u32[]{:S(2)}, u32[]{:S(2)}) collective-permute-start(bf16[128,512]{1,0:T(8,128)(2,1)S(1)} %get-tuple-element.71.refs_5_), channel_id=1, source_target_pairs={{0,16},{8,24},{16,0},{24,8},{1,17},{9,25},{17,1},{25,9},{2,18},{10... | collective-permute-start | bytes 393224 | tf_op jit(solution)/shard_map/ppermute | solution.py:371
  30.2 1.6 %collective-permute-start.10 = (bf16[128,1024]{1,0:T(8,128)(2,1)S(1)}, bf16[128,1024]{1,0:T(8,128)(2,1)S(1)}, u32[]{:S(2)}, u32[]{:S(2)}) collective-permute-start(bf16[128,1024]{1,0:T(8,128)(2,1)S(1)} %shard_map.116), channel_id=1, source_target_pairs={{0,8},{8,0},{16,24},{24,16},{1,9},{9,1},{17,25},{25,17},{2,10},{10... | collective-permute-start | bytes 786440 | tf_op jit(solution)/shard_map/ppermute | solution.py:375
  30.4 2.7 %collective-permute-start.9 = (bf16[128,1024]{1,0:T(8,128)(2,1)S(1)}, bf16[128,1024]{1,0:T(8,128)(2,1)S(1)}, u32[]{:S(2)}, u32[]{:S(2)}) collective-permute-start(bf16[128,1024]{1,0:T(8,128)(2,1)S(1)} %get-tuple-element.79), channel_id=1, source_target_pairs={{0,8},{8,0},{16,24},{24,16},{1,9},{9,1},{17,25},{25,17},{2,10},{10... | collective-permute-start | bytes 786440 | tf_op jit(solution)/shard_map/ppermute | solution.py:375
  32.1 5.6 %collective-permute-start.11 = (bf16[128,512]{1,0:T(8,128)(2,1)S(1)}, bf16[128,512]{1,0:T(8,128)(2,1)S(1)}, u32[]{:S(2)}, u32[]{:S(2)}) collective-permute-start(bf16[128,512]{1,0:T(8,128)(2,1)S(1)} %get-tuple-element.84.refs_7_), channel_id=1, source_target_pairs={{0,16},{8,24},{16,0},{24,8},{1,17},{9,25},{17,1},{25,9},{2,18},{10... | collective-permute-start | bytes 393224 | tf_op jit(solution)/shard_map/ppermute | solution.py:371
  37.7 1.6 %collective-permute-start.13 = (bf16[144,1024]{1,0:T(8,128)(2,1)S(1)}, bf16[144,1024]{1,0:T(8,128)(2,1)S(1)}, u32[]{:S(2)}, u32[]{:S(2)}) collective-permute-start(bf16[144,1024]{1,0:T(8,128)(2,1)S(1)} %shard_map.120), channel_id=1, source_target_pairs={{0,8},{8,0},{16,24},{24,16},{1,9},{9,1},{17,25},{25,17},{2,10},{10... | collective-permute-start | bytes 884744 | tf_op jit(solution)/shard_map/ppermute | solution.py:375
  37.8 9.9 %collective-permute-start.12 = (bf16[128,512]{1,0:T(8,128)(2,1)S(1)}, bf16[128,512]{1,0:T(8,128)(2,1)S(1)}, u32[]{:S(2)}, u32[]{:S(2)}) collective-permute-start(bf16[128,512]{1,0:T(8,128)(2,1)S(1)} %shard_map.119.refs_5_), channel_id=1, source_target_pairs={{0,1},{2,3},{4,5},{6,7},{1,0},{3,2},{5,4},{7,6},{8,9},{10,11},{12,... | collective-permute-start | bytes 393224 | tf_op jit(solution)/shard_map/ppermute | solution.py:379
  39.5 6.0 %collective-permute-start.15 = (bf16[144,512]{1,0:T(8,128)(2,1)S(1)}, bf16[144,512]{1,0:T(8,128)(2,1)S(1)}, u32[]{:S(2)}, u32[]{:S(2)}) collective-permute-start(bf16[144,512]{1,0:T(8,128)(2,1)S(1)} %get-tuple-element.97.refs_3_), channel_id=1, source_target_pairs={{0,16},{8,24},{16,0},{24,8},{1,17},{9,25},{17,1},{25,9},{2,18},{10... | collective-permute-start | bytes 442376 | tf_op jit(solution)/shard_map/ppermute | solution.py:371
  40.6 7.1 %collective-permute-start.14 = (bf16[128,512]{1,0:T(8,128)(2,1)S(1)}, bf16[128,512]{1,0:T(8,128)(2,1)S(1)}, u32[]{:S(2)}, u32[]{:S(2)}) collective-permute-start(bf16[128,512]{1,0:T(8,128)(2,1)S(1)} %shard_map.122), channel_id=1, source_target_pairs={{1,2},{3,4},{5,6},{2,1},{4,3},{6,5},{9,10},{11,12},{13,14},{10,9},... | collective-permute-start | bytes 393224 | tf_op jit(solution)/shard_map/ppermute | solution.py:379
  45.5 8.0 %collective-permute-start.16 = (bf16[128,512]{1,0:T(8,128)(2,1)S(1)}, bf16[128,512]{1,0:T(8,128)(2,1)S(1)}, u32[]{:S(2)}, u32[]{:S(2)}) collective-permute-start(bf16[128,512]{1,0:T(8,128)(2,1)S(1)} %shard_map.123.refs_5_), channel_id=1, source_target_pairs={{0,1},{2,3},{4,5},{6,7},{1,0},{3,2},{5,4},{7,6},{8,9},{10,11},{12,... | collective-permute-start | bytes 393224 | tf_op jit(solution)/shard_map/ppermute | solution.py:379
  47.0 6.5 %collective-permute-start.17 = (bf16[128,512]{1,0:T(8,128)(2,1)S(1)}, bf16[128,512]{1,0:T(8,128)(2,1)S(1)}, u32[]{:S(2)}, u32[]{:S(2)}) collective-permute-start(bf16[128,512]{1,0:T(8,128)(2,1)S(1)} %shard_map.128), channel_id=1, source_target_pairs={{1,2},{3,4},{5,6},{2,1},{4,3},{6,5},{9,10},{11,12},{13,14},{10,9},... | collective-permute-start | bytes 393224 | tf_op jit(solution)/shard_map/ppermute | solution.py:379
  47.8 10.6 %collective-permute-start.18 = (bf16[128,512]{1,0:T(8,128)(2,1)S(1)}, bf16[128,512]{1,0:T(8,128)(2,1)S(1)}, u32[]{:S(2)}, u32[]{:S(2)}) collective-permute-start(bf16[128,512]{1,0:T(8,128)(2,1)S(1)} %get-tuple-element.99.refs_11_), channel_id=1, source_target_pairs={{0,16},{8,24},{16,0},{24,8},{1,17},{9,25},{17,1},{25,9},{2,18},{10... | collective-permute-start | bytes 393224 | tf_op jit(solution)/shard_map/ppermute | solution.py:371
  53.6 5.0 %collective-permute-start.19 = (bf16[128,512]{1,0:T(8,128)(2,1)S(1)}, bf16[128,512]{1,0:T(8,128)(2,1)S(1)}, u32[]{:S(2)}, u32[]{:S(2)}) collective-permute-start(bf16[128,512]{1,0:T(8,128)(2,1)S(1)} %get-tuple-element.103.refs_13_), channel_id=1, source_target_pairs={{0,16},{8,24},{16,0},{24,8},{1,17},{9,25},{17,1},{25,9},{2,18},{10... | collective-permute-start | bytes 393224 | tf_op jit(solution)/shard_map/ppermute | solution.py:371
